TPU v7x, 32 devices: a whole 2x2x4 slice. The times are simulated.
32 devices in a mesh: groups: 2 (over y), dp: 16 (over z, x, core).
Axes of the slice: x: 2, y: 2, z: 4, core: 2. Of those that a mesh axis runs over, the one named last changes fastest.
Arguments:
- node_feats: bfloat16 [4096, 3712], P(('groups', 'dp')), parts along dimension 0, may hold values from -6 to 6
- node_grad: bfloat16 [4096, 3712], P(('groups', 'dp')), parts along dimension 0, may hold values from -6 to 6
- flat_params: bfloat16 [21888, 128], P('dp'), may hold values from -0.21875 to 0.21875
- rot_table: bfloat16 [64, 29, 29], replicated, may hold values from -0.41 to 1.41
- edge_src: int32 [4096], P(('groups', 'dp')), parts along dimension 0, may hold values from 0 to 127
- edge_dst: int32 [4096], P(('groups', 'dp')), parts along dimension 0, may hold values from 0 to 127
- edge_rot: int32 [4096], P(('groups', 'dp')), parts along dimension 0, may hold values from 0 to 63
- edge_owner: int32 [4096, 1], P(('groups', 'dp')), parts along dimension 0, may hold values from 0 to 15, as said below
Outputs:
- node_out: bfloat16 [4096, 3712], P(('groups', 'dp')), parts along dimension 0
- weight_grad: float32 [43776, 128], P(('groups', 'dp')), parts along dimension 0
There are 2 independent parts, one for each index of `groups`. A program takes and returns all parts, laid end to end along the dimension named above; an argument that names none is the same for every part. Nothing has to cross between parts.
Inputs may be any that keep to these rules, and one draw needn't show every extreme that they name: `edge_owner`: dp indices form aligned runs of 8; an edge's owner lies in the run of the edge's own device, at most two indices away from it; exactly half of each device's 128 edges are owned by the device itself, and no other owner is named by more than 32 of them.
All inputs are finite; a program needn't handle non-finite values.
Results may differ from a plain program's by a relative error of at most 0.0058.
Values may be sent and summed in bfloat16 or wider, within the bound.
No kernel may reach another device: no remote copies, remote signals or barrier semaphores. Data moves between devices by JAX's collectives and lax.ppermute only.
A program may use at most 128 MiB of HBM per device.

v0:
```python
import math

import jax
import jax.numpy as jnp
from jax import lax
from jax.sharding import PartitionSpec as P

K = 29


def from_behind(block, axis, distance):
    devices = range(lax.axis_size(axis))
    route = [(i - distance, i) for i in devices if i - distance in devices]
    return lax.ppermute(block, axis, route)


def unpack(flat_vector, channels):
    first_size = 49 * channels * channels
    second_size = 36 * channels * channels
    third_size = 25 * channels * channels
    offset = 0
    first = flat_vector[offset : offset + first_size].reshape(7 * channels, 7 * channels)
    offset = offset + first_size
    one_real = flat_vector[offset : offset + second_size].reshape(6 * channels, 6 * channels)
    offset = offset + second_size
    one_imag = flat_vector[offset : offset + second_size].reshape(6 * channels, 6 * channels)
    offset = offset + second_size
    two_real = flat_vector[offset : offset + third_size].reshape(5 * channels, 5 * channels)
    offset = offset + third_size
    two_imag = flat_vector[offset : offset + third_size].reshape(5 * channels, 5 * channels)
    return (first, one_real, one_imag, two_real, two_imag)


def blocks_of(rows, channels):
    edges_at = [0, 7, 13, 19, 24, 29]
    return [rows[:, edges_at[i] * channels : edges_at[i + 1] * channels] for i in range(5)]


def multiply(left, right):
    return jnp.dot(left, right, preferred_element_type=jnp.float32)


def convolve(rotated, weights, channels):
    first, one_real, one_imag, two_real, two_imag = weights
    zero_part, real_one, imag_one, real_two, imag_two = blocks_of(rotated, channels)
    out_zero = multiply(zero_part, first)
    out_real1 = multiply(real_one, one_real) - multiply(imag_one, one_imag)
    out_imag1 = multiply(real_one, one_imag) + multiply(imag_one, one_real)
    out_real2 = multiply(real_two, two_real) - multiply(imag_two, two_imag)
    out_imag2 = multiply(real_two, two_imag) + multiply(imag_two, two_real)
    joined = jnp.concatenate([out_zero, out_real1, out_imag1, out_real2, out_imag2], axis=1)
    return joined.astype(jnp.bfloat16)


def outer_sum(left, right):
    return lax.dot_general(
        left, right, (((0,), (0,)), ((), ())), preferred_element_type=jnp.float32
    )


def weight_terms(rotated, upstream, channels):
    zero_part, real_one, imag_one, real_two, imag_two = blocks_of(rotated, channels)
    up_zero, up_real1, up_imag1, up_real2, up_imag2 = blocks_of(upstream, channels)
    grad_first = outer_sum(zero_part, up_zero)
    grad_real1 = outer_sum(real_one, up_real1) + outer_sum(imag_one, up_imag1)
    grad_imag1 = outer_sum(real_one, up_imag1) - outer_sum(imag_one, up_real1)
    grad_real2 = outer_sum(real_two, up_real2) + outer_sum(imag_two, up_imag2)
    grad_imag2 = outer_sum(real_two, up_imag2) - outer_sum(imag_two, up_real2)
    return jnp.concatenate(
        [
            grad_first.reshape(-1),
            grad_real1.reshape(-1),
            grad_imag1.reshape(-1),
            grad_real2.reshape(-1),
            grad_imag2.reshape(-1),
        ]
    )


def deliver(message, target_ids, turn_ids, node_grad, rot_table, channels):
    slot_count = message.shape[0]
    flat_width = message.shape[1]
    matrices = rot_table[turn_ids]
    spread = jnp.einsum(
        "sjk,sjc->skc",
        matrices,
        message.reshape(slot_count, K, channels),
        preferred_element_type=jnp.float32,
    )
    totals = (
        jnp.zeros((node_grad.shape[0] + 1, flat_width), jnp.float32)
        .at[target_ids]
        .add(spread.reshape(slot_count, flat_width))
    )
    node_out = totals[1:].astype(jnp.bfloat16)
    padded_grad = jnp.concatenate([jnp.zeros((1, flat_width), jnp.bfloat16), node_grad], axis=0)
    incoming = padded_grad[target_ids].reshape(slot_count, K, channels)
    upstream = jnp.einsum("skj,sjc->skc", matrices, incoming, preferred_element_type=jnp.float32)
    return (node_out, upstream.astype(jnp.bfloat16).reshape(slot_count, flat_width))


def on_device(
    node_feats, node_grad, flat_params, rot_table, edge_src, edge_dst, edge_rot, edge_owner
):
    devices_dp = lax.axis_size("dp")
    edges_here = edge_src.shape[0]
    flat_width = node_feats.shape[1]
    channels = flat_width // K
    local_slots = edges_here // 2
    capacity = edges_here // 4
    total_slots = local_slots + 4 * capacity
    neighbor_steps = [-2, -1, 1, 2]
    weights_all = lax.all_gather(flat_params, "dp", axis=0, tiled=True)
    weights = unpack(weights_all.reshape(-1), channels)
    offsets_seen = edge_owner[:, 0] - lax.axis_index("dp")
    reach = jnp.array([0, -2, -1, 1, 2], jnp.int32)
    onehot = (offsets_seen[:, None] == reach[None, :]).astype(jnp.int32)
    starts = jnp.array(
        [
            0,
            local_slots,
            local_slots + capacity,
            local_slots + 2 * capacity,
            local_slots + 3 * capacity,
        ],
        jnp.int32,
    )
    slot_index = jnp.sum((jnp.cumsum(onehot, axis=0) - 1 + starts[None, :]) * onehot, axis=1)
    matrices = rot_table[edge_rot]
    sources = node_feats[edge_src].reshape(edges_here, K, channels)
    rotated = jnp.einsum("ekj,ejc->ekc", matrices, sources, preferred_element_type=jnp.float32)
    rotated = rotated.astype(jnp.bfloat16).reshape(edges_here, flat_width)
    target_ids = jnp.zeros((total_slots,), jnp.int32).at[slot_index].set(edge_dst + 1)
    turn_ids = jnp.zeros((total_slots,), jnp.int32).at[slot_index].set(edge_rot)
    message = convolve(rotated, weights, channels)
    outbound = jnp.zeros((total_slots, flat_width), jnp.bfloat16).at[slot_index].set(message)
    rows_in = [outbound[:local_slots]]
    targets_in = [target_ids[:local_slots]]
    turns_in = [turn_ids[:local_slots]]
    for which, step in enumerate(neighbor_steps):
        lower = local_slots + which * capacity
        got_rows, got_targets, got_turns = from_behind(
            (
                outbound[lower : lower + capacity],
                target_ids[lower : lower + capacity],
                turn_ids[lower : lower + capacity],
            ),
            "dp",
            step,
        )
        rows_in.append(got_rows)
        targets_in.append(got_targets)
        turns_in.append(got_turns)
    node_out, upstream = deliver(
        jnp.concatenate(rows_in, axis=0),
        jnp.concatenate(targets_in),
        jnp.concatenate(turns_in),
        node_grad,
        rot_table,
        channels,
    )
    back_rows = [upstream[:local_slots]]
    for which, step in enumerate(neighbor_steps):
        lower = local_slots + which * capacity
        back_rows.append(from_behind(upstream[lower : lower + capacity], "dp", -step))
    edge_upstream = jnp.concatenate(back_rows, axis=0)[slot_index]
    grad_sum = weight_terms(rotated, edge_upstream, channels)
    scaled = grad_sum * (1.0 / math.sqrt(edges_here * devices_dp))
    rows_all = flat_params.shape[0] * devices_dp
    padded = jnp.concatenate(
        [scaled, jnp.zeros((rows_all * 128 - scaled.shape[0],), jnp.float32)]
    ).reshape(rows_all, 128)
    weight_grad = lax.psum_scatter(padded, "dp", scatter_dimension=0, tiled=True)
    return (node_out, weight_grad)


def solution(mesh):
    placed = (
        P(("groups", "dp"), None),
        P(("groups", "dp"), None),
        P("dp", None),
        P(),
        P(("groups", "dp")),
        P(("groups", "dp")),
        P(("groups", "dp")),
        P(("groups", "dp"), None),
    )
    return jax.shard_map(
        on_device,
        mesh=mesh,
        in_specs=placed,
        out_specs=(P(("groups", "dp"), None), P(("groups", "dp"), None)),
        check_vma=False,
    )
```

profile of v0, /device:TPU:0, one launch (start us, length us, event | category | flops | bytes accessed | tf_op | source)
XLA Modules:
  0.0 281.9 jit_solution(790651230285757049)
XLA Ops:
  11.5 1.3 collective-permute-start
  12.7 1.3 collective-permute-start.1
  14.0 3.0 %collective-permute-start.2 = (s32[32]{0:T(128)S(1)}, s32[32]{0:T(128)S(1)}, u32[]{:S(2)}, u32[]{:S(2)}) collective-permute-start(s32[32]{0:T(128)S(1)} %get-tuple-element.19), channel_id=1, source_target_pairs={{0,1},{1,2},{2,3},{3,4},{4,5},{5,6},{6,7},{7,8},{8,9},{9,10},{10,1... | collective-permute-start | bytes 392 | tf_op jit(solution)/shard_map/ppermute | solution.py:14
  17.1 5.5 %collective-permute-start.3 = (s32[32]{0:T(128)S(1)}, s32[32]{0:T(128)S(1)}, u32[]{:S(2)}, u32[]{:S(2)}) collective-permute-start(s32[32]{0:T(128)S(1)} %get-tuple-element.18), channel_id=1, source_target_pairs={{0,2},{1,3},{2,4},{3,5},{4,6},{5,7},{6,8},{7,9},{8,10},{9,11},{10,... | collective-permute-start | bytes 392 | tf_op jit(solution)/shard_map/ppermute | solution.py:14
  23.8 1.4 collective-permute-start.4
  25.9 1.8 copy.21
  28.5 1.8 gather_fusion.1
  30.5 1.3 collective-permute-start.5
  31.8 4.8 %collective-permute-start.6 = (s32[32]{0:T(128)S(1)}, s32[32]{0:T(128)S(1)}, u32[]{:S(2)}, u32[]{:S(2)}) collective-permute-start(s32[32]{0:T(128)S(1)} %get-tuple-element.15), channel_id=1, source_target_pairs={{0,1},{1,2},{2,3},{3,4},{4,5},{5,6},{6,7},{7,8},{8,9},{9,10},{10,1... | collective-permute-start | bytes 392 | tf_op jit(solution)/shard_map/ppermute | solution.py:14
  36.6 4.3 %collective-permute-start.7 = (s32[32]{0:T(128)S(1)}, s32[32]{0:T(128)S(1)}, u32[]{:S(2)}, u32[]{:S(2)}) collective-permute-start(s32[32]{0:T(128)S(1)} %get-tuple-element.14), channel_id=1, source_target_pairs={{0,2},{1,3},{2,4},{3,5},{4,6},{5,7},{6,8},{7,9},{8,10},{9,11},{10,... | collective-permute-start | bytes 392 | tf_op jit(solution)/shard_map/ppermute | solution.py:14
  42.2 2.0 gather_fusion
  44.3 2.6 gather_fusion.3
  46.9 3.7 %reshape.482 = bf16[192,29,128]{2,1,0:T(8,128)(2,1)} reshape(bf16[192,3712]{1,0:T(8,128)(2,1)} %gather_fusion.3) | data formatting | bytes 2850816 | tf_op jit(solution)/shard_map/reshape | solution.py:97
  50.5 2.0 convolution_convert_fusion
  54.0 1.2 gather_fusion.2
  55.2 1.2 copy.23
  56.4 1.9 copy.24
  59.4 5.1 %collective-permute-start.12 = (bf16[32,3712]{1,0:T(8,128)(2,1)}, bf16[32,3712]{1,0:T(8,128)(2,1)}, u32[]{:S(2)}, u32[]{:S(2)}) collective-permute-start(bf16[32,3712]{1,0:T(8,128)(2,1)} %bitcast.62), channel_id=1, source_target_pairs={{0,2},{1,3},{2,4},{3,5},{4,6},{5,7},{6,8},{7,9},{8,10},{9,11},{10,... | collective-permute-start | bytes 712712 | tf_op jit(solution)/shard_map/ppermute | solution.py:14
  64.5 1.5 convolution_convert_fusion.1
  66.0 2.2 copy.25
  68.4 2.9 %collective-permute-start.13 = (bf16[32,3712]{1,0:T(8,128)(2,1)S(1)}, bf16[32,3712]{1,0:T(8,128)(2,1)S(1)}, u32[]{:S(2)}, u32[]{:S(2)}) collective-permute-start(bf16[32,3712]{1,0:T(8,128)(2,1)S(1)} %bitcast.90), channel_id=1, source_target_pairs={{0,1},{1,2},{2,3},{3,4},{4,5},{5,6},{6,7},{7,8},{8,9},{9,10},{10,1... | collective-permute-start | bytes 712712 | tf_op jit(solution)/shard_map/ppermute | solution.py:14
  71.5 1.3 collective-permute-start.14
  72.9 1.3 collective-permute-start.15
  76.3 9.5 %collective-permute-done.15 = bf16[32,3712]{1,0:T(8,128)(2,1)S(1)} collective-permute-done((bf16[32,3712]{1,0:T(8,128)(2,1)S(1)}, bf16[32,3712]{1,0:T(8,128)(2,1)S(1)}, u32[]{:S(2)}, u32[]{:S(2)}) %collective-permute-start.15) | collective-permute-done | bytes 237600 | tf_op jit(solution)/shard_map/ppermute | solution.py:14
  85.8 1.2 gather_fusion.4
  87.0 2.3 fusion.15
  89.2 1.8 fusion.20
  91.1 2.0 fusion.22
  93.1 1.5 fusion.26
  94.6 1.6 fusion.28
  96.2 4.4 %reshape.483 = f32[802816]{0:T(1024)} reshape(f32[896,896]{1,0:T(8,128)} %fusion.15) | data formatting | bytes 6422528 | tf_op jit(solution)/shard_map/reshape | solution.py:71
  100.7 4.0 %constant_dynamic-update-slice_fusion.8 = f32[2801664]{0:T(1024)} fusion(f32[802816]{0:T(1024)} %reshape.483), kind=kLoop, calls=%fused_computation.90 | loop fusion | bytes 6422528
  104.6 1.4 convolution_add_fusion
  106.0 1.5 reshape.484
  107.5 2.2 convolution_subtract_fusion
  109.8 1.6 reshape.485
  111.3 1.9 convolution_add_fusion.1
  113.2 1.3 reshape.486
  114.5 3.1 %convolution_subtract_fusion.1 = f32[640,640]{1,0:T(8,128)} fusion(f32[640,640]{1,0:T(8,128)} %fusion.28, bf16[128,3712]{1,0:T(8,128)(2,1)} %copy-done.9, bf16[128,3712]{0,1:T(8,128)(2,1)S(1)} %bitcast.71), kind=kOutput, calls=%fused_computation.17 | convolution fusion | flops 105267200 | bytes 3604480 | tf_op jit(solution)/shard_map/dot_general | solution.py:56
  117.7 2.6 reshape.487
  120.3 1.6 constant_dynamic-update-slice_fusion.12
  122.8 1.6 constant_dynamic-update-slice_fusion.11
  125.1 1.3 constant_dynamic-update-slice_fusion.10
  127.1 1.4 constant_dynamic-update-slice_fusion.9
  128.5 9.4 %multiply_bitcast_fusion = f32[21888,128]{1,0:T(8,128)} fusion(f32[2801664]{0:T(1024)} %constant_dynamic-update-slice_fusion.9), kind=kLoop, calls=%fused_computation.9 | loop fusion | flops 2801664 | bytes 22413312 | tf_op jit(solution)/shard_map/mul | solution.py:168
  138.0 1.4 slice-done
  139.4 2.5 reshape.475
  141.9 2.8 fusion.58
  145.8 2.6 reshape.477
  148.4 2.6 fusion.57
  151.0 2.4 reshape.478
  153.4 2.4 reshape.479
  155.8 1.6 fusion.49
  164.7 3.1 %scatter_custom_fusion.2 = bf16[192,3712]{1,0:T(8,128)(2,1)S(1)} fusion(s32[128]{0:T(128)S(1)} %fusion.52, bf16[128,3712]{1,0:T(8,128)(2,1)} %fusion.11, bf16[]{:T(256)} %constant.9.clone.1), kind=kCustom, calls=%fused_computation.35 | custom fusion | bytes 1425920 | tf_op jit(solution)/shard_map/scatter | solution.py:136
  167.9 1.3 collective-permute-start.8
  170.0 1.3 collective-permute-start.9
  171.3 5.1 %collective-permute-start.10 = (bf16[32,3712]{1,0:T(8,128)(2,1)S(1)}, bf16[32,3712]{1,0:T(8,128)(2,1)S(1)}, u32[]{:S(2)}, u32[]{:S(2)}) collective-permute-start(bf16[32,3712]{1,0:T(8,128)(2,1)S(1)} %get-tuple-element.11), channel_id=1, source_target_pairs={{0,1},{1,2},{2,3},{3,4},{4,5},{5,6},{6,7},{7,8},{8,9},{9,10},{10,1... | collective-permute-start | bytes 712712 | tf_op jit(solution)/shard_map/ppermute | solution.py:14
  176.3 5.7 %collective-permute-start.11 = (bf16[32,3712]{1,0:T(8,128)(2,1)S(1)}, bf16[32,3712]{1,0:T(8,128)(2,1)S(1)}, u32[]{:S(2)}, u32[]{:S(2)}) collective-permute-start(bf16[32,3712]{1,0:T(8,128)(2,1)S(1)} %get-tuple-element.10), channel_id=1, source_target_pairs={{0,2},{1,3},{2,4},{3,5},{4,6},{5,7},{6,8},{7,9},{8,10},{9,11},{10,... | collective-permute-start | bytes 712712 | tf_op jit(solution)/shard_map/ppermute | solution.py:14
  182.0 1.5 collective-permute-done.8
  185.7 8.9 %collective-permute-done.11 = bf16[32,3712]{1,0:T(8,128)(2,1)S(1)} collective-permute-done((bf16[32,3712]{1,0:T(8,128)(2,1)S(1)}, bf16[32,3712]{1,0:T(8,128)(2,1)S(1)}, u32[]{:S(2)}, u32[]{:S(2)}) %collective-permute-start.11) | collective-permute-done | bytes 237600 | tf_op jit(solution)/shard_map/ppermute | solution.py:14
  195.4 3.7 %reshape.480 = bf16[192,29,128]{2,1,0:T(8,128)(2,1)} reshape(bf16[192,3712]{1,0:T(8,128)(2,1)} %constant_dynamic-update-slice_fusion) | data formatting | bytes 2850816 | tf_op jit(solution)/shard_map/reshape | solution.py:87
  199.0 3.8 %fusion.63 = f32[192,29,128]{2,1,0:T(8,128)} fusion(bf16[192,29,29]{2,1,0:T(8,128)(2,1)S(1)} %copy-done.3, bf16[192,29,128]{2,1,0:T(8,128)(2,1)} %reshape.480), kind=kOutput, calls=%fused_computation.120 | convolution fusion | flops 41336832 | bytes 4599168 | tf_op jit(solution)/shard_map/sjk,sjc->skc/dot_general | solution.py:84
  202.9 7.8 %scatter_custom_fusion.3 = f32[129,3712]{1,0:T(8,128)S(1)} fusion(s32[192]{0:T(256)S(1)} %bitcast.92, f32[24,8,29,128]{3,2,1,0:T(8,128)} %bitcast.81, f32[]{:T(128)} %constant.13.clone.1), kind=kCustom, calls=%fused_computation.10 | custom fusion | flops 712704 | bytes 4766212 | tf_op jit(solution)/shard_map/scatter-add | solution.py:93
  211.7 63.3 %reduce-scatter.4.cloned.1.call-done = f32[1368,128]{1,0:T(8,128)} async-done(((f32[21888,128]{1,0:T(8,128)}), f32[1368,128]{1,0:T(8,128)}) %reduce-scatter.4.cloned.1.call-update) | async-done | bytes 700432
  (112 shorter events, 28.8 us)
Async XLA Ops:
  7.2 46.8 %copy-start = (bf16[128,3712]{1,0:T(8,128)(2,1)S(1)}, bf16[128,3712]{1,0:T(8,128)(2,1)}, u32[]{:S(2)}) copy-start(bf16[128,3712]{1,0:T(8,128)(2,1)} %param.10) | copy-start | bytes 2850820
  7.2 130.8 %all-gather.2.cloned.1.call-start = ((), (), s32[]{:S(2)}) async-start(), calls=%async_computation.1 | async-start | bytes 5953536 | tf_op jit(solution)/shard_map/all_gather | solution.py:113
  11.5 19.0 %collective-permute-start = (s32[32]{0:T(128)S(1)}, s32[32]{0:T(128)S(1)}, u32[]{:S(2)}, u32[]{:S(2)}) collective-permute-start(s32[32]{0:T(128)S(1)} %get-tuple-element.21), channel_id=1, source_target_pairs={{2,0},{3,1},{4,2},{5,3},{6,4},{7,5},{8,6},{9,7},{10,8},{11,9},{12,... | collective-permute-start | bytes 392 | tf_op jit(solution)/shard_map/ppermute | solution.py:14
  12.7 19.0 %collective-permute-start.1 = (s32[32]{0:T(128)S(1)}, s32[32]{0:T(128)S(1)}, u32[]{:S(2)}, u32[]{:S(2)}) collective-permute-start(s32[32]{0:T(128)S(1)} %get-tuple-element.20), channel_id=1, source_target_pairs={{1,0},{2,1},{3,2},{4,3},{5,4},{6,5},{7,6},{8,7},{9,8},{10,9},{11,1... | collective-permute-start | bytes 392 | tf_op jit(solution)/shard_map/ppermute | solution.py:14
  14.0 22.5 %collective-permute-start.2 = (s32[32]{0:T(128)S(1)}, s32[32]{0:T(128)S(1)}, u32[]{:S(2)}, u32[]{:S(2)}) collective-permute-start(s32[32]{0:T(128)S(1)} %get-tuple-element.19), channel_id=1, source_target_pairs={{0,1},{1,2},{2,3},{3,4},{4,5},{5,6},{6,7},{7,8},{8,9},{9,10},{10,1... | collective-permute-start | bytes 392 | tf_op jit(solution)/shard_map/ppermute | solution.py:14
  17.1 23.8 %collective-permute-start.3 = (s32[32]{0:T(128)S(1)}, s32[32]{0:T(128)S(1)}, u32[]{:S(2)}, u32[]{:S(2)}) collective-permute-start(s32[32]{0:T(128)S(1)} %get-tuple-element.18), channel_id=1, source_target_pairs={{0,2},{1,3},{2,4},{3,5},{4,6},{5,7},{6,8},{7,9},{8,10},{9,11},{10,... | collective-permute-start | bytes 392 | tf_op jit(solution)/shard_map/ppermute | solution.py:14
  23.8 6.5 %copy-start.20 = (bf16[128,3712]{1,0:T(8,128)(2,1)S(1)}, bf16[128,3712]{1,0:T(8,128)(2,1)}, u32[]{:S(2)}) copy-start(bf16[128,3712]{1,0:T(8,128)(2,1)} %param.11) | copy-start | bytes 2850820
  23.8 17.2 %collective-permute-start.4 = (s32[32]{0:T(128)S(1)}, s32[32]{0:T(128)S(1)}, u32[]{:S(2)}, u32[]{:S(2)}) collective-permute-start(s32[32]{0:T(128)S(1)} %get-tuple-element.17), channel_id=1, source_target_pairs={{2,0},{3,1},{4,2},{5,3},{6,4},{7,5},{8,6},{9,7},{10,8},{11,9},{12,... | collective-permute-start | bytes 392 | tf_op jit(solution)/shard_map/ppermute | solution.py:14
  25.2 249.8 %reduce-scatter.4.cloned.1.call-start = ((), (), s32[]{:S(2)}) async-start(), calls=%async_computation.2 | async-start | bytes 11907072
  30.5 10.5 %collective-permute-start.5 = (s32[32]{0:T(128)S(1)}, s32[32]{0:T(128)S(1)}, u32[]{:S(2)}, u32[]{:S(2)}) collective-permute-start(s32[32]{0:T(128)S(1)} %get-tuple-element.16), channel_id=1, source_target_pairs={{1,0},{2,1},{3,2},{4,3},{5,4},{6,5},{7,6},{8,7},{9,8},{10,9},{11,1... | collective-permute-start | bytes 392 | tf_op jit(solution)/shard_map/ppermute | solution.py:14
  31.8 9.2 %collective-permute-start.6 = (s32[32]{0:T(128)S(1)}, s32[32]{0:T(128)S(1)}, u32[]{:S(2)}, u32[]{:S(2)}) collective-permute-start(s32[32]{0:T(128)S(1)} %get-tuple-element.15), channel_id=1, source_target_pairs={{0,1},{1,2},{2,3},{3,4},{4,5},{5,6},{6,7},{7,8},{8,9},{9,10},{10,1... | collective-permute-start | bytes 392 | tf_op jit(solution)/shard_map/ppermute | solution.py:14
  36.6 5.6 %collective-permute-start.7 = (s32[32]{0:T(128)S(1)}, s32[32]{0:T(128)S(1)}, u32[]{:S(2)}, u32[]{:S(2)}) collective-permute-start(s32[32]{0:T(128)S(1)} %get-tuple-element.14), channel_id=1, source_target_pairs={{0,2},{1,3},{2,4},{3,5},{4,6},{5,7},{6,8},{7,9},{8,10},{9,11},{10,... | collective-permute-start | bytes 392 | tf_op jit(solution)/shard_map/ppermute | solution.py:14
  46.9 3.7 %copy-start.2 = (bf16[192,29,29]{2,1,0:T(8,128)(2,1)S(1)}, bf16[192,29,29]{2,1,0:T(8,128)(2,1)}, u32[]{:S(2)}) copy-start(bf16[192,29,29]{2,1,0:T(8,128)(2,1)} %gather_fusion) | copy-start | bytes 968836
  52.5 1.5 copy-start.13
  55.2 3.2 %slice-start.1 = ((bf16[192,29,128]{2,1,0:T(8,128)(2,1)}), bf16[64,29,128]{2,1,0:T(8,128)(2,1)S(1)}, s32[]{:S(2)}) async-start(bf16[192,29,128]{2,1,0:T(8,128)(2,1)} %copy-done.13), calls=%async_computation.4 | async-start | bytes 1048576 | tf_op jit(solution)/shard_map/slice | solution.py:162
  56.4 2.1 copy-start.19
  56.4 8.1 %copy-start.14 = (bf16[128,29,29]{2,1,0:T(8,128)(2,1)S(1)}, bf16[128,29,29]{2,1,0:T(8,128)(2,1)}, u32[]{:S(2)}) copy-start(bf16[128,29,29]{2,1,0:T(8,128)(2,1)} %gather_fusion.1) | copy-start | bytes 645892
  58.4 6.1 %copy-start.15 = (bf16[128,29,128]{2,1,0:T(8,128)(2,1)S(1)}, bf16[128,29,128]{2,1,0:T(8,128)(2,1)}, u32[]{:S(2)}) copy-start(bf16[128,29,128]{2,1,0:T(8,128)(2,1)} %copy.24) | copy-start | bytes 2850820
  59.4 15.8 %collective-permute-start.12 = (bf16[32,3712]{1,0:T(8,128)(2,1)}, bf16[32,3712]{1,0:T(8,128)(2,1)}, u32[]{:S(2)}, u32[]{:S(2)}) collective-permute-start(bf16[32,3712]{1,0:T(8,128)(2,1)} %bitcast.62), channel_id=1, source_target_pairs={{0,2},{1,3},{2,4},{3,5},{4,6},{5,7},{6,8},{7,9},{8,10},{9,11},{10,... | collective-permute-start | bytes 712712 | tf_op jit(solution)/shard_map/ppermute | solution.py:14
  66.0 2.2 copy-start.18
  66.0 5.3 %copy-start.17 = (bf16[32,29,128]{2,1,0:T(8,128)(2,1)S(1)}, bf16[32,29,128]{2,1,0:T(8,128)(2,1)}, u32[]{:S(2)}) copy-start(bf16[32,29,128]{2,1,0:T(8,128)(2,1)} %get-tuple-element.7) | copy-start | bytes 712708
  66.0 6.7 %copy-start.16 = (bf16[32,29,128]{2,1,0:T(8,128)(2,1)S(1)}, bf16[32,29,128]{2,1,0:T(8,128)(2,1)}, u32[]{:S(2)}) copy-start(bf16[32,29,128]{2,1,0:T(8,128)(2,1)} %get-tuple-element.6) | copy-start | bytes 712708
  68.4 7.8 %collective-permute-start.13 = (bf16[32,3712]{1,0:T(8,128)(2,1)S(1)}, bf16[32,3712]{1,0:T(8,128)(2,1)S(1)}, u32[]{:S(2)}, u32[]{:S(2)}) collective-permute-start(bf16[32,3712]{1,0:T(8,128)(2,1)S(1)} %bitcast.90), channel_id=1, source_target_pairs={{0,1},{1,2},{2,3},{3,4},{4,5},{5,6},{6,7},{7,8},{8,9},{9,10},{10,1... | collective-permute-start | bytes 712712 | tf_op jit(solution)/shard_map/ppermute | solution.py:14
  71.5 4.8 %collective-permute-start.14 = (bf16[32,3712]{1,0:T(8,128)(2,1)S(1)}, bf16[32,3712]{1,0:T(8,128)(2,1)S(1)}, u32[]{:S(2)}, u32[]{:S(2)}) collective-permute-start(bf16[32,3712]{1,0:T(8,128)(2,1)S(1)} %bitcast.88), channel_id=1, source_target_pairs={{1,0},{2,1},{3,2},{4,3},{5,4},{6,5},{7,6},{8,7},{9,8},{10,9},{11,1... | collective-permute-start | bytes 712712 | tf_op jit(solution)/shard_map/ppermute | solution.py:14
  72.9 12.9 %collective-permute-start.15 = (bf16[32,3712]{1,0:T(8,128)(2,1)S(1)}, bf16[32,3712]{1,0:T(8,128)(2,1)S(1)}, u32[]{:S(2)}, u32[]{:S(2)}) collective-permute-start(bf16[32,3712]{1,0:T(8,128)(2,1)S(1)} %bitcast.89), channel_id=1, source_target_pairs={{2,0},{3,1},{4,2},{5,3},{6,4},{7,5},{8,6},{9,7},{10,8},{11,9},{12,... | collective-permute-start | bytes 712712 | tf_op jit(solution)/shard_map/ppermute | solution.py:14
  87.0 7.6 %copy-start.9 = (bf16[128,3712]{1,0:T(8,128)(2,1)}, bf16[128,3712]{1,0:T(8,128)(2,1)S(1)}, u32[]{:S(2)}) copy-start(bf16[128,3712]{1,0:T(8,128)(2,1)S(1)} %gather_fusion.4) | copy-start | bytes 2850820
  100.7 4.0 %copy-start.6 = (f32[768,768]{1,0:T(8,128)S(1)}, f32[768,768]{1,0:T(8,128)}, u32[]{:S(2)}) copy-start(f32[768,768]{1,0:T(8,128)} %fusion.20) | copy-start | bytes 7077892
  117.7 2.7 copy-start.4
  120.3 2.5 copy-start.5
  122.8 2.2 copy-start.10
  125.1 2.0 copy-start.11
  138.0 1.4 slice-start
  155.8 1.6 copy-start.8
  157.8 1.6 copy-start.12
  161.6 2.1 copy-start.7
  167.9 15.7 %collective-permute-start.8 = (bf16[32,3712]{1,0:T(8,128)(2,1)S(1)}, bf16[32,3712]{1,0:T(8,128)(2,1)S(1)}, u32[]{:S(2)}, u32[]{:S(2)}) collective-permute-start(bf16[32,3712]{1,0:T(8,128)(2,1)S(1)} %get-tuple-element.13), channel_id=1, source_target_pairs={{2,0},{3,1},{4,2},{5,3},{6,4},{7,5},{8,6},{9,7},{10,8},{11,9},{12,... | collective-permute-start | bytes 712712 | tf_op jit(solution)/shard_map/ppermute | solution.py:14
  170.0 14.3 %collective-permute-start.9 = (bf16[32,3712]{1,0:T(8,128)(2,1)S(1)}, bf16[32,3712]{1,0:T(8,128)(2,1)S(1)}, u32[]{:S(2)}, u32[]{:S(2)}) collective-permute-start(bf16[32,3712]{1,0:T(8,128)(2,1)S(1)} %get-tuple-element.12), channel_id=1, source_target_pairs={{1,0},{2,1},{3,2},{4,3},{5,4},{6,5},{7,6},{8,7},{9,8},{10,9},{11,1... | collective-permute-start | bytes 712712 | tf_op jit(solution)/shard_map/ppermute | solution.py:14
  171.3 13.7 %collective-permute-start.10 = (bf16[32,3712]{1,0:T(8,128)(2,1)S(1)}, bf16[32,3712]{1,0:T(8,128)(2,1)S(1)}, u32[]{:S(2)}, u32[]{:S(2)}) collective-permute-start(bf16[32,3712]{1,0:T(8,128)(2,1)S(1)} %get-tuple-element.11), channel_id=1, source_target_pairs={{0,1},{1,2},{2,3},{3,4},{4,5},{5,6},{6,7},{7,8},{8,9},{9,10},{10,1... | collective-permute-start | bytes 712712 | tf_op jit(solution)/shard_map/ppermute | solution.py:14
  176.3 18.3 %collective-permute-start.11 = (bf16[32,3712]{1,0:T(8,128)(2,1)S(1)}, bf16[32,3712]{1,0:T(8,128)(2,1)S(1)}, u32[]{:S(2)}, u32[]{:S(2)}) collective-permute-start(bf16[32,3712]{1,0:T(8,128)(2,1)S(1)} %get-tuple-element.10), channel_id=1, source_target_pairs={{0,2},{1,3},{2,4},{3,5},{4,6},{5,7},{6,8},{7,9},{8,10},{9,11},{10,... | collective-permute-start | bytes 712712 | tf_op jit(solution)/shard_map/ppermute | solution.py:14
  195.4 3.7 %copy-start.3 = (bf16[192,29,29]{2,1,0:T(8,128)(2,1)S(1)}, bf16[192,29,29]{2,1,0:T(8,128)(2,1)}, u32[]{:S(2)}) copy-start(bf16[192,29,29]{2,1,0:T(8,128)(2,1)} %gather_fusion) | copy-start | bytes 968836
  202.9 72.2 %copy-start.1 = (bf16[128,3712]{1,0:T(8,128)(2,1)S(1)}, bf16[128,3712]{1,0:T(8,128)(2,1)}, u32[]{:S(2)}) copy-start(bf16[128,3712]{1,0:T(8,128)(2,1)} %param.10) | copy-start | bytes 2850820
Sparse Core Ops, SparseCore 0:
  25.3 70.2 all-gather.1
  138.1 136.9 reduce-scatter.3
where the time goes:
time: 283 us; the launch traced here: 282 us
  waiting for transfers between devices  85.5 us (30%)
  local copies, waits for them, and re-layouts  80.1 us (28%)
  starting transfers between devices  46.9 us (17%)
  matrix products  33.1 us (12%)
  other arithmetic  21.7 us (8%)
  between operations  14.6 us (5%)
    unnamed x3, waiting for transfers between devices  63.3 us
    ppermute x16, starting transfers between devices, from_behind(): return lax.ppermute(block, axis, route)  46.8 us
    ppermute x16, waiting for transfers between devices, from_behind(): return lax.ppermute(block, axis, route)  22.1 us
    unnamed x59, local copies, waits for them, and re-layouts  19.1 us
    dot_general x9, matrix products, outer_sum(): lax.dot_general(left, right, (((0,), (0,)), ((), ())), preferred_element_...  17.9 us
    mul x1, other arithmetic, on_device(): scaled = grad_sum * (1.0 / math.sqrt(edges_here * devices_dp))  9.44 us
    dot_general x9, matrix products, multiply(): return jnp.dot(left, right, preferred_element_type=jnp.float32)  7.91 us
    scatter-add x1, other arithmetic, deliver(): totals = jnp.zeros((node_grad.shape[0] + 1, flat_width), jnp.float32).at[...  7.78 us
  transfers between devices with their start and end apart: 18, of which 6 were waited for; matrix products, arithmetic and copies ran while one was open for 45% of the time, Pallas kernels for 0%

commit v1 on v0

v1 whole, which is shorter than its diff:
```python
import math

import jax
import jax.numpy as jnp
import numpy as np
from jax import lax
from jax.experimental import pallas as pl
from jax.experimental.pallas import tpu as pltpu
from jax.sharding import Mesh, PartitionSpec as P

K = 29
SPAN = 8
STEPS = (-2, -1, 1, 2)
BLOCKS_AT = (0, 7, 13, 19, 24, 29)
F32 = jnp.float32
BF16 = jnp.bfloat16
ALL = ("z", "x", "core")


def params(mib):
    return pltpu.CompilerParams(vmem_limit_bytes=mib * 1024 * 1024)


def dot(a, b):
    return jnp.dot(a, b, preferred_element_type=F32)


def iota(shape, dim):
    return lax.broadcasted_iota(jnp.int32, shape, dim)


def hot(cond):
    return jnp.where(cond, 1.0, 0.0).astype(BF16)


def column(row):
    n = row.shape[1]
    eye = iota((n, n), 0) == iota((n, n), 1)
    return jnp.sum(jnp.where(eye, row.astype(F32), 0.0), axis=1, keepdims=True)


def dp_index(n_x):
    return (lax.axis_index("z") * n_x + lax.axis_index("x")) * 2 + lax.axis_index("core")


def prep_kernel(me_ref, owner_ref, dst_ref, *outs):
    req_refs, take_ref, put_ref = outs[:4], outs[4], outs[5]
    n = owner_ref.shape[0]
    cap = n // 4
    off = (owner_ref[...] - me_ref[0]).astype(F32)
    eye = iota((n, n), 0) == iota((n, n), 1)
    off_row = jnp.sum(jnp.where(eye, off, 0.0), axis=0, keepdims=True)
    dst_row = dst_ref[...].astype(F32)
    dst = column(dst_ref[...])
    same = off == off_row
    earlier = same & (iota((n, n), 1) < iota((n, n), 0))
    pos = jnp.sum(jnp.where(earlier, 1.0, 0.0), axis=1, keepdims=True)
    before = same & (iota((n, n), 0) < iota((n, n), 1))
    pos_row = jnp.sum(jnp.where(before, 1.0, 0.0), axis=0, keepdims=True)
    base, base_row = jnp.full_like(off, -1000.0), jnp.full_like(off_row, -1000.0)
    for q, step in enumerate(STEPS):
        base = jnp.where(off == step, float(q * cap), base)
        base_row = jnp.where(off_row == step, float(q * cap), base_row)
        mine = (off == step) & (pos == iota((n, cap), 1).astype(F32))
        ids = jnp.sum(jnp.where(mine, dst + 1.0, 0.0), axis=0, keepdims=True)
        req_refs[q][...] = ids.astype(jnp.int32)
    slot, slot_row = base + pos, base_row + pos_row
    lanes = iota((n, n), 1).astype(F32)
    rows = iota((n, n), 0).astype(F32)
    take_ref[:, :n] = hot((off == 0.0) & (dst == lanes))
    take_ref[:, n:] = hot(slot == lanes)
    put_ref[:n, :] = hot((off_row == 0.0) & (dst_row == rows))
    put_ref[n:, :] = hot(slot_row == rows)


def serve_kernel(r0, r1, r2, r3, grad_ref, o0, o1, o2, o3):
    n = grad_ref.shape[0]
    cap = r0.shape[1]
    for r, o in ((r0, o0), (r1, o1), (r2, o2), (r3, o3)):
        pick = hot(iota((n, cap), 0) + 1 == r[...])
        o[...] = lax.dot_general(
            pick, grad_ref[...], (((0,), (0,)), ((), ())), preferred_element_type=F32
        ).astype(BF16)


def turn(mats_ref, src_ref, res_ref):
    n = src_ref.shape[1]
    for g in range(n // 8):
        rhs = src_ref[:, 8 * g : 8 * g + 8, :].reshape(256, 128).astype(BF16)
        res = dot(mats_ref[g], rhs)
        res_ref[:, 8 * g : 8 * g + 8, :] = res.reshape(30, 8, 128)


def build(table_ref, rot_hot, mats_ref, tmp_ref):
    n = rot_hot.shape[0]
    n_rot = rot_hot.shape[1]
    spread = hot(iota((K, 256), 1) // 8 == iota((K, 256), 0))
    wide = dot(table_ref[...], spread).astype(BF16)
    own = (iota((n, 256), 1) % 8) == (iota((n, 256), 0) % 8)
    for k in range(K):
        tmp_ref[k] = jnp.where(own, dot(rot_hot, wide[k * n_rot : (k + 1) * n_rot]), 0.0)
    tmp_ref[K] = jnp.zeros((n, 256), F32)
    for g in range(n // 8):
        mats_ref[g] = tmp_ref[:, 8 * g : 8 * g + 8, :].reshape(240, 256).astype(BF16)


def fill(dst_ref, j, wide):
    for i in range(wide.shape[1] // 128):
        dst_ref[j + i] = wide[:, 128 * i : 128 * i + 128]


def chunks():
    j = 0
    while j < K:
        w = min(4, K - j)
        yield j, w
        j += w


def source_kernel(
    src_ref, rot_ref, tab_ref, tabt_ref, feats_ref, mats_ref, matst_ref, h_ref, ht_ref,
    tmp_ref, in_ref, res_ref,
):
    n = feats_ref.shape[0]
    n_rot = tab_ref.shape[0] // K
    rot_hot = hot(column(rot_ref[...]) == iota((n, n_rot), 1).astype(F32))
    src_hot = hot(column(src_ref[...]) == iota((n, n), 1).astype(F32))
    for j, w in chunks():
        fill(in_ref, j, dot(src_hot, feats_ref[:, j * 128 : (j + w) * 128]))
    for j in range(K, 32):
        in_ref[j] = jnp.zeros((n, 128), F32)
    build(tab_ref, rot_hot, mats_ref, tmp_ref)
    turn(mats_ref, in_ref, res_ref)
    for k in range(K):
        h_ref[:, k * 128 : (k + 1) * 128] = res_ref[k].astype(BF16)
        ht_ref[k * 128 : (k + 1) * 128, :] = res_ref[k].T.astype(BF16)
    build(tabt_ref, rot_hot, matst_ref, tmp_ref)


def upstream_kernel(take_ref, mats_ref, grad_ref, r0, r1, r2, r3, u_ref, in_ref, res_ref):
    n = grad_ref.shape[0]
    for j, w in chunks():
        cols = slice(j * 128, (j + w) * 128)
        rows = jnp.concatenate([grad_ref[:, cols]] + [r[:, cols] for r in (r0, r1, r2, r3)], axis=0)
        fill(in_ref, j, dot(take_ref[...], rows))
    for j in range(K, 32):
        in_ref[j] = jnp.zeros((n, 128), F32)
    turn(mats_ref, in_ref, res_ref)
    for k in range(K):
        u_ref[:, k * 128 : (k + 1) * 128] = res_ref[k].astype(BF16)


def rank(n_z, z, target):
    order = sorted(range(n_z), key=lambda t: (-abs(t - z), -t))
    return order.index(target)


def by_rank(n_z, i):
    return [next(t for t in range(n_z) if rank(n_z, z, t) == i) for z in range(n_z)]


def choose(z, values):
    out = jnp.int32(values[0])
    for at in range(1, len(values)):
        out = jnp.where(z == at, jnp.int32(values[at]), out)
    return out


def grad_kernel(n_z, n_x, pos_ref, hta, htb, ua, ub, *outs_and_scratch):
    outs, flat = outs_and_scratch[:-1], outs_and_scratch[-1]
    z, x, core = pos_ref[0], pos_ref[1], pos_ref[2]

    def left(first, start, size):
        at = slice(first * 128 + start, first * 128 + start + size)
        return [hta[at, :], htb[at, :]]

    def right(first, width):
        at = slice(first * 128, (first + width) * 128)
        return [ua[:, at], ub[:, at]]

    def emit(base, width, start, res):
        for b in range(width):
            flat[pl.ds(base + start * width + b, res.shape[0], stride=width), :] = res[
                :, b * 128 : (b + 1) * 128
            ]

    base = 0
    rows0 = jnp.concatenate(right(0, 7), axis=0)
    for i in range(7):
        emit(base, 7, 128 * i, dot(jnp.concatenate(left(0, 128 * i, 128), axis=1), rows0))
    base += 49 * 128
    for first, width in ((7, 6), (19, 5)):
        real, imag = right(first, width), right(first + width, width)
        same = jnp.concatenate(real + imag, axis=0)
        cross = jnp.concatenate(imag + [-v for v in real], axis=0)
        for i in range(width):
            lhs = jnp.concatenate(
                left(first, 128 * i, 128) + left(first + width, 128 * i, 128), axis=1
            )
            emit(base, width, 128 * i, dot(lhs, same))
            emit(base + width * width * 128, width, 128 * i, dot(lhs, cross))
        base += 2 * width * width * 128

    rows = outs[0].shape[0]
    at_out = 0
    for o in list(range(1, n_x)) + [0]:
        for i in range(n_z):
            target = choose(z, by_rank(n_z, i))
            start = ((target * n_x + (x + o) % n_x) * 2 + core) * rows
            if rows % 8 == 0:
                start = pl.multiple_of(start, 8)
            ref = outs[at_out]
            ref[...] = flat[pl.ds(start, rows), :].astype(ref.dtype)
            at_out += 1


def message_kernel(n_half, rows, core_ref, wa, wb, h_ref, matst_ref, put_ref, *rest):
    local_ref, outs = rest[0], rest[1:5]
    flat, in_ref, res_ref, wide_ref = rest[5:]
    n = h_ref.shape[0]
    cap = n // 4
    piece = wa.shape[1]
    core = core_ref[0]
    for ref, who in ((wa, core), (wb, 1 - core)):
        for p in range(wa.shape[0]):
            half, chip = divmod(p, wa.shape[0] // n_half)
            start = (chip * 2 + who) * rows + half * (rows - piece)
            if rows % 8 == 0:
                start = pl.multiple_of(start, 8)
            flat[pl.ds(start, piece), :] = ref[p].astype(F32)

    def weight(base, width, b, many):
        parts = [
            flat[pl.ds(base + b + t, width * 128, stride=width), :].astype(BF16)
            for t in range(many)
        ]
        return parts[0] if many == 1 else jnp.concatenate(parts, axis=1)

    def rounded(v):
        return v.astype(BF16).astype(F32)

    def pairs(width):
        return [(b, min(2, width - b)) for b in range(0, width, 2)]

    for b, many in pairs(7):
        fill(in_ref, b, rounded(dot(h_ref[:, : 7 * 128], weight(0, 7, b, many))))
    base = 49 * 128
    for first, width in ((7, 6), (19, 5)):
        mid, end = (first + width) * 128, (first + 2 * width) * 128
        both = jnp.concatenate([h_ref[:, first * 128 : mid], h_ref[:, mid:end]], axis=0)
        for b, many in pairs(width):
            real = dot(both, weight(base, width, b, many))
            imag = dot(both, weight(base + width * width * 128, width, b, many))
            fill(in_ref, first + b, rounded(real[:n] - imag[n:]))
            fill(in_ref, first + width + b, rounded(imag[:n] + real[n:]))
        base += 2 * width * width * 128
    for j in range(K, 32):
        in_ref[j] = jnp.zeros((n, 128), F32)
    turn(matst_ref, in_ref, res_ref)
    for k in range(K):
        wide_ref[:, k * 128 : (k + 1) * 128] = res_ref[k].astype(BF16)
    for j, w in chunks():
        cols = slice(j * 128, (j + w) * 128)
        res = dot(put_ref[...], wide_ref[:, cols])
        local_ref[:, cols] = res[:n]
        for q in range(4):
            outs[q][:, cols] = res[n + q * cap : n + (q + 1) * cap].astype(BF16)


def collect_kernel(local_ref, r0, r1, r2, r3, m0, m1, m2, m3, out_ref):
    n = local_ref.shape[0]
    cap = r0.shape[1]
    hots = [hot(iota((n, cap), 0) + 1 == r[...]) for r in (r0, r1, r2, r3)]
    for j, w in chunks():
        cols = slice(j * 128, (j + w) * 128)
        total = local_ref[:, cols]
        for pick, m in zip(hots, (m0, m1, m2, m3)):
            total = total + dot(pick, m[:, cols])
        out_ref[:, cols] = total.astype(BF16)


def shape(dims, kind):
    return jax.ShapeDtypeStruct(dims, kind)


def on_device(
    n_z, n_x, node_feats, node_grad, flat_params, rot_table, edge_src, edge_dst, edge_rot,
    edge_owner,
):
    n = edge_src.shape[0]
    cap = n // 4
    width = node_feats.shape[1]
    rows = flat_params.shape[0]
    n_dp = n_z * n_x * 2
    n_rot = rot_table.shape[0]
    groups = lax.axis_size("groups")
    group, z, x, core = (lax.axis_index(a) for a in ("groups", "z", "x", "core"))
    me = dp_index(n_x)
    vmem = pl.BlockSpec(memory_space=pltpu.VMEM)
    smem = pl.BlockSpec(memory_space=pltpu.SMEM)

    def shift(block, step):
        route = [
            (i, i + step) for i in range(n_dp)
            if 0 <= i + step and i // SPAN == (i + step) // SPAN
        ]
        return lax.ppermute(block, ALL, route)

    def swap(block):
        return lax.ppermute(block, "core", [(0, 1), (1, 0)])

    piece = -(-rows // (16 * groups)) * 16
    part = lax.dynamic_slice_in_dim(flat_params, group * (rows - piece), piece, 0)
    w_own = lax.all_gather(part, ("groups", "z", "x"), axis=0)
    w_other = swap(w_own)

    row = lambda v: v.reshape(1, n)
    *req, take, put = pl.pallas_call(
        prep_kernel,
        out_shape=[shape((1, cap), jnp.int32)] * 4 + [shape((n, 2 * n), BF16), shape((2 * n, n), BF16)],
        in_specs=[smem, vmem, vmem],
        out_specs=[vmem] * 6,
        name="slots",
    )(me.reshape(1), edge_owner, row(edge_dst))
    got = [shift(r, s) for r, s in zip(req, STEPS)]
    served = pl.pallas_call(
        serve_kernel,
        out_shape=[shape((cap, width), BF16)] * 4,
        in_specs=[vmem] * 5,
        out_specs=[vmem] * 4,
        compiler_params=params(32),
        name="serve",
    )(*got, node_grad)
    back = [shift(r, -s) for r, s in zip(served, STEPS)]

    tab = rot_table.transpose(1, 0, 2).reshape(K * n_rot, K)
    tabt = rot_table.transpose(2, 0, 1).reshape(K * n_rot, K)
    mats, matst, h, ht = pl.pallas_call(
        source_kernel,
        out_shape=[
            shape((n // 8, 240, 256), BF16), shape((n // 8, 240, 256), BF16),
            shape((n, width), BF16), shape((width, n), BF16),
        ],
        in_specs=[vmem] * 5,
        out_specs=[vmem] * 4,
        scratch_shapes=[
            pltpu.VMEM((30, n, 256), F32), pltpu.VMEM((32, n, 128), F32),
            pltpu.VMEM((30, n, 128), F32),
        ],
        compiler_params=params(40),
        name="source",
    )(row(edge_src), row(edge_rot), tab, tabt, node_feats)
    ht_other = swap(ht)
    u = pl.pallas_call(
        upstream_kernel,
        out_shape=shape((n, width), BF16),
        in_specs=[vmem] * 7,
        out_specs=vmem,
        scratch_shapes=[pltpu.VMEM((32, n, 128), F32), pltpu.VMEM((30, n, 128), F32)],
        compiler_params=params(32),
        name="upstream",
    )(take, mats, node_grad, *back)
    u_other = swap(u)

    n_send = n_z * (n_x - 1)
    blocks = pl.pallas_call(
        lambda *refs: grad_kernel(n_z, n_x, *refs),
        out_shape=[shape((rows, 128), BF16)] * n_send + [shape((rows, 128), F32)] * n_z,
        in_specs=[smem] + [vmem] * 4,
        out_specs=[vmem] * (n_send + n_z),
        scratch_shapes=[pltpu.VMEM((rows * n_dp, 128), F32)],
        compiler_params=params(48),
        name="weight_terms",
    )(jnp.stack([z, x, core]), ht, ht_other, u, u_other)
    sums = []
    for i in range(n_z):
        total = blocks[n_send + i]
        for o in range(1, n_x):
            got_part = lax.ppermute(
                blocks[(o - 1) * n_z + i], "x", [(s, (s + o) % n_x) for s in range(n_x)]
            )
            total = total + got_part.astype(F32)
        sums.append(total)
    result = sums[n_z - 1]
    for way in (1, -1):
        arrived = None
        for k in range(n_z - 1, 0, -1):
            senders = [s for s in range(n_z) if 0 <= s + way * k < n_z]
            term = sums[rank(n_z, senders[0], senders[0] + way * k)]
            for s in senders[1:]:
                term = jnp.where(z == s, sums[rank(n_z, s, s + way * k)], term)
            if arrived is not None:
                term = term + arrived.astype(F32)
            arrived = lax.ppermute(term.astype(BF16), "z", [(s, s + way) for s in senders])
        if arrived is not None:
            result = result + arrived.astype(F32)
    weight_grad = result * (1.0 / math.sqrt(n * n_dp))

    local, *outbound = pl.pallas_call(
        lambda *refs: message_kernel(groups, rows, *refs),
        out_shape=[shape((n, width), F32)] + [shape((cap, width), BF16)] * 4,
        in_specs=[smem] + [vmem] * 5,
        out_specs=[vmem] * 5,
        scratch_shapes=[
            pltpu.VMEM((rows * n_dp, 128), F32), pltpu.VMEM((32, n, 128), F32),
            pltpu.VMEM((30, n, 128), F32), pltpu.VMEM((n, width), BF16),
        ],
        compiler_params=params(48),
        name="messages",
    )(core.reshape(1), w_own, w_other, h, matst, put)
    arrived = [shift(m, s) for m, s in zip(outbound, STEPS)]
    node_out = pl.pallas_call(
        collect_kernel,
        out_shape=shape((n, width), BF16),
        in_specs=[vmem] * 9,
        out_specs=vmem,
        compiler_params=params(32),
        name="collect",
    )(local, *got, *arrived)
    return (node_out, weight_grad)


def chips(mesh):
    n_dp = mesh.shape["dp"]
    line = list(mesh.devices.reshape(-1, n_dp)[0])
    coords = [getattr(d, "coords", None) for d in line]
    n_x = 2 if coords[0] is None else len({c[0] for c in coords})
    return n_dp // (2 * n_x), n_x


def solution(mesh):
    n_z, n_x = chips(mesh)
    fine = Mesh(
        np.asarray(mesh.devices).reshape(mesh.shape["groups"], n_z, n_x, 2),
        ("groups", "z", "x", "core"),
    )
    every = ("groups",) + ALL
    placed = (
        P(every, None),
        P(every, None),
        P(ALL, None),
        P(),
        P(every),
        P(every),
        P(every),
        P(every, None),
    )
    return jax.shard_map(
        lambda *args: on_device(n_z, n_x, *args),
        mesh=fine,
        in_specs=placed,
        out_specs=(P(every, None), P(every, None)),
        check_vma=False,
    )
```

time: 283 us -> 163 us (0.58)
  local copies, waits for them, and re-layouts: 80.1 us -> 10.2 us
  waiting for transfers between devices: 85.5 us -> 49 us
  matrix products: 33.1 us -> 0 us
  Pallas kernels: 0 us -> 22.3 us
  other arithmetic: 21.7 us -> 5.31 us
  starting transfers between devices: 46.9 us -> 59.7 us
    unnamed x3 -> x1, waiting for transfers between devices: 63.3 us -> 0.02 us
    dot_general x21 -> x0, matrix products: 33.1 us -> none  [the longest x9 17.9 us: outer_sum(): lax.dot_general(left, right, (((0,), (0,)), ((), ())), preferred_element_...]
    reshape x13 -> x0, local copies, waits for them, and re-layouts: 31.7 us -> none  [the longest x2 4.8 us: unpack(): flat_vector[offset:offset + third_size].reshape(5 * channels, 5 * channels)]
    all_gather x1, waiting for transfers between devices: 0.02 us -> 23.7 us  [on_device(): w_own = lax.all_gather(part, ('groups', 'z', 'x'), axis=0)]
    pallas_call x0 -> x7, Pallas kernels: none -> 22.3 us  [the longest x1 6.43 us: on_device(): pl.pallas_call(lambda *refs: message_kernel(groups, rows, *refs), out_sha...]
    ppermute x16 -> x25, starting transfers between devices: 46.8 us -> 59.7 us  [the longest x12 31.9 us: shift(): return lax.ppermute(block, ALL, route)]
    unnamed x59 -> x37, local copies, waits for them, and re-layouts: 19.1 us -> 6.98 us
    gather x6 -> x0, local copies, waits for them, and re-layouts: 9.96 us -> none  [the longest x1 2.58 us: deliver(): incoming = padded_grad[target_ids].reshape(slot_count, K, channels)]
  transfers between devices with their start and end apart: 18 -> 26, of which waited for: 6 -> 7; matrix products, arithmetic and copies ran while one was open for 45% -> 6% of each run, Pallas kernels for 0% -> 13%
where the time goes in v1:
time: 163 us; the launch traced here: 161 us
  starting transfers between devices  59.7 us (37%)
  waiting for transfers between devices  49 us (30%)
  Pallas kernels  22.3 us (14%)
  between operations  14.4 us (9%)
  local copies, waits for them, and re-layouts  10.2 us (6%)
  other arithmetic  5.31 us (3%)
    ppermute x12, starting transfers between devices, shift(): return lax.ppermute(block, ALL, route)  31.9 us
    all_gather x1, waiting for transfers between devices, on_device(): w_own = lax.all_gather(part, ('groups', 'z', 'x'), axis=0)  23.7 us
    ppermute x6, starting transfers between devices, on_device(): lax.ppermute(term.astype(BF16), 'z', [(s, s + way) for s in senders])  19.9 us
    ppermute x12, waiting for transfers between devices, shift(): return lax.ppermute(block, ALL, route)  14.6 us
    unnamed x37, local copies, waits for them, and re-layouts  6.98 us
    pallas_call x1, Pallas kernels, on_device(): pl.pallas_call(lambda *refs: message_kernel(groups, rows, *refs), out_sha...  6.43 us
    pallas_call x1, Pallas kernels, on_device(): pl.pallas_call(lambda *refs: grad_kernel(n_z, n_x, *refs), out_shape=[sha...  5.5 us
    ppermute x4, starting transfers between devices, on_device(): lax.ppermute(blocks[(o - 1) * n_z + i], 'x', [(s, (s + o) % n_x) for s in...  5.22 us
  transfers between devices with their start and end apart: 26, of which 7 were waited for; matrix products, arithmetic and copies ran while one was open for 6% of the time, Pallas kernels for 13%

profile of v1, /device:TPU:0, one launch (start us, length us, event | category | flops | bytes accessed | tf_op | source)
XLA Modules:
  0.0 160.9 jit_solution(3486021845438079954)
XLA Ops:
  7.2 0.0 copy-start
  7.2 0.0 all-gather.3.cloned.1.call-start
  7.3 0.9 copy-done
  8.2 0.7 constant_dynamic-slice_fusion
  8.8 0.0 all-gather.3.cloned.1.call-update
  8.9 1.4 copy.12.owner_ref
  10.3 1.8 %slots.1 = (s32[1,32]{1,0:T(1,128)}, s32[1,32]{1,0:T(1,128)}, s32[1,32]{1,0:T(1,128)}, s32[1,32]{1,0:T(1,128)}, bf16[128,256]{1,0:T(8,128)(2,1)}, /*index=5*/bf16[256,128]{1,0:T(8,128)(2,1)}) custom-call(s32[1]{0:T(128)} %bitcast.8.me_ref, s32[128,1]{1,0:T(8,128)} %copy.12.owner_ref, s32[1,128]{1,0:T(1,128)} %bitcast.20), custom_call_target="tpu_custom_call" | custom-call | tf_op jit(solution)/shard_map/slots/pallas_call | solution.py:318
  12.1 1.3 collective-permute-start.1
  13.4 1.3 collective-permute-start.2
  14.7 3.0 %collective-permute-start.3 = (s32[1,32]{1,0:T(1,128)}, s32[1,32]{1,0:T(1,128)S(1)}, u32[]{:S(2)}, u32[]{:S(2)}) collective-permute-start(s32[1,32]{1,0:T(1,128)} %get-tuple-element.35), channel_id=1, source_target_pairs={{0,1},{1,2},{2,3},{3,4},{4,5},{5,6},{6,7},{8,9},{9,10},{10,11},{11... | collective-permute-start | bytes 392 | tf_op jit(solution)/shard_map/ppermute | solution.py:307
  17.7 5.5 %collective-permute-start.4 = (s32[1,32]{1,0:T(1,128)}, s32[1,32]{1,0:T(1,128)S(1)}, u32[]{:S(2)}, u32[]{:S(2)}) collective-permute-start(s32[1,32]{1,0:T(1,128)} %get-tuple-element.36), channel_id=1, source_target_pairs={{0,2},{1,3},{2,4},{3,5},{4,6},{5,7},{8,10},{9,11},{10,12},{11,13},... | collective-permute-start | bytes 392 | tf_op jit(solution)/shard_map/ppermute | solution.py:307
  23.2 0.0 collective-permute-done.1.r0
  23.2 0.0 collective-permute-done.2.r1
  23.2 1.5 collective-permute-done.4.r3
  24.7 1.2 copy-done.1
  25.9 1.4 serve.1
  27.3 4.8 %collective-permute-start.10 = (bf16[32,3712]{1,0:T(8,128)(2,1)}, bf16[32,3712]{1,0:T(8,128)(2,1)S(1)}, u32[]{:S(2)}, u32[]{:S(2)}) collective-permute-start(bf16[32,3712]{1,0:T(8,128)(2,1)} %get-tuple-element.44), channel_id=1, source_target_pairs={{0,2},{1,3},{2,4},{3,5},{4,6},{5,7},{8,10},{9,11},{10,12},{11,13},... | collective-permute-start | bytes 712712 | tf_op jit(solution)/shard_map/ppermute | solution.py:307
  32.1 3.3 %collective-permute-start.11 = (bf16[32,3712]{1,0:T(8,128)(2,1)}, bf16[32,3712]{1,0:T(8,128)(2,1)}, u32[]{:S(2)}, u32[]{:S(2)}) collective-permute-start(bf16[32,3712]{1,0:T(8,128)(2,1)} %get-tuple-element.45), channel_id=1, source_target_pairs={{0,1},{1,2},{2,3},{3,4},{4,5},{5,6},{6,7},{8,9},{9,10},{10,11},{11... | collective-permute-start | bytes 712712 | tf_op jit(solution)/shard_map/ppermute | solution.py:307
  35.4 1.3 collective-permute-start.12
  36.7 1.3 collective-permute-start.13
  38.0 1.2 copy.10
  39.2 1.3 copy.11
  40.6 2.8 %source.1 = (bf16[16,240,256]{2,1,0:T(8,128)(2,1)S(1)}, bf16[16,240,256]{2,1,0:T(8,128)(2,1)S(1)}, bf16[128,3712]{1,0:T(8,128)(2,1)S(1)}, bf16[3712,128]{1,0:T(8,128)(2,1)S(1)}) custom-call(s32[1,128]{1,0:T(1,128)S(1)} %bitcast.14, s32[1,128]{1,0:T(1,128)S(1)} %bitcast.15, bf16[1856,29]{1,0:T(8,128)(2,1)S(1)} %bitcast.12, bf16[1856,29]{1,0:T(8,128)(2,1)S(1)} %bitcast.13, ...), custom_call_target="tpu_custom_call" | custom-call | tf_op jit(solution)/shard_map/source/pallas_call | solution.py:338
  43.4 0.0 copy-start.7
  43.4 2.6 %collective-permute-start.9 = (bf16[3712,128]{1,0:T(8,128)(2,1)S(1)}, bf16[3712,128]{1,0:T(8,128)(2,1)S(1)}, u32[]{:S(2)}, u32[]{:S(2)}) collective-permute-start(bf16[3712,128]{1,0:T(8,128)(2,1)S(1)} %get-tuple-element.41.refs_1_), channel_id=1, source_target_pairs={{0,1},{1,0},{2,3},{3,2},{4,5},{5,4},{6,7},{7,6},{8,9},{9,8},{10,11... | collective-permute-start | bytes 2850824 | tf_op jit(solution)/shard_map/ppermute | solution.py:310
  46.0 0.0 collective-permute-done.10.r0
  46.0 0.0 collective-permute-done.11.r1
  46.0 0.0 collective-permute-done.12.r2
  46.0 8.0 %collective-permute-done.13.r3 = bf16[32,3712]{1,0:T(8,128)(2,1)} collective-permute-done((bf16[32,3712]{1,0:T(8,128)(2,1)}, bf16[32,3712]{1,0:T(8,128)(2,1)}, u32[]{:S(2)}, u32[]{:S(2)}) %collective-permute-start.13) | collective-permute-done | bytes 237600 | tf_op jit(solution)/shard_map/ppermute | solution.py:307
  54.0 2.3 %upstream.1.refs_3_ = bf16[128,3712]{1,0:T(8,128)(2,1)S(1)} custom-call(bf16[128,256]{1,0:T(8,128)(2,1)S(1)} %copy-done.13, bf16[16,240,256]{2,1,0:T(8,128)(2,1)S(1)} %get-tuple-element.43.mats_ref, bf16[128,3712]{1,0:T(8,128)(2,1)S(1)} %copy-done.2, bf16[32,3712]{1,0:T(8,128)(2,1)S(1)} %collective-permute-done.10.r0, ...), custom_call_target="tpu_custom_call" | custom-call | tf_op jit(solution)/shard_map/upstream/pallas_call | solution.py:354
  56.3 0.1 collective-permute-start.14
  56.4 0.1 pad_add_fusion.refs_0_
  56.4 2.4 %collective-permute-done.14.refs_4_ = bf16[128,3712]{1,0:T(8,128)(2,1)S(1)} collective-permute-done((bf16[128,3712]{1,0:T(8,128)(2,1)S(1)}, bf16[128,3712]{1,0:T(8,128)(2,1)S(1)}, u32[]{:S(2)}, u32[]{:S(2)}) %collective-permute-start.14) | collective-permute-done | bytes 950304 | tf_op jit(solution)/shard_map/ppermute | solution.py:310
  58.9 0.9 copy-done.17
  59.8 5.5 %weight_terms.1 = (bf16[1368,128]{1,0:T(8,128)(2,1)S(1)}, bf16[1368,128]{1,0:T(8,128)(2,1)S(1)}, bf16[1368,128]{1,0:T(8,128)(2,1)}, bf16[1368,128]{1,0:T(8,128)(...) custom-call(s32[3]{0:T(128)S(1)} %pad_add_fusion.refs_0_, ...), custom_call_target="tpu_custom_call" | custom-call | tf_op jit(solution)/shard_map/weight_terms/pallas_call | solution.py:366
  65.3 0.9 copy-done.9
  66.2 0.8 copy-done.11
  67.1 1.5 collective-permute-start.18
  68.6 23.7 %all-gather.3.cloned.1.call-done = bf16[11008,128]{1,0:T(8,128)(2,1)} async-done(((bf16[688,128]{1,0:T(8,128)(2,1)}), bf16[11008,128]{1,0:T(8,128)(2,1)}) %all-gather.3.cloned.1.call-update) | async-done | bytes 2818064 | tf_op jit(solution)/shard_map/all_gather | solution.py:314
  92.3 0.0 collective-permute-start
  92.3 0.6 collective-permute-start.16
  92.9 0.0 collective-permute-done.18
  92.9 0.1 fusion.2
  93.0 2.8 %collective-permute-start.19 = (bf16[1368,128]{1,0:T(8,128)(2,1)S(1)}, bf16[1368,128]{1,0:T(8,128)(2,1)}, u32[]{:S(2)}, u32[]{:S(2)}) collective-permute-start(bf16[1368,128]{1,0:T(8,128)(2,1)S(1)} %fusion.2), channel_id=1, source_target_pairs={{0,4},{1,5},{2,6},{3,7},{16,20},{17,21},{18,22},{19,23}} | collective-permute-start | bytes 1050632 | tf_op jit(solution)/shard_map/ppermute | solution.py:394
  95.8 1.4 collective-permute-start.22
  97.2 1.6 collective-permute-start.17
  98.8 4.6 %collective-permute-done.16 = bf16[1368,128]{1,0:T(8,128)(2,1)S(1)} collective-permute-done((bf16[1368,128]{1,0:T(8,128)(2,1)S(1)}, bf16[1368,128]{1,0:T(8,128)(2,1)S(1)}, u32[]{:S(2)}, u32[]{:S(2)}) %collective-permute-start.16) | collective-permute-done | bytes 350240 | tf_op jit(solution)/shard_map/ppermute | solution.py:379
  103.3 0.7 copy-done.16
  104.1 2.3 %add_convert_fusion.2 = (bf16[1368,128]{1,0:T(8,128)(2,1)}, bf16[1368,128]{1,0:T(8,128)(2,1)}) fusion(bf16[1368,128]{1,0:T(8,128)(2,1)} %collective-permute-done.19, pred[]{:T(512)S(6)} %eq.13, f32[1368,128]{1,0:T(8,128)S(1)} %get-tuple-element.50, bf16[1368,128]{1,0:T(8,128)(2,1)S(1)} %collective-permute-done.16, f32[1368,128]{1,0:T(8,128)S(1)} %get-tuple-element.54, ...), kind=kLoop, calls=%fused_computation.6 | loop fusion | flops 2101248 | bytes 3502082 | tf_op jit(solution)/shard_map/convert_element_type | solution.py:394
  106.4 4.2 %collective-permute-start.20 = (bf16[1368,128]{1,0:T(8,128)(2,1)}, bf16[1368,128]{1,0:T(8,128)(2,1)}, u32[]{:S(2)}, u32[]{:S(2)}) collective-permute-start(bf16[1368,128]{1,0:T(8,128)(2,1)} %get-tuple-element.56), channel_id=1, source_target_pairs={{0,4},{4,8},{1,5},{5,9},{2,6},{6,10},{3,7},{7,11},{16,20},{20,24},... | collective-permute-start | bytes 1050632 | tf_op jit(solution)/shard_map/ppermute | solution.py:394
  110.6 1.4 collective-permute-start.23
  112.0 1.6 collective-permute-start.15
  113.6 3.6 %collective-permute-done.20 = bf16[1368,128]{1,0:T(8,128)(2,1)} collective-permute-done((bf16[1368,128]{1,0:T(8,128)(2,1)}, bf16[1368,128]{1,0:T(8,128)(2,1)}, u32[]{:S(2)}, u32[]{:S(2)}) %collective-permute-start.20) | collective-permute-done | bytes 350240 | tf_op jit(solution)/shard_map/ppermute | solution.py:394
  117.2 1.8 %fusion.1 = (bf16[1368,128]{1,0:T(8,128)(2,1)S(1)}, bf16[1368,128]{1,0:T(8,128)(2,1)S(1)}) fusion(bf16[1368,128]{1,0:T(8,128)(2,1)} %collective-permute-done.20, f32[1368,128]{1,0:T(8,128)} %copy-done.11, bf16[1368,128]{1,0:T(8,128)(2,1)} %collective-permute-done.17, pred[]{:T(512)S(6)} %eq.13, pred[]{:T(512)S(6)} %eq.12, ...), kind=kLoop, calls=%fused_computation.2 | loop fusion | flops 2101248 | bytes 3502082 | tf_op jit(solution)/shard_map/convert_element_type | solution.py:394
  119.0 8.6 %collective-permute-start.21 = (bf16[1368,128]{1,0:T(8,128)(2,1)S(1)}, bf16[1368,128]{1,0:T(8,128)(2,1)S(1)}, u32[]{:S(2)}, u32[]{:S(2)}) collective-permute-start(bf16[1368,128]{1,0:T(8,128)(2,1)S(1)} %get-tuple-element.58), channel_id=1, source_target_pairs={{0,4},{4,8},{8,12},{1,5},{5,9},{9,13},{2,6},{6,10},{10,14},{3,7},{... | collective-permute-start | bytes 1050632 | tf_op jit(solution)/shard_map/ppermute | solution.py:394
  127.6 1.5 collective-permute-start.24
  129.1 6.4 %messages.1 = (f32[128,3712]{1,0:T(8,128)S(1)}, bf16[32,3712]{1,0:T(8,128)(2,1)S(1)}, bf16[32,3712]{1,0:T(8,128)(2,1)S(1)}, bf16[32,3712]{1,0:T(8,128)(2,1)S(1)}, bf16[32,3712]{1,0:T(8,128)(2,1)S(1)}) custom-call(s32[1]{0:T(128)} %bitcast.refs_0_, bf16[16,688,128]{2,1,0:T(8,128)(2,1)} %bitcast.17, bf16[16,688,128]{2,1,0:T(8,128)(2,1)} %collective-permute-done.refs_2_, ...), custom_call_target="tpu_custom_call" | custom-call | tf_op jit(solution)/shard_map/messages/pallas_call | solution.py:399
  135.5 1.3 collective-permute-start.5
  136.8 1.3 collective-permute-start.6
  138.1 3.0 %collective-permute-start.7 = (bf16[32,3712]{1,0:T(8,128)(2,1)S(1)}, bf16[32,3712]{1,0:T(8,128)(2,1)S(1)}, u32[]{:S(2)}, u32[]{:S(2)}) collective-permute-start(bf16[32,3712]{1,0:T(8,128)(2,1)S(1)} %get-tuple-element.39), channel_id=1, source_target_pairs={{0,1},{1,2},{2,3},{3,4},{4,5},{5,6},{6,7},{8,9},{9,10},{10,11},{11... | collective-permute-start | bytes 712712 | tf_op jit(solution)/shard_map/ppermute | solution.py:307
  141.2 4.6 %collective-permute-start.8 = (bf16[32,3712]{1,0:T(8,128)(2,1)S(1)}, bf16[32,3712]{1,0:T(8,128)(2,1)S(1)}, u32[]{:S(2)}, u32[]{:S(2)}) collective-permute-start(bf16[32,3712]{1,0:T(8,128)(2,1)S(1)} %get-tuple-element.40), channel_id=1, source_target_pairs={{0,2},{1,3},{2,4},{3,5},{4,6},{5,7},{8,10},{9,11},{10,12},{11,13},... | collective-permute-start | bytes 712712 | tf_op jit(solution)/shard_map/ppermute | solution.py:307
  145.8 1.0 add_multiply_fusion
  146.8 5.1 %collective-permute-done.8.m3 = bf16[32,3712]{1,0:T(8,128)(2,1)S(1)} collective-permute-done((bf16[32,3712]{1,0:T(8,128)(2,1)S(1)}, bf16[32,3712]{1,0:T(8,128)(2,1)S(1)}, u32[]{:S(2)}, u32[]{:S(2)}) %collective-permute-start.8) | collective-permute-done | bytes 237600 | tf_op jit(solution)/shard_map/ppermute | solution.py:307
  152.0 2.1 %collect.1 = bf16[128,3712]{1,0:T(8,128)(2,1)} custom-call(f32[128,3712]{1,0:T(8,128)S(1)} %get-tuple-element.32.local_ref, s32[1,32]{1,0:T(1,128)S(1)} %collective-permute-done.1.r0, s32[1,32]{1,0:T(1,128)S(1)} %collective-permute-done.2.r1, s32[1,32]{1,0:T(1,128)S(1)} %collective-permute-done.3.r2, s32[1,32]{1,0:T(1,128)S(1)} %collective-permute-done.4.r3, ...), custom_call_target="tpu_custom_call" | custom-call | tf_op jit(solution)/shard_map/collect/pallas_call | solution.py:412
  (41 shorter events, 0.1 us)
Async XLA Ops:
  7.2 1.0 copy-start
  7.2 33.4 %copy-start.14 = (s32[128]{0:T(128)S(1)}, s32[128]{0:T(128)}, u32[]{:S(2)}) copy-start(s32[128]{0:T(128)} %param.12) | copy-start | bytes 1540
  7.2 33.4 %copy-start.15 = (s32[128]{0:T(128)S(1)}, s32[128]{0:T(128)}, u32[]{:S(2)}) copy-start(s32[128]{0:T(128)} %param.14) | copy-start | bytes 1540
  7.2 85.1 %all-gather.3.cloned.1.call-start = ((), (), s32[]{:S(2)}) async-start(), calls=%async_computation | async-start | bytes 2994176 | tf_op jit(solution)/shard_map/all_gather | solution.py:314
  12.1 11.1 %collective-permute-start.1 = (s32[1,32]{1,0:T(1,128)}, s32[1,32]{1,0:T(1,128)S(1)}, u32[]{:S(2)}, u32[]{:S(2)}) collective-permute-start(s32[1,32]{1,0:T(1,128)} %get-tuple-element.33), channel_id=1, source_target_pairs={{2,0},{3,1},{4,2},{5,3},{6,4},{7,5},{10,8},{11,9},{12,10},{13,11},... | collective-permute-start | bytes 392 | tf_op jit(solution)/shard_map/ppermute | solution.py:307
  13.4 9.8 %collective-permute-start.2 = (s32[1,32]{1,0:T(1,128)}, s32[1,32]{1,0:T(1,128)S(1)}, u32[]{:S(2)}, u32[]{:S(2)}) collective-permute-start(s32[1,32]{1,0:T(1,128)} %get-tuple-element.34), channel_id=1, source_target_pairs={{1,0},{2,1},{3,2},{4,3},{5,4},{6,5},{7,6},{9,8},{10,9},{11,10},{12... | collective-permute-start | bytes 392 | tf_op jit(solution)/shard_map/ppermute | solution.py:307
  14.7 8.5 %collective-permute-start.3 = (s32[1,32]{1,0:T(1,128)}, s32[1,32]{1,0:T(1,128)S(1)}, u32[]{:S(2)}, u32[]{:S(2)}) collective-permute-start(s32[1,32]{1,0:T(1,128)} %get-tuple-element.35), channel_id=1, source_target_pairs={{0,1},{1,2},{2,3},{3,4},{4,5},{5,6},{6,7},{8,9},{9,10},{10,11},{11... | collective-permute-start | bytes 392 | tf_op jit(solution)/shard_map/ppermute | solution.py:307
  17.7 7.0 %collective-permute-start.4 = (s32[1,32]{1,0:T(1,128)}, s32[1,32]{1,0:T(1,128)S(1)}, u32[]{:S(2)}, u32[]{:S(2)}) collective-permute-start(s32[1,32]{1,0:T(1,128)} %get-tuple-element.36), channel_id=1, source_target_pairs={{0,2},{1,3},{2,4},{3,5},{4,6},{5,7},{8,10},{9,11},{10,12},{11,13},... | collective-permute-start | bytes 392 | tf_op jit(solution)/shard_map/ppermute | solution.py:307
  24.7 1.2 copy-start.1
  25.9 14.7 %copy-start.6 = (bf16[128,3712]{1,0:T(8,128)(2,1)S(1)}, bf16[128,3712]{1,0:T(8,128)(2,1)}, u32[]{:S(2)}) copy-start(bf16[128,3712]{1,0:T(8,128)(2,1)} %feats_ref.1) | copy-start | bytes 2850820
  25.9 28.1 %copy-start.2 = (bf16[128,3712]{1,0:T(8,128)(2,1)S(1)}, bf16[128,3712]{1,0:T(8,128)(2,1)}, u32[]{:S(2)}) copy-start(bf16[128,3712]{1,0:T(8,128)(2,1)} %grad_ref.3) | copy-start | bytes 2850820
  25.9 28.1 %copy-start.13 = (bf16[128,256]{1,0:T(8,128)(2,1)S(1)}, bf16[128,256]{1,0:T(8,128)(2,1)}, u32[]{:S(2)}) copy-start(bf16[128,256]{1,0:T(8,128)(2,1)} %get-tuple-element.42.take_ref) | copy-start | bytes 196612
  27.3 18.7 %collective-permute-start.10 = (bf16[32,3712]{1,0:T(8,128)(2,1)}, bf16[32,3712]{1,0:T(8,128)(2,1)S(1)}, u32[]{:S(2)}, u32[]{:S(2)}) collective-permute-start(bf16[32,3712]{1,0:T(8,128)(2,1)} %get-tuple-element.44), channel_id=1, source_target_pairs={{0,2},{1,3},{2,4},{3,5},{4,6},{5,7},{8,10},{9,11},{10,12},{11,13},... | collective-permute-start | bytes 712712 | tf_op jit(solution)/shard_map/ppermute | solution.py:307
  32.1 13.9 %collective-permute-start.11 = (bf16[32,3712]{1,0:T(8,128)(2,1)}, bf16[32,3712]{1,0:T(8,128)(2,1)}, u32[]{:S(2)}, u32[]{:S(2)}) collective-permute-start(bf16[32,3712]{1,0:T(8,128)(2,1)} %get-tuple-element.45), channel_id=1, source_target_pairs={{0,1},{1,2},{2,3},{3,4},{4,5},{5,6},{6,7},{8,9},{9,10},{10,11},{11... | collective-permute-start | bytes 712712 | tf_op jit(solution)/shard_map/ppermute | solution.py:307
  35.4 10.6 %collective-permute-start.12 = (bf16[32,3712]{1,0:T(8,128)(2,1)}, bf16[32,3712]{1,0:T(8,128)(2,1)}, u32[]{:S(2)}, u32[]{:S(2)}) collective-permute-start(bf16[32,3712]{1,0:T(8,128)(2,1)} %get-tuple-element.46), channel_id=1, source_target_pairs={{1,0},{2,1},{3,2},{4,3},{5,4},{6,5},{7,6},{9,8},{10,9},{11,10},{12... | collective-permute-start | bytes 712712 | tf_op jit(solution)/shard_map/ppermute | solution.py:307
  36.7 17.3 %collective-permute-start.13 = (bf16[32,3712]{1,0:T(8,128)(2,1)}, bf16[32,3712]{1,0:T(8,128)(2,1)}, u32[]{:S(2)}, u32[]{:S(2)}) collective-permute-start(bf16[32,3712]{1,0:T(8,128)(2,1)} %get-tuple-element.47), channel_id=1, source_target_pairs={{2,0},{3,1},{4,2},{5,3},{6,4},{7,5},{10,8},{11,9},{12,10},{13,11},... | collective-permute-start | bytes 712712 | tf_op jit(solution)/shard_map/ppermute | solution.py:307
  43.4 12.9 %copy-start.4 = (bf16[16,240,256]{2,1,0:T(8,128)(2,1)}, bf16[16,240,256]{2,1,0:T(8,128)(2,1)S(1)}, u32[]{:S(2)}) copy-start(bf16[16,240,256]{2,1,0:T(8,128)(2,1)S(1)} %get-tuple-element.30.refs_4_) | copy-start | bytes 5898244
  43.4 12.9 %copy-start.7 = (bf16[128,3712]{1,0:T(8,128)(2,1)}, bf16[128,3712]{1,0:T(8,128)(2,1)S(1)}, u32[]{:S(2)}) copy-start(bf16[128,3712]{1,0:T(8,128)(2,1)S(1)} %get-tuple-element.29.refs_3_) | copy-start | bytes 2850820
  43.4 13.0 %collective-permute-start.9 = (bf16[3712,128]{1,0:T(8,128)(2,1)S(1)}, bf16[3712,128]{1,0:T(8,128)(2,1)S(1)}, u32[]{:S(2)}, u32[]{:S(2)}) collective-permute-start(bf16[3712,128]{1,0:T(8,128)(2,1)S(1)} %get-tuple-element.41.refs_1_), channel_id=1, source_target_pairs={{0,1},{1,0},{2,3},{3,2},{4,5},{5,4},{6,7},{7,6},{8,9},{9,8},{10,11... | collective-permute-start | bytes 2850824 | tf_op jit(solution)/shard_map/ppermute | solution.py:310
  56.3 2.6 %copy-start.3 = (bf16[128,3712]{1,0:T(8,128)(2,1)}, bf16[128,3712]{1,0:T(8,128)(2,1)S(1)}, u32[]{:S(2)}) copy-start(bf16[128,3712]{1,0:T(8,128)(2,1)S(1)} %upstream.1.refs_3_) | copy-start | bytes 2850820
  56.3 2.6 %collective-permute-start.14 = (bf16[128,3712]{1,0:T(8,128)(2,1)S(1)}, bf16[128,3712]{1,0:T(8,128)(2,1)S(1)}, u32[]{:S(2)}, u32[]{:S(2)}) collective-permute-start(bf16[128,3712]{1,0:T(8,128)(2,1)S(1)} %upstream.1.refs_3_), channel_id=1, source_target_pairs={{0,1},{1,0},{2,3},{3,2},{4,5},{5,4},{6,7},{7,6},{8,9},{9,8},{10,11... | collective-permute-start | bytes 2850824 | tf_op jit(solution)/shard_map/ppermute | solution.py:310
  58.9 1.0 copy-start.17
  65.3 0.9 copy-start.9
  66.2 0.9 copy-start.11
  67.1 25.8 %collective-permute-start.18 = (bf16[1368,128]{1,0:T(8,128)(2,1)S(1)}, bf16[1368,128]{1,0:T(8,128)(2,1)S(1)}, u32[]{:S(2)}, u32[]{:S(2)}) collective-permute-start(bf16[1368,128]{1,0:T(8,128)(2,1)S(1)} %get-tuple-element.55), channel_id=1, source_target_pairs={{0,2},{2,0},{1,3},{3,1},{4,6},{6,4},{5,7},{7,5},{8,10},{10,8},{9,1... | collective-permute-start | bytes 1050632 | tf_op jit(solution)/shard_map/ppermute | solution.py:379
  92.3 36.7 %collective-permute-start = (bf16[16,688,128]{2,1,0:T(8,128)(2,1)}, bf16[16,688,128]{2,1,0:T(8,128)(2,1)}, u32[]{:S(2)}, u32[]{:S(2)}) collective-permute-start(bf16[16,688,128]{2,1,0:T(8,128)(2,1)} %bitcast.16), channel_id=1, source_target_pairs={{0,1},{1,0},{2,3},{3,2},{4,5},{5,4},{6,7},{7,6},{8,9},{9,8},{10,11... | collective-permute-start | bytes 8454152 | tf_op jit(solution)/shard_map/ppermute | solution.py:310
  92.3 11.0 %collective-permute-start.16 = (bf16[1368,128]{1,0:T(8,128)(2,1)S(1)}, bf16[1368,128]{1,0:T(8,128)(2,1)S(1)}, u32[]{:S(2)}, u32[]{:S(2)}) collective-permute-start(bf16[1368,128]{1,0:T(8,128)(2,1)S(1)} %get-tuple-element.51), channel_id=1, source_target_pairs={{0,2},{2,0},{1,3},{3,1},{4,6},{6,4},{5,7},{7,5},{8,10},{10,8},{9,1... | collective-permute-start | bytes 1050632 | tf_op jit(solution)/shard_map/ppermute | solution.py:379
  93.0 10.3 %collective-permute-start.19 = (bf16[1368,128]{1,0:T(8,128)(2,1)S(1)}, bf16[1368,128]{1,0:T(8,128)(2,1)}, u32[]{:S(2)}, u32[]{:S(2)}) collective-permute-start(bf16[1368,128]{1,0:T(8,128)(2,1)S(1)} %fusion.2), channel_id=1, source_target_pairs={{0,4},{1,5},{2,6},{3,7},{16,20},{17,21},{18,22},{19,23}} | collective-permute-start | bytes 1050632 | tf_op jit(solution)/shard_map/ppermute | solution.py:394
  95.8 7.5 %collective-permute-start.22 = (bf16[1368,128]{1,0:T(8,128)(2,1)S(1)}, bf16[1368,128]{1,0:T(8,128)(2,1)}, u32[]{:S(2)}, u32[]{:S(2)}) collective-permute-start(bf16[1368,128]{1,0:T(8,128)(2,1)S(1)} %fusion.2), channel_id=1, source_target_pairs={{12,8},{13,9},{14,10},{15,11},{28,24},{29,25},{30,26},{31,27}} | collective-permute-start | bytes 1050632 | tf_op jit(solution)/shard_map/ppermute | solution.py:394
  97.2 16.3 %collective-permute-start.17 = (bf16[1368,128]{1,0:T(8,128)(2,1)}, bf16[1368,128]{1,0:T(8,128)(2,1)}, u32[]{:S(2)}, u32[]{:S(2)}) collective-permute-start(bf16[1368,128]{1,0:T(8,128)(2,1)} %get-tuple-element.53), channel_id=1, source_target_pairs={{0,2},{2,0},{1,3},{3,1},{4,6},{6,4},{5,7},{7,5},{8,10},{10,8},{9,1... | collective-permute-start | bytes 1050632 | tf_op jit(solution)/shard_map/ppermute | solution.py:379
  103.3 0.7 copy-start.16
  106.4 22.7 %copy-start.5 = (bf16[16,240,256]{2,1,0:T(8,128)(2,1)S(1)}, bf16[16,240,256]{2,1,0:T(8,128)(2,1)}, u32[]{:S(2)}) copy-start(bf16[16,240,256]{2,1,0:T(8,128)(2,1)} %copy-done.4) | copy-start | bytes 5898244
  106.4 22.7 %copy-start.12 = (bf16[256,128]{1,0:T(8,128)(2,1)S(1)}, bf16[256,128]{1,0:T(8,128)(2,1)}, u32[]{:S(2)}) copy-start(bf16[256,128]{1,0:T(8,128)(2,1)} %get-tuple-element.31.refs_5_) | copy-start | bytes 196612
  106.4 10.8 %collective-permute-start.20 = (bf16[1368,128]{1,0:T(8,128)(2,1)}, bf16[1368,128]{1,0:T(8,128)(2,1)}, u32[]{:S(2)}, u32[]{:S(2)}) collective-permute-start(bf16[1368,128]{1,0:T(8,128)(2,1)} %get-tuple-element.56), channel_id=1, source_target_pairs={{0,4},{4,8},{1,5},{5,9},{2,6},{6,10},{3,7},{7,11},{16,20},{20,24},... | collective-permute-start | bytes 1050632 | tf_op jit(solution)/shard_map/ppermute | solution.py:394
  110.6 6.6 %collective-permute-start.23 = (bf16[1368,128]{1,0:T(8,128)(2,1)}, bf16[1368,128]{1,0:T(8,128)(2,1)}, u32[]{:S(2)}, u32[]{:S(2)}) collective-permute-start(bf16[1368,128]{1,0:T(8,128)(2,1)} %get-tuple-element.57), channel_id=1, source_target_pairs={{8,4},{12,8},{9,5},{13,9},{10,6},{14,10},{11,7},{15,11},{24,20},{2... | collective-permute-start | bytes 1050632 | tf_op jit(solution)/shard_map/ppermute | solution.py:394
  112.0 17.1 %copy-start.8 = (bf16[128,3712]{1,0:T(8,128)(2,1)S(1)}, bf16[128,3712]{1,0:T(8,128)(2,1)}, u32[]{:S(2)}) copy-start(bf16[128,3712]{1,0:T(8,128)(2,1)} %copy-done.7) | copy-start | bytes 2850820
  112.0 26.1 %collective-permute-start.15 = (bf16[1368,128]{1,0:T(8,128)(2,1)S(1)}, bf16[1368,128]{1,0:T(8,128)(2,1)S(1)}, u32[]{:S(2)}, u32[]{:S(2)}) collective-permute-start(bf16[1368,128]{1,0:T(8,128)(2,1)S(1)} %get-tuple-element.49), channel_id=1, source_target_pairs={{0,2},{2,0},{1,3},{3,1},{4,6},{6,4},{5,7},{7,5},{8,10},{10,8},{9,1... | collective-permute-start | bytes 1050632 | tf_op jit(solution)/shard_map/ppermute | solution.py:379
  119.0 22.2 %collective-permute-start.21 = (bf16[1368,128]{1,0:T(8,128)(2,1)S(1)}, bf16[1368,128]{1,0:T(8,128)(2,1)S(1)}, u32[]{:S(2)}, u32[]{:S(2)}) collective-permute-start(bf16[1368,128]{1,0:T(8,128)(2,1)S(1)} %get-tuple-element.58), channel_id=1, source_target_pairs={{0,4},{4,8},{8,12},{1,5},{5,9},{9,13},{2,6},{6,10},{10,14},{3,7},{... | collective-permute-start | bytes 1050632 | tf_op jit(solution)/shard_map/ppermute | solution.py:394
  127.6 18.2 %collective-permute-start.24 = (bf16[1368,128]{1,0:T(8,128)(2,1)S(1)}, bf16[1368,128]{1,0:T(8,128)(2,1)S(1)}, u32[]{:S(2)}, u32[]{:S(2)}) collective-permute-start(bf16[1368,128]{1,0:T(8,128)(2,1)S(1)} %get-tuple-element.59), channel_id=1, source_target_pairs={{4,0},{8,4},{12,8},{5,1},{9,5},{13,9},{6,2},{10,6},{14,10},{7,3},{... | collective-permute-start | bytes 1050632 | tf_op jit(solution)/shard_map/ppermute | solution.py:394
  129.1 16.7 %copy-start.10 = (f32[1368,128]{1,0:T(8,128)S(1)}, f32[1368,128]{1,0:T(8,128)}, u32[]{:S(2)}) copy-start(f32[1368,128]{1,0:T(8,128)} %copy-done.9) | copy-start | bytes 2101252
  135.5 11.3 %collective-permute-start.5 = (bf16[32,3712]{1,0:T(8,128)(2,1)S(1)}, bf16[32,3712]{1,0:T(8,128)(2,1)S(1)}, u32[]{:S(2)}, u32[]{:S(2)}) collective-permute-start(bf16[32,3712]{1,0:T(8,128)(2,1)S(1)} %get-tuple-element.37), channel_id=1, source_target_pairs={{2,0},{3,1},{4,2},{5,3},{6,4},{7,5},{10,8},{11,9},{12,10},{13,11},... | collective-permute-start | bytes 712712 | tf_op jit(solution)/shard_map/ppermute | solution.py:307
  136.8 10.0 %collective-permute-start.6 = (bf16[32,3712]{1,0:T(8,128)(2,1)S(1)}, bf16[32,3712]{1,0:T(8,128)(2,1)S(1)}, u32[]{:S(2)}, u32[]{:S(2)}) collective-permute-start(bf16[32,3712]{1,0:T(8,128)(2,1)S(1)} %get-tuple-element.38), channel_id=1, source_target_pairs={{1,0},{2,1},{3,2},{4,3},{5,4},{6,5},{7,6},{9,8},{10,9},{11,10},{12... | collective-permute-start | bytes 712712 | tf_op jit(solution)/shard_map/ppermute | solution.py:307
  138.1 8.7 %collective-permute-start.7 = (bf16[32,3712]{1,0:T(8,128)(2,1)S(1)}, bf16[32,3712]{1,0:T(8,128)(2,1)S(1)}, u32[]{:S(2)}, u32[]{:S(2)}) collective-permute-start(bf16[32,3712]{1,0:T(8,128)(2,1)S(1)} %get-tuple-element.39), channel_id=1, source_target_pairs={{0,1},{1,2},{2,3},{3,4},{4,5},{5,6},{6,7},{8,9},{9,10},{10,11},{11... | collective-permute-start | bytes 712712 | tf_op jit(solution)/shard_map/ppermute | solution.py:307
  141.2 10.8 %collective-permute-start.8 = (bf16[32,3712]{1,0:T(8,128)(2,1)S(1)}, bf16[32,3712]{1,0:T(8,128)(2,1)S(1)}, u32[]{:S(2)}, u32[]{:S(2)}) collective-permute-start(bf16[32,3712]{1,0:T(8,128)(2,1)S(1)} %get-tuple-element.40), channel_id=1, source_target_pairs={{0,2},{1,3},{2,4},{3,5},{4,6},{5,7},{8,10},{9,11},{10,12},{11,13},... | collective-permute-start | bytes 712712 | tf_op jit(solution)/shard_map/ppermute | solution.py:307
Sparse Core Ops, SparseCore 0:
  10.7 81.5 all-gather.2

commit v2 on v1

v2 whole, which is shorter than its diff:
```python
import math

import jax
import jax.numpy as jnp
import numpy as np
from jax import lax
from jax.experimental import pallas as pl
from jax.experimental.pallas import tpu as pltpu
from jax.sharding import Mesh, PartitionSpec as P

K = 29
SPAN = 8
STEPS = (-2, -1, 1, 2)
F32 = jnp.float32
BF16 = jnp.bfloat16
ALL = ("z", "x", "core")


def params(mib):
    return pltpu.CompilerParams(vmem_limit_bytes=mib * 1024 * 1024)


def dot(a, b):
    return jnp.dot(a, b, preferred_element_type=F32)


def iota(shape, dim):
    return lax.broadcasted_iota(jnp.int32, shape, dim)


def hot(cond):
    return jnp.where(cond, 1.0, 0.0).astype(BF16)


def column(row):
    n = row.shape[1]
    eye = iota((n, n), 0) == iota((n, n), 1)
    return jnp.sum(jnp.where(eye, row.astype(F32), 0.0), axis=1, keepdims=True)


def dp_index(n_x):
    return (lax.axis_index("z") * n_x + lax.axis_index("x")) * 2 + lax.axis_index("core")


def send_kernel(me_ref, owner_ref, src_ref, dst_ref, rot_ref, feats_ref, *outs):
    n = feats_ref.shape[0]
    width = feats_ref.shape[1]
    half, cap = n // 2, n // 4
    off_row = (owner_ref[...] - me_ref[0]).astype(F32)
    off = column(off_row)
    before = (off == off_row) & (iota((n, n), 0) < iota((n, n), 1))
    slot = jnp.sum(jnp.where(before, 1.0, 0.0), axis=0, keepdims=True)
    for q, step in enumerate(STEPS):
        slot = jnp.where(off_row == step, slot + float(half + q * cap), slot)
    slots = half + 4 * cap
    here = slot == iota((slots, n), 0).astype(F32)

    def pick(row):
        return jnp.sum(jnp.where(here, row, 0.0), axis=1, keepdims=True)

    source = pick(src_ref[...].astype(F32) + 1.0) - 1.0
    target = pick(dst_ref[...].astype(F32) + 1.0)
    turns = pick(rot_ref[...].astype(F32))
    source_hot = hot(source == iota((slots, n), 1).astype(F32))
    lane = iota((slots, 128), 1)
    ids = jnp.where(lane == 0, target, jnp.where(lane == 1, turns, 0.0)).astype(BF16)
    spans = [(0, half)] + [(half + q * cap, cap) for q in range(4)]
    for o, (at, size) in zip(outs, spans):
        o[:, width:] = ids[at : at + size]
    for j, w in chunks():
        cols = slice(j * 128, (j + w) * 128)
        rows = dot(source_hot, feats_ref[:, cols]).astype(BF16)
        for o, (at, size) in zip(outs, spans):
            o[:, cols] = rows[at : at + size]


def turn(mats_ref, src_ref, res_ref):
    lanes = src_ref.shape[2]
    for g in range(src_ref.shape[1] // 8):
        rhs = src_ref[:, 8 * g : 8 * g + 8, :].reshape(256, lanes).astype(BF16)
        res = dot(mats_ref[g], rhs)
        res_ref[:, 8 * g : 8 * g + 8, :] = res.reshape(30, 8, lanes)


def build(table_ref, rot_hot, mats_ref, tmp_ref):
    n = rot_hot.shape[0]
    n_rot = rot_hot.shape[1]
    spread = hot(iota((K, 256), 1) // 8 == iota((K, 256), 0))
    wide = dot(table_ref[...], spread).astype(BF16)
    own = (iota((n, 256), 1) % 8) == (iota((n, 256), 0) % 8)
    for k in range(K):
        tmp_ref[k] = jnp.where(own, dot(rot_hot, wide[k * n_rot : (k + 1) * n_rot]), 0.0)
    tmp_ref[K] = jnp.zeros((n, 256), F32)
    for g in range(n // 8):
        mats_ref[g] = tmp_ref[:, 8 * g : 8 * g + 8, :].reshape(240, 256).astype(BF16)


def chunks():
    j = 0
    while j < K:
        w = min(4, K - j)
        yield j, w
        j += w


def joined(refs, cols):
    return jnp.concatenate([r[:, cols] for r in refs], axis=0)


def number(ids, lane):
    at = iota(ids.shape, 1) == lane
    return jnp.sum(jnp.where(at, ids.astype(F32), 0.0), axis=1, keepdims=True)


def rotate_kernel(count, *refs):
    raw, (tab_ref, tabt_ref, grad_ref) = refs[:count], refs[count : count + 3]
    both_ref, matst_ref, hot_ref, mats_ref, tmp_ref, in_ref, res_ref = refs[count + 3 :]
    n = grad_ref.shape[0]
    n_rot = tab_ref.shape[0] // K
    width = grad_ref.shape[1]
    ids = joined(raw, slice(width, width + 128))
    slots = ids.shape[0]
    target_hot = hot(number(ids, 0) - 1.0 == iota((slots, n), 1).astype(F32))
    rot_hot = hot(number(ids, 1) == iota((slots, n_rot), 1).astype(F32))
    hot_ref[...] = target_hot
    for j, w in chunks():
        cols = slice(j * 128, (j + w) * 128)
        rows = joined(raw, cols).astype(F32)
        back = dot(target_hot, grad_ref[:, cols])
        for i in range(w):
            in_ref[j + i, :, :128] = rows[:, 128 * i : 128 * i + 128]
            in_ref[j + i, :, 128:] = back[:, 128 * i : 128 * i + 128]
    for j in range(K, 32):
        in_ref[j] = jnp.zeros((slots, 256), F32)
    build(tab_ref, rot_hot, mats_ref, tmp_ref)
    turn(mats_ref, in_ref, res_ref)
    for k in range(K):
        cols = slice(k * 128, (k + 1) * 128)
        both_ref[:slots, cols] = res_ref[k, :, :128].astype(BF16)
        both_ref[slots:, cols] = res_ref[k, :, 128:].astype(BF16)
    build(tabt_ref, rot_hot, matst_ref, tmp_ref)


def rank(n_z, z, target):
    order = sorted(range(n_z), key=lambda t: (-abs(t - z), -t))
    return order.index(target)


def by_rank(n_z, i):
    return [next(t for t in range(n_z) if rank(n_z, z, t) == i) for z in range(n_z)]


def choose(z, values):
    out = jnp.int32(values[0])
    for at in range(1, len(values)):
        out = jnp.where(z == at, jnp.int32(values[at]), out)
    return out


def grad_kernel(n_z, n_x, pos_ref, *refs):
    parts, outs, flat = refs[:4], refs[4:-1], refs[-1]
    z, x, core = pos_ref[0], pos_ref[1], pos_ref[2]

    def left(first):
        at = slice(first * 128, (first + 1) * 128)
        return [p[: p.shape[0] // 2, at] for p in parts]

    def right(first, width):
        at = slice(first * 128, (first + width) * 128)
        return [p[p.shape[0] // 2 :, at] for p in parts]

    def outer(lhs, rhs):
        return lax.dot_general(lhs, rhs, (((0,), (0,)), ((), ())), preferred_element_type=F32)

    def emit(base, width, start, res):
        for b in range(width):
            flat[pl.ds(base + start * width + b, res.shape[0], stride=width), :] = res[
                :, b * 128 : (b + 1) * 128
            ]

    rows0 = jnp.concatenate(right(0, 7), axis=0)
    for i in range(7):
        emit(0, 7, 128 * i, outer(jnp.concatenate(left(i), axis=0), rows0))
    base = 49 * 128
    for first, width in ((7, 6), (19, 5)):
        real, imag = right(first, width), right(first + width, width)
        same = jnp.concatenate(real + imag, axis=0)
        cross = jnp.concatenate(imag + [-v for v in real], axis=0)
        for i in range(width):
            lhs = jnp.concatenate(left(first + i) + left(first + width + i), axis=0)
            emit(base, width, 128 * i, outer(lhs, same))
            emit(base + width * width * 128, width, 128 * i, outer(lhs, cross))
        base += 2 * width * width * 128

    rows = outs[0].shape[0]
    at_out = 0
    for o in list(range(1, n_x)) + [0]:
        for i in range(n_z):
            target = choose(z, by_rank(n_z, i))
            start = ((target * n_x + (x + o) % n_x) * 2 + core) * rows
            if rows % 8 == 0:
                start = pl.multiple_of(start, 8)
            ref = outs[at_out]
            ref[...] = flat[pl.ds(start, rows), :].astype(ref.dtype)
            at_out += 1


def message_kernel(w_ref, *refs):
    both, mats, hots = refs[0:2], refs[2:4], refs[4:6]
    out_ref, flat, in_ref, res_ref, wide_ref = refs[6:]
    n = out_ref.shape[0]
    slots = in_ref.shape[1]
    part = w_ref.shape[0] // 16
    for p in range(16):
        flat[p * part : (p + 1) * part, :] = w_ref[p * part : (p + 1) * part, :].astype(F32)

    def h(first, end):
        return jnp.concatenate(
            [r[: r.shape[0] // 2, first * 128 : end * 128] for r in both], axis=0
        )

    def fill(j, wide):
        for i in range(wide.shape[1] // 128):
            in_ref[j + i] = wide[:, 128 * i : 128 * i + 128]

    def weight(base, width, b, many):
        parts = [
            flat[pl.ds(base + b + t, width * 128, stride=width), :].astype(BF16)
            for t in range(many)
        ]
        return parts[0] if many == 1 else jnp.concatenate(parts, axis=1)

    def rounded(v):
        return v.astype(BF16).astype(F32)

    def pairs(width):
        return [(b, min(2, width - b)) for b in range(0, width, 2)]

    h0 = h(0, 7)
    for b, many in pairs(7):
        fill(b, rounded(dot(h0, weight(0, 7, b, many))))
    base = 49 * 128
    for first, width in ((7, 6), (19, 5)):
        mid, end = first + width, first + 2 * width
        pair = jnp.concatenate([h(first, mid), h(mid, end)], axis=0)
        for b, many in pairs(width):
            real = dot(pair, weight(base, width, b, many))
            imag = dot(pair, weight(base + width * width * 128, width, b, many))
            fill(first + b, rounded(real[:slots] - imag[slots:]))
            fill(mid + b, rounded(imag[:slots] + real[slots:]))
        base += 2 * width * width * 128
    for j in range(K, 32):
        in_ref[j] = jnp.zeros((slots, 128), F32)
    at = 0
    for m in mats:
        size = m.shape[0] * 8
        turn(m, in_ref.at[:, at : at + size, :], res_ref.at[:, at : at + size, :])
        at += size
    for k in range(K):
        wide_ref[:, k * 128 : (k + 1) * 128] = res_ref[k].astype(BF16)
    target = jnp.concatenate([r[...] for r in hots], axis=0).astype(F32).T.astype(BF16)
    for j, w in chunks():
        cols = slice(j * 128, (j + w) * 128)
        out_ref[:, cols] = dot(target, wide_ref[:, cols]).astype(BF16)


def shape(dims, kind):
    return jax.ShapeDtypeStruct(dims, kind)


def on_device(
    n_z, n_x, node_feats, node_grad, flat_params, rot_table, edge_src, edge_dst, edge_rot,
    edge_owner,
):
    n = edge_src.shape[0]
    cap = n // 4
    width = node_feats.shape[1]
    rows = flat_params.shape[0]
    n_dp = n_z * n_x * 2
    n_rot = rot_table.shape[0]
    z, x, core = (lax.axis_index(a) for a in ALL)
    me = dp_index(n_x)
    vmem = pl.BlockSpec(memory_space=pltpu.VMEM)
    smem = pl.BlockSpec(memory_space=pltpu.SMEM)

    def shift(block, step):
        route = [
            (i, i + step) for i in range(n_dp)
            if 0 <= i + step and i // SPAN == (i + step) // SPAN
        ]
        return lax.ppermute(block, ALL, route)

    def swap(block):
        return lax.ppermute(block, "core", [(0, 1), (1, 0)])

    weights = lax.all_gather(flat_params, ALL, axis=0, tiled=True)

    row = lambda v: v.reshape(1, n)
    here, *outbound = pl.pallas_call(
        send_kernel,
        out_shape=[shape((n // 2, width + 128), BF16)] + [shape((cap, width + 128), BF16)] * 4,
        in_specs=[smem] + [vmem] * 5,
        out_specs=[vmem] * 5,
        compiler_params=params(32),
        name="send",
    )(me.reshape(1), row(edge_owner), row(edge_src), row(edge_dst), row(edge_rot), node_feats)
    arrived = [shift(r, s) for r, s in zip(outbound, STEPS)]

    tab = rot_table.transpose(1, 0, 2).reshape(K * n_rot, K)
    tabt = rot_table.transpose(2, 0, 1).reshape(K * n_rot, K)

    def rotate(rows_in, name):
        slots = sum(r.shape[0] for r in rows_in)
        return pl.pallas_call(
            lambda *refs: rotate_kernel(len(rows_in), *refs),
            out_shape=[
                shape((2 * slots, width), BF16), shape((slots // 8, 240, 256), BF16),
                shape((slots, n), BF16),
            ],
            in_specs=[vmem] * (len(rows_in) + 3),
            out_specs=[vmem] * 3,
            scratch_shapes=[
                pltpu.VMEM((slots // 8, 240, 256), BF16), pltpu.VMEM((30, slots, 256), F32),
                pltpu.VMEM((32, slots, 256), F32), pltpu.VMEM((30, slots, 256), F32),
            ],
            compiler_params=params(40),
            name=name,
        )(*rows_in, tab, tabt, node_grad)

    both_near, matst_near, hot_near = rotate([here], "rotate_near")
    both_near_other = swap(both_near)
    both_far, matst_far, hot_far = rotate(arrived, "rotate_far")
    both_far_other = swap(both_far)

    n_send = n_z * (n_x - 1)
    blocks = pl.pallas_call(
        lambda *refs: grad_kernel(n_z, n_x, *refs),
        out_shape=[shape((rows, 128), BF16)] * n_send + [shape((rows, 128), F32)] * n_z,
        in_specs=[smem] + [vmem] * 4,
        out_specs=[vmem] * (n_send + n_z),
        scratch_shapes=[pltpu.VMEM((rows * n_dp, 128), F32)],
        compiler_params=params(48),
        name="weight_terms",
    )(jnp.stack([z, x, core]), both_near, both_near_other, both_far, both_far_other)
    sums = []
    for i in range(n_z):
        total = blocks[n_send + i]
        for o in range(1, n_x):
            got_part = lax.ppermute(
                blocks[(o - 1) * n_z + i], "x", [(s, (s + o) % n_x) for s in range(n_x)]
            )
            total = total + got_part.astype(F32)
        sums.append(total)
    result = sums[n_z - 1]
    for way in (1, -1):
        arrived = None
        for k in range(n_z - 1, 0, -1):
            senders = [s for s in range(n_z) if 0 <= s + way * k < n_z]
            term = sums[rank(n_z, senders[0], senders[0] + way * k)]
            for s in senders[1:]:
                term = jnp.where(z == s, sums[rank(n_z, s, s + way * k)], term)
            if arrived is not None:
                term = term + arrived.astype(F32)
            term = term.astype(BF16)
            arrived = lax.ppermute(term, "z", [(s, s + way) for s in senders])
        if arrived is not None:
            result = result + arrived.astype(F32)
    weight_grad = result * (1.0 / math.sqrt(n * n_dp))

    weights, _ = lax.optimization_barrier((weights, term))
    slots = n // 2 + 4 * cap
    node_out = pl.pallas_call(
        message_kernel,
        out_shape=shape((n, width), BF16),
        in_specs=[vmem] * 7,
        out_specs=vmem,
        scratch_shapes=[
            pltpu.VMEM((rows * n_dp, 128), F32), pltpu.VMEM((32, slots, 128), F32),
            pltpu.VMEM((30, slots, 128), F32), pltpu.VMEM((slots, width), BF16),
        ],
        compiler_params=params(48),
        name="messages",
    )(weights, both_near, both_far, matst_near, matst_far, hot_near, hot_far)
    return (node_out, weight_grad)


def chips(mesh):
    n_dp = mesh.shape["dp"]
    line = list(mesh.devices.reshape(-1, n_dp)[0])
    coords = [getattr(d, "coords", None) for d in line]
    n_x = 2 if coords[0] is None else len({c[0] for c in coords})
    return n_dp // (2 * n_x), n_x


def solution(mesh):
    n_z, n_x = chips(mesh)
    fine = Mesh(
        np.asarray(mesh.devices).reshape(mesh.shape["groups"], n_z, n_x, 2),
        ("groups", "z", "x", "core"),
    )
    every = ("groups",) + ALL
    placed = (
        P(every, None),
        P(every, None),
        P(ALL, None),
        P(),
        P(every),
        P(every),
        P(every),
        P(every, None),
    )
    return jax.shard_map(
        lambda *args: on_device(n_z, n_x, *args),
        mesh=fine,
        in_specs=placed,
        out_specs=(P(every, None), P(every, None)),
        check_vma=False,
    )
```

time: 163 us -> 138 us (0.85)
  starting transfers between devices: 59.7 us -> 39.1 us
  waiting for transfers between devices: 49 us -> 39.8 us
  local copies, waits for them, and re-layouts: 10.2 us -> 16.6 us
  other arithmetic: 5.31 us -> 6.94 us
    all_gather x1, waiting for transfers between devices: 23.7 us -> 0.01 us  [on_device(): weights = lax.all_gather(flat_params, ALL, axis=0, tiled=True)]
    ppermute x12 -> x4, starting transfers between devices: 31.9 us -> 11.1 us  [shift(): return lax.ppermute(block, ALL, route)]
    ppermute x6, waiting for transfers between devices: 3.64 us -> 18.7 us  [on_device(): arrived = lax.ppermute(term, 'z', [(s, s + way) for s in senders])]
    unnamed x37 -> x42, local copies, waits for them, and re-layouts: 6.98 us -> 14.1 us
    ppermute x12 -> x4, waiting for transfers between devices: 14.6 us -> 9.34 us  [shift(): return lax.ppermute(block, ALL, route)]
    ppermute x4, waiting for transfers between devices: 4.56 us -> 9.01 us  [on_device(): lax.ppermute(blocks[(o - 1) * n_z + i], 'x', [(s, (s + o) % n_x) for s in...]
    pallas_call x6 -> x4, Pallas kernels: 16.8 us -> 13 us  [the longest x1 7.66 us: on_device(): pl.pallas_call(message_kernel, out_shape=shape((n, width), BF16), in_spec...]
    pallas_call x1, Pallas kernels: 5.5 us -> 7.71 us  [on_device(): pl.pallas_call(lambda *refs: grad_kernel(n_z, n_x, *refs), out_shape=[sha...]
  transfers between devices with their start and end apart: 26 -> 17, of which waited for: 7 -> 7; matrix products, arithmetic and copies ran while one was open for 6% -> 7% of each run, Pallas kernels for 13% -> 9%
where the time goes in v2:
time: 138 us; the launch traced here: 137 us
  waiting for transfers between devices  39.8 us (29%)
  starting transfers between devices  39.1 us (28%)
  Pallas kernels  20.7 us (15%)
  local copies, waits for them, and re-layouts  16.6 us (12%)
  between operations  14.2 us (10%)
  other arithmetic  6.94 us (5%)
    ppermute x6, starting transfers between devices, on_device(): arrived = lax.ppermute(term, 'z', [(s, s + way) for s in senders])  21.5 us
    ppermute x6, waiting for transfers between devices, on_device(): arrived = lax.ppermute(term, 'z', [(s, s + way) for s in senders])  18.7 us
    unnamed x42, local copies, waits for them, and re-layouts  14.1 us
    ppermute x4, starting transfers between devices, shift(): return lax.ppermute(block, ALL, route)  11.1 us
    ppermute x4, waiting for transfers between devices, shift(): return lax.ppermute(block, ALL, route)  9.34 us
    ppermute x4, waiting for transfers between devices, on_device(): lax.ppermute(blocks[(o - 1) * n_z + i], 'x', [(s, (s + o) % n_x) for s in...  9.01 us
    pallas_call x1, Pallas kernels, on_device(): pl.pallas_call(lambda *refs: grad_kernel(n_z, n_x, *refs), out_shape=[sha...  7.71 us
    pallas_call x1, Pallas kernels, on_device(): pl.pallas_call(message_kernel, out_shape=shape((n, width), BF16), in_spec...  7.66 us
  transfers between devices with their start and end apart: 17, of which 7 were waited for; matrix products, arithmetic and copies ran while one was open for 7% of the time, Pallas kernels for 9%

profile of v2, /device:TPU:0, one launch (start us, length us, event | category | flops | bytes accessed | tf_op | source)
XLA Modules:
  0.0 137.4 jit_solution(5083676534730284011)
XLA Ops:
  7.2 0.0 all-gather.2.cloned.1.call-start
  7.2 0.7 all-gather.2.cloned.1.call-update
  7.9 0.0 copy-start.10
  7.9 1.2 copy-done.10
  9.1 0.7 copy-done.16
  9.8 0.7 copy-done.17
  10.4 0.7 copy-done.18
  11.1 0.7 copy-done.19
  11.7 0.7 send.1
  12.4 1.3 collective-permute-start.1
  13.7 1.3 collective-permute-start.2
  15.0 3.0 %collective-permute-start.3 = (bf16[32,3840]{1,0:T(8,128)(2,1)S(1)}, bf16[32,3840]{1,0:T(8,128)(2,1)S(1)}, u32[]{:S(2)}, u32[]{:S(2)}) collective-permute-start(bf16[32,3840]{1,0:T(8,128)(2,1)S(1)} %get-tuple-element.26), channel_id=1, source_target_pairs={{0,1},{1,2},{2,3},{3,4},{4,5},{5,6},{6,7},{8,9},{9,10},{10,11},{11... | collective-permute-start | bytes 737288 | tf_op jit(solution)/shard_map/ppermute | solution.py:291
  18.1 5.5 %collective-permute-start.4 = (bf16[32,3840]{1,0:T(8,128)(2,1)S(1)}, bf16[32,3840]{1,0:T(8,128)(2,1)S(1)}, u32[]{:S(2)}, u32[]{:S(2)}) collective-permute-start(bf16[32,3840]{1,0:T(8,128)(2,1)S(1)} %get-tuple-element.27), channel_id=1, source_target_pairs={{0,2},{1,3},{2,4},{3,5},{4,6},{5,7},{8,10},{9,11},{10,12},{11,13},... | collective-permute-start | bytes 737288 | tf_op jit(solution)/shard_map/ppermute | solution.py:291
  23.6 1.3 copy.11
  24.9 1.2 copy.10
  26.1 0.0 collective-permute-done.1.refs_0_
  26.1 0.0 collective-permute-done.2.refs_1_
  26.1 0.0 collective-permute-done.3.refs_2_
  26.1 9.3 %collective-permute-done.4.refs_3_ = bf16[32,3840]{1,0:T(8,128)(2,1)S(1)} collective-permute-done((bf16[32,3840]{1,0:T(8,128)(2,1)S(1)}, bf16[32,3840]{1,0:T(8,128)(2,1)S(1)}, u32[]{:S(2)}, u32[]{:S(2)}) %collective-permute-start.4) | collective-permute-done | bytes 245792 | tf_op jit(solution)/shard_map/ppermute | solution.py:291
  35.5 1.2 copy-done.2
  36.7 2.8 %rotate_far.1 = (bf16[256,3712]{1,0:T(8,128)(2,1)S(1)}, bf16[16,240,256]{2,1,0:T(8,128)(2,1)S(1)}, bf16[128,128]{1,0:T(8,128)(2,1)S(1)}) custom-call(bf16[32,3840]{1,0:T(8,128)(2,1)S(1)} %collective-permute-done.1.refs_0_, bf16[32,3840]{1,0:T(8,128)(2,1)S(1)} %collective-permute-done.2.refs_1_, bf16[32,3840]{1,0:T(8,128)(2,1)S(1)} %collective-permute-done.3.refs_2_, ...), custom_call_target="tpu_custom_call" | custom-call | tf_op jit(solution)/shard_map/rotate_far/pallas_call | solution.py:314
  39.4 1.3 copy-done.6
  40.7 2.3 %collective-permute-start.5 = (bf16[256,3712]{1,0:T(8,128)(2,1)S(1)}, bf16[256,3712]{1,0:T(8,128)(2,1)S(1)}, u32[]{:S(2)}, u32[]{:S(2)}) collective-permute-start(bf16[256,3712]{1,0:T(8,128)(2,1)S(1)} %get-tuple-element.28.refs_3_.refs_1_), channel_id=1, source_target_pairs={{0,1},{1,0},{2,3},{3,2},{4,5},{5,4},{6,7},{7,6},{8,9},{9,8},{10,11... | collective-permute-start | bytes 5701640 | tf_op jit(solution)/shard_map/ppermute | solution.py:294
  43.0 1.2 copy-done.3
  44.2 1.9 %rotate_near.1 = (bf16[128,3712]{1,0:T(8,128)(2,1)S(1)}, bf16[8,240,256]{2,1,0:T(8,128)(2,1)S(1)}, bf16[64,128]{1,0:T(8,128)(2,1)S(1)}) custom-call(bf16[64,3840]{1,0:T(8,128)(2,1)S(1)} %get-tuple-element.22.refs_0_, bf16[1856,29]{1,0:T(8,128)(2,1)S(1)} %bitcast.15, bf16[1856,29]{1,0:T(8,128)(2,1)S(1)} %bitcast.13, bf16[128,3712]{1,0:T(8,128)(2,1)S(1)} %copy-done.3), custom_call_target="tpu_custom_call" | custom-call | tf_op jit(solution)/shard_map/rotate_near/pallas_call | solution.py:314
  46.2 0.0 copy-start.8
  46.2 1.0 copy-done.8
  47.2 0.6 copy-done.14
  47.8 0.7 collective-permute-start
  48.5 0.1 pad_add_fusion.refs_0_
  48.5 2.1 %collective-permute-done.refs_2_ = bf16[128,3712]{1,0:T(8,128)(2,1)S(1)} collective-permute-done((bf16[128,3712]{1,0:T(8,128)(2,1)S(1)}, bf16[128,3712]{1,0:T(8,128)(2,1)S(1)}, u32[]{:S(2)}, u32[]{:S(2)}) %collective-permute-start) | collective-permute-done | bytes 950304 | tf_op jit(solution)/shard_map/ppermute | solution.py:294
  50.6 0.0 collective-permute-done.5.refs_4_
  50.6 0.0 copy-done
  50.6 1.4 copy-done.20
  52.0 7.7 %weight_terms.1 = (bf16[1368,128]{1,0:T(8,128)(2,1)S(1)}, bf16[1368,128]{1,0:T(8,128)(2,1)S(1)}, bf16[1368,128]{1,0:T(8,128)(2,1)S(1)}, bf16[1368,128]{1,0:T(8,1...) custom-call(s32[3]{0:T(128)S(1)} %pad_add_fusion.refs_0_, ...), custom_call_target="tpu_custom_call" | custom-call | tf_op jit(solution)/shard_map/weight_terms/pallas_call | solution.py:336
  59.7 0.8 copy-done.11
  60.5 2.8 %collective-permute-start.8 = (bf16[1368,128]{1,0:T(8,128)(2,1)S(1)}, bf16[1368,128]{1,0:T(8,128)(2,1)S(1)}, u32[]{:S(2)}, u32[]{:S(2)}) collective-permute-start(bf16[1368,128]{1,0:T(8,128)(2,1)S(1)} %get-tuple-element.34), channel_id=1, source_target_pairs={{0,2},{2,0},{1,3},{3,1},{4,6},{6,4},{5,7},{7,5},{8,10},{10,8},{9,1... | collective-permute-start | bytes 1050632 | tf_op jit(solution)/shard_map/ppermute | solution.py:349
  63.3 0.0 collective-permute-start.7
  63.3 9.0 %collective-permute-done.8 = bf16[1368,128]{1,0:T(8,128)(2,1)S(1)} collective-permute-done((bf16[1368,128]{1,0:T(8,128)(2,1)S(1)}, bf16[1368,128]{1,0:T(8,128)(2,1)S(1)}, u32[]{:S(2)}, u32[]{:S(2)}) %collective-permute-start.8) | collective-permute-done | bytes 350240 | tf_op jit(solution)/shard_map/ppermute | solution.py:349
  72.3 0.9 fusion.2
  73.2 6.2 %collective-permute-start.12 = (bf16[1368,128]{1,0:T(8,128)(2,1)}, bf16[1368,128]{1,0:T(8,128)(2,1)}, u32[]{:S(2)}, u32[]{:S(2)}) collective-permute-start(bf16[1368,128]{1,0:T(8,128)(2,1)} %fusion.2), channel_id=1, source_target_pairs={{0,4},{1,5},{2,6},{3,7},{16,20},{17,21},{18,22},{19,23}} | collective-permute-start | bytes 1050632 | tf_op jit(solution)/shard_map/ppermute | solution.py:365
  79.4 1.4 %collective-permute-start.9 = (bf16[1368,128]{1,0:T(8,128)(2,1)}, bf16[1368,128]{1,0:T(8,128)(2,1)}, u32[]{:S(2)}, u32[]{:S(2)}) collective-permute-start(bf16[1368,128]{1,0:T(8,128)(2,1)} %fusion.2), channel_id=1, source_target_pairs={{12,8},{13,9},{14,10},{15,11},{28,24},{29,25},{30,26},{31,27}} | collective-permute-start | bytes 1050632 | tf_op jit(solution)/shard_map/ppermute | solution.py:365
  80.8 0.0 collective-permute-start.6
  80.8 0.0 collective-permute-done.7
  80.8 4.8 %collective-permute-done.12 = bf16[1368,128]{1,0:T(8,128)(2,1)} collective-permute-done((bf16[1368,128]{1,0:T(8,128)(2,1)}, bf16[1368,128]{1,0:T(8,128)(2,1)}, u32[]{:S(2)}, u32[]{:S(2)}) %collective-permute-start.12) | collective-permute-done | bytes 350240 | tf_op jit(solution)/shard_map/ppermute | solution.py:365
  85.6 0.0 collective-permute-done.9
  85.6 2.4 %add_convert_fusion = (bf16[1368,128]{1,0:T(8,128)(2,1)}, bf16[1368,128]{1,0:T(8,128)(2,1)}) fusion(bf16[1368,128]{1,0:T(8,128)(2,1)} %collective-permute-done.12, pred[]{:T(512)S(6)} %eq.14, f32[1368,128]{1,0:T(8,128)S(1)} %get-tuple-element.31, bf16[1368,128]{1,0:T(8,128)(2,1)} %collective-permute-done.7, f32[1368,128]{1,0:T(8,128)S(1)} %get-tuple-element.33, ...), kind=kLoop, calls=%fused_computation.4 | loop fusion | flops 2101248 | bytes 3502082 | tf_op jit(solution)/shard_map/convert_element_type | solution.py:364
  88.0 0.7 collective-permute-start.10
  88.7 5.0 %collective-permute-start.13 = (bf16[1368,128]{1,0:T(8,128)(2,1)}, bf16[1368,128]{1,0:T(8,128)(2,1)S(1)}, u32[]{:S(2)}, u32[]{:S(2)}) collective-permute-start(bf16[1368,128]{1,0:T(8,128)(2,1)} %get-tuple-element.42), channel_id=1, source_target_pairs={{0,4},{4,8},{1,5},{5,9},{2,6},{6,10},{3,7},{7,11},{16,20},{20,24},... | collective-permute-start | bytes 1050632 | tf_op jit(solution)/shard_map/ppermute | solution.py:365
  93.7 0.6 collective-permute-start.11
  94.3 0.0 collective-permute-done.6
  94.3 0.0 collective-permute-done.10
  94.3 5.4 %collective-permute-done.13 = bf16[1368,128]{1,0:T(8,128)(2,1)S(1)} collective-permute-done((bf16[1368,128]{1,0:T(8,128)(2,1)}, bf16[1368,128]{1,0:T(8,128)(2,1)S(1)}, u32[]{:S(2)}, u32[]{:S(2)}) %collective-permute-start.13) | collective-permute-done | bytes 350240 | tf_op jit(solution)/shard_map/ppermute | solution.py:365
  99.8 1.5 %fusion.1 = (bf16[1368,128]{1,0:T(8,128)(2,1)S(1)}, bf16[1368,128]{1,0:T(8,128)(2,1)S(1)}) fusion(bf16[1368,128]{1,0:T(8,128)(2,1)S(1)} %collective-permute-done.13, f32[1368,128]{1,0:T(8,128)S(1)} %get-tuple-element.29, bf16[1368,128]{1,0:T(8,128)(2,1)} %collective-permute-done.6, pred[]{:T(512)S(6)} %eq.14, pred[]{:T(512)S(6)} %eq.13, ...), kind=kLoop, calls=%fused_computation.2 | loop fusion | flops 2101248 | bytes 3502082 | tf_op jit(solution)/shard_map/convert_element_type | solution.py:364
  101.3 6.9 %collective-permute-start.14 = (bf16[1368,128]{1,0:T(8,128)(2,1)S(1)}, bf16[1368,128]{1,0:T(8,128)(2,1)S(1)}, u32[]{:S(2)}, u32[]{:S(2)}) collective-permute-start(bf16[1368,128]{1,0:T(8,128)(2,1)S(1)} %get-tuple-element.44), channel_id=1, source_target_pairs={{0,4},{4,8},{8,12},{1,5},{5,9},{9,13},{2,6},{6,10},{10,14},{3,7},{... | collective-permute-start | bytes 1050632 | tf_op jit(solution)/shard_map/ppermute | solution.py:365
  108.2 1.3 collective-permute-start.15
  109.5 0.0 collective-permute-done.11
  109.6 3.7 %collective-permute-done.14 = bf16[1368,128]{1,0:T(8,128)(2,1)S(1)} collective-permute-done((bf16[1368,128]{1,0:T(8,128)(2,1)S(1)}, bf16[1368,128]{1,0:T(8,128)(2,1)S(1)}, u32[]{:S(2)}, u32[]{:S(2)}) %collective-permute-start.14) | collective-permute-done | bytes 350240 | tf_op jit(solution)/shard_map/ppermute | solution.py:365
  113.2 4.8 %collective-permute-done.15 = bf16[1368,128]{1,0:T(8,128)(2,1)S(1)} collective-permute-done((bf16[1368,128]{1,0:T(8,128)(2,1)S(1)}, bf16[1368,128]{1,0:T(8,128)(2,1)S(1)}, u32[]{:S(2)}, u32[]{:S(2)}) %collective-permute-start.15) | collective-permute-done | bytes 350240 | tf_op jit(solution)/shard_map/ppermute | solution.py:365
  118.0 2.1 %add_multiply_fusion = f32[1368,128]{1,0:T(8,128)} fusion(bf16[1368,128]{1,0:T(8,128)(2,1)S(1)} %collective-permute-done.15, bf16[1368,128]{1,0:T(8,128)(2,1)S(1)} %collective-permute-done.14, f32[1368,128]{1,0:T(8,128)} %copy-done.11, bf16[1368,128]{1,0:T(8,128)(2,1)S(1)} %collective-permute-done.11), kind=kLoop, calls=%fused_computation.3 | loop fusion | flops 1225728 | bytes 2451456 | tf_op jit(solution)/shard_map/mul | solution.py:368
  120.1 0.0 copy-done.5
  120.2 1.5 %copy-done.7 = bf16[16,240,256]{2,1,0:T(8,128)(2,1)S(1)} copy-done((bf16[16,240,256]{2,1,0:T(8,128)(2,1)S(1)}, bf16[16,240,256]{2,1,0:T(8,128)(2,1)}, u32[]{:S(2)}) %copy-start.7) | copy-done | bytes 1966104
  121.7 1.2 copy-done.9
  122.9 7.7 %messages.1 = bf16[128,3712]{1,0:T(8,128)(2,1)} custom-call(bf16[21888,128]{1,0:T(8,128)(2,1)} %all-gather.2.cloned.1.call-done.w_ref, bf16[128,3712]{1,0:T(8,128)(2,1)S(1)} %copy-done.5, bf16[256,3712]{1,0:T(8,128)(2,1)S(1)} %copy-done.1, bf16[8,240,256]{2,1,0:T(8,128)(2,1)S(1)} %copy-done.9, bf16[16,240,256]{2,1,0:T(8,128)(2,1)S(1)} %copy-done.7, ...), custom_call_target="tpu_custom_call" | custom-call | tf_op jit(solution)/shard_map/messages/pallas_call | solution.py:372
  (25 shorter events, 0.0 us)
Async XLA Ops:
  7.2 113.0 %all-gather.2.cloned.1.call-start = ((), (), s32[]{:S(2)}) async-start(), calls=%async_computation | async-start | bytes 5953536 | tf_op jit(solution)/shard_map/all_gather | solution.py:296
  7.9 1.2 copy-start.10
  9.1 0.7 copy-start.16
  9.8 0.7 copy-start.17
  10.4 0.7 copy-start.18
  11.1 0.7 copy-start.19
  12.4 13.7 %collective-permute-start.1 = (bf16[32,3840]{1,0:T(8,128)(2,1)S(1)}, bf16[32,3840]{1,0:T(8,128)(2,1)S(1)}, u32[]{:S(2)}, u32[]{:S(2)}) collective-permute-start(bf16[32,3840]{1,0:T(8,128)(2,1)S(1)} %get-tuple-element.24), channel_id=1, source_target_pairs={{2,0},{3,1},{4,2},{5,3},{6,4},{7,5},{10,8},{11,9},{12,10},{13,11},... | collective-permute-start | bytes 737288 | tf_op jit(solution)/shard_map/ppermute | solution.py:291
  13.7 12.4 %collective-permute-start.2 = (bf16[32,3840]{1,0:T(8,128)(2,1)S(1)}, bf16[32,3840]{1,0:T(8,128)(2,1)S(1)}, u32[]{:S(2)}, u32[]{:S(2)}) collective-permute-start(bf16[32,3840]{1,0:T(8,128)(2,1)S(1)} %get-tuple-element.25), channel_id=1, source_target_pairs={{1,0},{2,1},{3,2},{4,3},{5,4},{6,5},{7,6},{9,8},{10,9},{11,10},{12... | collective-permute-start | bytes 737288 | tf_op jit(solution)/shard_map/ppermute | solution.py:291
  15.0 11.1 %collective-permute-start.3 = (bf16[32,3840]{1,0:T(8,128)(2,1)S(1)}, bf16[32,3840]{1,0:T(8,128)(2,1)S(1)}, u32[]{:S(2)}, u32[]{:S(2)}) collective-permute-start(bf16[32,3840]{1,0:T(8,128)(2,1)S(1)} %get-tuple-element.26), channel_id=1, source_target_pairs={{0,1},{1,2},{2,3},{3,4},{4,5},{5,6},{6,7},{8,9},{9,10},{10,11},{11... | collective-permute-start | bytes 737288 | tf_op jit(solution)/shard_map/ppermute | solution.py:291
  18.1 17.4 %collective-permute-start.4 = (bf16[32,3840]{1,0:T(8,128)(2,1)S(1)}, bf16[32,3840]{1,0:T(8,128)(2,1)S(1)}, u32[]{:S(2)}, u32[]{:S(2)}) collective-permute-start(bf16[32,3840]{1,0:T(8,128)(2,1)S(1)} %get-tuple-element.27), channel_id=1, source_target_pairs={{0,2},{1,3},{2,4},{3,5},{4,6},{5,7},{8,10},{9,11},{10,12},{11,13},... | collective-permute-start | bytes 737288 | tf_op jit(solution)/shard_map/ppermute | solution.py:291
  35.5 1.2 copy-start.2
  39.4 1.3 copy-start.6
  40.7 9.9 %copy-start.12 = (bf16[128,128]{1,0:T(8,128)(2,1)}, bf16[128,128]{1,0:T(8,128)(2,1)S(1)}, u32[]{:S(2)}) copy-start(bf16[128,128]{1,0:T(8,128)(2,1)S(1)} %get-tuple-element.39.refs_5_) | copy-start | bytes 98308
  40.7 9.9 %copy-start = (bf16[256,3712]{1,0:T(8,128)(2,1)}, bf16[256,3712]{1,0:T(8,128)(2,1)S(1)}, u32[]{:S(2)}) copy-start(bf16[256,3712]{1,0:T(8,128)(2,1)S(1)} %get-tuple-element.28.refs_3_.refs_1_) | copy-start | bytes 5701636
  40.7 9.9 %collective-permute-start.5 = (bf16[256,3712]{1,0:T(8,128)(2,1)S(1)}, bf16[256,3712]{1,0:T(8,128)(2,1)S(1)}, u32[]{:S(2)}, u32[]{:S(2)}) collective-permute-start(bf16[256,3712]{1,0:T(8,128)(2,1)S(1)} %get-tuple-element.28.refs_3_.refs_1_), channel_id=1, source_target_pairs={{0,1},{1,0},{2,3},{3,2},{4,5},{5,4},{6,7},{7,6},{8,9},{9,8},{10,11... | collective-permute-start | bytes 5701640 | tf_op jit(solution)/shard_map/ppermute | solution.py:294
  43.0 1.2 copy-start.3
  46.2 1.0 copy-start.8
  47.2 0.6 copy-start.14
  47.8 11.9 %copy-start.4 = (bf16[128,3712]{1,0:T(8,128)(2,1)}, bf16[128,3712]{1,0:T(8,128)(2,1)S(1)}, u32[]{:S(2)}) copy-start(bf16[128,3712]{1,0:T(8,128)(2,1)S(1)} %get-tuple-element.23.refs_1_.refs_0_) | copy-start | bytes 2850820
  47.8 2.8 %collective-permute-start = (bf16[128,3712]{1,0:T(8,128)(2,1)S(1)}, bf16[128,3712]{1,0:T(8,128)(2,1)S(1)}, u32[]{:S(2)}, u32[]{:S(2)}) collective-permute-start(bf16[128,3712]{1,0:T(8,128)(2,1)S(1)} %get-tuple-element.23.refs_1_.refs_0_), channel_id=1, source_target_pairs={{0,1},{1,0},{2,3},{3,2},{4,5},{5,4},{6,7},{7,6},{8,9},{9,8},{10,11... | collective-permute-start | bytes 2850824 | tf_op jit(solution)/shard_map/ppermute | solution.py:294
  50.6 1.4 copy-start.20
  59.7 0.9 copy-start.11
  60.5 11.8 %collective-permute-start.8 = (bf16[1368,128]{1,0:T(8,128)(2,1)S(1)}, bf16[1368,128]{1,0:T(8,128)(2,1)S(1)}, u32[]{:S(2)}, u32[]{:S(2)}) collective-permute-start(bf16[1368,128]{1,0:T(8,128)(2,1)S(1)} %get-tuple-element.34), channel_id=1, source_target_pairs={{0,2},{2,0},{1,3},{3,1},{4,6},{6,4},{5,7},{7,5},{8,10},{10,8},{9,1... | collective-permute-start | bytes 1050632 | tf_op jit(solution)/shard_map/ppermute | solution.py:349
  63.3 17.5 %collective-permute-start.7 = (bf16[1368,128]{1,0:T(8,128)(2,1)S(1)}, bf16[1368,128]{1,0:T(8,128)(2,1)}, u32[]{:S(2)}, u32[]{:S(2)}) collective-permute-start(bf16[1368,128]{1,0:T(8,128)(2,1)S(1)} %get-tuple-element.32), channel_id=1, source_target_pairs={{0,2},{2,0},{1,3},{3,1},{4,6},{6,4},{5,7},{7,5},{8,10},{10,8},{9,1... | collective-permute-start | bytes 1050632 | tf_op jit(solution)/shard_map/ppermute | solution.py:349
  73.2 12.5 %collective-permute-start.12 = (bf16[1368,128]{1,0:T(8,128)(2,1)}, bf16[1368,128]{1,0:T(8,128)(2,1)}, u32[]{:S(2)}, u32[]{:S(2)}) collective-permute-start(bf16[1368,128]{1,0:T(8,128)(2,1)} %fusion.2), channel_id=1, source_target_pairs={{0,4},{1,5},{2,6},{3,7},{16,20},{17,21},{18,22},{19,23}} | collective-permute-start | bytes 1050632 | tf_op jit(solution)/shard_map/ppermute | solution.py:365
  79.4 6.3 %collective-permute-start.9 = (bf16[1368,128]{1,0:T(8,128)(2,1)}, bf16[1368,128]{1,0:T(8,128)(2,1)}, u32[]{:S(2)}, u32[]{:S(2)}) collective-permute-start(bf16[1368,128]{1,0:T(8,128)(2,1)} %fusion.2), channel_id=1, source_target_pairs={{12,8},{13,9},{14,10},{15,11},{28,24},{29,25},{30,26},{31,27}} | collective-permute-start | bytes 1050632 | tf_op jit(solution)/shard_map/ppermute | solution.py:365
  80.8 13.6 %collective-permute-start.6 = (bf16[1368,128]{1,0:T(8,128)(2,1)S(1)}, bf16[1368,128]{1,0:T(8,128)(2,1)}, u32[]{:S(2)}, u32[]{:S(2)}) collective-permute-start(bf16[1368,128]{1,0:T(8,128)(2,1)S(1)} %get-tuple-element.30), channel_id=1, source_target_pairs={{0,2},{2,0},{1,3},{3,1},{4,6},{6,4},{5,7},{7,5},{8,10},{10,8},{9,1... | collective-permute-start | bytes 1050632 | tf_op jit(solution)/shard_map/ppermute | solution.py:349
  88.0 6.3 %collective-permute-start.10 = (bf16[1368,128]{1,0:T(8,128)(2,1)}, bf16[1368,128]{1,0:T(8,128)(2,1)S(1)}, u32[]{:S(2)}, u32[]{:S(2)}) collective-permute-start(bf16[1368,128]{1,0:T(8,128)(2,1)} %get-tuple-element.43), channel_id=1, source_target_pairs={{8,4},{12,8},{9,5},{13,9},{10,6},{14,10},{11,7},{15,11},{24,20},{2... | collective-permute-start | bytes 1050632 | tf_op jit(solution)/shard_map/ppermute | solution.py:365
  88.7 11.1 %collective-permute-start.13 = (bf16[1368,128]{1,0:T(8,128)(2,1)}, bf16[1368,128]{1,0:T(8,128)(2,1)S(1)}, u32[]{:S(2)}, u32[]{:S(2)}) collective-permute-start(bf16[1368,128]{1,0:T(8,128)(2,1)} %get-tuple-element.42), channel_id=1, source_target_pairs={{0,4},{4,8},{1,5},{5,9},{2,6},{6,10},{3,7},{7,11},{16,20},{20,24},... | collective-permute-start | bytes 1050632 | tf_op jit(solution)/shard_map/ppermute | solution.py:365
  93.7 15.8 %collective-permute-start.11 = (bf16[1368,128]{1,0:T(8,128)(2,1)}, bf16[1368,128]{1,0:T(8,128)(2,1)S(1)}, u32[]{:S(2)}, u32[]{:S(2)}) collective-permute-start(bf16[1368,128]{1,0:T(8,128)(2,1)} %get-tuple-element.41), channel_id=1, source_target_pairs={{0,2},{2,0},{1,3},{3,1},{4,6},{6,4},{5,7},{7,5},{8,10},{10,8},{9,1... | collective-permute-start | bytes 1050632 | tf_op jit(solution)/shard_map/ppermute | solution.py:349
  99.8 20.4 %copy-start.5 = (bf16[128,3712]{1,0:T(8,128)(2,1)S(1)}, bf16[128,3712]{1,0:T(8,128)(2,1)}, u32[]{:S(2)}) copy-start(bf16[128,3712]{1,0:T(8,128)(2,1)} %copy-done.4) | copy-start | bytes 2850820
  101.3 18.9 %copy-start.1 = (bf16[256,3712]{1,0:T(8,128)(2,1)S(1)}, bf16[256,3712]{1,0:T(8,128)(2,1)}, u32[]{:S(2)}) copy-start(bf16[256,3712]{1,0:T(8,128)(2,1)} %copy-done) | copy-start | bytes 5701636
  101.3 18.9 %copy-start.13 = (bf16[128,128]{1,0:T(8,128)(2,1)S(1)}, bf16[128,128]{1,0:T(8,128)(2,1)}, u32[]{:S(2)}) copy-start(bf16[128,128]{1,0:T(8,128)(2,1)} %copy-done.12) | copy-start | bytes 98308
  101.3 18.9 %copy-start.15 = (bf16[64,128]{1,0:T(8,128)(2,1)S(1)}, bf16[64,128]{1,0:T(8,128)(2,1)}, u32[]{:S(2)}) copy-start(bf16[64,128]{1,0:T(8,128)(2,1)} %copy-done.14) | copy-start | bytes 49156
  101.3 11.9 %collective-permute-start.14 = (bf16[1368,128]{1,0:T(8,128)(2,1)S(1)}, bf16[1368,128]{1,0:T(8,128)(2,1)S(1)}, u32[]{:S(2)}, u32[]{:S(2)}) collective-permute-start(bf16[1368,128]{1,0:T(8,128)(2,1)S(1)} %get-tuple-element.44), channel_id=1, source_target_pairs={{0,4},{4,8},{8,12},{1,5},{5,9},{9,13},{2,6},{6,10},{10,14},{3,7},{... | collective-permute-start | bytes 1050632 | tf_op jit(solution)/shard_map/ppermute | solution.py:365
  108.2 9.7 %collective-permute-start.15 = (bf16[1368,128]{1,0:T(8,128)(2,1)S(1)}, bf16[1368,128]{1,0:T(8,128)(2,1)S(1)}, u32[]{:S(2)}, u32[]{:S(2)}) collective-permute-start(bf16[1368,128]{1,0:T(8,128)(2,1)S(1)} %get-tuple-element.45), channel_id=1, source_target_pairs={{4,0},{8,4},{12,8},{5,1},{9,5},{13,9},{6,2},{10,6},{14,10},{7,3},{... | collective-permute-start | bytes 1050632 | tf_op jit(solution)/shard_map/ppermute | solution.py:365
  120.2 1.5 %copy-start.7 = (bf16[16,240,256]{2,1,0:T(8,128)(2,1)S(1)}, bf16[16,240,256]{2,1,0:T(8,128)(2,1)}, u32[]{:S(2)}) copy-start(bf16[16,240,256]{2,1,0:T(8,128)(2,1)} %copy-done.6) | copy-start | bytes 5898244
  121.7 1.2 copy-start.9
Sparse Core Ops, SparseCore 0:
  10.2 66.9 all-gather.1

commit v3 on v2

--- a/solution.py
+++ b/solution.py
@@ -14,10 +14,6 @@
 F32 = jnp.float32
 BF16 = jnp.bfloat16
 ALL = ("z", "x", "core")
-
-
-def params(mib):
-    return pltpu.CompilerParams(vmem_limit_bytes=mib * 1024 * 1024)
 
 
 def dot(a, b):
@@ -141,20 +137,8 @@
     build(tabt_ref, rot_hot, matst_ref, tmp_ref)
 
 
-def rank(n_z, z, target):
-    order = sorted(range(n_z), key=lambda t: (-abs(t - z), -t))
-    return order.index(target)
-
-
-def by_rank(n_z, i):
-    return [next(t for t in range(n_z) if rank(n_z, z, t) == i) for z in range(n_z)]
-
-
-def choose(z, values):
-    out = jnp.int32(values[0])
-    for at in range(1, len(values)):
-        out = jnp.where(z == at, jnp.int32(values[at]), out)
-    return out
+def shifts(n_z):
+    return sorted(range(n_z), key=lambda i: (i == 0, abs(i - n_z // 2)))
 
 
 def grad_kernel(n_z, n_x, pos_ref, *refs):
@@ -195,9 +179,8 @@
     rows = outs[0].shape[0]
     at_out = 0
     for o in list(range(1, n_x)) + [0]:
-        for i in range(n_z):
-            target = choose(z, by_rank(n_z, i))
-            start = ((target * n_x + (x + o) % n_x) * 2 + core) * rows
+        for i in shifts(n_z):
+            start = (((z + i) % n_z * n_x + (x + o) % n_x) * 2 + core) * rows
             if rows % 8 == 0:
                 start = pl.multiple_of(start, 8)
             ref = outs[at_out]
@@ -205,14 +188,21 @@
             at_out += 1
 
 
-def message_kernel(w_ref, *refs):
-    both, mats, hots = refs[0:2], refs[2:4], refs[4:6]
-    out_ref, flat, in_ref, res_ref, wide_ref = refs[6:]
+def message_kernel(rows, pos_ref, *refs):
+    pieces, both, mats, hots = refs[:4], refs[4:6], refs[6:8], refs[8:10]
+    out_ref, flat, in_ref, res_ref, wide_ref = refs[10:]
     n = out_ref.shape[0]
     slots = in_ref.shape[1]
-    part = w_ref.shape[0] // 16
-    for p in range(16):
-        flat[p * part : (p + 1) * part, :] = w_ref[p * part : (p + 1) * part, :].astype(F32)
+    group, core = pos_ref[0], pos_ref[1]
+    for at, ref in enumerate(pieces):
+        which = group if at < 2 else 1 - group
+        who = core if at % 2 == 0 else 1 - core
+        size = ref.shape[1]
+        for chip in range(ref.shape[0]):
+            start = (chip * 2 + who) * rows + which * (rows - size)
+            if rows % 8 == 0:
+                start = pl.multiple_of(start, 8)
+            flat[pl.ds(start, size), :] = ref[chip].astype(F32)
 
     def h(first, end):
         return jnp.concatenate(
@@ -268,6 +258,25 @@
     return jax.ShapeDtypeStruct(dims, kind)
 
 
+def whole(like):
+    zeros = (0,) * len(like.shape)
+    return pl.BlockSpec(like.shape, lambda i: zeros, pipeline_mode=pl.Buffered(1))
+
+
+def call(kernel, name, mib, outs, operands, scratch=(), numbers=None):
+    first = [] if numbers is None else [pl.BlockSpec(memory_space=pltpu.SMEM)]
+    return pl.pallas_call(
+        kernel,
+        grid=(1,),
+        out_shape=outs,
+        in_specs=first + [whole(v) for v in operands],
+        out_specs=[whole(o) for o in outs],
+        scratch_shapes=list(scratch),
+        compiler_params=pltpu.CompilerParams(vmem_limit_bytes=mib * 1024 * 1024),
+        name=name,
+    )(*(() if numbers is None else (numbers,)), *operands)
+
+
 def on_device(
     n_z, n_x, node_feats, node_grad, flat_params, rot_table, edge_src, edge_dst, edge_rot,
     edge_owner,
@@ -280,7 +289,6 @@
     n_rot = rot_table.shape[0]
     z, x, core = (lax.axis_index(a) for a in ALL)
     me = dp_index(n_x)
-    vmem = pl.BlockSpec(memory_space=pltpu.VMEM)
     smem = pl.BlockSpec(memory_space=pltpu.SMEM)
 
     def shift(block, step):
@@ -293,17 +301,20 @@
     def swap(block):
         return lax.ppermute(block, "core", [(0, 1), (1, 0)])
 
-    weights = lax.all_gather(flat_params, ALL, axis=0, tiled=True)
+    group = lax.axis_index("groups")
+    piece = -(-rows // 32) * 16
+    part = lax.dynamic_slice_in_dim(flat_params, group * (rows - piece), piece, 0)
+    gathered = lax.all_gather(part, ("z", "x"), axis=0)
+    crossed = lax.ppermute(gathered, "groups", [(0, 1), (1, 0)])
+    weights = [gathered, swap(gathered), crossed, swap(crossed)]
 
     row = lambda v: v.reshape(1, n)
-    here, *outbound = pl.pallas_call(
-        send_kernel,
-        out_shape=[shape((n // 2, width + 128), BF16)] + [shape((cap, width + 128), BF16)] * 4,
-        in_specs=[smem] + [vmem] * 5,
-        out_specs=[vmem] * 5,
-        compiler_params=params(32),
-        name="send",
-    )(me.reshape(1), row(edge_owner), row(edge_src), row(edge_dst), row(edge_rot), node_feats)
+    here, *outbound = call(
+        send_kernel, "send", 60,
+        [shape((n // 2, width + 128), BF16)] + [shape((cap, width + 128), BF16)] * 4,
+        [row(edge_owner), row(edge_src), row(edge_dst), row(edge_rot), node_feats],
+        numbers=me.reshape(1),
+    )
     arrived = [shift(r, s) for r, s in zip(outbound, STEPS)]
 
     tab = rot_table.transpose(1, 0, 2).reshape(K * n_rot, K)
@@ -311,76 +322,63 @@
 
     def rotate(rows_in, name):
         slots = sum(r.shape[0] for r in rows_in)
-        return pl.pallas_call(
-            lambda *refs: rotate_kernel(len(rows_in), *refs),
-            out_shape=[
+        return call(
+            lambda *refs: rotate_kernel(len(rows_in), *refs), name, 60,
+            [
                 shape((2 * slots, width), BF16), shape((slots // 8, 240, 256), BF16),
                 shape((slots, n), BF16),
             ],
-            in_specs=[vmem] * (len(rows_in) + 3),
-            out_specs=[vmem] * 3,
-            scratch_shapes=[
+            [*rows_in, tab, tabt, node_grad],
+            [
                 pltpu.VMEM((slots // 8, 240, 256), BF16), pltpu.VMEM((30, slots, 256), F32),
                 pltpu.VMEM((32, slots, 256), F32), pltpu.VMEM((30, slots, 256), F32),
             ],
-            compiler_params=params(40),
-            name=name,
-        )(*rows_in, tab, tabt, node_grad)
+        )
 
     both_near, matst_near, hot_near = rotate([here], "rotate_near")
     both_near_other = swap(both_near)
+    arrived, both_near, matst_near, hot_near = lax.optimization_barrier(
+        (arrived, both_near, matst_near, hot_near)
+    )
     both_far, matst_far, hot_far = rotate(arrived, "rotate_far")
     both_far_other = swap(both_far)
 
     n_send = n_z * (n_x - 1)
-    blocks = pl.pallas_call(
-        lambda *refs: grad_kernel(n_z, n_x, *refs),
-        out_shape=[shape((rows, 128), BF16)] * n_send + [shape((rows, 128), F32)] * n_z,
-        in_specs=[smem] + [vmem] * 4,
-        out_specs=[vmem] * (n_send + n_z),
-        scratch_shapes=[pltpu.VMEM((rows * n_dp, 128), F32)],
-        compiler_params=params(48),
-        name="weight_terms",
-    )(jnp.stack([z, x, core]), both_near, both_near_other, both_far, both_far_other)
-    sums = []
-    for i in range(n_z):
-        total = blocks[n_send + i]
+    blocks = call(
+        lambda *refs: grad_kernel(n_z, n_x, *refs), "weight_terms", 60,
+        [shape((rows, 128), BF16)] * n_send + [shape((rows, 128), F32)] * n_z,
+        [both_near, both_near_other, both_far, both_far_other],
+        [pltpu.VMEM((rows * n_dp, 128), F32)],
+        numbers=jnp.stack([z, x, core]),
+    )
+    arrived = []
+    for at, i in enumerate(shifts(n_z)):
+        total = blocks[n_send + at]
         for o in range(1, n_x):
-            got_part = lax.ppermute(
-                blocks[(o - 1) * n_z + i], "x", [(s, (s + o) % n_x) for s in range(n_x)]
+            got = lax.ppermute(
+                blocks[(o - 1) * n_z + at], "x", [(s, (s + o) % n_x) for s in range(n_x)]
             )
-            total = total + got_part.astype(F32)
-        sums.append(total)
-    result = sums[n_z - 1]
-    for way in (1, -1):
-        arrived = None
-        for k in range(n_z - 1, 0, -1):
-            senders = [s for s in range(n_z) if 0 <= s + way * k < n_z]
-            term = sums[rank(n_z, senders[0], senders[0] + way * k)]
-            for s in senders[1:]:
-                term = jnp.where(z == s, sums[rank(n_z, s, s + way * k)], term)
-            if arrived is not None:
-                term = term + arrived.astype(F32)
-            term = term.astype(BF16)
-            arrived = lax.ppermute(term, "z", [(s, s + way) for s in senders])
-        if arrived is not None:
-            result = result + arrived.astype(F32)
+            total = total + got.astype(F32)
+        if i:
+            term = total.astype(BF16)
+            arrived.append(lax.ppermute(term, "z", [(s, (s + i) % n_z) for s in range(n_z)]))
+    result = total
+    for got in arrived:
+        result = result + got.astype(F32)
     weight_grad = result * (1.0 / math.sqrt(n * n_dp))
 
-    weights, _ = lax.optimization_barrier((weights, term))
+    weights[3], _ = lax.optimization_barrier((weights[3], term))
     slots = n // 2 + 4 * cap
-    node_out = pl.pallas_call(
-        message_kernel,
-        out_shape=shape((n, width), BF16),
-        in_specs=[vmem] * 7,
-        out_specs=vmem,
-        scratch_shapes=[
+    (node_out,) = call(
+        lambda *refs: message_kernel(rows, *refs), "messages", 60,
+        [shape((n, width), BF16)],
+        [*weights, both_near, both_far, matst_near, matst_far, hot_near, hot_far],
+        [
             pltpu.VMEM((rows * n_dp, 128), F32), pltpu.VMEM((32, slots, 128), F32),
             pltpu.VMEM((30, slots, 128), F32), pltpu.VMEM((slots, width), BF16),
         ],
-        compiler_params=params(48),
-        name="messages",
-    )(weights, both_near, both_far, matst_near, matst_far, hot_near, hot_far)
+        numbers=jnp.stack([group, core]),
+    )
     return (node_out, weight_grad)
 
 

time: 138 us -> 140 us (1.014)
  waiting for transfers between devices: 39.8 us -> 58.1 us
  starting transfers between devices: 39.1 us -> 24 us
  Pallas kernels: 20.7 us -> 32.5 us
  local copies, waits for them, and re-layouts: 16.6 us -> 7.39 us
  other arithmetic: 6.94 us -> 3.65 us
    all_gather x1, waiting for transfers between devices: 0.01 us -> 17 us  [on_device(): gathered = lax.all_gather(part, ('z', 'x'), axis=0)]
    ppermute x10 -> x8, starting transfers between devices: 25 us -> 10.5 us  [the longest x3 4.89 us: on_device(): lax.ppermute(term, 'z', [(s, (s + i) % n_z) for s in range(n_z)])]
    pallas_call x5, Pallas kernels: 20.7 us -> 32.5 us  [call(): pl.pallas_call(kernel, grid=(1,), out_shape=outs, in_specs=first + [whole...]
    ppermute x10 -> x8, waiting for transfers between devices: 27.7 us -> 37.6 us  [the longest x4 23.3 us: on_device(): lax.ppermute(blocks[(o - 1) * n_z + at], 'x', [(s, (s + o) % n_x) for s i...]
    unnamed x42 -> x26, local copies, waits for them, and re-layouts: 14.1 us -> 4.46 us
    ppermute x4, waiting for transfers between devices: 9.34 us -> 3.54 us  [shift(): return lax.ppermute(block, ALL, route)]
    convert_element_type x3, other arithmetic: 4.72 us -> 1.35 us  [on_device(): term = total.astype(BF16)]
    ppermute x2 -> x4, waiting for transfers between devices: 2.07 us -> 0.01 us  [swap(): return lax.ppermute(block, 'core', [(0, 1), (1, 0)])]
  transfers between devices with their start and end apart: 17 -> 17, of which waited for: 7 -> 8; matrix products, arithmetic and copies ran while one was open for 7% -> 4% of each run, Pallas kernels for 9% -> 14%
where the time goes in v3:
time: 140 us
  waiting for transfers between devices  58.1 us (42%)
  Pallas kernels  32.5 us (23%)
  starting transfers between devices  24 us (17%)
  between operations  14.2 us (10%)
  local copies, waits for them, and re-layouts  7.39 us (5%)
  other arithmetic  3.65 us (3%)
    pallas_call x5, Pallas kernels, call(): pl.pallas_call(kernel, grid=(1,), out_shape=outs, in_specs=first + [whole...  32.5 us
    ppermute x4, waiting for transfers between devices, on_device(): lax.ppermute(blocks[(o - 1) * n_z + at], 'x', [(s, (s + o) % n_x) for s i...  23.3 us
    all_gather x1, waiting for transfers between devices, on_device(): gathered = lax.all_gather(part, ('z', 'x'), axis=0)  17 us
    ppermute x3, waiting for transfers between devices, on_device(): lax.ppermute(term, 'z', [(s, (s + i) % n_z) for s in range(n_z)])  14.2 us
    ppermute x4, starting transfers between devices, shift(): return lax.ppermute(block, ALL, route)  11.1 us
    ppermute x3, starting transfers between devices, on_device(): lax.ppermute(term, 'z', [(s, (s + i) % n_z) for s in range(n_z)])  4.89 us
    unnamed x26, local copies, waits for them, and re-layouts  4.46 us
    ppermute x4, starting transfers between devices, on_device(): lax.ppermute(blocks[(o - 1) * n_z + at], 'x', [(s, (s + o) % n_x) for s i...  4.12 us
  transfers between devices with their start and end apart: 17, of which 8 were waited for; matrix products, arithmetic and copies ran while one was open for 4% of the time, Pallas kernels for 14%

profile of v3, /device:TPU:0, one launch (start us, length us, event | category | flops | bytes accessed | tf_op | source)
XLA Modules:
  0.0 139.9 jit_solution(16461854168951954841)
XLA Ops:
  7.2 0.0 copy-start
  7.2 0.0 copy-start.5
  7.2 0.0 all-gather.3.cloned.1.call-start
  7.2 0.9 copy-done
  8.2 0.7 constant_dynamic-slice_fusion
  8.8 0.0 all-gather.3.cloned.1.call-update
  8.9 3.1 %send.1 = (bf16[64,3840]{1,0:T(8,128)(2,1)}, bf16[32,3840]{1,0:T(8,128)(2,1)}, bf16[32,3840]{1,0:T(8,128)(2,1)}, bf16[32,3840]{1,0:T(8,128)(2,1)}, bf16[32,3840]{1,0:T(8,128)(2,1)}) custom-call(s32[1]{0:T(128)} %bitcast.5.me_ref, s32[1,128]{1,0:T(1,128)} %bitcast.23, s32[1,128]{1,0:T(1,128)} %bitcast.24, s32[1,128]{1,0:T(1,128)} %bitcast.25, ...), custom_call_target="tpu_custom_call" | custom-call | tf_op jit(solution)/shard_map/send/pallas_call | solution.py:268
  11.9 1.3 collective-permute-start.3
  13.2 1.3 collective-permute-start.4
  14.5 3.0 %collective-permute-start.5 = (bf16[32,3840]{1,0:T(8,128)(2,1)}, bf16[32,3840]{1,0:T(8,128)(2,1)S(1)}, u32[]{:S(2)}, u32[]{:S(2)}) collective-permute-start(bf16[32,3840]{1,0:T(8,128)(2,1)} %get-tuple-element.31), channel_id=1, source_target_pairs={{0,1},{1,2},{2,3},{3,4},{4,5},{5,6},{6,7},{8,9},{9,10},{10,11},{11... | collective-permute-start | bytes 737288 | tf_op jit(solution)/shard_map/ppermute | solution.py:299
  17.6 5.5 %collective-permute-start.6 = (bf16[32,3840]{1,0:T(8,128)(2,1)}, bf16[32,3840]{1,0:T(8,128)(2,1)S(1)}, u32[]{:S(2)}, u32[]{:S(2)}) collective-permute-start(bf16[32,3840]{1,0:T(8,128)(2,1)} %get-tuple-element.32), channel_id=1, source_target_pairs={{0,2},{1,3},{2,4},{3,5},{4,6},{5,7},{8,10},{9,11},{10,12},{11,13},... | collective-permute-start | bytes 737288 | tf_op jit(solution)/shard_map/ppermute | solution.py:299
  23.1 0.0 copy-done.5
  23.1 1.0 copy.10
  24.1 1.2 copy.11
  25.3 4.5 %rotate_near.1 = (bf16[128,3712]{1,0:T(8,128)(2,1)}, bf16[8,240,256]{2,1,0:T(8,128)(2,1)}, bf16[64,128]{1,0:T(8,128)(2,1)}) custom-call(bf16[64,3840]{1,0:T(8,128)(2,1)} %get-tuple-element.33.refs_0_, bf16[1856,29]{1,0:T(8,128)(2,1)} %bitcast.14, bf16[1856,29]{1,0:T(8,128)(2,1)} %bitcast.16, bf16[128,3712]{1,0:T(8,128)(2,1)} %refs_6_.1), custom_call_target="tpu_custom_call" | custom-call | tf_op jit(solution)/shard_map/rotate_near/pallas_call | solution.py:268
  29.8 0.0 collective-permute-done.3.refs_0_
  29.8 0.0 collective-permute-done.4.refs_1_
  29.8 0.0 copy-start.10
  29.9 0.0 collective-permute-done.5.refs_2_
  29.9 0.0 copy-start.11
  29.9 3.5 %collective-permute-done.6.refs_3_ = bf16[32,3840]{1,0:T(8,128)(2,1)S(1)} collective-permute-done((bf16[32,3840]{1,0:T(8,128)(2,1)}, bf16[32,3840]{1,0:T(8,128)(2,1)S(1)}, u32[]{:S(2)}, u32[]{:S(2)}) %collective-permute-start.6) | collective-permute-done | bytes 245792 | tf_op jit(solution)/shard_map/ppermute | solution.py:299
  33.4 0.0 copy-done.9
  33.4 0.0 copy-done.10
  33.4 0.0 copy-done.11
  33.4 0.7 copy-done.12
  34.1 6.0 %rotate_far.1 = (bf16[256,3712]{1,0:T(8,128)(2,1)}, bf16[16,240,256]{2,1,0:T(8,128)(2,1)}, bf16[128,128]{1,0:T(8,128)(2,1)}) custom-call(bf16[32,3840]{1,0:T(8,128)(2,1)} %copy-done.9, bf16[32,3840]{1,0:T(8,128)(2,1)} %copy-done.10, bf16[32,3840]{1,0:T(8,128)(2,1)} %copy-done.11, bf16[32,3840]{1,0:T(8,128)(2,1)} %copy-done.12, bf16[1856,29]{1,0:T(8,128)(2,1)} %bitcast.15, ...), custom_call_target="tpu_custom_call" | custom-call | tf_op jit(solution)/shard_map/rotate_far/pallas_call | solution.py:268
  40.1 2.3 %collective-permute-start.8 = (bf16[256,3712]{1,0:T(8,128)(2,1)}, bf16[256,3712]{1,0:T(8,128)(2,1)S(1)}, u32[]{:S(2)}, u32[]{:S(2)}) collective-permute-start(bf16[256,3712]{1,0:T(8,128)(2,1)} %get-tuple-element.42.refs_3_.refs_6_), channel_id=1, source_target_pairs={{0,1},{1,0},{2,3},{3,2},{4,5},{5,4},{6,7},{7,6},{8,9},{9,8},{10,11... | collective-permute-start | bytes 5701640 | tf_op jit(solution)/shard_map/ppermute | solution.py:302
  42.5 0.1 collective-permute-start.7
  42.5 17.0 %all-gather.3.cloned.1.call-done = bf16[5504,128]{1,0:T(8,128)(2,1)} async-done(((bf16[688,128]{1,0:T(8,128)(2,1)}), bf16[5504,128]{1,0:T(8,128)(2,1)}) %all-gather.3.cloned.1.call-update) | async-done | bytes 1409040 | tf_op jit(solution)/shard_map/all_gather | solution.py:307
  59.5 1.5 %collective-permute-start.1 = (bf16[8,688,128]{2,1,0:T(8,128)(2,1)}, bf16[8,688,128]{2,1,0:T(8,128)(2,1)}, u32[]{:S(2)}, u32[]{:S(2)}) collective-permute-start(bf16[8,688,128]{2,1,0:T(8,128)(2,1)} %bitcast.18), channel_id=1, source_target_pairs={{0,16},{16,0},{1,17},{17,1},{2,18},{18,2},{3,19},{19,3},{4,20},{20... | collective-permute-start | bytes 4227080 | tf_op jit(solution)/shard_map/ppermute | solution.py:308
  61.0 0.6 pad_add_fusion.1.refs_0_
  61.6 0.0 collective-permute-done.7.refs_2_
  61.6 0.0 collective-permute-done.8.refs_4_
  61.6 1.3 copy-done.2
  62.8 9.3 %weight_terms.1 = (bf16[1368,128]{1,0:T(8,128)(2,1)}, bf16[1368,128]{1,0:T(8,128)(2,1)}, bf16[1368,128]{1,0:T(8,128)(2,1)}, bf16[1368,128]{1,0:T(8,128)(2,1)}, f...) custom-call(s32[3]{0:T(128)} %pad_add_fusion.1.refs_0_, ...), custom_call_target="tpu_custom_call" | custom-call | tf_op jit(solution)/shard_map/weight_terms/pallas_call | solution.py:268
  72.2 0.5 collective-permute-start.11
  72.6 1.6 %collective-permute-start.13 = (bf16[1368,128]{1,0:T(8,128)(2,1)}, bf16[1368,128]{1,0:T(8,128)(2,1)S(1)}, u32[]{:S(2)}, u32[]{:S(2)}) collective-permute-start(bf16[1368,128]{1,0:T(8,128)(2,1)} %get-tuple-element.55), channel_id=1, source_target_pairs={{0,2},{2,0},{1,3},{3,1},{4,6},{6,4},{5,7},{7,5},{8,10},{10,8},{9,1... | collective-permute-start | bytes 1050632 | tf_op jit(solution)/shard_map/ppermute | solution.py:358
  74.2 0.4 collective-permute-start.9
  74.7 1.6 %collective-permute-start.10 = (bf16[1368,128]{1,0:T(8,128)(2,1)}, bf16[1368,128]{1,0:T(8,128)(2,1)S(1)}, u32[]{:S(2)}, u32[]{:S(2)}) collective-permute-start(bf16[1368,128]{1,0:T(8,128)(2,1)} %get-tuple-element.51), channel_id=1, source_target_pairs={{0,2},{2,0},{1,3},{3,1},{4,6},{6,4},{5,7},{7,5},{8,10},{10,8},{9,1... | collective-permute-start | bytes 1050632 | tf_op jit(solution)/shard_map/ppermute | solution.py:358
  76.3 7.3 %collective-permute-done.11 = bf16[1368,128]{1,0:T(8,128)(2,1)S(1)} collective-permute-done((bf16[1368,128]{1,0:T(8,128)(2,1)}, bf16[1368,128]{1,0:T(8,128)(2,1)S(1)}, u32[]{:S(2)}, u32[]{:S(2)}) %collective-permute-start.11) | collective-permute-done | bytes 350240 | tf_op jit(solution)/shard_map/ppermute | solution.py:358
  83.6 0.0 collective-permute-start
  83.6 1.2 add_convert_fusion.1
  84.8 6.3 %collective-permute-done.13 = bf16[1368,128]{1,0:T(8,128)(2,1)S(1)} collective-permute-done((bf16[1368,128]{1,0:T(8,128)(2,1)}, bf16[1368,128]{1,0:T(8,128)(2,1)S(1)}, u32[]{:S(2)}, u32[]{:S(2)}) %collective-permute-start.13) | collective-permute-done | bytes 350240 | tf_op jit(solution)/shard_map/ppermute | solution.py:358
  91.1 1.6 %collective-permute-start.12 = (bf16[1368,128]{1,0:T(8,128)(2,1)S(1)}, bf16[1368,128]{1,0:T(8,128)(2,1)S(1)}, u32[]{:S(2)}, u32[]{:S(2)}) collective-permute-start(bf16[1368,128]{1,0:T(8,128)(2,1)S(1)} %add_convert_fusion.1), channel_id=1, source_target_pairs={{0,8},{4,12},{8,0},{12,4},{1,9},{5,13},{9,1},{13,5},{2,10},{6,14},... | collective-permute-start | bytes 1050632 | tf_op jit(solution)/shard_map/ppermute | solution.py:364
  92.7 0.0 collective-permute-done.1.refs_3_
  92.7 0.0 collective-permute-start.2
  92.7 0.1 add_convert_fusion
  92.8 5.8 %collective-permute-done.9 = bf16[1368,128]{1,0:T(8,128)(2,1)S(1)} collective-permute-done((bf16[1368,128]{1,0:T(8,128)(2,1)}, bf16[1368,128]{1,0:T(8,128)(2,1)S(1)}, u32[]{:S(2)}, u32[]{:S(2)}) %collective-permute-start.9) | collective-permute-done | bytes 350240 | tf_op jit(solution)/shard_map/ppermute | solution.py:358
  98.6 1.4 %collective-permute-start.14 = (bf16[1368,128]{1,0:T(8,128)(2,1)S(1)}, bf16[1368,128]{1,0:T(8,128)(2,1)S(1)}, u32[]{:S(2)}, u32[]{:S(2)}) collective-permute-start(bf16[1368,128]{1,0:T(8,128)(2,1)S(1)} %add_convert_fusion), channel_id=1, source_target_pairs={{0,4},{4,8},{8,12},{12,0},{1,5},{5,9},{9,13},{13,1},{2,6},{6,10},{... | collective-permute-start | bytes 1050632 | tf_op jit(solution)/shard_map/ppermute | solution.py:364
  100.0 0.0 copy-done.7
  100.0 0.1 add_convert_fusion.2
  100.1 3.9 %collective-permute-done.10 = bf16[1368,128]{1,0:T(8,128)(2,1)S(1)} collective-permute-done((bf16[1368,128]{1,0:T(8,128)(2,1)}, bf16[1368,128]{1,0:T(8,128)(2,1)S(1)}, u32[]{:S(2)}, u32[]{:S(2)}) %collective-permute-start.10) | collective-permute-done | bytes 350240 | tf_op jit(solution)/shard_map/ppermute | solution.py:358
  104.0 1.8 %collective-permute-start.15 = (bf16[1368,128]{1,0:T(8,128)(2,1)S(1)}, bf16[1368,128]{1,0:T(8,128)(2,1)S(1)}, u32[]{:S(2)}, u32[]{:S(2)}) collective-permute-start(bf16[1368,128]{1,0:T(8,128)(2,1)S(1)} %add_convert_fusion.2), channel_id=1, source_target_pairs={{0,12},{4,0},{8,4},{12,8},{1,13},{5,1},{9,5},{13,9},{2,14},{6,2},{... | collective-permute-start | bytes 1050632 | tf_op jit(solution)/shard_map/ppermute | solution.py:364
  105.9 0.6 pad_add_fusion.refs_0_
  106.5 7.9 %collective-permute-done.12 = bf16[1368,128]{1,0:T(8,128)(2,1)S(1)} collective-permute-done((bf16[1368,128]{1,0:T(8,128)(2,1)S(1)}, bf16[1368,128]{1,0:T(8,128)(2,1)S(1)}, u32[]{:S(2)}, u32[]{:S(2)}) %collective-permute-start.12) | collective-permute-done | bytes 350240 | tf_op jit(solution)/shard_map/ppermute | solution.py:364
  114.4 0.0 collective-permute-done.14
  114.4 6.3 %collective-permute-done.15 = bf16[1368,128]{1,0:T(8,128)(2,1)S(1)} collective-permute-done((bf16[1368,128]{1,0:T(8,128)(2,1)S(1)}, bf16[1368,128]{1,0:T(8,128)(2,1)S(1)}, u32[]{:S(2)}, u32[]{:S(2)}) %collective-permute-start.15) | collective-permute-done | bytes 350240 | tf_op jit(solution)/shard_map/ppermute | solution.py:364
  120.7 1.1 add_multiply_fusion
  121.8 0.0 collective-permute-done.2.refs_4_
  121.8 0.0 collective-permute-done.refs_2_
  121.8 0.0 copy-start.3
  121.8 1.1 copy-done.4
  122.9 0.5 copy-done.3
  123.4 9.7 %messages.1 = bf16[128,3712]{1,0:T(8,128)(2,1)} custom-call(s32[2]{0:T(128)} %pad_add_fusion.refs_0_, bf16[8,688,128]{2,1,0:T(8,128)(2,1)} %bitcast.20, bf16[8,688,128]{2,1,0:T(8,128)(2,1)} %copy-done.3, bf16[8,688,128]{2,1,0:T(8,128)(2,1)} %collective-permute-done.1.refs_3_, bf16[8,688,128]{2,1,0:T(8,128)(2,1)} %copy-done.4, ...), custom_call_target="tpu_custom_call" | custom-call | tf_op jit(solution)/shard_map/messages/pallas_call | solution.py:268
  (11 shorter events, 0.0 us)
Async XLA Ops:
  7.2 1.0 copy-start
  7.2 15.9 %copy-start.5 = (bf16[64,29,29]{0,2,1:T(8,128)(2,1)S(1)}, bf16[64,29,29]{0,2,1:T(8,128)(2,1)}, u32[]{:S(2)}) copy-start(bf16[64,29,29]{0,2,1:T(8,128)(2,1)} %param.11) | copy-start | bytes 322948
  7.2 52.3 %all-gather.3.cloned.1.call-start = ((), (), s32[]{:S(2)}) async-start(), calls=%async_computation | async-start | bytes 1585152 | tf_op jit(solution)/shard_map/all_gather | solution.py:307
  11.9 17.9 %collective-permute-start.3 = (bf16[32,3840]{1,0:T(8,128)(2,1)}, bf16[32,3840]{1,0:T(8,128)(2,1)S(1)}, u32[]{:S(2)}, u32[]{:S(2)}) collective-permute-start(bf16[32,3840]{1,0:T(8,128)(2,1)} %get-tuple-element.29), channel_id=1, source_target_pairs={{2,0},{3,1},{4,2},{5,3},{6,4},{7,5},{10,8},{11,9},{12,10},{13,11},... | collective-permute-start | bytes 737288 | tf_op jit(solution)/shard_map/ppermute | solution.py:299
  13.2 16.6 %collective-permute-start.4 = (bf16[32,3840]{1,0:T(8,128)(2,1)}, bf16[32,3840]{1,0:T(8,128)(2,1)S(1)}, u32[]{:S(2)}, u32[]{:S(2)}) collective-permute-start(bf16[32,3840]{1,0:T(8,128)(2,1)} %get-tuple-element.30), channel_id=1, source_target_pairs={{1,0},{2,1},{3,2},{4,3},{5,4},{6,5},{7,6},{9,8},{10,9},{11,10},{12... | collective-permute-start | bytes 737288 | tf_op jit(solution)/shard_map/ppermute | solution.py:299
  14.5 15.3 %collective-permute-start.5 = (bf16[32,3840]{1,0:T(8,128)(2,1)}, bf16[32,3840]{1,0:T(8,128)(2,1)S(1)}, u32[]{:S(2)}, u32[]{:S(2)}) collective-permute-start(bf16[32,3840]{1,0:T(8,128)(2,1)} %get-tuple-element.31), channel_id=1, source_target_pairs={{0,1},{1,2},{2,3},{3,4},{4,5},{5,6},{6,7},{8,9},{9,10},{10,11},{11... | collective-permute-start | bytes 737288 | tf_op jit(solution)/shard_map/ppermute | solution.py:299
  17.6 15.8 %collective-permute-start.6 = (bf16[32,3840]{1,0:T(8,128)(2,1)}, bf16[32,3840]{1,0:T(8,128)(2,1)S(1)}, u32[]{:S(2)}, u32[]{:S(2)}) collective-permute-start(bf16[32,3840]{1,0:T(8,128)(2,1)} %get-tuple-element.32), channel_id=1, source_target_pairs={{0,2},{1,3},{2,4},{3,5},{4,6},{5,7},{8,10},{9,11},{10,12},{11,13},... | collective-permute-start | bytes 737288 | tf_op jit(solution)/shard_map/ppermute | solution.py:299
  29.8 3.6 %copy-start.9 = (bf16[32,3840]{1,0:T(8,128)(2,1)}, bf16[32,3840]{1,0:T(8,128)(2,1)S(1)}, u32[]{:S(2)}) copy-start(bf16[32,3840]{1,0:T(8,128)(2,1)S(1)} %collective-permute-done.3.refs_0_) | copy-start | bytes 737284
  29.8 3.6 %copy-start.10 = (bf16[32,3840]{1,0:T(8,128)(2,1)}, bf16[32,3840]{1,0:T(8,128)(2,1)S(1)}, u32[]{:S(2)}) copy-start(bf16[32,3840]{1,0:T(8,128)(2,1)S(1)} %collective-permute-done.4.refs_1_) | copy-start | bytes 737284
  29.9 3.6 %copy-start.11 = (bf16[32,3840]{1,0:T(8,128)(2,1)}, bf16[32,3840]{1,0:T(8,128)(2,1)S(1)}, u32[]{:S(2)}) copy-start(bf16[32,3840]{1,0:T(8,128)(2,1)S(1)} %collective-permute-done.5.refs_2_) | copy-start | bytes 737284
  33.4 0.7 copy-start.12
  34.1 8.3 %copy-start.1 = (bf16[128,3712]{1,0:T(8,128)(2,1)S(1)}, bf16[128,3712]{1,0:T(8,128)(2,1)}, u32[]{:S(2)}) copy-start(bf16[128,3712]{1,0:T(8,128)(2,1)} %get-tuple-element.37.refs_1_.refs_5_) | copy-start | bytes 2850820
  40.1 21.4 %collective-permute-start.8 = (bf16[256,3712]{1,0:T(8,128)(2,1)}, bf16[256,3712]{1,0:T(8,128)(2,1)S(1)}, u32[]{:S(2)}, u32[]{:S(2)}) collective-permute-start(bf16[256,3712]{1,0:T(8,128)(2,1)} %get-tuple-element.42.refs_3_.refs_6_), channel_id=1, source_target_pairs={{0,1},{1,0},{2,3},{3,2},{4,5},{5,4},{6,7},{7,6},{8,9},{9,8},{10,11... | collective-permute-start | bytes 5701640 | tf_op jit(solution)/shard_map/ppermute | solution.py:302
  42.5 19.1 %collective-permute-start.7 = (bf16[128,3712]{1,0:T(8,128)(2,1)S(1)}, bf16[128,3712]{1,0:T(8,128)(2,1)}, u32[]{:S(2)}, u32[]{:S(2)}) collective-permute-start(bf16[128,3712]{1,0:T(8,128)(2,1)S(1)} %copy-done.1), channel_id=1, source_target_pairs={{0,1},{1,0},{2,3},{3,2},{4,5},{5,4},{6,7},{7,6},{8,9},{9,8},{10,11... | collective-permute-start | bytes 2850824 | tf_op jit(solution)/shard_map/ppermute | solution.py:302
  59.5 33.2 %collective-permute-start.1 = (bf16[8,688,128]{2,1,0:T(8,128)(2,1)}, bf16[8,688,128]{2,1,0:T(8,128)(2,1)}, u32[]{:S(2)}, u32[]{:S(2)}) collective-permute-start(bf16[8,688,128]{2,1,0:T(8,128)(2,1)} %bitcast.18), channel_id=1, source_target_pairs={{0,16},{16,0},{1,17},{17,1},{2,18},{18,2},{3,19},{19,3},{4,20},{20... | collective-permute-start | bytes 4227080 | tf_op jit(solution)/shard_map/ppermute | solution.py:308
  61.6 1.3 copy-start.2
  72.1 20.5 %copy-start.8 = (f32[1368,128]{1,0:T(8,128)S(1)}, f32[1368,128]{1,0:T(8,128)}, u32[]{:S(2)}) copy-start(f32[1368,128]{1,0:T(8,128)} %get-tuple-element.54) | copy-start | bytes 2101252
  72.1 27.9 %copy-start.7 = (f32[1368,128]{1,0:T(8,128)S(1)}, f32[1368,128]{1,0:T(8,128)}, u32[]{:S(2)}) copy-start(f32[1368,128]{1,0:T(8,128)} %get-tuple-element.43) | copy-start | bytes 2101252
  72.2 11.4 %collective-permute-start.11 = (bf16[1368,128]{1,0:T(8,128)(2,1)}, bf16[1368,128]{1,0:T(8,128)(2,1)S(1)}, u32[]{:S(2)}, u32[]{:S(2)}) collective-permute-start(bf16[1368,128]{1,0:T(8,128)(2,1)} %get-tuple-element.53), channel_id=1, source_target_pairs={{0,2},{2,0},{1,3},{3,1},{4,6},{6,4},{5,7},{7,5},{8,10},{10,8},{9,1... | collective-permute-start | bytes 1050632 | tf_op jit(solution)/shard_map/ppermute | solution.py:358
  72.6 18.4 %collective-permute-start.13 = (bf16[1368,128]{1,0:T(8,128)(2,1)}, bf16[1368,128]{1,0:T(8,128)(2,1)S(1)}, u32[]{:S(2)}, u32[]{:S(2)}) collective-permute-start(bf16[1368,128]{1,0:T(8,128)(2,1)} %get-tuple-element.55), channel_id=1, source_target_pairs={{0,2},{2,0},{1,3},{3,1},{4,6},{6,4},{5,7},{7,5},{8,10},{10,8},{9,1... | collective-permute-start | bytes 1050632 | tf_op jit(solution)/shard_map/ppermute | solution.py:358
  74.2 24.3 %collective-permute-start.9 = (bf16[1368,128]{1,0:T(8,128)(2,1)}, bf16[1368,128]{1,0:T(8,128)(2,1)S(1)}, u32[]{:S(2)}, u32[]{:S(2)}) collective-permute-start(bf16[1368,128]{1,0:T(8,128)(2,1)} %get-tuple-element.44), channel_id=1, source_target_pairs={{0,2},{2,0},{1,3},{3,1},{4,6},{6,4},{5,7},{7,5},{8,10},{10,8},{9,1... | collective-permute-start | bytes 1050632 | tf_op jit(solution)/shard_map/ppermute | solution.py:358
  74.7 29.4 %collective-permute-start.10 = (bf16[1368,128]{1,0:T(8,128)(2,1)}, bf16[1368,128]{1,0:T(8,128)(2,1)S(1)}, u32[]{:S(2)}, u32[]{:S(2)}) collective-permute-start(bf16[1368,128]{1,0:T(8,128)(2,1)} %get-tuple-element.51), channel_id=1, source_target_pairs={{0,2},{2,0},{1,3},{3,1},{4,6},{6,4},{5,7},{7,5},{8,10},{10,8},{9,1... | collective-permute-start | bytes 1050632 | tf_op jit(solution)/shard_map/ppermute | solution.py:358
  83.6 38.2 %collective-permute-start = (bf16[8,688,128]{2,1,0:T(8,128)(2,1)}, bf16[8,688,128]{2,1,0:T(8,128)(2,1)S(1)}, u32[]{:S(2)}, u32[]{:S(2)}) collective-permute-start(bf16[8,688,128]{2,1,0:T(8,128)(2,1)} %bitcast.19), channel_id=1, source_target_pairs={{0,1},{1,0},{2,3},{3,2},{4,5},{5,4},{6,7},{7,6},{8,9},{9,8},{10,11... | collective-permute-start | bytes 4227080 | tf_op jit(solution)/shard_map/ppermute | solution.py:302
  84.7 36.0 %copy-start.6 = (f32[1368,128]{1,0:T(8,128)S(1)}, f32[1368,128]{1,0:T(8,128)}, u32[]{:S(2)}) copy-start(f32[1368,128]{1,0:T(8,128)} %get-tuple-element.50) | copy-start | bytes 2101252
  91.1 23.3 %collective-permute-start.12 = (bf16[1368,128]{1,0:T(8,128)(2,1)S(1)}, bf16[1368,128]{1,0:T(8,128)(2,1)S(1)}, u32[]{:S(2)}, u32[]{:S(2)}) collective-permute-start(bf16[1368,128]{1,0:T(8,128)(2,1)S(1)} %add_convert_fusion.1), channel_id=1, source_target_pairs={{0,8},{4,12},{8,0},{12,4},{1,9},{5,13},{9,1},{13,5},{2,10},{6,14},... | collective-permute-start | bytes 1050632 | tf_op jit(solution)/shard_map/ppermute | solution.py:364
  92.7 29.1 %collective-permute-start.2 = (bf16[8,688,128]{2,1,0:T(8,128)(2,1)}, bf16[8,688,128]{2,1,0:T(8,128)(2,1)S(1)}, u32[]{:S(2)}, u32[]{:S(2)}) collective-permute-start(bf16[8,688,128]{2,1,0:T(8,128)(2,1)} %collective-permute-done.1.refs_3_), channel_id=1, source_target_pairs={{0,1},{1,0},{2,3},{3,2},{4,5},{5,4},{6,7},{7,6},{8,9},{9,8},{10,11... | collective-permute-start | bytes 4227080 | tf_op jit(solution)/shard_map/ppermute | solution.py:302
  98.6 15.8 %collective-permute-start.14 = (bf16[1368,128]{1,0:T(8,128)(2,1)S(1)}, bf16[1368,128]{1,0:T(8,128)(2,1)S(1)}, u32[]{:S(2)}, u32[]{:S(2)}) collective-permute-start(bf16[1368,128]{1,0:T(8,128)(2,1)S(1)} %add_convert_fusion), channel_id=1, source_target_pairs={{0,4},{4,8},{8,12},{12,0},{1,5},{5,9},{9,13},{13,1},{2,6},{6,10},{... | collective-permute-start | bytes 1050632 | tf_op jit(solution)/shard_map/ppermute | solution.py:364
  104.0 16.7 %collective-permute-start.15 = (bf16[1368,128]{1,0:T(8,128)(2,1)S(1)}, bf16[1368,128]{1,0:T(8,128)(2,1)S(1)}, u32[]{:S(2)}, u32[]{:S(2)}) collective-permute-start(bf16[1368,128]{1,0:T(8,128)(2,1)S(1)} %add_convert_fusion.2), channel_id=1, source_target_pairs={{0,12},{4,0},{8,4},{12,8},{1,13},{5,1},{9,5},{13,9},{2,14},{6,2},{... | collective-permute-start | bytes 1050632 | tf_op jit(solution)/shard_map/ppermute | solution.py:364
  121.8 1.1 copy-start.4
  121.8 1.5 %copy-start.3 = (bf16[8,688,128]{2,1,0:T(8,128)(2,1)}, bf16[8,688,128]{2,1,0:T(8,128)(2,1)S(1)}, u32[]{:S(2)}) copy-start(bf16[8,688,128]{2,1,0:T(8,128)(2,1)S(1)} %collective-permute-done.refs_2_) | copy-start | bytes 4227076
Sparse Core Ops, SparseCore 0:
  10.2 49.2 all-gather.2

commit v4 on v3

--- a/solution.py
+++ b/solution.py
@@ -109,8 +109,8 @@
 
 
 def rotate_kernel(count, *refs):
-    raw, (tab_ref, tabt_ref, grad_ref) = refs[:count], refs[count : count + 3]
-    both_ref, matst_ref, hot_ref, mats_ref, tmp_ref, in_ref, res_ref = refs[count + 3 :]
+    raw, (tab_ref, grad_ref) = refs[:count], refs[count : count + 2]
+    both_ref, hot_ref, turn_ref, mats_ref, tmp_ref, in_ref, res_ref = refs[count + 2 :]
     n = grad_ref.shape[0]
     n_rot = tab_ref.shape[0] // K
     width = grad_ref.shape[1]
@@ -119,6 +119,7 @@
     target_hot = hot(number(ids, 0) - 1.0 == iota((slots, n), 1).astype(F32))
     rot_hot = hot(number(ids, 1) == iota((slots, n_rot), 1).astype(F32))
     hot_ref[...] = target_hot
+    turn_ref[...] = rot_hot
     for j, w in chunks():
         cols = slice(j * 128, (j + w) * 128)
         rows = joined(raw, cols).astype(F32)
@@ -134,7 +135,11 @@
         cols = slice(k * 128, (k + 1) * 128)
         both_ref[:slots, cols] = res_ref[k, :, :128].astype(BF16)
         both_ref[slots:, cols] = res_ref[k, :, 128:].astype(BF16)
-    build(tabt_ref, rot_hot, matst_ref, tmp_ref)
+
+
+def back_kernel(near_ref, far_ref, tabt_ref, near_out, far_out, near_tmp, far_tmp):
+    build(tabt_ref, near_ref[...], near_out, near_tmp)
+    build(tabt_ref, far_ref[...], far_out, far_tmp)
 
 
 def shifts(n_z):
@@ -145,8 +150,8 @@
     parts, outs, flat = refs[:4], refs[4:-1], refs[-1]
     z, x, core = pos_ref[0], pos_ref[1], pos_ref[2]
 
-    def left(first):
-        at = slice(first * 128, (first + 1) * 128)
+    def left(first, width):
+        at = slice(first * 128, (first + width) * 128)
         return [p[: p.shape[0] // 2, at] for p in parts]
 
     def right(first, width):
@@ -156,25 +161,19 @@
     def outer(lhs, rhs):
         return lax.dot_general(lhs, rhs, (((0,), (0,)), ((), ())), preferred_element_type=F32)
 
-    def emit(base, width, start, res):
+    def emit(base, width, res):
         for b in range(width):
-            flat[pl.ds(base + start * width + b, res.shape[0], stride=width), :] = res[
-                :, b * 128 : (b + 1) * 128
-            ]
-
-    rows0 = jnp.concatenate(right(0, 7), axis=0)
-    for i in range(7):
-        emit(0, 7, 128 * i, outer(jnp.concatenate(left(i), axis=0), rows0))
+            flat[pl.ds(base + b, width * 128, stride=width), :] = res[:, b * 128 : (b + 1) * 128]
+
+    emit(0, 7, outer(jnp.concatenate(left(0, 7), axis=0), jnp.concatenate(right(0, 7), axis=0)))
     base = 49 * 128
     for first, width in ((7, 6), (19, 5)):
+        lhs = jnp.concatenate(left(first, width) + left(first + width, width), axis=0)
         real, imag = right(first, width), right(first + width, width)
-        same = jnp.concatenate(real + imag, axis=0)
-        cross = jnp.concatenate(imag + [-v for v in real], axis=0)
-        for i in range(width):
-            lhs = jnp.concatenate(left(first + i) + left(first + width + i), axis=0)
-            emit(base, width, 128 * i, outer(lhs, same))
-            emit(base + width * width * 128, width, 128 * i, outer(lhs, cross))
-        base += 2 * width * width * 128
+        emit(base, width, outer(lhs, jnp.concatenate(real + imag, axis=0)))
+        base += width * width * 128
+        emit(base, width, outer(lhs, jnp.concatenate(imag + [-v for v in real], axis=0)))
+        base += width * width * 128
 
     rows = outs[0].shape[0]
     at_out = 0
@@ -188,21 +187,14 @@
             at_out += 1
 
 
-def message_kernel(rows, pos_ref, *refs):
-    pieces, both, mats, hots = refs[:4], refs[4:6], refs[6:8], refs[8:10]
-    out_ref, flat, in_ref, res_ref, wide_ref = refs[10:]
+def message_kernel(w_ref, *refs):
+    both, mats, hots = refs[0:2], refs[2:4], refs[4:6]
+    out_ref, flat, in_ref, res_ref, wide_ref = refs[6:]
     n = out_ref.shape[0]
     slots = in_ref.shape[1]
-    group, core = pos_ref[0], pos_ref[1]
-    for at, ref in enumerate(pieces):
-        which = group if at < 2 else 1 - group
-        who = core if at % 2 == 0 else 1 - core
-        size = ref.shape[1]
-        for chip in range(ref.shape[0]):
-            start = (chip * 2 + who) * rows + which * (rows - size)
-            if rows % 8 == 0:
-                start = pl.multiple_of(start, 8)
-            flat[pl.ds(start, size), :] = ref[chip].astype(F32)
+    part = w_ref.shape[0] // 16
+    for p in range(16):
+        flat[p * part : (p + 1) * part, :] = w_ref[p * part : (p + 1) * part, :].astype(F32)
 
     def h(first, end):
         return jnp.concatenate(
@@ -301,12 +293,7 @@
     def swap(block):
         return lax.ppermute(block, "core", [(0, 1), (1, 0)])
 
-    group = lax.axis_index("groups")
-    piece = -(-rows // 32) * 16
-    part = lax.dynamic_slice_in_dim(flat_params, group * (rows - piece), piece, 0)
-    gathered = lax.all_gather(part, ("z", "x"), axis=0)
-    crossed = lax.ppermute(gathered, "groups", [(0, 1), (1, 0)])
-    weights = [gathered, swap(gathered), crossed, swap(crossed)]
+    weights = lax.all_gather(flat_params, ALL, axis=0, tiled=True)
 
     row = lambda v: v.reshape(1, n)
     here, *outbound = call(
@@ -325,22 +312,20 @@
         return call(
             lambda *refs: rotate_kernel(len(rows_in), *refs), name, 60,
             [
-                shape((2 * slots, width), BF16), shape((slots // 8, 240, 256), BF16),
-                shape((slots, n), BF16),
+                shape((2 * slots, width), BF16), shape((slots, n), BF16),
+                shape((slots, n_rot), BF16),
             ],
-            [*rows_in, tab, tabt, node_grad],
+            [*rows_in, tab, node_grad],
             [
                 pltpu.VMEM((slots // 8, 240, 256), BF16), pltpu.VMEM((30, slots, 256), F32),
                 pltpu.VMEM((32, slots, 256), F32), pltpu.VMEM((30, slots, 256), F32),
             ],
         )
 
-    both_near, matst_near, hot_near = rotate([here], "rotate_near")
+    both_near, hot_near, turn_near = rotate([here], "rotate_near")
     both_near_other = swap(both_near)
-    arrived, both_near, matst_near, hot_near = lax.optimization_barrier(
-        (arrived, both_near, matst_near, hot_near)
-    )
-    both_far, matst_far, hot_far = rotate(arrived, "rotate_far")
+    arrived, both_near = lax.optimization_barrier((arrived, both_near))
+    both_far, hot_far, turn_far = rotate(arrived, "rotate_far")
     both_far_other = swap(both_far)
 
     n_send = n_z * (n_x - 1)
@@ -351,7 +336,14 @@
         [pltpu.VMEM((rows * n_dp, 128), F32)],
         numbers=jnp.stack([z, x, core]),
     )
-    arrived = []
+    turn_far, blocks = lax.optimization_barrier((turn_far, blocks))
+    matst_near, matst_far = call(
+        back_kernel, "back", 60,
+        [shape((t.shape[0] // 8, 240, 256), BF16) for t in (turn_near, turn_far)],
+        [turn_near, turn_far, tabt],
+        [pltpu.VMEM((30, t.shape[0], 256), F32) for t in (turn_near, turn_far)],
+    )
+    arrived, terms = [], []
     for at, i in enumerate(shifts(n_z)):
         total = blocks[n_send + at]
         for o in range(1, n_x):
@@ -360,25 +352,24 @@
             )
             total = total + got.astype(F32)
         if i:
-            term = total.astype(BF16)
-            arrived.append(lax.ppermute(term, "z", [(s, (s + i) % n_z) for s in range(n_z)]))
+            terms.append(total.astype(BF16))
+            arrived.append(lax.ppermute(terms[-1], "z", [(s, (s + i) % n_z) for s in range(n_z)]))
+    weights, _ = lax.optimization_barrier((weights, terms[-1]))
+    slots = n // 2 + 4 * cap
+    (node_out,) = call(
+        message_kernel, "messages", 60,
+        [shape((n, width), BF16)],
+        [weights, both_near, both_far, matst_near, matst_far, hot_near, hot_far],
+        [
+            pltpu.VMEM((rows * n_dp, 128), F32), pltpu.VMEM((32, slots, 128), F32),
+            pltpu.VMEM((30, slots, 128), F32), pltpu.VMEM((slots, width), BF16),
+        ],
+    )
+    arrived[-1], node_out = lax.optimization_barrier((arrived[-1], node_out))
     result = total
     for got in arrived:
         result = result + got.astype(F32)
     weight_grad = result * (1.0 / math.sqrt(n * n_dp))
-
-    weights[3], _ = lax.optimization_barrier((weights[3], term))
-    slots = n // 2 + 4 * cap
-    (node_out,) = call(
-        lambda *refs: message_kernel(rows, *refs), "messages", 60,
-        [shape((n, width), BF16)],
-        [*weights, both_near, both_far, matst_near, matst_far, hot_near, hot_far],
-        [
-            pltpu.VMEM((rows * n_dp, 128), F32), pltpu.VMEM((32, slots, 128), F32),
-            pltpu.VMEM((30, slots, 128), F32), pltpu.VMEM((slots, width), BF16),
-        ],
-        numbers=jnp.stack([group, core]),
-    )
     return (node_out, weight_grad)
 
 

time: 140 us -> 119 us (0.85)
  waiting for transfers between devices: 58.1 us -> 28.1 us
  starting transfers between devices: 24 us -> 31.7 us
  Pallas kernels: 32.5 us -> 34.3 us
    all_gather x1, waiting for transfers between devices: 17 us -> 0.01 us  [on_device(): weights = lax.all_gather(flat_params, ALL, axis=0, tiled=True)]
    ppermute x4 -> x3, waiting for transfers between devices: 14.2 us -> 0.01 us  [on_device(): lax.ppermute(terms[-1], 'z', [(s, (s + i) % n_z) for s in range(n_z)])]
    ppermute x4, waiting for transfers between devices: 23.3 us -> 17.2 us  [on_device(): lax.ppermute(blocks[(o - 1) * n_z + at], 'x', [(s, (s + o) % n_x) for s i...]
    ppermute x4, starting transfers between devices: 4.12 us -> 8.38 us  [on_device(): lax.ppermute(blocks[(o - 1) * n_z + at], 'x', [(s, (s + o) % n_x) for s i...]
    ppermute x4 -> x2, waiting for transfers between devices: 0.01 us -> 4.05 us  [swap(): return lax.ppermute(block, 'core', [(0, 1), (1, 0)])]
    ppermute x4 -> x3, starting transfers between devices: 6.36 us -> 9.58 us  [on_device(): lax.ppermute(terms[-1], 'z', [(s, (s + i) % n_z) for s in range(n_z)])]
    ppermute x4, waiting for transfers between devices: 3.54 us -> 6.2 us  [shift(): return lax.ppermute(block, ALL, route)]
    pallas_call x5 -> x6, Pallas kernels: 32.5 us -> 34.3 us  [call(): pl.pallas_call(kernel, grid=(1,), out_shape=outs, in_specs=first + [whole...]
  transfers between devices with their start and end apart: 17 -> 14, of which waited for: 8 -> 4; matrix products, arithmetic and copies ran while one was open for 4% -> 5% of each run, Pallas kernels for 14% -> 26%
where the time goes in v4:
time: 119 us; the launch traced here: 118 us
  Pallas kernels  34.3 us (29%)
  starting transfers between devices  31.7 us (27%)
  waiting for transfers between devices  28.1 us (24%)
  between operations  14.2 us (12%)
  local copies, waits for them, and re-layouts  6 us (5%)
  other arithmetic  4.14 us (3%)
    pallas_call x6, Pallas kernels, call(): pl.pallas_call(kernel, grid=(1,), out_shape=outs, in_specs=first + [whole...  34.3 us
    ppermute x4, waiting for transfers between devices, on_device(): lax.ppermute(blocks[(o - 1) * n_z + at], 'x', [(s, (s + o) % n_x) for s i...  17.2 us
    ppermute x4, starting transfers between devices, shift(): return lax.ppermute(block, ALL, route)  11.1 us
    ppermute x3, starting transfers between devices, on_device(): lax.ppermute(terms[-1], 'z', [(s, (s + i) % n_z) for s in range(n_z)])  9.58 us
    ppermute x4, starting transfers between devices, on_device(): lax.ppermute(blocks[(o - 1) * n_z + at], 'x', [(s, (s + o) % n_x) for s i...  8.38 us
    ppermute x4, waiting for transfers between devices, shift(): return lax.ppermute(block, ALL, route)  6.2 us
    ppermute x2, waiting for transfers between devices, swap(): return lax.ppermute(block, 'core', [(0, 1), (1, 0)])  4.05 us
    unnamed x20, local copies, waits for them, and re-layouts  2.89 us
  transfers between devices with their start and end apart: 14, of which 4 were waited for; matrix products, arithmetic and copies ran while one was open for 5% of the time, Pallas kernels for 26%

profile of v4, /device:TPU:0, one launch (start us, length us, event | category | flops | bytes accessed | tf_op | source)
XLA Modules:
  0.0 118.4 jit_solution(7017439906251926666)
XLA Ops:
  7.2 0.0 all-gather.2.cloned.1.call-start
  7.2 0.7 all-gather.2.cloned.1.call-update
  7.9 3.1 %send.1 = (bf16[64,3840]{1,0:T(8,128)(2,1)}, bf16[32,3840]{1,0:T(8,128)(2,1)}, bf16[32,3840]{1,0:T(8,128)(2,1)}, bf16[32,3840]{1,0:T(8,128)(2,1)}, bf16[32,3840]{1,0:T(8,128)(2,1)}) custom-call(s32[1]{0:T(128)} %bitcast.me_ref, s32[1,128]{1,0:T(1,128)} %bitcast.17, s32[1,128]{1,0:T(1,128)} %bitcast.18, s32[1,128]{1,0:T(1,128)} %bitcast.19, ...), custom_call_target="tpu_custom_call" | custom-call | tf_op jit(solution)/shard_map/send/pallas_call | solution.py:260
  11.0 1.3 %collective-permute-start = (bf16[32,3840]{1,0:T(8,128)(2,1)}, bf16[32,3840]{1,0:T(8,128)(2,1)S(1)}, u32[]{:S(2)}, u32[]{:S(2)}) collective-permute-start(bf16[32,3840]{1,0:T(8,128)(2,1)} %get-tuple-element.40), channel_id=1, source_target_pairs={{2,0},{3,1},{4,2},{5,3},{6,4},{7,5},{10,8},{11,9},{12,10},{13,11},... | collective-permute-start | bytes 737288 | tf_op jit(solution)/shard_map/ppermute | solution.py:291
  12.3 1.3 %collective-permute-start.1 = (bf16[32,3840]{1,0:T(8,128)(2,1)}, bf16[32,3840]{1,0:T(8,128)(2,1)S(1)}, u32[]{:S(2)}, u32[]{:S(2)}) collective-permute-start(bf16[32,3840]{1,0:T(8,128)(2,1)} %get-tuple-element.41), channel_id=1, source_target_pairs={{1,0},{2,1},{3,2},{4,3},{5,4},{6,5},{7,6},{9,8},{10,9},{11,10},{12... | collective-permute-start | bytes 737288 | tf_op jit(solution)/shard_map/ppermute | solution.py:291
  13.6 3.0 %collective-permute-start.2 = (bf16[32,3840]{1,0:T(8,128)(2,1)}, bf16[32,3840]{1,0:T(8,128)(2,1)S(1)}, u32[]{:S(2)}, u32[]{:S(2)}) collective-permute-start(bf16[32,3840]{1,0:T(8,128)(2,1)} %get-tuple-element.42), channel_id=1, source_target_pairs={{0,1},{1,2},{2,3},{3,4},{4,5},{5,6},{6,7},{8,9},{9,10},{10,11},{11... | collective-permute-start | bytes 737288 | tf_op jit(solution)/shard_map/ppermute | solution.py:291
  16.6 5.5 %collective-permute-start.3 = (bf16[32,3840]{1,0:T(8,128)(2,1)}, bf16[32,3840]{1,0:T(8,128)(2,1)S(1)}, u32[]{:S(2)}, u32[]{:S(2)}) collective-permute-start(bf16[32,3840]{1,0:T(8,128)(2,1)} %get-tuple-element.43), channel_id=1, source_target_pairs={{0,2},{1,3},{2,4},{3,5},{4,6},{5,7},{8,10},{9,11},{10,12},{11,13},... | collective-permute-start | bytes 737288 | tf_op jit(solution)/shard_map/ppermute | solution.py:291
  22.1 2.0 %copy.10 = bf16[29,64,29]{2,1,0:T(8,128)(2,1)} copy(bf16[29,64,29]{1,2,0:T(8,128)(2,1)} %bitcast.15) | data formatting | bytes 215296 | tf_op jit(solution)/shard_map/transpose | solution.py:307
  24.1 3.7 %rotate_near.1 = (bf16[128,3712]{1,0:T(8,128)(2,1)}, bf16[64,128]{1,0:T(8,128)(2,1)}, bf16[64,64]{1,0:T(8,128)(2,1)}) custom-call(bf16[64,3840]{1,0:T(8,128)(2,1)} %get-tuple-element.44.refs_0_, bf16[1856,29]{1,0:T(8,128)(2,1)} %bitcast.12, bf16[128,3712]{1,0:T(8,128)(2,1)} %refs_5_.1), custom_call_target="tpu_custom_call" | custom-call | tf_op jit(solution)/shard_map/rotate_near/pallas_call | solution.py:260
  27.8 0.0 copy-start
  27.8 0.0 collective-permute-done.refs_0_
  27.8 0.0 copy-start.6
  27.8 0.0 collective-permute-done.1.refs_1_
  27.8 0.0 copy-start.7
  27.8 0.0 collective-permute-done.2.refs_2_
  27.9 0.0 copy-start.8
  27.9 6.2 %collective-permute-done.3.refs_3_ = bf16[32,3840]{1,0:T(8,128)(2,1)S(1)} collective-permute-done((bf16[32,3840]{1,0:T(8,128)(2,1)}, bf16[32,3840]{1,0:T(8,128)(2,1)S(1)}, u32[]{:S(2)}, u32[]{:S(2)}) %collective-permute-start.3) | collective-permute-done | bytes 245792 | tf_op jit(solution)/shard_map/ppermute | solution.py:291
  34.1 0.0 copy-start.9
  34.1 0.0 copy-done.6
  34.1 0.0 copy-done.7
  34.1 0.0 copy-done.8
  34.1 0.7 copy-done.9
  34.8 5.1 %rotate_far.1 = (bf16[256,3712]{1,0:T(8,128)(2,1)}, bf16[128,128]{1,0:T(8,128)(2,1)}, bf16[128,64]{1,0:T(8,128)(2,1)}) custom-call(bf16[32,3840]{1,0:T(8,128)(2,1)} %copy-done.6, bf16[32,3840]{1,0:T(8,128)(2,1)} %copy-done.7, bf16[32,3840]{1,0:T(8,128)(2,1)} %copy-done.8, bf16[32,3840]{1,0:T(8,128)(2,1)} %copy-done.9, bf16[1856,29]{1,0:T(8,128)(2,1)} %bitcast.13, ...), custom_call_target="tpu_custom_call" | custom-call | tf_op jit(solution)/shard_map/rotate_far/pallas_call | solution.py:260
  39.8 2.6 %collective-permute-start.5 = (bf16[256,3712]{1,0:T(8,128)(2,1)}, bf16[256,3712]{1,0:T(8,128)(2,1)S(1)}, u32[]{:S(2)}, u32[]{:S(2)}) collective-permute-start(bf16[256,3712]{1,0:T(8,128)(2,1)} %get-tuple-element.52.refs_3_.refs_1_), channel_id=1, source_target_pairs={{0,1},{1,0},{2,3},{3,2},{4,5},{5,4},{6,7},{7,6},{8,9},{9,8},{10,11... | collective-permute-start | bytes 5701640 | tf_op jit(solution)/shard_map/ppermute | solution.py:294
  42.4 0.0 copy-done
  42.4 0.1 collective-permute-start.4
  42.5 0.6 pad_add_fusion.refs_0_
  43.1 4.0 %collective-permute-done.4.refs_2_ = bf16[128,3712]{1,0:T(8,128)(2,1)S(1)} collective-permute-done((bf16[128,3712]{1,0:T(8,128)(2,1)S(1)}, bf16[128,3712]{1,0:T(8,128)(2,1)S(1)}, u32[]{:S(2)}, u32[]{:S(2)}) %collective-permute-start.4) | collective-permute-done | bytes 950304 | tf_op jit(solution)/shard_map/ppermute | solution.py:294
  47.1 0.0 copy-start.3
  47.1 0.9 copy-done.3
  48.0 0.0 collective-permute-done.5.refs_4_
  48.1 0.0 copy-start.1
  48.1 1.3 %copy-done.1 = bf16[256,3712]{1,0:T(8,128)(2,1)} copy-done((bf16[256,3712]{1,0:T(8,128)(2,1)}, bf16[256,3712]{1,0:T(8,128)(2,1)S(1)}, u32[]{:S(2)}) %copy-start.1) | copy-done | bytes 1900568
  49.3 9.2 %weight_terms.1 = (bf16[1368,128]{1,0:T(8,128)(2,1)}, bf16[1368,128]{1,0:T(8,128)(2,1)}, bf16[1368,128]{1,0:T(8,128)(2,1)}, bf16[1368,128]{1,0:T(8,128)(2,1)}, f...) custom-call(s32[3]{0:T(128)} %pad_add_fusion.refs_0_, ...), custom_call_target="tpu_custom_call" | custom-call | tf_op jit(solution)/shard_map/weight_terms/pallas_call | solution.py:260
  58.5 0.0 copy-start.5
  58.5 0.0 copy-start.2
  58.5 6.3 %collective-permute-start.9 = (bf16[1368,128]{1,0:T(8,128)(2,1)}, bf16[1368,128]{1,0:T(8,128)(2,1)S(1)}, u32[]{:S(2)}, u32[]{:S(2)}) collective-permute-start(bf16[1368,128]{1,0:T(8,128)(2,1)} %get-tuple-element.74), channel_id=1, source_target_pairs={{0,2},{2,0},{1,3},{3,1},{4,6},{6,4},{5,7},{7,5},{8,10},{10,8},{9,1... | collective-permute-start | bytes 1050632 | tf_op jit(solution)/shard_map/ppermute | solution.py:350
  64.8 0.1 collective-permute-start.11
  64.9 1.9 %collective-permute-start.6 = (bf16[1368,128]{1,0:T(8,128)(2,1)}, bf16[1368,128]{1,0:T(8,128)(2,1)S(1)}, u32[]{:S(2)}, u32[]{:S(2)}) collective-permute-start(bf16[1368,128]{1,0:T(8,128)(2,1)} %get-tuple-element.62), channel_id=1, source_target_pairs={{0,2},{2,0},{1,3},{3,1},{4,6},{6,4},{5,7},{7,5},{8,10},{10,8},{9,1... | collective-permute-start | bytes 1050632 | tf_op jit(solution)/shard_map/ppermute | solution.py:350
  66.8 0.1 collective-permute-start.8
  66.9 7.1 %collective-permute-done.9 = bf16[1368,128]{1,0:T(8,128)(2,1)S(1)} collective-permute-done((bf16[1368,128]{1,0:T(8,128)(2,1)}, bf16[1368,128]{1,0:T(8,128)(2,1)S(1)}, u32[]{:S(2)}, u32[]{:S(2)}) %collective-permute-start.9) | collective-permute-done | bytes 350240 | tf_op jit(solution)/shard_map/ppermute | solution.py:350
  74.0 1.2 %add_convert_fusion.1 = bf16[1368,128]{1,0:T(8,128)(2,1)S(1)} fusion(f32[1368,128]{1,0:T(8,128)} %get-tuple-element.73, bf16[1368,128]{1,0:T(8,128)(2,1)S(1)} %collective-permute-done.9), kind=kLoop, calls=%fused_computation.2 | loop fusion | flops 525312 | bytes 1400832 | tf_op jit(solution)/shard_map/convert_element_type | solution.py:355
  75.2 3.7 %collective-permute-start.10 = (bf16[1368,128]{1,0:T(8,128)(2,1)S(1)}, bf16[1368,128]{1,0:T(8,128)(2,1)S(1)}, u32[]{:S(2)}, u32[]{:S(2)}) collective-permute-start(bf16[1368,128]{1,0:T(8,128)(2,1)S(1)} %add_convert_fusion.1), channel_id=1, source_target_pairs={{0,8},{4,12},{8,0},{12,4},{1,9},{5,13},{9,1},{13,5},{2,10},{6,14},... | collective-permute-start | bytes 1050632 | tf_op jit(solution)/shard_map/ppermute | solution.py:356
  78.9 10.1 %collective-permute-done.6 = bf16[1368,128]{1,0:T(8,128)(2,1)S(1)} collective-permute-done((bf16[1368,128]{1,0:T(8,128)(2,1)}, bf16[1368,128]{1,0:T(8,128)(2,1)S(1)}, u32[]{:S(2)}, u32[]{:S(2)}) %collective-permute-start.6) | collective-permute-done | bytes 350240 | tf_op jit(solution)/shard_map/ppermute | solution.py:350
  89.0 1.2 add_convert_fusion.2
  90.2 5.6 %collective-permute-start.7 = (bf16[1368,128]{1,0:T(8,128)(2,1)S(1)}, bf16[1368,128]{1,0:T(8,128)(2,1)S(1)}, u32[]{:S(2)}, u32[]{:S(2)}) collective-permute-start(bf16[1368,128]{1,0:T(8,128)(2,1)S(1)} %add_convert_fusion.2), channel_id=1, source_target_pairs={{0,12},{4,0},{8,4},{12,8},{1,13},{5,1},{9,5},{13,9},{2,14},{6,2},{... | collective-permute-start | bytes 1050632 | tf_op jit(solution)/shard_map/ppermute | solution.py:356
  95.8 0.0 collective-permute-done.11
  95.8 0.0 copy-done.5
  95.8 0.1 add_convert_fusion
  95.9 0.2 collective-permute-start.12
  96.1 0.0 copy-done.2
  96.2 1.1 copy.11
  97.3 3.8 %back.1 = (bf16[8,240,256]{2,1,0:T(8,128)(2,1)}, bf16[16,240,256]{2,1,0:T(8,128)(2,1)}) custom-call(bf16[64,64]{1,0:T(8,128)(2,1)} %get-tuple-element.64.near_ref, bf16[128,64]{1,0:T(8,128)(2,1)} %get-tuple-element.65.far_ref, bf16[1856,29]{1,0:T(8,128)(2,1)} %bitcast.14), custom_call_target="tpu_custom_call" | custom-call | tf_op jit(solution)/shard_map/back/pallas_call | solution.py:260
  101.1 0.0 all-gather.2.cloned.1.call-done.w_ref
  101.1 0.0 copy-start.4
  101.1 9.4 %messages.1 = bf16[128,3712]{1,0:T(8,128)(2,1)} custom-call(bf16[21888,128]{1,0:T(8,128)(2,1)} %all-gather.2.cloned.1.call-done.w_ref, bf16[128,3712]{1,0:T(8,128)(2,1)} %get-tuple-element.51.refs_1_.refs_0_, bf16[256,3712]{1,0:T(8,128)(2,1)} %get-tuple-element.52.refs_3_.refs_1_, bf16[8,240,256]{2,1,0:T(8,128)(2,1)} %get-tuple-element.66.refs_2_, ...), custom_call_target="tpu_custom_call" | custom-call | tf_op jit(solution)/shard_map/messages/pallas_call | solution.py:260
  110.5 0.0 collective-permute-done.7
  110.5 0.0 collective-permute-done.8
  110.5 0.0 collective-permute-done.10
  110.5 0.0 collective-permute-done.12
  110.5 0.0 copy-done.4
  110.5 1.1 add_multiply_fusion
Async XLA Ops:
  7.2 94.0 %all-gather.2.cloned.1.call-start = ((), (), s32[]{:S(2)}) async-start(), calls=%async_computation | async-start | bytes 5953536 | tf_op jit(solution)/shard_map/all_gather | solution.py:296
  11.0 16.8 %collective-permute-start = (bf16[32,3840]{1,0:T(8,128)(2,1)}, bf16[32,3840]{1,0:T(8,128)(2,1)S(1)}, u32[]{:S(2)}, u32[]{:S(2)}) collective-permute-start(bf16[32,3840]{1,0:T(8,128)(2,1)} %get-tuple-element.40), channel_id=1, source_target_pairs={{2,0},{3,1},{4,2},{5,3},{6,4},{7,5},{10,8},{11,9},{12,10},{13,11},... | collective-permute-start | bytes 737288 | tf_op jit(solution)/shard_map/ppermute | solution.py:291
  12.3 15.6 %collective-permute-start.1 = (bf16[32,3840]{1,0:T(8,128)(2,1)}, bf16[32,3840]{1,0:T(8,128)(2,1)S(1)}, u32[]{:S(2)}, u32[]{:S(2)}) collective-permute-start(bf16[32,3840]{1,0:T(8,128)(2,1)} %get-tuple-element.41), channel_id=1, source_target_pairs={{1,0},{2,1},{3,2},{4,3},{5,4},{6,5},{7,6},{9,8},{10,9},{11,10},{12... | collective-permute-start | bytes 737288 | tf_op jit(solution)/shard_map/ppermute | solution.py:291
  13.6 14.3 %collective-permute-start.2 = (bf16[32,3840]{1,0:T(8,128)(2,1)}, bf16[32,3840]{1,0:T(8,128)(2,1)S(1)}, u32[]{:S(2)}, u32[]{:S(2)}) collective-permute-start(bf16[32,3840]{1,0:T(8,128)(2,1)} %get-tuple-element.42), channel_id=1, source_target_pairs={{0,1},{1,2},{2,3},{3,4},{4,5},{5,6},{6,7},{8,9},{9,10},{10,11},{11... | collective-permute-start | bytes 737288 | tf_op jit(solution)/shard_map/ppermute | solution.py:291
  16.6 17.4 %collective-permute-start.3 = (bf16[32,3840]{1,0:T(8,128)(2,1)}, bf16[32,3840]{1,0:T(8,128)(2,1)S(1)}, u32[]{:S(2)}, u32[]{:S(2)}) collective-permute-start(bf16[32,3840]{1,0:T(8,128)(2,1)} %get-tuple-element.43), channel_id=1, source_target_pairs={{0,2},{1,3},{2,4},{3,5},{4,6},{5,7},{8,10},{9,11},{10,12},{11,13},... | collective-permute-start | bytes 737288 | tf_op jit(solution)/shard_map/ppermute | solution.py:291
  27.8 14.6 %copy-start = (bf16[128,3712]{1,0:T(8,128)(2,1)S(1)}, bf16[128,3712]{1,0:T(8,128)(2,1)}, u32[]{:S(2)}) copy-start(bf16[128,3712]{1,0:T(8,128)(2,1)} %get-tuple-element.51.refs_1_.refs_0_) | copy-start | bytes 2850820
  27.8 6.2 %copy-start.6 = (bf16[32,3840]{1,0:T(8,128)(2,1)}, bf16[32,3840]{1,0:T(8,128)(2,1)S(1)}, u32[]{:S(2)}) copy-start(bf16[32,3840]{1,0:T(8,128)(2,1)S(1)} %collective-permute-done.refs_0_) | copy-start | bytes 737284
  27.8 6.2 %copy-start.7 = (bf16[32,3840]{1,0:T(8,128)(2,1)}, bf16[32,3840]{1,0:T(8,128)(2,1)S(1)}, u32[]{:S(2)}) copy-start(bf16[32,3840]{1,0:T(8,128)(2,1)S(1)} %collective-permute-done.1.refs_1_) | copy-start | bytes 737284
  27.9 6.2 %copy-start.8 = (bf16[32,3840]{1,0:T(8,128)(2,1)}, bf16[32,3840]{1,0:T(8,128)(2,1)S(1)}, u32[]{:S(2)}) copy-start(bf16[32,3840]{1,0:T(8,128)(2,1)S(1)} %collective-permute-done.2.refs_2_) | copy-start | bytes 737284
  34.1 0.7 copy-start.9
  39.8 8.2 %collective-permute-start.5 = (bf16[256,3712]{1,0:T(8,128)(2,1)}, bf16[256,3712]{1,0:T(8,128)(2,1)S(1)}, u32[]{:S(2)}, u32[]{:S(2)}) collective-permute-start(bf16[256,3712]{1,0:T(8,128)(2,1)} %get-tuple-element.52.refs_3_.refs_1_), channel_id=1, source_target_pairs={{0,1},{1,0},{2,3},{3,2},{4,5},{5,4},{6,7},{7,6},{8,9},{9,8},{10,11... | collective-permute-start | bytes 5701640 | tf_op jit(solution)/shard_map/ppermute | solution.py:294
  42.4 4.7 %collective-permute-start.4 = (bf16[128,3712]{1,0:T(8,128)(2,1)S(1)}, bf16[128,3712]{1,0:T(8,128)(2,1)S(1)}, u32[]{:S(2)}, u32[]{:S(2)}) collective-permute-start(bf16[128,3712]{1,0:T(8,128)(2,1)S(1)} %copy-done), channel_id=1, source_target_pairs={{0,1},{1,0},{2,3},{3,2},{4,5},{5,4},{6,7},{7,6},{8,9},{9,8},{10,11... | collective-permute-start | bytes 2850824 | tf_op jit(solution)/shard_map/ppermute | solution.py:294
  47.1 0.9 copy-start.3
  48.1 1.3 %copy-start.1 = (bf16[256,3712]{1,0:T(8,128)(2,1)}, bf16[256,3712]{1,0:T(8,128)(2,1)S(1)}, u32[]{:S(2)}) copy-start(bf16[256,3712]{1,0:T(8,128)(2,1)S(1)} %collective-permute-done.5.refs_4_) | copy-start | bytes 5701636
  58.5 37.3 %copy-start.5 = (f32[1368,128]{1,0:T(8,128)S(1)}, f32[1368,128]{1,0:T(8,128)}, u32[]{:S(2)}) copy-start(f32[1368,128]{1,0:T(8,128)} %get-tuple-element.75) | copy-start | bytes 2101252
  58.5 37.6 %copy-start.2 = (bf16[64,29,29]{0,2,1:T(8,128)(2,1)S(1)}, bf16[64,29,29]{0,2,1:T(8,128)(2,1)}, u32[]{:S(2)}) copy-start(bf16[64,29,29]{0,2,1:T(8,128)(2,1)} %param.11) | copy-start | bytes 322948
  58.5 15.5 %collective-permute-start.9 = (bf16[1368,128]{1,0:T(8,128)(2,1)}, bf16[1368,128]{1,0:T(8,128)(2,1)S(1)}, u32[]{:S(2)}, u32[]{:S(2)}) collective-permute-start(bf16[1368,128]{1,0:T(8,128)(2,1)} %get-tuple-element.74), channel_id=1, source_target_pairs={{0,2},{2,0},{1,3},{3,1},{4,6},{6,4},{5,7},{7,5},{8,10},{10,8},{9,1... | collective-permute-start | bytes 1050632 | tf_op jit(solution)/shard_map/ppermute | solution.py:350
  64.8 31.0 %collective-permute-start.11 = (bf16[1368,128]{1,0:T(8,128)(2,1)}, bf16[1368,128]{1,0:T(8,128)(2,1)S(1)}, u32[]{:S(2)}, u32[]{:S(2)}) collective-permute-start(bf16[1368,128]{1,0:T(8,128)(2,1)} %get-tuple-element.76), channel_id=1, source_target_pairs={{0,2},{2,0},{1,3},{3,1},{4,6},{6,4},{5,7},{7,5},{8,10},{10,8},{9,1... | collective-permute-start | bytes 1050632 | tf_op jit(solution)/shard_map/ppermute | solution.py:350
  64.9 24.1 %collective-permute-start.6 = (bf16[1368,128]{1,0:T(8,128)(2,1)}, bf16[1368,128]{1,0:T(8,128)(2,1)S(1)}, u32[]{:S(2)}, u32[]{:S(2)}) collective-permute-start(bf16[1368,128]{1,0:T(8,128)(2,1)} %get-tuple-element.62), channel_id=1, source_target_pairs={{0,2},{2,0},{1,3},{3,1},{4,6},{6,4},{5,7},{7,5},{8,10},{10,8},{9,1... | collective-permute-start | bytes 1050632 | tf_op jit(solution)/shard_map/ppermute | solution.py:350
  66.8 43.7 %collective-permute-start.8 = (bf16[1368,128]{1,0:T(8,128)(2,1)}, bf16[1368,128]{1,0:T(8,128)(2,1)S(1)}, u32[]{:S(2)}, u32[]{:S(2)}) collective-permute-start(bf16[1368,128]{1,0:T(8,128)(2,1)} %get-tuple-element.72), channel_id=1, source_target_pairs={{0,2},{2,0},{1,3},{3,1},{4,6},{6,4},{5,7},{7,5},{8,10},{10,8},{9,1... | collective-permute-start | bytes 1050632 | tf_op jit(solution)/shard_map/ppermute | solution.py:350
  75.2 35.3 %collective-permute-start.10 = (bf16[1368,128]{1,0:T(8,128)(2,1)S(1)}, bf16[1368,128]{1,0:T(8,128)(2,1)S(1)}, u32[]{:S(2)}, u32[]{:S(2)}) collective-permute-start(bf16[1368,128]{1,0:T(8,128)(2,1)S(1)} %add_convert_fusion.1), channel_id=1, source_target_pairs={{0,8},{4,12},{8,0},{12,4},{1,9},{5,13},{9,1},{13,5},{2,10},{6,14},... | collective-permute-start | bytes 1050632 | tf_op jit(solution)/shard_map/ppermute | solution.py:356
  90.2 20.3 %collective-permute-start.7 = (bf16[1368,128]{1,0:T(8,128)(2,1)S(1)}, bf16[1368,128]{1,0:T(8,128)(2,1)S(1)}, u32[]{:S(2)}, u32[]{:S(2)}) collective-permute-start(bf16[1368,128]{1,0:T(8,128)(2,1)S(1)} %add_convert_fusion.2), channel_id=1, source_target_pairs={{0,12},{4,0},{8,4},{12,8},{1,13},{5,1},{9,5},{13,9},{2,14},{6,2},{... | collective-permute-start | bytes 1050632 | tf_op jit(solution)/shard_map/ppermute | solution.py:356
  95.9 14.6 %collective-permute-start.12 = (bf16[1368,128]{1,0:T(8,128)(2,1)S(1)}, bf16[1368,128]{1,0:T(8,128)(2,1)S(1)}, u32[]{:S(2)}, u32[]{:S(2)}) collective-permute-start(bf16[1368,128]{1,0:T(8,128)(2,1)S(1)} %add_convert_fusion), channel_id=1, source_target_pairs={{0,4},{4,8},{8,12},{12,0},{1,5},{5,9},{9,13},{13,1},{2,6},{6,10},{... | collective-permute-start | bytes 1050632 | tf_op jit(solution)/shard_map/ppermute | solution.py:356
  101.1 9.4 %copy-start.4 = (f32[1368,128]{1,0:T(8,128)S(1)}, f32[1368,128]{1,0:T(8,128)}, u32[]{:S(2)}) copy-start(f32[1368,128]{1,0:T(8,128)} %get-tuple-element.71) | copy-start | bytes 2101252
Sparse Core Ops, SparseCore 0:
  10.2 66.7 all-gather.1

commit v5 on v4

--- a/solution.py
+++ b/solution.py
@@ -10,7 +10,7 @@
 
 K = 29
 SPAN = 8
-STEPS = (-2, -1, 1, 2)
+STEPS = (-2, 2, -1, 1)
 F32 = jnp.float32
 BF16 = jnp.bfloat16
 ALL = ("z", "x", "core")
@@ -137,18 +137,19 @@
         both_ref[slots:, cols] = res_ref[k, :, 128:].astype(BF16)
 
 
-def back_kernel(near_ref, far_ref, tabt_ref, near_out, far_out, near_tmp, far_tmp):
-    build(tabt_ref, near_ref[...], near_out, near_tmp)
-    build(tabt_ref, far_ref[...], far_out, far_tmp)
+def back_kernel(tabt_ref, *refs):
+    for i in range(2):
+        build(tabt_ref, refs[i][...], refs[2 + i], refs[4 + i])
 
 
 def shifts(n_z):
     return sorted(range(n_z), key=lambda i: (i == 0, abs(i - n_z // 2)))
 
 
-def grad_kernel(n_z, n_x, pos_ref, *refs):
+def grad_kernel(n_z, n_x, me_ref, *refs):
     parts, outs, flat = refs[:4], refs[4:-1], refs[-1]
-    z, x, core = pos_ref[0], pos_ref[1], pos_ref[2]
+    chip, core = me_ref[0] // 2, me_ref[0] % 2
+    z, x = chip // n_x, chip % n_x
 
     def left(first, width):
         at = slice(first * 128, (first + width) * 128)
@@ -255,7 +256,7 @@
     return pl.BlockSpec(like.shape, lambda i: zeros, pipeline_mode=pl.Buffered(1))
 
 
-def call(kernel, name, mib, outs, operands, scratch=(), numbers=None):
+def call(kernel, name, mib, outs, operands, scratch=(), numbers=None, cost=None):
     first = [] if numbers is None else [pl.BlockSpec(memory_space=pltpu.SMEM)]
     return pl.pallas_call(
         kernel,
@@ -265,6 +266,7 @@
         out_specs=[whole(o) for o in outs],
         scratch_shapes=list(scratch),
         compiler_params=pltpu.CompilerParams(vmem_limit_bytes=mib * 1024 * 1024),
+        cost_estimate=cost,
         name=name,
     )(*(() if numbers is None else (numbers,)), *operands)
 
@@ -279,7 +281,6 @@
     rows = flat_params.shape[0]
     n_dp = n_z * n_x * 2
     n_rot = rot_table.shape[0]
-    z, x, core = (lax.axis_index(a) for a in ALL)
     me = dp_index(n_x)
     smem = pl.BlockSpec(memory_space=pltpu.SMEM)
 
@@ -297,7 +298,7 @@
 
     row = lambda v: v.reshape(1, n)
     here, *outbound = call(
-        send_kernel, "send", 60,
+        send_kernel, "send", 62,
         [shape((n // 2, width + 128), BF16)] + [shape((cap, width + 128), BF16)] * 4,
         [row(edge_owner), row(edge_src), row(edge_dst), row(edge_rot), node_feats],
         numbers=me.reshape(1),
@@ -307,10 +308,10 @@
     tab = rot_table.transpose(1, 0, 2).reshape(K * n_rot, K)
     tabt = rot_table.transpose(2, 0, 1).reshape(K * n_rot, K)
 
-    def rotate(rows_in, name):
+    def rotate(rows_in, name, cost=None):
         slots = sum(r.shape[0] for r in rows_in)
         return call(
-            lambda *refs: rotate_kernel(len(rows_in), *refs), name, 60,
+            lambda *refs: rotate_kernel(len(rows_in), *refs), name, 62,
             [
                 shape((2 * slots, width), BF16), shape((slots, n), BF16),
                 shape((slots, n_rot), BF16),
@@ -320,32 +321,52 @@
                 pltpu.VMEM((slots // 8, 240, 256), BF16), pltpu.VMEM((30, slots, 256), F32),
                 pltpu.VMEM((32, slots, 256), F32), pltpu.VMEM((30, slots, 256), F32),
             ],
+            cost=cost,
         )
 
-    both_near, hot_near, turn_near = rotate([here], "rotate_near")
-    both_near_other = swap(both_near)
-    arrived, both_near = lax.optimization_barrier((arrived, both_near))
-    both_far, hot_far, turn_far = rotate(arrived, "rotate_far")
-    both_far_other = swap(both_far)
+    both_a, hot_a, turn_a = rotate([here] + arrived[:2], "rotate_first")
+    both_a_other = swap(both_a)
+    last, both_a = lax.optimization_barrier((arrived[2:], both_a))
+    both_b, hot_b, turn_b = rotate(
+        last, "rotate_last",
+        pl.CostEstimate(flops=10**10, bytes_accessed=10**8, transcendentals=0),
+    )
+    both_b_other = swap(both_b)
+    both, hots, turns = [both_a, both_b], [hot_a, hot_b], [turn_a, turn_b]
 
     n_send = n_z * (n_x - 1)
     blocks = call(
-        lambda *refs: grad_kernel(n_z, n_x, *refs), "weight_terms", 60,
+        lambda *refs: grad_kernel(n_z, n_x, *refs), "weight_terms", 62,
         [shape((rows, 128), BF16)] * n_send + [shape((rows, 128), F32)] * n_z,
-        [both_near, both_near_other, both_far, both_far_other],
+        both + [both_a_other, both_b_other],
         [pltpu.VMEM((rows * n_dp, 128), F32)],
-        numbers=jnp.stack([z, x, core]),
-    )
-    turn_far, blocks = lax.optimization_barrier((turn_far, blocks))
-    matst_near, matst_far = call(
-        back_kernel, "back", 60,
-        [shape((t.shape[0] // 8, 240, 256), BF16) for t in (turn_near, turn_far)],
-        [turn_near, turn_far, tabt],
-        [pltpu.VMEM((30, t.shape[0], 256), F32) for t in (turn_near, turn_far)],
-    )
+        numbers=me.reshape(1),
+    )
+    turns, blocks = lax.optimization_barrier((turns, list(blocks)))
+    mats = call(
+        back_kernel, "back", 62,
+        [shape((t.shape[0] // 8, 240, 256), BF16) for t in turns],
+        [tabt] + turns,
+        [pltpu.VMEM((30, t.shape[0], 256), F32) for t in turns],
+    )
+    kept = blocks[n_send:]
+    kept[0], mats = lax.optimization_barrier((kept[0], mats))
     arrived, terms = [], []
     for at, i in enumerate(shifts(n_z)):
-        total = blocks[n_send + at]
+        total = kept[at]
+        if at == 2:
+            weights, _ = lax.optimization_barrier((weights, terms[1]))
+            slots = n // 2 + 4 * cap
+            (node_out,) = call(
+                message_kernel, "messages", 62,
+                [shape((n, width), BF16)],
+                [weights, *both, *mats, *hots],
+                [
+                    pltpu.VMEM((rows * n_dp, 128), F32), pltpu.VMEM((32, slots, 128), F32),
+                    pltpu.VMEM((30, slots, 128), F32), pltpu.VMEM((slots, width), BF16),
+                ],
+            )
+            total, node_out = lax.optimization_barrier((total, node_out))
         for o in range(1, n_x):
             got = lax.ppermute(
                 blocks[(o - 1) * n_z + at], "x", [(s, (s + o) % n_x) for s in range(n_x)]
@@ -354,18 +375,6 @@
         if i:
             terms.append(total.astype(BF16))
             arrived.append(lax.ppermute(terms[-1], "z", [(s, (s + i) % n_z) for s in range(n_z)]))
-    weights, _ = lax.optimization_barrier((weights, terms[-1]))
-    slots = n // 2 + 4 * cap
-    (node_out,) = call(
-        message_kernel, "messages", 60,
-        [shape((n, width), BF16)],
-        [weights, both_near, both_far, matst_near, matst_far, hot_near, hot_far],
-        [
-            pltpu.VMEM((rows * n_dp, 128), F32), pltpu.VMEM((32, slots, 128), F32),
-            pltpu.VMEM((30, slots, 128), F32), pltpu.VMEM((slots, width), BF16),
-        ],
-    )
-    arrived[-1], node_out = lax.optimization_barrier((arrived[-1], node_out))
     result = total
     for got in arrived:
         result = result + got.astype(F32)

time: 119 us -> 116 us (0.975)
  starting transfers between devices: 31.7 us -> 23.1 us
  waiting for transfers between devices: 28.1 us -> 33.7 us
    ppermute x3, waiting for transfers between devices: 0.01 us -> 13.5 us  [on_device(): lax.ppermute(terms[-1], 'z', [(s, (s + i) % n_z) for s in range(n_z)])]
    ppermute x4, waiting for transfers between devices: 17.2 us -> 7.79 us  [on_device(): lax.ppermute(blocks[(o - 1) * n_z + at], 'x', [(s, (s + o) % n_x) for s i...]
    ppermute x4, starting transfers between devices: 8.38 us -> 4.48 us  [on_device(): lax.ppermute(blocks[(o - 1) * n_z + at], 'x', [(s, (s + o) % n_x) for s i...]
    ppermute x3, starting transfers between devices: 9.58 us -> 6.3 us  [on_device(): lax.ppermute(terms[-1], 'z', [(s, (s + i) % n_z) for s in range(n_z)])]
    ppermute x4, waiting for transfers between devices: 6.2 us -> 9.2 us  [shift(): return lax.ppermute(block, ALL, route)]
    ppermute x2, starting transfers between devices: 2.63 us -> 0.5 us  [swap(): return lax.ppermute(block, 'core', [(0, 1), (1, 0)])]
    ppermute x2, waiting for transfers between devices: 4.05 us -> 2.49 us  [swap(): return lax.ppermute(block, 'core', [(0, 1), (1, 0)])]
    unnamed x20 -> x12, local copies, waits for them, and re-layouts: 2.89 us -> 1.96 us
  transfers between devices with their start and end apart: 14 -> 14, of which waited for: 4 -> 7; matrix products, arithmetic and copies ran while one was open for 5% -> 6% of each run, Pallas kernels for 26% -> 27%
where the time goes in v5:
time: 116 us
  Pallas kernels  34 us (29%)
  waiting for transfers between devices  33.7 us (29%)
  starting transfers between devices  23.1 us (20%)
  between operations  14.1 us (12%)
  local copies, waits for them, and re-layouts  6.01 us (5%)
  other arithmetic  5.06 us (4%)
    pallas_call x6, Pallas kernels, call(): pl.pallas_call(kernel, grid=(1,), out_shape=outs, in_specs=first + [whole...  34 us
    ppermute x3, waiting for transfers between devices, on_device(): lax.ppermute(terms[-1], 'z', [(s, (s + i) % n_z) for s in range(n_z)])  13.5 us
    ppermute x4, starting transfers between devices, shift(): return lax.ppermute(block, ALL, route)  11.8 us
    ppermute x4, waiting for transfers between devices, shift(): return lax.ppermute(block, ALL, route)  9.2 us
    ppermute x4, waiting for transfers between devices, on_device(): lax.ppermute(blocks[(o - 1) * n_z + at], 'x', [(s, (s + o) % n_x) for s i...  7.79 us
    ppermute x3, starting transfers between devices, on_device(): lax.ppermute(terms[-1], 'z', [(s, (s + i) % n_z) for s in range(n_z)])  6.3 us
    ppermute x4, starting transfers between devices, on_device(): lax.ppermute(blocks[(o - 1) * n_z + at], 'x', [(s, (s + o) % n_x) for s i...  4.48 us
    convert_element_type x3, other arithmetic, on_device(): terms.append(total.astype(BF16))  2.81 us
  transfers between devices with their start and end apart: 14, of which 7 were waited for; matrix products, arithmetic and copies ran while one was open for 6% of the time, Pallas kernels for 27%

profile of v5, /device:TPU:0, one launch (start us, length us, event | category | flops | bytes accessed | tf_op | source)
XLA Modules:
  0.0 116.0 jit_solution(11608284683330341651)
XLA Ops:
  7.2 0.0 all-gather.2.cloned.1.call-start
  7.2 0.7 all-gather.2.cloned.1.call-update
  7.9 3.1 %send.1 = (bf16[64,3840]{1,0:T(8,128)(2,1)}, bf16[32,3840]{1,0:T(8,128)(2,1)}, bf16[32,3840]{1,0:T(8,128)(2,1)}, bf16[32,3840]{1,0:T(8,128)(2,1)}, bf16[32,3840]{1,0:T(8,128)(2,1)}) custom-call(s32[1]{0:T(128)} %bitcast.me_ref.refs_0_, s32[1,128]{1,0:T(1,128)} %bitcast.14, s32[1,128]{1,0:T(1,128)} %bitcast.15, s32[1,128]{1,0:T(1,128)} %bitcast.16, ...), custom_call_target="tpu_custom_call" | custom-call | tf_op jit(solution)/shard_map/send/pallas_call | solution.py:261
  11.0 1.3 %collective-permute-start = (bf16[32,3840]{1,0:T(8,128)(2,1)}, bf16[32,3840]{1,0:T(8,128)(2,1)S(1)}, u32[]{:S(2)}, u32[]{:S(2)}) collective-permute-start(bf16[32,3840]{1,0:T(8,128)(2,1)} %get-tuple-element.43), channel_id=1, source_target_pairs={{2,0},{3,1},{4,2},{5,3},{6,4},{7,5},{10,8},{11,9},{12,10},{13,11},... | collective-permute-start | bytes 737288 | tf_op jit(solution)/shard_map/ppermute | solution.py:292
  12.3 5.5 %collective-permute-start.1 = (bf16[32,3840]{1,0:T(8,128)(2,1)}, bf16[32,3840]{1,0:T(8,128)(2,1)S(1)}, u32[]{:S(2)}, u32[]{:S(2)}) collective-permute-start(bf16[32,3840]{1,0:T(8,128)(2,1)} %get-tuple-element.44), channel_id=1, source_target_pairs={{0,2},{1,3},{2,4},{3,5},{4,6},{5,7},{8,10},{9,11},{10,12},{11,13},... | collective-permute-start | bytes 737288 | tf_op jit(solution)/shard_map/ppermute | solution.py:292
  17.8 1.3 %collective-permute-start.2 = (bf16[32,3840]{1,0:T(8,128)(2,1)}, bf16[32,3840]{1,0:T(8,128)(2,1)}, u32[]{:S(2)}, u32[]{:S(2)}) collective-permute-start(bf16[32,3840]{1,0:T(8,128)(2,1)} %get-tuple-element.46), channel_id=1, source_target_pairs={{1,0},{2,1},{3,2},{4,3},{5,4},{6,5},{7,6},{9,8},{10,9},{11,10},{12... | collective-permute-start | bytes 737288 | tf_op jit(solution)/shard_map/ppermute | solution.py:292
  19.1 3.7 %collective-permute-start.3 = (bf16[32,3840]{1,0:T(8,128)(2,1)}, bf16[32,3840]{1,0:T(8,128)(2,1)}, u32[]{:S(2)}, u32[]{:S(2)}) collective-permute-start(bf16[32,3840]{1,0:T(8,128)(2,1)} %get-tuple-element.47), channel_id=1, source_target_pairs={{0,1},{1,2},{2,3},{3,4},{4,5},{5,6},{6,7},{8,9},{9,10},{10,11},{11... | collective-permute-start | bytes 737288 | tf_op jit(solution)/shard_map/ppermute | solution.py:292
  22.8 2.0 %copy.10 = bf16[29,64,29]{2,1,0:T(8,128)(2,1)} copy(bf16[29,64,29]{1,2,0:T(8,128)(2,1)} %bitcast.12) | data formatting | bytes 215296 | tf_op jit(solution)/shard_map/transpose | solution.py:308
  24.8 0.0 collective-permute-done.refs_1_
  24.8 0.0 copy-start.4
  24.8 9.2 %collective-permute-done.1.refs_2_ = bf16[32,3840]{1,0:T(8,128)(2,1)S(1)} collective-permute-done((bf16[32,3840]{1,0:T(8,128)(2,1)}, bf16[32,3840]{1,0:T(8,128)(2,1)S(1)}, u32[]{:S(2)}, u32[]{:S(2)}) %collective-permute-start.1) | collective-permute-done | bytes 245792 | tf_op jit(solution)/shard_map/ppermute | solution.py:292
  34.0 0.0 copy-start.5
  34.0 0.0 copy-done.4
  34.0 0.7 copy-done.5
  34.7 5.0 %rotate_first.1 = (bf16[256,3712]{1,0:T(8,128)(2,1)}, bf16[128,128]{1,0:T(8,128)(2,1)}, bf16[128,64]{1,0:T(8,128)(2,1)}) custom-call(bf16[64,3840]{1,0:T(8,128)(2,1)} %get-tuple-element.42.refs_0_, bf16[32,3840]{1,0:T(8,128)(2,1)} %copy-done.4, bf16[32,3840]{1,0:T(8,128)(2,1)} %copy-done.5, bf16[1856,29]{1,0:T(8,128)(2,1)} %bitcast.9, bf16[128,3712]{1,0:T(8,128)(2,1)} %refs_3_.1), custom_call_target="tpu_custom_call" | custom-call | tf_op jit(solution)/shard_map/rotate_first/pallas_call | solution.py:261
  39.6 0.0 collective-permute-start.4
  39.6 0.0 collective-permute-done.2.refs_0_
  39.6 0.0 collective-permute-done.3.refs_1_
  39.7 3.8 %rotate_last.1 = (bf16[128,3712]{1,0:T(8,128)(2,1)}, bf16[64,128]{1,0:T(8,128)(2,1)}, bf16[64,64]{1,0:T(8,128)(2,1)}) custom-call(bf16[32,3840]{1,0:T(8,128)(2,1)} %collective-permute-done.2.refs_0_, bf16[32,3840]{1,0:T(8,128)(2,1)} %collective-permute-done.3.refs_1_, bf16[1856,29]{1,0:T(8,128)(2,1)} %bitcast.10, bf16[128,3712]{1,0:T(8,128)(2,1)} %refs_3_.1), custom_call_target="tpu_custom_call" | custom-call | flops 10000000000 | bytes 100000000 | tf_op jit(solution)/shard_map/rotate_last/pallas_call | solution.py:261
  43.5 0.5 collective-permute-start.5
  44.0 2.5 %collective-permute-done.5.refs_4_ = bf16[128,3712]{1,0:T(8,128)(2,1)} collective-permute-done((bf16[128,3712]{1,0:T(8,128)(2,1)}, bf16[128,3712]{1,0:T(8,128)(2,1)}, u32[]{:S(2)}, u32[]{:S(2)}) %collective-permute-start.5) | collective-permute-done | bytes 950304 | tf_op jit(solution)/shard_map/ppermute | solution.py:295
  46.5 0.0 collective-permute-done.4.refs_3_
  46.5 0.0 copy-start
  46.5 1.3 %copy-done = bf16[256,3712]{1,0:T(8,128)(2,1)} copy-done((bf16[256,3712]{1,0:T(8,128)(2,1)}, bf16[256,3712]{1,0:T(8,128)(2,1)S(1)}, u32[]{:S(2)}) %copy-start) | copy-done | bytes 1900568
  47.7 9.1 %weight_terms.1 = (bf16[1368,128]{1,0:T(8,128)(2,1)}, bf16[1368,128]{1,0:T(8,128)(2,1)}, bf16[1368,128]{1,0:T(8,128)(2,1)}, bf16[1368,128]{1,0:T(8,128)(2,1)}, f...) custom-call(s32[1]{0:T(128)} %bitcast.me_ref.refs_0_, ...), custom_call_target="tpu_custom_call" | custom-call | tf_op jit(solution)/shard_map/weight_terms/pallas_call | solution.py:261
  56.8 0.0 copy-start.3
  56.8 2.4 %collective-permute-start.8 = (bf16[1368,128]{1,0:T(8,128)(2,1)}, bf16[1368,128]{1,0:T(8,128)(2,1)S(1)}, u32[]{:S(2)}, u32[]{:S(2)}) collective-permute-start(bf16[1368,128]{1,0:T(8,128)(2,1)} %get-tuple-element.79), channel_id=1, source_target_pairs={{0,2},{2,0},{1,3},{3,1},{4,6},{6,4},{5,7},{7,5},{8,10},{10,8},{9,1... | collective-permute-start | bytes 1050632 | tf_op jit(solution)/shard_map/ppermute | solution.py:371
  59.2 2.1 %copy.11 = bf16[29,64,29]{2,1,0:T(8,128)(2,1)} copy(bf16[29,64,29]{1,0,2:T(8,128)(2,1)} %bitcast.13) | data formatting | bytes 215296 | tf_op jit(solution)/shard_map/transpose | solution.py:309
  61.3 3.7 %back.1 = (bf16[16,240,256]{2,1,0:T(8,128)(2,1)}, bf16[8,240,256]{2,1,0:T(8,128)(2,1)}) custom-call(bf16[1856,29]{1,0:T(8,128)(2,1)} %bitcast.11, bf16[128,64]{1,0:T(8,128)(2,1)} %get-tuple-element.67.refs_0_, bf16[64,64]{1,0:T(8,128)(2,1)} %get-tuple-element.68.refs_1_), custom_call_target="tpu_custom_call" | custom-call | tf_op jit(solution)/shard_map/back/pallas_call | solution.py:261
  65.0 0.1 collective-permute-start.6
  65.1 2.0 %collective-permute-start.11 = (bf16[1368,128]{1,0:T(8,128)(2,1)}, bf16[1368,128]{1,0:T(8,128)(2,1)S(1)}, u32[]{:S(2)}, u32[]{:S(2)}) collective-permute-start(bf16[1368,128]{1,0:T(8,128)(2,1)} %get-tuple-element.81), channel_id=1, source_target_pairs={{0,2},{2,0},{1,3},{3,1},{4,6},{6,4},{5,7},{7,5},{8,10},{10,8},{9,1... | collective-permute-start | bytes 1050632 | tf_op jit(solution)/shard_map/ppermute | solution.py:371
  67.0 0.1 collective-permute-start.7
  67.1 3.8 %collective-permute-done.8 = bf16[1368,128]{1,0:T(8,128)(2,1)S(1)} collective-permute-done((bf16[1368,128]{1,0:T(8,128)(2,1)}, bf16[1368,128]{1,0:T(8,128)(2,1)S(1)}, u32[]{:S(2)}, u32[]{:S(2)}) %collective-permute-start.8) | collective-permute-done | bytes 350240 | tf_op jit(solution)/shard_map/ppermute | solution.py:371
  70.8 1.9 %add_convert_fusion.1 = bf16[1368,128]{1,0:T(8,128)(2,1)} fusion(f32[1368,128]{1,0:T(8,128)} %get-tuple-element.78, bf16[1368,128]{1,0:T(8,128)(2,1)S(1)} %collective-permute-done.8), kind=kLoop, calls=%fused_computation.2 | loop fusion | flops 525312 | bytes 1400832 | tf_op jit(solution)/shard_map/convert_element_type | solution.py:376
  72.8 2.4 %collective-permute-start.9 = (bf16[1368,128]{1,0:T(8,128)(2,1)}, bf16[1368,128]{1,0:T(8,128)(2,1)}, u32[]{:S(2)}, u32[]{:S(2)}) collective-permute-start(bf16[1368,128]{1,0:T(8,128)(2,1)} %add_convert_fusion.1), channel_id=1, source_target_pairs={{0,8},{4,12},{8,0},{12,4},{1,9},{5,13},{9,1},{13,5},{2,10},{6,14},... | collective-permute-start | bytes 1050632 | tf_op jit(solution)/shard_map/ppermute | solution.py:377
  75.2 3.1 %collective-permute-done.6 = bf16[1368,128]{1,0:T(8,128)(2,1)S(1)} collective-permute-done((bf16[1368,128]{1,0:T(8,128)(2,1)}, bf16[1368,128]{1,0:T(8,128)(2,1)S(1)}, u32[]{:S(2)}, u32[]{:S(2)}) %collective-permute-start.6) | collective-permute-done | bytes 350240 | tf_op jit(solution)/shard_map/ppermute | solution.py:371
  78.3 0.0 copy-done.3
  78.3 0.8 add_convert_fusion.2
  79.1 1.6 %collective-permute-start.10 = (bf16[1368,128]{1,0:T(8,128)(2,1)}, bf16[1368,128]{1,0:T(8,128)(2,1)}, u32[]{:S(2)}, u32[]{:S(2)}) collective-permute-start(bf16[1368,128]{1,0:T(8,128)(2,1)} %add_convert_fusion.2), channel_id=1, source_target_pairs={{0,4},{4,8},{8,12},{12,0},{1,5},{5,9},{9,13},{13,1},{2,6},{6,10},{... | collective-permute-start | bytes 1050632 | tf_op jit(solution)/shard_map/ppermute | solution.py:377
  80.7 0.0 all-gather.2.cloned.1.call-done.w_ref
  80.7 0.0 copy-start.2
  80.8 0.0 copy-start.1
  80.8 9.4 %messages.1 = bf16[128,3712]{1,0:T(8,128)(2,1)} custom-call(bf16[21888,128]{1,0:T(8,128)(2,1)} %all-gather.2.cloned.1.call-done.w_ref, bf16[256,3712]{1,0:T(8,128)(2,1)} %get-tuple-element.52.refs_1_.refs_0_, bf16[128,3712]{1,0:T(8,128)(2,1)} %get-tuple-element.53.refs_2_.refs_1_, bf16[16,240,256]{2,1,0:T(8,128)(2,1)} %get-tuple-element.71.refs_2_, ...), custom_call_target="tpu_custom_call" | custom-call | tf_op jit(solution)/shard_map/messages/pallas_call | solution.py:261
  90.1 0.0 collective-permute-done.11
  90.1 0.0 copy-done.2
  90.1 0.1 add_convert_fusion
  90.2 2.3 %collective-permute-start.12 = (bf16[1368,128]{1,0:T(8,128)(2,1)S(1)}, bf16[1368,128]{1,0:T(8,128)(2,1)S(1)}, u32[]{:S(2)}, u32[]{:S(2)}) collective-permute-start(bf16[1368,128]{1,0:T(8,128)(2,1)S(1)} %add_convert_fusion), channel_id=1, source_target_pairs={{0,12},{4,0},{8,4},{12,8},{1,13},{5,1},{9,5},{13,9},{2,14},{6,2},{... | collective-permute-start | bytes 1050632 | tf_op jit(solution)/shard_map/ppermute | solution.py:377
  92.5 0.9 collective-permute-done.7
  93.4 6.7 %collective-permute-done.9 = bf16[1368,128]{1,0:T(8,128)(2,1)} collective-permute-done((bf16[1368,128]{1,0:T(8,128)(2,1)}, bf16[1368,128]{1,0:T(8,128)(2,1)}, u32[]{:S(2)}, u32[]{:S(2)}) %collective-permute-start.9) | collective-permute-done | bytes 350240 | tf_op jit(solution)/shard_map/ppermute | solution.py:377
  100.1 0.0 collective-permute-done.10
  100.1 6.8 %collective-permute-done.12 = bf16[1368,128]{1,0:T(8,128)(2,1)S(1)} collective-permute-done((bf16[1368,128]{1,0:T(8,128)(2,1)S(1)}, bf16[1368,128]{1,0:T(8,128)(2,1)S(1)}, u32[]{:S(2)}, u32[]{:S(2)}) %collective-permute-start.12) | collective-permute-done | bytes 350240 | tf_op jit(solution)/shard_map/ppermute | solution.py:377
  106.9 0.0 copy-done.1
  106.9 2.2 %add_multiply_fusion = f32[1368,128]{1,0:T(8,128)} fusion(bf16[1368,128]{1,0:T(8,128)(2,1)S(1)} %collective-permute-done.12, bf16[1368,128]{1,0:T(8,128)(2,1)} %collective-permute-done.10, bf16[1368,128]{1,0:T(8,128)(2,1)} %collective-permute-done.9, f32[1368,128]{1,0:T(8,128)S(1)} %copy-done.1, bf16[1368,128]{1,0:T(8,128)(2,1)} %collective-permute-done.7), kind=kLoop, calls=%fused_computation | loop fusion | flops 1575936 | bytes 2801664 | tf_op jit(solution)/shard_map/mul | solution.py:381
Async XLA Ops:
  7.2 73.6 %all-gather.2.cloned.1.call-start = ((), (), s32[]{:S(2)}) async-start(), calls=%async_computation | async-start | bytes 5953536 | tf_op jit(solution)/shard_map/all_gather | solution.py:297
  11.0 13.8 %collective-permute-start = (bf16[32,3840]{1,0:T(8,128)(2,1)}, bf16[32,3840]{1,0:T(8,128)(2,1)S(1)}, u32[]{:S(2)}, u32[]{:S(2)}) collective-permute-start(bf16[32,3840]{1,0:T(8,128)(2,1)} %get-tuple-element.43), channel_id=1, source_target_pairs={{2,0},{3,1},{4,2},{5,3},{6,4},{7,5},{10,8},{11,9},{12,10},{13,11},... | collective-permute-start | bytes 737288 | tf_op jit(solution)/shard_map/ppermute | solution.py:292
  12.3 21.7 %collective-permute-start.1 = (bf16[32,3840]{1,0:T(8,128)(2,1)}, bf16[32,3840]{1,0:T(8,128)(2,1)S(1)}, u32[]{:S(2)}, u32[]{:S(2)}) collective-permute-start(bf16[32,3840]{1,0:T(8,128)(2,1)} %get-tuple-element.44), channel_id=1, source_target_pairs={{0,2},{1,3},{2,4},{3,5},{4,6},{5,7},{8,10},{9,11},{10,12},{11,13},... | collective-permute-start | bytes 737288 | tf_op jit(solution)/shard_map/ppermute | solution.py:292
  17.8 21.9 %collective-permute-start.2 = (bf16[32,3840]{1,0:T(8,128)(2,1)}, bf16[32,3840]{1,0:T(8,128)(2,1)}, u32[]{:S(2)}, u32[]{:S(2)}) collective-permute-start(bf16[32,3840]{1,0:T(8,128)(2,1)} %get-tuple-element.46), channel_id=1, source_target_pairs={{1,0},{2,1},{3,2},{4,3},{5,4},{6,5},{7,6},{9,8},{10,9},{11,10},{12... | collective-permute-start | bytes 737288 | tf_op jit(solution)/shard_map/ppermute | solution.py:292
  19.1 20.6 %collective-permute-start.3 = (bf16[32,3840]{1,0:T(8,128)(2,1)}, bf16[32,3840]{1,0:T(8,128)(2,1)}, u32[]{:S(2)}, u32[]{:S(2)}) collective-permute-start(bf16[32,3840]{1,0:T(8,128)(2,1)} %get-tuple-element.47), channel_id=1, source_target_pairs={{0,1},{1,2},{2,3},{3,4},{4,5},{5,6},{6,7},{8,9},{9,10},{10,11},{11... | collective-permute-start | bytes 737288 | tf_op jit(solution)/shard_map/ppermute | solution.py:292
  24.8 9.2 %copy-start.4 = (bf16[32,3840]{1,0:T(8,128)(2,1)}, bf16[32,3840]{1,0:T(8,128)(2,1)S(1)}, u32[]{:S(2)}) copy-start(bf16[32,3840]{1,0:T(8,128)(2,1)S(1)} %collective-permute-done.refs_1_) | copy-start | bytes 737284
  34.0 0.7 copy-start.5
  39.6 6.8 %collective-permute-start.4 = (bf16[256,3712]{1,0:T(8,128)(2,1)}, bf16[256,3712]{1,0:T(8,128)(2,1)S(1)}, u32[]{:S(2)}, u32[]{:S(2)}) collective-permute-start(bf16[256,3712]{1,0:T(8,128)(2,1)} %get-tuple-element.52.refs_1_.refs_0_), channel_id=1, source_target_pairs={{0,1},{1,0},{2,3},{3,2},{4,5},{5,4},{6,7},{7,6},{8,9},{9,8},{10,11... | collective-permute-start | bytes 5701640 | tf_op jit(solution)/shard_map/ppermute | solution.py:295
  43.5 3.0 %collective-permute-start.5 = (bf16[128,3712]{1,0:T(8,128)(2,1)}, bf16[128,3712]{1,0:T(8,128)(2,1)}, u32[]{:S(2)}, u32[]{:S(2)}) collective-permute-start(bf16[128,3712]{1,0:T(8,128)(2,1)} %get-tuple-element.53.refs_2_.refs_1_), channel_id=1, source_target_pairs={{0,1},{1,0},{2,3},{3,2},{4,5},{5,4},{6,7},{7,6},{8,9},{9,8},{10,11... | collective-permute-start | bytes 2850824 | tf_op jit(solution)/shard_map/ppermute | solution.py:295
  46.5 1.3 %copy-start = (bf16[256,3712]{1,0:T(8,128)(2,1)}, bf16[256,3712]{1,0:T(8,128)(2,1)S(1)}, u32[]{:S(2)}) copy-start(bf16[256,3712]{1,0:T(8,128)(2,1)S(1)} %collective-permute-done.4.refs_3_) | copy-start | bytes 5701636
  56.8 21.5 %copy-start.3 = (f32[1368,128]{1,0:T(8,128)S(1)}, f32[1368,128]{1,0:T(8,128)}, u32[]{:S(2)}) copy-start(f32[1368,128]{1,0:T(8,128)} %get-tuple-element.63) | copy-start | bytes 2101252
  56.8 14.0 %collective-permute-start.8 = (bf16[1368,128]{1,0:T(8,128)(2,1)}, bf16[1368,128]{1,0:T(8,128)(2,1)S(1)}, u32[]{:S(2)}, u32[]{:S(2)}) collective-permute-start(bf16[1368,128]{1,0:T(8,128)(2,1)} %get-tuple-element.79), channel_id=1, source_target_pairs={{0,2},{2,0},{1,3},{3,1},{4,6},{6,4},{5,7},{7,5},{8,10},{10,8},{9,1... | collective-permute-start | bytes 1050632 | tf_op jit(solution)/shard_map/ppermute | solution.py:371
  65.0 13.4 %collective-permute-start.6 = (bf16[1368,128]{1,0:T(8,128)(2,1)}, bf16[1368,128]{1,0:T(8,128)(2,1)S(1)}, u32[]{:S(2)}, u32[]{:S(2)}) collective-permute-start(bf16[1368,128]{1,0:T(8,128)(2,1)} %get-tuple-element.64), channel_id=1, source_target_pairs={{0,2},{2,0},{1,3},{3,1},{4,6},{6,4},{5,7},{7,5},{8,10},{10,8},{9,1... | collective-permute-start | bytes 1050632 | tf_op jit(solution)/shard_map/ppermute | solution.py:371
  65.1 25.1 %collective-permute-start.11 = (bf16[1368,128]{1,0:T(8,128)(2,1)}, bf16[1368,128]{1,0:T(8,128)(2,1)S(1)}, u32[]{:S(2)}, u32[]{:S(2)}) collective-permute-start(bf16[1368,128]{1,0:T(8,128)(2,1)} %get-tuple-element.81), channel_id=1, source_target_pairs={{0,2},{2,0},{1,3},{3,1},{4,6},{6,4},{5,7},{7,5},{8,10},{10,8},{9,1... | collective-permute-start | bytes 1050632 | tf_op jit(solution)/shard_map/ppermute | solution.py:371
  67.0 26.4 %collective-permute-start.7 = (bf16[1368,128]{1,0:T(8,128)(2,1)}, bf16[1368,128]{1,0:T(8,128)(2,1)}, u32[]{:S(2)}, u32[]{:S(2)}) collective-permute-start(bf16[1368,128]{1,0:T(8,128)(2,1)} %get-tuple-element.77), channel_id=1, source_target_pairs={{0,2},{2,0},{1,3},{3,1},{4,6},{6,4},{5,7},{7,5},{8,10},{10,8},{9,1... | collective-permute-start | bytes 1050632 | tf_op jit(solution)/shard_map/ppermute | solution.py:371
  72.8 27.3 %collective-permute-start.9 = (bf16[1368,128]{1,0:T(8,128)(2,1)}, bf16[1368,128]{1,0:T(8,128)(2,1)}, u32[]{:S(2)}, u32[]{:S(2)}) collective-permute-start(bf16[1368,128]{1,0:T(8,128)(2,1)} %add_convert_fusion.1), channel_id=1, source_target_pairs={{0,8},{4,12},{8,0},{12,4},{1,9},{5,13},{9,1},{13,5},{2,10},{6,14},... | collective-permute-start | bytes 1050632 | tf_op jit(solution)/shard_map/ppermute | solution.py:377
  79.1 20.9 %collective-permute-start.10 = (bf16[1368,128]{1,0:T(8,128)(2,1)}, bf16[1368,128]{1,0:T(8,128)(2,1)}, u32[]{:S(2)}, u32[]{:S(2)}) collective-permute-start(bf16[1368,128]{1,0:T(8,128)(2,1)} %add_convert_fusion.2), channel_id=1, source_target_pairs={{0,4},{4,8},{8,12},{12,0},{1,5},{5,9},{9,13},{13,1},{2,6},{6,10},{... | collective-permute-start | bytes 1050632 | tf_op jit(solution)/shard_map/ppermute | solution.py:377
  80.7 9.4 %copy-start.2 = (f32[1368,128]{1,0:T(8,128)S(1)}, f32[1368,128]{1,0:T(8,128)}, u32[]{:S(2)}) copy-start(f32[1368,128]{1,0:T(8,128)} %get-tuple-element.80) | copy-start | bytes 2101252
  80.8 26.1 %copy-start.1 = (f32[1368,128]{1,0:T(8,128)S(1)}, f32[1368,128]{1,0:T(8,128)}, u32[]{:S(2)}) copy-start(f32[1368,128]{1,0:T(8,128)} %get-tuple-element.76) | copy-start | bytes 2101252
  90.2 16.7 %collective-permute-start.12 = (bf16[1368,128]{1,0:T(8,128)(2,1)S(1)}, bf16[1368,128]{1,0:T(8,128)(2,1)S(1)}, u32[]{:S(2)}, u32[]{:S(2)}) collective-permute-start(bf16[1368,128]{1,0:T(8,128)(2,1)S(1)} %add_convert_fusion), channel_id=1, source_target_pairs={{0,12},{4,0},{8,4},{12,8},{1,13},{5,1},{9,5},{13,9},{2,14},{6,2},{... | collective-permute-start | bytes 1050632 | tf_op jit(solution)/shard_map/ppermute | solution.py:377
Sparse Core Ops, SparseCore 0:
  10.2 69.3 all-gather.1

commit v6 on v5

--- a/solution.py
+++ b/solution.py
@@ -142,10 +142,6 @@
         build(tabt_ref, refs[i][...], refs[2 + i], refs[4 + i])
 
 
-def shifts(n_z):
-    return sorted(range(n_z), key=lambda i: (i == 0, abs(i - n_z // 2)))
-
-
 def grad_kernel(n_z, n_x, me_ref, *refs):
     parts, outs, flat = refs[:4], refs[4:-1], refs[-1]
     chip, core = me_ref[0] // 2, me_ref[0] % 2
@@ -179,8 +175,8 @@
     rows = outs[0].shape[0]
     at_out = 0
     for o in list(range(1, n_x)) + [0]:
-        for i in shifts(n_z):
-            start = (((z + i) % n_z * n_x + (x + o) % n_x) * 2 + core) * rows
+        for r in reversed(range(n_z)):
+            start = (((z ^ r) * n_x + (x + o) % n_x) * 2 + core) * rows
             if rows % 8 == 0:
                 start = pl.multiple_of(start, 8)
             ref = outs[at_out]
@@ -351,33 +347,36 @@
     )
     kept = blocks[n_send:]
     kept[0], mats = lax.optimization_barrier((kept[0], mats))
-    arrived, terms = [], []
-    for at, i in enumerate(shifts(n_z)):
+    sums = {}
+    for at, r in enumerate(reversed(range(n_z))):
         total = kept[at]
-        if at == 2:
-            weights, _ = lax.optimization_barrier((weights, terms[1]))
-            slots = n // 2 + 4 * cap
-            (node_out,) = call(
-                message_kernel, "messages", 62,
-                [shape((n, width), BF16)],
-                [weights, *both, *mats, *hots],
-                [
-                    pltpu.VMEM((rows * n_dp, 128), F32), pltpu.VMEM((32, slots, 128), F32),
-                    pltpu.VMEM((30, slots, 128), F32), pltpu.VMEM((slots, width), BF16),
-                ],
-            )
-            total, node_out = lax.optimization_barrier((total, node_out))
         for o in range(1, n_x):
             got = lax.ppermute(
                 blocks[(o - 1) * n_z + at], "x", [(s, (s + o) % n_x) for s in range(n_x)]
             )
             total = total + got.astype(F32)
-        if i:
-            terms.append(total.astype(BF16))
-            arrived.append(lax.ppermute(terms[-1], "z", [(s, (s + i) % n_z) for s in range(n_z)]))
-    result = total
-    for got in arrived:
-        result = result + got.astype(F32)
+        sums[r] = total
+    for bit in [1 << i for i in range(n_z.bit_length() - 1)]:
+        for r in reversed(range(bit, n_z, 2 * bit)):
+            term = sums[r].astype(BF16)
+            if (bit, r) == (1, 1):
+                last_term = term
+            got = lax.ppermute(term, "z", [(s, s ^ bit) for s in range(n_z)])
+            if 2 * bit < n_z:
+                sums[r ^ bit] = sums[r ^ bit] + got.astype(F32)
+    weights, _ = lax.optimization_barrier((weights, last_term))
+    slots = n // 2 + 4 * cap
+    (node_out,) = call(
+        message_kernel, "messages", 62,
+        [shape((n, width), BF16)],
+        [weights, *both, *mats, *hots],
+        [
+            pltpu.VMEM((rows * n_dp, 128), F32), pltpu.VMEM((32, slots, 128), F32),
+            pltpu.VMEM((30, slots, 128), F32), pltpu.VMEM((slots, width), BF16),
+        ],
+    )
+    got, node_out = lax.optimization_barrier((got, node_out))
+    result = sums[0] + got.astype(F32)
     weight_grad = result * (1.0 / math.sqrt(n * n_dp))
     return (node_out, weight_grad)
 

time: 116 us -> 114 us (0.983)
  starting transfers between devices: 23.1 us -> 21 us
    ppermute x3, starting transfers between devices: 6.3 us -> 4.23 us  [on_device(): got = lax.ppermute(term, 'z', [(s, s ^ bit) for s in range(n_z)])]
  transfers between devices with their start and end apart: 14 -> 14, of which waited for: 7 -> 8; matrix products, arithmetic and copies ran while one was open for 6% -> 5% of each run, Pallas kernels for 27% -> 27%
where the time goes in v6:
time: 114 us; the launch traced here: 113 us
  Pallas kernels  34.1 us (30%)
  waiting for transfers between devices  33.9 us (30%)
  starting transfers between devices  21 us (18%)
  between operations  14.1 us (12%)
  local copies, waits for them, and re-layouts  6.01 us (5%)
  other arithmetic  4.23 us (4%)
    pallas_call x6, Pallas kernels, call(): pl.pallas_call(kernel, grid=(1,), out_shape=outs, in_specs=first + [whole...  34.1 us
    ppermute x3, waiting for transfers between devices, on_device(): got = lax.ppermute(term, 'z', [(s, s ^ bit) for s in range(n_z)])  12.9 us
    ppermute x4, starting transfers between devices, shift(): return lax.ppermute(block, ALL, route)  11.8 us
    ppermute x4, waiting for transfers between devices, shift(): return lax.ppermute(block, ALL, route)  9.2 us
    ppermute x4, waiting for transfers between devices, on_device(): lax.ppermute(blocks[(o - 1) * n_z + at], 'x', [(s, (s + o) % n_x) for s i...  8.61 us
    ppermute x4, starting transfers between devices, on_device(): lax.ppermute(blocks[(o - 1) * n_z + at], 'x', [(s, (s + o) % n_x) for s i...  4.48 us
    ppermute x3, starting transfers between devices, on_device(): got = lax.ppermute(term, 'z', [(s, s ^ bit) for s in range(n_z)])  4.23 us
    ppermute x2, waiting for transfers between devices, swap(): return lax.ppermute(block, 'core', [(0, 1), (1, 0)])  2.49 us
  transfers between devices with their start and end apart: 14, of which 8 were waited for; matrix products, arithmetic and copies ran while one was open for 5% of the time, Pallas kernels for 27%

profile of v6, /device:TPU:0, one launch (start us, length us, event | category | flops | bytes accessed | tf_op | source)
XLA Modules:
  0.0 113.3 jit_solution(15800993267339599194)
XLA Ops:
  7.2 0.0 all-gather.2.cloned.1.call-start
  7.2 0.7 all-gather.2.cloned.1.call-update
  7.9 3.1 %send.1 = (bf16[64,3840]{1,0:T(8,128)(2,1)}, bf16[32,3840]{1,0:T(8,128)(2,1)}, bf16[32,3840]{1,0:T(8,128)(2,1)}, bf16[32,3840]{1,0:T(8,128)(2,1)}, bf16[32,3840]{1,0:T(8,128)(2,1)}) custom-call(s32[1]{0:T(128)} %bitcast.me_ref.refs_0_, s32[1,128]{1,0:T(1,128)} %bitcast.14, s32[1,128]{1,0:T(1,128)} %bitcast.15, s32[1,128]{1,0:T(1,128)} %bitcast.16, ...), custom_call_target="tpu_custom_call" | custom-call | tf_op jit(solution)/shard_map/send/pallas_call | solution.py:257
  11.0 1.3 %collective-permute-start = (bf16[32,3840]{1,0:T(8,128)(2,1)}, bf16[32,3840]{1,0:T(8,128)(2,1)S(1)}, u32[]{:S(2)}, u32[]{:S(2)}) collective-permute-start(bf16[32,3840]{1,0:T(8,128)(2,1)} %get-tuple-element.43), channel_id=1, source_target_pairs={{2,0},{3,1},{4,2},{5,3},{6,4},{7,5},{10,8},{11,9},{12,10},{13,11},... | collective-permute-start | bytes 737288 | tf_op jit(solution)/shard_map/ppermute | solution.py:288
  12.3 5.5 %collective-permute-start.1 = (bf16[32,3840]{1,0:T(8,128)(2,1)}, bf16[32,3840]{1,0:T(8,128)(2,1)S(1)}, u32[]{:S(2)}, u32[]{:S(2)}) collective-permute-start(bf16[32,3840]{1,0:T(8,128)(2,1)} %get-tuple-element.44), channel_id=1, source_target_pairs={{0,2},{1,3},{2,4},{3,5},{4,6},{5,7},{8,10},{9,11},{10,12},{11,13},... | collective-permute-start | bytes 737288 | tf_op jit(solution)/shard_map/ppermute | solution.py:288
  17.8 1.3 %collective-permute-start.2 = (bf16[32,3840]{1,0:T(8,128)(2,1)}, bf16[32,3840]{1,0:T(8,128)(2,1)}, u32[]{:S(2)}, u32[]{:S(2)}) collective-permute-start(bf16[32,3840]{1,0:T(8,128)(2,1)} %get-tuple-element.46), channel_id=1, source_target_pairs={{1,0},{2,1},{3,2},{4,3},{5,4},{6,5},{7,6},{9,8},{10,9},{11,10},{12... | collective-permute-start | bytes 737288 | tf_op jit(solution)/shard_map/ppermute | solution.py:288
  19.1 3.7 %collective-permute-start.3 = (bf16[32,3840]{1,0:T(8,128)(2,1)}, bf16[32,3840]{1,0:T(8,128)(2,1)}, u32[]{:S(2)}, u32[]{:S(2)}) collective-permute-start(bf16[32,3840]{1,0:T(8,128)(2,1)} %get-tuple-element.47), channel_id=1, source_target_pairs={{0,1},{1,2},{2,3},{3,4},{4,5},{5,6},{6,7},{8,9},{9,10},{10,11},{11... | collective-permute-start | bytes 737288 | tf_op jit(solution)/shard_map/ppermute | solution.py:288
  22.8 2.0 %copy.10 = bf16[29,64,29]{2,1,0:T(8,128)(2,1)} copy(bf16[29,64,29]{1,2,0:T(8,128)(2,1)} %bitcast.12) | data formatting | bytes 215296 | tf_op jit(solution)/shard_map/transpose | solution.py:304
  24.8 0.0 collective-permute-done.refs_1_
  24.8 0.0 copy-start.4
  24.8 9.2 %collective-permute-done.1.refs_2_ = bf16[32,3840]{1,0:T(8,128)(2,1)S(1)} collective-permute-done((bf16[32,3840]{1,0:T(8,128)(2,1)}, bf16[32,3840]{1,0:T(8,128)(2,1)S(1)}, u32[]{:S(2)}, u32[]{:S(2)}) %collective-permute-start.1) | collective-permute-done | bytes 245792 | tf_op jit(solution)/shard_map/ppermute | solution.py:288
  34.0 0.0 copy-start.5
  34.0 0.0 copy-done.4
  34.0 0.7 copy-done.5
  34.7 5.0 %rotate_first.1 = (bf16[256,3712]{1,0:T(8,128)(2,1)}, bf16[128,128]{1,0:T(8,128)(2,1)}, bf16[128,64]{1,0:T(8,128)(2,1)}) custom-call(bf16[64,3840]{1,0:T(8,128)(2,1)} %get-tuple-element.42.refs_0_, bf16[32,3840]{1,0:T(8,128)(2,1)} %copy-done.4, bf16[32,3840]{1,0:T(8,128)(2,1)} %copy-done.5, bf16[1856,29]{1,0:T(8,128)(2,1)} %bitcast.9, bf16[128,3712]{1,0:T(8,128)(2,1)} %refs_3_.1), custom_call_target="tpu_custom_call" | custom-call | tf_op jit(solution)/shard_map/rotate_first/pallas_call | solution.py:257
  39.6 0.0 collective-permute-start.4
  39.6 0.0 collective-permute-done.2.refs_0_
  39.7 0.0 collective-permute-done.3.refs_1_
  39.7 3.8 %rotate_last.1 = (bf16[128,3712]{1,0:T(8,128)(2,1)}, bf16[64,128]{1,0:T(8,128)(2,1)}, bf16[64,64]{1,0:T(8,128)(2,1)}) custom-call(bf16[32,3840]{1,0:T(8,128)(2,1)} %collective-permute-done.2.refs_0_, bf16[32,3840]{1,0:T(8,128)(2,1)} %collective-permute-done.3.refs_1_, bf16[1856,29]{1,0:T(8,128)(2,1)} %bitcast.10, bf16[128,3712]{1,0:T(8,128)(2,1)} %refs_3_.1), custom_call_target="tpu_custom_call" | custom-call | flops 10000000000 | bytes 100000000 | tf_op jit(solution)/shard_map/rotate_last/pallas_call | solution.py:257
  43.5 0.5 collective-permute-start.5
  44.0 2.5 %collective-permute-done.5.refs_4_ = bf16[128,3712]{1,0:T(8,128)(2,1)} collective-permute-done((bf16[128,3712]{1,0:T(8,128)(2,1)}, bf16[128,3712]{1,0:T(8,128)(2,1)}, u32[]{:S(2)}, u32[]{:S(2)}) %collective-permute-start.5) | collective-permute-done | bytes 950304 | tf_op jit(solution)/shard_map/ppermute | solution.py:291
  46.5 0.0 collective-permute-done.4.refs_3_
  46.5 0.0 copy-start
  46.5 1.3 %copy-done = bf16[256,3712]{1,0:T(8,128)(2,1)} copy-done((bf16[256,3712]{1,0:T(8,128)(2,1)}, bf16[256,3712]{1,0:T(8,128)(2,1)S(1)}, u32[]{:S(2)}) %copy-start) | copy-done | bytes 1900568
  47.7 9.1 %weight_terms.1 = (bf16[1368,128]{1,0:T(8,128)(2,1)}, bf16[1368,128]{1,0:T(8,128)(2,1)}, bf16[1368,128]{1,0:T(8,128)(2,1)}, bf16[1368,128]{1,0:T(8,128)(2,1)}, f...) custom-call(s32[1]{0:T(128)} %bitcast.me_ref.refs_0_, ...), custom_call_target="tpu_custom_call" | custom-call | tf_op jit(solution)/shard_map/weight_terms/pallas_call | solution.py:257
  56.8 0.0 copy-start.3
  56.8 2.4 %collective-permute-start.7 = (bf16[1368,128]{1,0:T(8,128)(2,1)}, bf16[1368,128]{1,0:T(8,128)(2,1)S(1)}, u32[]{:S(2)}, u32[]{:S(2)}) collective-permute-start(bf16[1368,128]{1,0:T(8,128)(2,1)} %get-tuple-element.70), channel_id=1, source_target_pairs={{0,2},{2,0},{1,3},{3,1},{4,6},{6,4},{5,7},{7,5},{8,10},{10,8},{9,1... | collective-permute-start | bytes 1050632 | tf_op jit(solution)/shard_map/ppermute | solution.py:354
  59.2 2.1 %copy.11 = bf16[29,64,29]{2,1,0:T(8,128)(2,1)} copy(bf16[29,64,29]{1,0,2:T(8,128)(2,1)} %bitcast.13) | data formatting | bytes 215296 | tf_op jit(solution)/shard_map/transpose | solution.py:305
  61.3 0.0 copy-start.2
  61.3 3.8 %back.1 = (bf16[16,240,256]{2,1,0:T(8,128)(2,1)}, bf16[8,240,256]{2,1,0:T(8,128)(2,1)}) custom-call(bf16[1856,29]{1,0:T(8,128)(2,1)} %bitcast.11, bf16[128,64]{1,0:T(8,128)(2,1)} %get-tuple-element.65.refs_0_, bf16[64,64]{1,0:T(8,128)(2,1)} %get-tuple-element.66.refs_1_), custom_call_target="tpu_custom_call" | custom-call | tf_op jit(solution)/shard_map/back/pallas_call | solution.py:257
  65.0 0.1 collective-permute-start.6
  65.1 5.7 %collective-permute-done.7 = bf16[1368,128]{1,0:T(8,128)(2,1)S(1)} collective-permute-done((bf16[1368,128]{1,0:T(8,128)(2,1)}, bf16[1368,128]{1,0:T(8,128)(2,1)S(1)}, u32[]{:S(2)}, u32[]{:S(2)}) %collective-permute-start.7) | collective-permute-done | bytes 350240 | tf_op jit(solution)/shard_map/ppermute | solution.py:354
  70.8 1.2 %add_convert_fusion.2 = bf16[1368,128]{1,0:T(8,128)(2,1)S(1)} fusion(f32[1368,128]{1,0:T(8,128)} %get-tuple-element.69, bf16[1368,128]{1,0:T(8,128)(2,1)S(1)} %collective-permute-done.7), kind=kLoop, calls=%fused_computation.3 | loop fusion | flops 525312 | bytes 1400832 | tf_op jit(solution)/shard_map/convert_element_type | solution.py:361
  72.0 1.7 %collective-permute-start.8 = (bf16[1368,128]{1,0:T(8,128)(2,1)S(1)}, bf16[1368,128]{1,0:T(8,128)(2,1)S(1)}, u32[]{:S(2)}, u32[]{:S(2)}) collective-permute-start(bf16[1368,128]{1,0:T(8,128)(2,1)S(1)} %add_convert_fusion.2), channel_id=1, source_target_pairs={{0,4},{4,0},{8,12},{12,8},{1,5},{5,1},{9,13},{13,9},{2,6},{6,2},{1... | collective-permute-start | bytes 1050632 | tf_op jit(solution)/shard_map/ppermute | solution.py:364
  73.7 0.5 collective-permute-start.10
  74.1 1.6 %collective-permute-start.11 = (bf16[1368,128]{1,0:T(8,128)(2,1)}, bf16[1368,128]{1,0:T(8,128)(2,1)}, u32[]{:S(2)}, u32[]{:S(2)}) collective-permute-start(bf16[1368,128]{1,0:T(8,128)(2,1)} %get-tuple-element.80), channel_id=1, source_target_pairs={{0,2},{2,0},{1,3},{3,1},{4,6},{6,4},{5,7},{7,5},{8,10},{10,8},{9,1... | collective-permute-start | bytes 1050632 | tf_op jit(solution)/shard_map/ppermute | solution.py:354
  75.7 2.6 %collective-permute-done.6 = bf16[1368,128]{1,0:T(8,128)(2,1)S(1)} collective-permute-done((bf16[1368,128]{1,0:T(8,128)(2,1)}, bf16[1368,128]{1,0:T(8,128)(2,1)S(1)}, u32[]{:S(2)}, u32[]{:S(2)}) %collective-permute-start.6) | collective-permute-done | bytes 350240 | tf_op jit(solution)/shard_map/ppermute | solution.py:354
  78.3 6.3 %collective-permute-done.8 = bf16[1368,128]{1,0:T(8,128)(2,1)S(1)} collective-permute-done((bf16[1368,128]{1,0:T(8,128)(2,1)S(1)}, bf16[1368,128]{1,0:T(8,128)(2,1)S(1)}, u32[]{:S(2)}, u32[]{:S(2)}) %collective-permute-start.8) | collective-permute-done | bytes 350240 | tf_op jit(solution)/shard_map/ppermute | solution.py:364
  84.7 0.0 copy-done.3
  84.7 0.1 add_convert_fusion.1
  84.8 0.8 collective-permute-start.9
  85.6 0.3 collective-permute-done.10
  85.8 0.0 copy-done.2
  85.8 0.8 add_convert_fusion
  86.7 1.8 %collective-permute-start.12 = (bf16[1368,128]{1,0:T(8,128)(2,1)}, bf16[1368,128]{1,0:T(8,128)(2,1)S(1)}, u32[]{:S(2)}, u32[]{:S(2)}) collective-permute-start(bf16[1368,128]{1,0:T(8,128)(2,1)} %add_convert_fusion), channel_id=1, source_target_pairs={{0,4},{4,0},{8,12},{12,8},{1,5},{5,1},{9,13},{13,9},{2,6},{6,2},{1... | collective-permute-start | bytes 1050632 | tf_op jit(solution)/shard_map/ppermute | solution.py:364
  88.5 0.0 all-gather.2.cloned.1.call-done.w_ref
  88.5 0.0 copy-start.1
  88.5 9.3 %messages.1 = bf16[128,3712]{1,0:T(8,128)(2,1)} custom-call(bf16[21888,128]{1,0:T(8,128)(2,1)} %all-gather.2.cloned.1.call-done.w_ref, bf16[256,3712]{1,0:T(8,128)(2,1)} %get-tuple-element.52.refs_1_.refs_0_, bf16[128,3712]{1,0:T(8,128)(2,1)} %get-tuple-element.53.refs_2_.refs_1_, bf16[16,240,256]{2,1,0:T(8,128)(2,1)} %get-tuple-element.74.refs_2_, ...), custom_call_target="tpu_custom_call" | custom-call | tf_op jit(solution)/shard_map/messages/pallas_call | solution.py:257
  97.8 5.4 %collective-permute-done.9 = bf16[1368,128]{1,0:T(8,128)(2,1)} collective-permute-done((bf16[1368,128]{1,0:T(8,128)(2,1)S(1)}, bf16[1368,128]{1,0:T(8,128)(2,1)}, u32[]{:S(2)}, u32[]{:S(2)}) %collective-permute-start.9) | collective-permute-done | bytes 350240 | tf_op jit(solution)/shard_map/ppermute | solution.py:364
  103.1 0.0 collective-permute-done.11
  103.1 1.2 %collective-permute-done.12 = bf16[1368,128]{1,0:T(8,128)(2,1)S(1)} collective-permute-done((bf16[1368,128]{1,0:T(8,128)(2,1)}, bf16[1368,128]{1,0:T(8,128)(2,1)S(1)}, u32[]{:S(2)}, u32[]{:S(2)}) %collective-permute-start.12) | collective-permute-done | bytes 350240 | tf_op jit(solution)/shard_map/ppermute | solution.py:364
  104.3 0.0 copy-done.1
  104.3 2.1 %add_multiply_fusion = f32[1368,128]{1,0:T(8,128)} fusion(bf16[1368,128]{1,0:T(8,128)(2,1)} %collective-permute-done.9, bf16[1368,128]{1,0:T(8,128)(2,1)S(1)} %collective-permute-done.12, f32[1368,128]{1,0:T(8,128)S(1)} %copy-done.1, bf16[1368,128]{1,0:T(8,128)(2,1)} %collective-permute-done.11), kind=kLoop, calls=%fused_computation | loop fusion | flops 1225728 | bytes 2451456 | tf_op jit(solution)/shard_map/mul | solution.py:380
Async XLA Ops:
  7.2 81.3 %all-gather.2.cloned.1.call-start = ((), (), s32[]{:S(2)}) async-start(), calls=%async_computation | async-start | bytes 5953536 | tf_op jit(solution)/shard_map/all_gather | solution.py:293
  11.0 13.8 %collective-permute-start = (bf16[32,3840]{1,0:T(8,128)(2,1)}, bf16[32,3840]{1,0:T(8,128)(2,1)S(1)}, u32[]{:S(2)}, u32[]{:S(2)}) collective-permute-start(bf16[32,3840]{1,0:T(8,128)(2,1)} %get-tuple-element.43), channel_id=1, source_target_pairs={{2,0},{3,1},{4,2},{5,3},{6,4},{7,5},{10,8},{11,9},{12,10},{13,11},... | collective-permute-start | bytes 737288 | tf_op jit(solution)/shard_map/ppermute | solution.py:288
  12.3 21.7 %collective-permute-start.1 = (bf16[32,3840]{1,0:T(8,128)(2,1)}, bf16[32,3840]{1,0:T(8,128)(2,1)S(1)}, u32[]{:S(2)}, u32[]{:S(2)}) collective-permute-start(bf16[32,3840]{1,0:T(8,128)(2,1)} %get-tuple-element.44), channel_id=1, source_target_pairs={{0,2},{1,3},{2,4},{3,5},{4,6},{5,7},{8,10},{9,11},{10,12},{11,13},... | collective-permute-start | bytes 737288 | tf_op jit(solution)/shard_map/ppermute | solution.py:288
  17.8 21.9 %collective-permute-start.2 = (bf16[32,3840]{1,0:T(8,128)(2,1)}, bf16[32,3840]{1,0:T(8,128)(2,1)}, u32[]{:S(2)}, u32[]{:S(2)}) collective-permute-start(bf16[32,3840]{1,0:T(8,128)(2,1)} %get-tuple-element.46), channel_id=1, source_target_pairs={{1,0},{2,1},{3,2},{4,3},{5,4},{6,5},{7,6},{9,8},{10,9},{11,10},{12... | collective-permute-start | bytes 737288 | tf_op jit(solution)/shard_map/ppermute | solution.py:288
  19.1 20.6 %collective-permute-start.3 = (bf16[32,3840]{1,0:T(8,128)(2,1)}, bf16[32,3840]{1,0:T(8,128)(2,1)}, u32[]{:S(2)}, u32[]{:S(2)}) collective-permute-start(bf16[32,3840]{1,0:T(8,128)(2,1)} %get-tuple-element.47), channel_id=1, source_target_pairs={{0,1},{1,2},{2,3},{3,4},{4,5},{5,6},{6,7},{8,9},{9,10},{10,11},{11... | collective-permute-start | bytes 737288 | tf_op jit(solution)/shard_map/ppermute | solution.py:288
  24.8 9.2 %copy-start.4 = (bf16[32,3840]{1,0:T(8,128)(2,1)}, bf16[32,3840]{1,0:T(8,128)(2,1)S(1)}, u32[]{:S(2)}) copy-start(bf16[32,3840]{1,0:T(8,128)(2,1)S(1)} %collective-permute-done.refs_1_) | copy-start | bytes 737284
  34.0 0.7 copy-start.5
  39.6 6.8 %collective-permute-start.4 = (bf16[256,3712]{1,0:T(8,128)(2,1)}, bf16[256,3712]{1,0:T(8,128)(2,1)S(1)}, u32[]{:S(2)}, u32[]{:S(2)}) collective-permute-start(bf16[256,3712]{1,0:T(8,128)(2,1)} %get-tuple-element.52.refs_1_.refs_0_), channel_id=1, source_target_pairs={{0,1},{1,0},{2,3},{3,2},{4,5},{5,4},{6,7},{7,6},{8,9},{9,8},{10,11... | collective-permute-start | bytes 5701640 | tf_op jit(solution)/shard_map/ppermute | solution.py:291
  43.5 3.0 %collective-permute-start.5 = (bf16[128,3712]{1,0:T(8,128)(2,1)}, bf16[128,3712]{1,0:T(8,128)(2,1)}, u32[]{:S(2)}, u32[]{:S(2)}) collective-permute-start(bf16[128,3712]{1,0:T(8,128)(2,1)} %get-tuple-element.53.refs_2_.refs_1_), channel_id=1, source_target_pairs={{0,1},{1,0},{2,3},{3,2},{4,5},{5,4},{6,7},{7,6},{8,9},{9,8},{10,11... | collective-permute-start | bytes 2850824 | tf_op jit(solution)/shard_map/ppermute | solution.py:291
  46.5 1.3 %copy-start = (bf16[256,3712]{1,0:T(8,128)(2,1)}, bf16[256,3712]{1,0:T(8,128)(2,1)S(1)}, u32[]{:S(2)}) copy-start(bf16[256,3712]{1,0:T(8,128)(2,1)S(1)} %collective-permute-done.4.refs_3_) | copy-start | bytes 5701636
  56.8 27.8 %copy-start.3 = (f32[1368,128]{1,0:T(8,128)S(1)}, f32[1368,128]{1,0:T(8,128)}, u32[]{:S(2)}) copy-start(f32[1368,128]{1,0:T(8,128)} %get-tuple-element.62) | copy-start | bytes 2101252
  56.8 14.0 %collective-permute-start.7 = (bf16[1368,128]{1,0:T(8,128)(2,1)}, bf16[1368,128]{1,0:T(8,128)(2,1)S(1)}, u32[]{:S(2)}, u32[]{:S(2)}) collective-permute-start(bf16[1368,128]{1,0:T(8,128)(2,1)} %get-tuple-element.70), channel_id=1, source_target_pairs={{0,2},{2,0},{1,3},{3,1},{4,6},{6,4},{5,7},{7,5},{8,10},{10,8},{9,1... | collective-permute-start | bytes 1050632 | tf_op jit(solution)/shard_map/ppermute | solution.py:354
  61.3 24.6 %copy-start.2 = (f32[1368,128]{1,0:T(8,128)S(1)}, f32[1368,128]{1,0:T(8,128)}, u32[]{:S(2)}) copy-start(f32[1368,128]{1,0:T(8,128)} %get-tuple-element.71) | copy-start | bytes 2101252
  65.0 13.3 %collective-permute-start.6 = (bf16[1368,128]{1,0:T(8,128)(2,1)}, bf16[1368,128]{1,0:T(8,128)(2,1)S(1)}, u32[]{:S(2)}, u32[]{:S(2)}) collective-permute-start(bf16[1368,128]{1,0:T(8,128)(2,1)} %get-tuple-element.63), channel_id=1, source_target_pairs={{0,2},{2,0},{1,3},{3,1},{4,6},{6,4},{5,7},{7,5},{8,10},{10,8},{9,1... | collective-permute-start | bytes 1050632 | tf_op jit(solution)/shard_map/ppermute | solution.py:354
  72.0 12.6 %collective-permute-start.8 = (bf16[1368,128]{1,0:T(8,128)(2,1)S(1)}, bf16[1368,128]{1,0:T(8,128)(2,1)S(1)}, u32[]{:S(2)}, u32[]{:S(2)}) collective-permute-start(bf16[1368,128]{1,0:T(8,128)(2,1)S(1)} %add_convert_fusion.2), channel_id=1, source_target_pairs={{0,4},{4,0},{8,12},{12,8},{1,5},{5,1},{9,13},{13,9},{2,6},{6,2},{1... | collective-permute-start | bytes 1050632 | tf_op jit(solution)/shard_map/ppermute | solution.py:364
  73.7 12.2 %collective-permute-start.10 = (bf16[1368,128]{1,0:T(8,128)(2,1)}, bf16[1368,128]{1,0:T(8,128)(2,1)S(1)}, u32[]{:S(2)}, u32[]{:S(2)}) collective-permute-start(bf16[1368,128]{1,0:T(8,128)(2,1)} %get-tuple-element.72), channel_id=1, source_target_pairs={{0,2},{2,0},{1,3},{3,1},{4,6},{6,4},{5,7},{7,5},{8,10},{10,8},{9,1... | collective-permute-start | bytes 1050632 | tf_op jit(solution)/shard_map/ppermute | solution.py:354
  74.1 29.0 %collective-permute-start.11 = (bf16[1368,128]{1,0:T(8,128)(2,1)}, bf16[1368,128]{1,0:T(8,128)(2,1)}, u32[]{:S(2)}, u32[]{:S(2)}) collective-permute-start(bf16[1368,128]{1,0:T(8,128)(2,1)} %get-tuple-element.80), channel_id=1, source_target_pairs={{0,2},{2,0},{1,3},{3,1},{4,6},{6,4},{5,7},{7,5},{8,10},{10,8},{9,1... | collective-permute-start | bytes 1050632 | tf_op jit(solution)/shard_map/ppermute | solution.py:354
  84.8 18.4 %collective-permute-start.9 = (bf16[1368,128]{1,0:T(8,128)(2,1)S(1)}, bf16[1368,128]{1,0:T(8,128)(2,1)}, u32[]{:S(2)}, u32[]{:S(2)}) collective-permute-start(bf16[1368,128]{1,0:T(8,128)(2,1)S(1)} %add_convert_fusion.1), channel_id=1, source_target_pairs={{0,8},{4,12},{8,0},{12,4},{1,9},{5,13},{9,1},{13,5},{2,10},{6,14},... | collective-permute-start | bytes 1050632 | tf_op jit(solution)/shard_map/ppermute | solution.py:364
  86.7 17.7 %collective-permute-start.12 = (bf16[1368,128]{1,0:T(8,128)(2,1)}, bf16[1368,128]{1,0:T(8,128)(2,1)S(1)}, u32[]{:S(2)}, u32[]{:S(2)}) collective-permute-start(bf16[1368,128]{1,0:T(8,128)(2,1)} %add_convert_fusion), channel_id=1, source_target_pairs={{0,4},{4,0},{8,12},{12,8},{1,5},{5,1},{9,13},{13,9},{2,6},{6,2},{1... | collective-permute-start | bytes 1050632 | tf_op jit(solution)/shard_map/ppermute | solution.py:364
  88.5 15.9 %copy-start.1 = (f32[1368,128]{1,0:T(8,128)S(1)}, f32[1368,128]{1,0:T(8,128)}, u32[]{:S(2)}) copy-start(f32[1368,128]{1,0:T(8,128)} %get-tuple-element.79) | copy-start | bytes 2101252
Sparse Core Ops, SparseCore 0:
  10.2 71.2 all-gather.1

commit v7 on v6

--- a/solution.py
+++ b/solution.py
@@ -173,25 +173,36 @@
         base += width * width * 128
 
     rows = outs[0].shape[0]
-    at_out = 0
     for o in list(range(1, n_x)) + [0]:
         for r in reversed(range(n_z)):
             start = (((z ^ r) * n_x + (x + o) % n_x) * 2 + core) * rows
             if rows % 8 == 0:
                 start = pl.multiple_of(start, 8)
-            ref = outs[at_out]
-            ref[...] = flat[pl.ds(start, rows), :].astype(ref.dtype)
-            at_out += 1
-
-
-def message_kernel(w_ref, *refs):
-    both, mats, hots = refs[0:2], refs[2:4], refs[4:6]
-    out_ref, flat, in_ref, res_ref, wide_ref = refs[6:]
+            block = flat[pl.ds(start, rows), :]
+            if o == 0:
+                outs[-1 - r][...] = block
+            elif r < 2:
+                outs[(o - 1) * (n_z - 1) + n_z - 2][1 - r] = block.astype(BF16)
+            else:
+                outs[(o - 1) * (n_z - 1) + n_z - 1 - r][...] = block.astype(BF16)
+
+
+def message_kernel(rows, place_ref, *refs):
+    pieces, both, mats, hots = refs[0:3], refs[3:5], refs[5:7], refs[7:9]
+    out_ref, flat, in_ref, res_ref, wide_ref = refs[9:]
     n = out_ref.shape[0]
     slots = in_ref.shape[1]
-    part = w_ref.shape[0] // 16
-    for p in range(16):
-        flat[p * part : (p + 1) * part, :] = w_ref[p * part : (p + 1) * part, :].astype(F32)
+    group, core = place_ref[0], place_ref[1]
+    half = pieces[1].shape[0]
+    for ref, which, first in zip(
+        pieces, (group, 1 - group, 1 - group), (0, core * half, (1 - core) * half)
+    ):
+        size = ref.shape[1]
+        for i in range(ref.shape[0]):
+            start = (first + i) * rows + which * (rows - size)
+            if rows % 8 == 0:
+                start = pl.multiple_of(start, 8)
+            flat[pl.ds(start, size), :] = ref[i].astype(F32)
 
     def h(first, end):
         return jnp.concatenate(
@@ -290,7 +301,11 @@
     def swap(block):
         return lax.ppermute(block, "core", [(0, 1), (1, 0)])
 
-    weights = lax.all_gather(flat_params, ALL, axis=0, tiled=True)
+    group, core = lax.axis_index("groups"), lax.axis_index("core")
+    piece = -(-rows // 32) * 16
+    part = lax.dynamic_slice_in_dim(flat_params, group * (rows - piece), piece, 0)
+    gathered = lax.all_gather(part, ALL, axis=0)
+    mine = lax.dynamic_slice_in_dim(gathered, core * (n_dp // 2), n_dp // 2, 0)
 
     row = lambda v: v.reshape(1, n)
     here, *outbound = call(
@@ -328,12 +343,15 @@
         pl.CostEstimate(flops=10**10, bytes_accessed=10**8, transcendentals=0),
     )
     both_b_other = swap(both_b)
+    both_b_other, mine = lax.optimization_barrier((both_b_other, mine))
+    crossed = lax.ppermute(mine, "groups", [(0, 1), (1, 0)])
     both, hots, turns = [both_a, both_b], [hot_a, hot_b], [turn_a, turn_b]
 
-    n_send = n_z * (n_x - 1)
+    n_send = (n_z - 1) * (n_x - 1)
+    sends = [shape((rows, 128), BF16)] * (n_z - 2) + [shape((2, rows, 128), BF16)]
     blocks = call(
         lambda *refs: grad_kernel(n_z, n_x, *refs), "weight_terms", 62,
-        [shape((rows, 128), BF16)] * n_send + [shape((rows, 128), F32)] * n_z,
+        sends * (n_x - 1) + [shape((rows, 128), F32)] * n_z,
         both + [both_a_other, both_b_other],
         [pltpu.VMEM((rows * n_dp, 128), F32)],
         numbers=me.reshape(1),
@@ -347,33 +365,38 @@
     )
     kept = blocks[n_send:]
     kept[0], mats = lax.optimization_barrier((kept[0], mats))
-    sums = {}
-    for at, r in enumerate(reversed(range(n_z))):
-        total = kept[at]
+    sums = {r: kept[n_z - 1 - r] for r in range(n_z)}
+    for at in range(n_z - 1):
         for o in range(1, n_x):
             got = lax.ppermute(
-                blocks[(o - 1) * n_z + at], "x", [(s, (s + o) % n_x) for s in range(n_x)]
-            )
-            total = total + got.astype(F32)
-        sums[r] = total
+                blocks[(o - 1) * (n_z - 1) + at], "x", [(s, (s + o) % n_x) for s in range(n_x)]
+            ).astype(F32)
+            if at < n_z - 2:
+                sums[n_z - 1 - at] += got
+            else:
+                sums[1] += got[0]
+                sums[0] += got[1]
+    terms = []
     for bit in [1 << i for i in range(n_z.bit_length() - 1)]:
         for r in reversed(range(bit, n_z, 2 * bit)):
             term = sums[r].astype(BF16)
-            if (bit, r) == (1, 1):
-                last_term = term
+            if bit == 1:
+                terms.append(term)
             got = lax.ppermute(term, "z", [(s, s ^ bit) for s in range(n_z)])
             if 2 * bit < n_z:
                 sums[r ^ bit] = sums[r ^ bit] + got.astype(F32)
-    weights, _ = lax.optimization_barrier((weights, last_term))
+    crossed, _ = lax.optimization_barrier((crossed, terms[0]))
+    swapped, _ = lax.optimization_barrier((swap(crossed), terms[-1]))
     slots = n // 2 + 4 * cap
     (node_out,) = call(
-        message_kernel, "messages", 62,
+        lambda *refs: message_kernel(rows, *refs), "messages", 62,
         [shape((n, width), BF16)],
-        [weights, *both, *mats, *hots],
+        [gathered, crossed, swapped, *both, *mats, *hots],
         [
             pltpu.VMEM((rows * n_dp, 128), F32), pltpu.VMEM((32, slots, 128), F32),
             pltpu.VMEM((30, slots, 128), F32), pltpu.VMEM((slots, width), BF16),
         ],
+        numbers=jnp.stack([group, core]),
     )
     got, node_out = lax.optimization_barrier((got, node_out))
     result = sums[0] + got.astype(F32)

time: 114 us -> 134 us (1.18)
  waiting for transfers between devices: 33.9 us -> 51.6 us
  other arithmetic: 4.23 us -> 5.89 us
    all_gather x1, waiting for transfers between devices: 0.01 us -> 17.9 us  [on_device(): gathered = lax.all_gather(part, ALL, axis=0)]
    ppermute x4, waiting for transfers between devices: 8.61 us -> 20.2 us  [the longest x3 12.3 us: on_device(): lax.ppermute(blocks[(o - 1) * (n_z - 1) + at], 'x', [(s, (s + o) % n_x) f...]
    ppermute x3, waiting for transfers between devices: 12.9 us -> 4.57 us  [on_device(): got = lax.ppermute(term, 'z', [(s, s ^ bit) for s in range(n_z)])]
    ppermute x2 -> x3, waiting for transfers between devices: 2.49 us -> 0.01 us  [swap(): return lax.ppermute(block, 'core', [(0, 1), (1, 0)])]
    dynamic_slice x0 -> x2, local copies, waits for them, and re-layouts: none -> 2.12 us  [the longest x1 1.44 us: on_device(): mine = lax.dynamic_slice_in_dim(gathered, core * (n_dp // 2), n_dp // 2, 0)]
    unnamed x12 -> x18, local copies, waits for them, and re-layouts: 1.96 us -> 3.01 us
  transfers between devices with their start and end apart: 14 -> 15, of which waited for: 8 -> 6; matrix products, arithmetic and copies ran while one was open for 5% -> 5% of each run, Pallas kernels for 27% -> 23%
where the time goes in v7:
time: 134 us; the launch traced here: 133 us
  waiting for transfers between devices  51.6 us (39%)
  Pallas kernels  34.3 us (26%)
  starting transfers between devices  20.2 us (15%)
  between operations  14.2 us (11%)
  local copies, waits for them, and re-layouts  7.31 us (5%)
  other arithmetic  5.89 us (4%)
    pallas_call x6, Pallas kernels, call(): pl.pallas_call(kernel, grid=(1,), out_shape=outs, in_specs=first + [whole...  34.3 us
    all_gather x1, waiting for transfers between devices, on_device(): gathered = lax.all_gather(part, ALL, axis=0)  17.9 us
    ppermute x3, waiting for transfers between devices, on_device(): lax.ppermute(blocks[(o - 1) * (n_z - 1) + at], 'x', [(s, (s + o) % n_x) f...  12.3 us
    ppermute x4, starting transfers between devices, shift(): return lax.ppermute(block, ALL, route)  11.1 us
    ppermute x4, waiting for transfers between devices, shift(): return lax.ppermute(block, ALL, route)  8.94 us
    ppermute x1, waiting for transfers between devices, on_device(): crossed = lax.ppermute(mine, 'groups', [(0, 1), (1, 0)])  7.88 us
    ppermute x3, waiting for transfers between devices, on_device(): got = lax.ppermute(term, 'z', [(s, s ^ bit) for s in range(n_z)])  4.57 us
    ppermute x3, starting transfers between devices, on_device(): got = lax.ppermute(term, 'z', [(s, s ^ bit) for s in range(n_z)])  4.45 us
  transfers between devices with their start and end apart: 15, of which 6 were waited for; matrix products, arithmetic and copies ran while one was open for 5% of the time, Pallas kernels for 23%

profile of v7, /device:TPU:0, one launch (start us, length us, event | category | flops | bytes accessed | tf_op | source)
XLA Modules:
  0.0 133.4 jit_solution(1514979311682718424)
XLA Ops:
  7.2 0.0 copy-start
  7.2 0.0 copy-start.1
  7.2 0.0 all-gather.3.cloned.1.call-start
  7.2 0.9 copy-done
  8.2 0.7 constant_dynamic-slice_fusion.1
  8.8 0.0 all-gather.3.cloned.1.call-update
  8.9 3.1 %send.1 = (bf16[64,3840]{1,0:T(8,128)(2,1)}, bf16[32,3840]{1,0:T(8,128)(2,1)}, bf16[32,3840]{1,0:T(8,128)(2,1)}, bf16[32,3840]{1,0:T(8,128)(2,1)}, bf16[32,3840]{1,0:T(8,128)(2,1)}) custom-call(s32[1]{0:T(128)} %bitcast.me_ref.refs_0_, s32[1,128]{1,0:T(1,128)} %bitcast.35, s32[1,128]{1,0:T(1,128)} %bitcast.36, s32[1,128]{1,0:T(1,128)} %bitcast.37, ...), custom_call_target="tpu_custom_call" | custom-call | tf_op jit(solution)/shard_map/send/pallas_call | solution.py:268
  11.9 1.3 collective-permute-start
  13.2 5.5 %collective-permute-start.1 = (bf16[32,3840]{1,0:T(8,128)(2,1)}, bf16[32,3840]{1,0:T(8,128)(2,1)S(1)}, u32[]{:S(2)}, u32[]{:S(2)}) collective-permute-start(bf16[32,3840]{1,0:T(8,128)(2,1)} %get-tuple-element.45), channel_id=1, source_target_pairs={{0,2},{1,3},{2,4},{3,5},{4,6},{5,7},{8,10},{9,11},{10,12},{11,13},... | collective-permute-start | bytes 737288 | tf_op jit(solution)/shard_map/ppermute | solution.py:299
  18.7 1.3 collective-permute-start.2
  20.0 3.0 %collective-permute-start.3 = (bf16[32,3840]{1,0:T(8,128)(2,1)}, bf16[32,3840]{1,0:T(8,128)(2,1)S(1)}, u32[]{:S(2)}, u32[]{:S(2)}) collective-permute-start(bf16[32,3840]{1,0:T(8,128)(2,1)} %get-tuple-element.48), channel_id=1, source_target_pairs={{0,1},{1,2},{2,3},{3,4},{4,5},{5,6},{6,7},{8,9},{9,10},{10,11},{11... | collective-permute-start | bytes 737288 | tf_op jit(solution)/shard_map/ppermute | solution.py:299
  23.1 0.0 copy-done.1
  23.1 1.0 copy.10
  24.1 0.0 collective-permute-done.refs_1_
  24.1 0.0 copy-start.5
  24.1 8.9 %collective-permute-done.1.refs_2_ = bf16[32,3840]{1,0:T(8,128)(2,1)S(1)} collective-permute-done((bf16[32,3840]{1,0:T(8,128)(2,1)}, bf16[32,3840]{1,0:T(8,128)(2,1)S(1)}, u32[]{:S(2)}, u32[]{:S(2)}) %collective-permute-start.1) | collective-permute-done | bytes 245792 | tf_op jit(solution)/shard_map/ppermute | solution.py:299
  33.1 0.0 copy-start.6
  33.1 0.0 copy-done.5
  33.1 0.7 copy-done.6
  33.7 4.9 %rotate_first.1 = (bf16[256,3712]{1,0:T(8,128)(2,1)}, bf16[128,128]{1,0:T(8,128)(2,1)}, bf16[128,64]{1,0:T(8,128)(2,1)}) custom-call(bf16[64,3840]{1,0:T(8,128)(2,1)} %get-tuple-element.43.refs_0_, bf16[32,3840]{1,0:T(8,128)(2,1)} %copy-done.5, bf16[32,3840]{1,0:T(8,128)(2,1)} %copy-done.6, bf16[1856,29]{1,0:T(8,128)(2,1)} %bitcast.30, bf16[128,3712]{1,0:T(8,128)(2,1)} %refs_3_.1), custom_call_target="tpu_custom_call" | custom-call | tf_op jit(solution)/shard_map/rotate_first/pallas_call | solution.py:268
  38.7 0.0 collective-permute-start.4
  38.7 0.0 collective-permute-done.2.refs_0_
  38.7 0.0 copy-start.7
  38.7 0.0 collective-permute-done.3.refs_1_
  38.7 0.7 copy-done.7
  39.4 0.0 copy-start.8
  39.4 0.7 copy-done.8
  40.1 3.8 %rotate_last.1 = (bf16[128,3712]{1,0:T(8,128)(2,1)}, bf16[64,128]{1,0:T(8,128)(2,1)}, bf16[64,64]{1,0:T(8,128)(2,1)}) custom-call(bf16[32,3840]{1,0:T(8,128)(2,1)} %copy-done.7, bf16[32,3840]{1,0:T(8,128)(2,1)} %copy-done.8, bf16[1856,29]{1,0:T(8,128)(2,1)} %bitcast.31, bf16[128,3712]{1,0:T(8,128)(2,1)} %refs_3_.1), custom_call_target="tpu_custom_call" | custom-call | flops 10000000000 | bytes 100000000 | tf_op jit(solution)/shard_map/rotate_last/pallas_call | solution.py:268
  43.9 0.5 collective-permute-start.5
  44.4 17.9 %all-gather.3.cloned.1.call-done = bf16[11008,128]{1,0:T(8,128)(2,1)} async-done(((bf16[688,128]{1,0:T(8,128)(2,1)}), bf16[11008,128]{1,0:T(8,128)(2,1)}) %all-gather.3.cloned.1.call-update) | async-done | bytes 2818064 | tf_op jit(solution)/shard_map/all_gather | solution.py:307
  62.3 1.4 %constant_dynamic-slice_fusion = bf16[8,688,128]{2,1,0:T(8,128)(2,1)S(1)} fusion(bf16[16,688,128]{2,1,0:T(8,128)(2,1)} %bitcast.28, s32[]{:T(128)S(6)} %select_n.7), kind=kLoop, calls=%fused_computation.11 | loop fusion | bytes 2818052 | tf_op jit(solution)/shard_map/dynamic_slice | solution.py:308
  63.7 0.0 collective-permute-done.5.refs_4_
  63.7 0.0 copy-start.2
  63.7 1.5 %collective-permute-start.10 = (bf16[8,688,128]{2,1,0:T(8,128)(2,1)S(1)}, bf16[8,688,128]{2,1,0:T(8,128)(2,1)}, u32[]{:S(2)}, u32[]{:S(2)}) collective-permute-start(bf16[8,688,128]{2,1,0:T(8,128)(2,1)S(1)} %constant_dynamic-slice_fusion), channel_id=1, source_target_pairs={{0,16},{16,0},{1,17},{17,1},{2,18},{18,2},{3,19},{19,3},{4,20},{20... | collective-permute-start | bytes 4227080 | tf_op jit(solution)/shard_map/ppermute | solution.py:347
  65.3 0.0 copy-done.2
  65.3 0.0 collective-permute-done.4.refs_3_
  65.3 9.1 %weight_terms.1 = (bf16[1368,128]{1,0:T(8,128)(2,1)}, bf16[1368,128]{1,0:T(8,128)(2,1)}, bf16[2,1368,128]{2,1,0:T(8,128)(2,1)}, f32[1368,128]{1,0:T(8,128)}, f32...) custom-call(s32[1]{0:T(128)} %bitcast.me_ref.refs_0_, ...), custom_call_target="tpu_custom_call" | custom-call | tf_op jit(solution)/shard_map/weight_terms/pallas_call | solution.py:268
  74.4 0.6 collective-permute-start.7
  75.0 1.1 copy.11
  76.1 3.7 %back.1 = (bf16[16,240,256]{2,1,0:T(8,128)(2,1)}, bf16[8,240,256]{2,1,0:T(8,128)(2,1)}) custom-call(bf16[1856,29]{1,0:T(8,128)(2,1)} %bitcast.32, bf16[128,64]{1,0:T(8,128)(2,1)} %get-tuple-element.66.refs_0_, bf16[64,64]{1,0:T(8,128)(2,1)} %get-tuple-element.67.refs_1_), custom_call_target="tpu_custom_call" | custom-call | tf_op jit(solution)/shard_map/back/pallas_call | solution.py:268
  79.8 0.0 copy-start.4
  79.8 1.5 %collective-permute-start.6 = (bf16[1368,128]{1,0:T(8,128)(2,1)}, bf16[1368,128]{1,0:T(8,128)(2,1)S(1)}, u32[]{:S(2)}, u32[]{:S(2)}) collective-permute-start(bf16[1368,128]{1,0:T(8,128)(2,1)} %get-tuple-element.64), channel_id=1, source_target_pairs={{0,2},{2,0},{1,3},{3,1},{4,6},{6,4},{5,7},{7,5},{8,10},{10,8},{9,1... | collective-permute-start | bytes 1050632 | tf_op jit(solution)/shard_map/ppermute | solution.py:371
  81.3 4.5 %collective-permute-done.7 = bf16[1368,128]{1,0:T(8,128)(2,1)} collective-permute-done((bf16[1368,128]{1,0:T(8,128)(2,1)}, bf16[1368,128]{1,0:T(8,128)(2,1)}, u32[]{:S(2)}, u32[]{:S(2)}) %collective-permute-start.7) | collective-permute-done | bytes 350240 | tf_op jit(solution)/shard_map/ppermute | solution.py:371
  85.8 1.3 add_convert_fusion.1
  87.0 1.5 %collective-permute-start.8 = (bf16[1368,128]{1,0:T(8,128)(2,1)S(1)}, bf16[1368,128]{1,0:T(8,128)(2,1)S(1)}, u32[]{:S(2)}, u32[]{:S(2)}) collective-permute-start(bf16[1368,128]{1,0:T(8,128)(2,1)S(1)} %add_convert_fusion.1), channel_id=1, source_target_pairs={{0,4},{4,0},{8,12},{12,8},{1,5},{5,1},{9,13},{13,9},{2,6},{6,2},{1... | collective-permute-start | bytes 1050632 | tf_op jit(solution)/shard_map/ppermute | solution.py:385
  88.5 0.6 collective-permute-start.12
  89.1 7.9 %collective-permute-done.10.refs_2_ = bf16[8,688,128]{2,1,0:T(8,128)(2,1)} collective-permute-done((bf16[8,688,128]{2,1,0:T(8,128)(2,1)S(1)}, bf16[8,688,128]{2,1,0:T(8,128)(2,1)}, u32[]{:S(2)}, u32[]{:S(2)}) %collective-permute-start.10) | collective-permute-done | bytes 1409056 | tf_op jit(solution)/shard_map/ppermute | solution.py:347
  96.9 0.0 collective-permute-start.11
  96.9 0.0 collective-permute-done.6
  96.9 0.0 collective-permute-done.8
  97.0 0.0 copy-done.4
  97.0 0.9 add_convert_fusion
  97.8 1.6 %collective-permute-start.9 = (bf16[1368,128]{1,0:T(8,128)(2,1)}, bf16[1368,128]{1,0:T(8,128)(2,1)}, u32[]{:S(2)}, u32[]{:S(2)}) collective-permute-start(bf16[1368,128]{1,0:T(8,128)(2,1)} %add_convert_fusion), channel_id=1, source_target_pairs={{0,8},{4,12},{8,0},{12,4},{1,9},{5,13},{9,1},{13,5},{2,10},{6,14},... | collective-permute-start | bytes 1050632 | tf_op jit(solution)/shard_map/ppermute | solution.py:385
  99.4 7.8 %collective-permute-done.12 = bf16[2,1368,128]{2,1,0:T(8,128)(2,1)S(1)} collective-permute-done((bf16[2,1368,128]{2,1,0:T(8,128)(2,1)}, bf16[2,1368,128]{2,1,0:T(8,128)(2,1)S(1)}, u32[]{:S(2)}, u32[]{:S(2)}) %collective-permute-start.12) | collective-permute-done | bytes 700448 | tf_op jit(solution)/shard_map/ppermute | solution.py:371
  107.2 0.1 convert_element_type.32
  107.3 0.0 copy-done.3
  107.3 0.8 fusion.5
  108.1 1.4 %collective-permute-start.13 = (bf16[1368,128]{1,0:T(8,128)(2,1)}, bf16[1368,128]{1,0:T(8,128)(2,1)}, u32[]{:S(2)}, u32[]{:S(2)}) collective-permute-start(bf16[1368,128]{1,0:T(8,128)(2,1)} %fusion.5), channel_id=1, source_target_pairs={{0,4},{4,0},{8,12},{12,8},{1,5},{5,1},{9,13},{13,9},{2,6},{6,2},{1... | collective-permute-start | bytes 1050632 | tf_op jit(solution)/shard_map/ppermute | solution.py:385
  109.5 0.6 pad_add_fusion.refs_0_
  110.1 0.0 collective-permute-done.11.refs_3_
  110.1 9.7 %messages.1 = bf16[128,3712]{1,0:T(8,128)(2,1)} custom-call(s32[2]{0:T(128)} %pad_add_fusion.refs_0_, bf16[16,688,128]{2,1,0:T(8,128)(2,1)} %bitcast.29, bf16[8,688,128]{2,1,0:T(8,128)(2,1)} %collective-permute-done.10.refs_2_, bf16[8,688,128]{2,1,0:T(8,128)(2,1)} %collective-permute-done.11.refs_3_, bf16[256,3712]{1,0:T(8,128)(2,1)} %get-tuple-element.53.refs_1_.refs_4_, ...), custom_call_target="tpu_custom_call" | custom-call | tf_op jit(solution)/shard_map/messages/pallas_call | solution.py:268
  119.7 0.0 collective-permute-done.9
  119.7 4.6 %collective-permute-done.13 = bf16[1368,128]{1,0:T(8,128)(2,1)} collective-permute-done((bf16[1368,128]{1,0:T(8,128)(2,1)}, bf16[1368,128]{1,0:T(8,128)(2,1)}, u32[]{:S(2)}, u32[]{:S(2)}) %collective-permute-start.13) | collective-permute-done | bytes 350240 | tf_op jit(solution)/shard_map/ppermute | solution.py:385
  124.3 2.3 %fusion.3 = f32[1368,128]{1,0:T(8,128)} fusion(f32[1368,128]{1,0:T(8,128)} %get-tuple-element.82, f32[2,1368,128]{2,1,0:T(8,128)S(1)} %convert_element_type.32, bf16[1368,128]{1,0:T(8,128)(2,1)} %collective-permute-done.9, bf16[1368,128]{1,0:T(8,128)(2,1)} %collective-permute-done.13), kind=kLoop, calls=%fused_computation.4 | loop fusion | flops 1050624 | bytes 2801664 | tf_op jit(solution)/shard_map/mul | solution.py:403
  (1 shorter events, 0.0 us)
Async XLA Ops:
  7.2 1.0 copy-start
  7.2 15.9 %copy-start.1 = (bf16[64,29,29]{0,2,1:T(8,128)(2,1)S(1)}, bf16[64,29,29]{0,2,1:T(8,128)(2,1)}, u32[]{:S(2)}) copy-start(bf16[64,29,29]{0,2,1:T(8,128)(2,1)} %param.11) | copy-start | bytes 322948
  7.2 55.1 %all-gather.3.cloned.1.call-start = ((), (), s32[]{:S(2)}) async-start(), calls=%async_computation | async-start | bytes 2994176 | tf_op jit(solution)/shard_map/all_gather | solution.py:307
  11.9 12.2 %collective-permute-start = (bf16[32,3840]{1,0:T(8,128)(2,1)}, bf16[32,3840]{1,0:T(8,128)(2,1)S(1)}, u32[]{:S(2)}, u32[]{:S(2)}) collective-permute-start(bf16[32,3840]{1,0:T(8,128)(2,1)} %get-tuple-element.44), channel_id=1, source_target_pairs={{2,0},{3,1},{4,2},{5,3},{6,4},{7,5},{10,8},{11,9},{12,10},{13,11},... | collective-permute-start | bytes 737288 | tf_op jit(solution)/shard_map/ppermute | solution.py:299
  13.2 19.8 %collective-permute-start.1 = (bf16[32,3840]{1,0:T(8,128)(2,1)}, bf16[32,3840]{1,0:T(8,128)(2,1)S(1)}, u32[]{:S(2)}, u32[]{:S(2)}) collective-permute-start(bf16[32,3840]{1,0:T(8,128)(2,1)} %get-tuple-element.45), channel_id=1, source_target_pairs={{0,2},{1,3},{2,4},{3,5},{4,6},{5,7},{8,10},{9,11},{10,12},{11,13},... | collective-permute-start | bytes 737288 | tf_op jit(solution)/shard_map/ppermute | solution.py:299
  18.7 20.0 %collective-permute-start.2 = (bf16[32,3840]{1,0:T(8,128)(2,1)}, bf16[32,3840]{1,0:T(8,128)(2,1)S(1)}, u32[]{:S(2)}, u32[]{:S(2)}) collective-permute-start(bf16[32,3840]{1,0:T(8,128)(2,1)} %get-tuple-element.47), channel_id=1, source_target_pairs={{1,0},{2,1},{3,2},{4,3},{5,4},{6,5},{7,6},{9,8},{10,9},{11,10},{12... | collective-permute-start | bytes 737288 | tf_op jit(solution)/shard_map/ppermute | solution.py:299
  20.0 18.7 %collective-permute-start.3 = (bf16[32,3840]{1,0:T(8,128)(2,1)}, bf16[32,3840]{1,0:T(8,128)(2,1)S(1)}, u32[]{:S(2)}, u32[]{:S(2)}) collective-permute-start(bf16[32,3840]{1,0:T(8,128)(2,1)} %get-tuple-element.48), channel_id=1, source_target_pairs={{0,1},{1,2},{2,3},{3,4},{4,5},{5,6},{6,7},{8,9},{9,10},{10,11},{11... | collective-permute-start | bytes 737288 | tf_op jit(solution)/shard_map/ppermute | solution.py:299
  24.1 8.9 %copy-start.5 = (bf16[32,3840]{1,0:T(8,128)(2,1)}, bf16[32,3840]{1,0:T(8,128)(2,1)S(1)}, u32[]{:S(2)}) copy-start(bf16[32,3840]{1,0:T(8,128)(2,1)S(1)} %collective-permute-done.refs_1_) | copy-start | bytes 737284
  33.1 0.7 copy-start.6
  38.7 26.6 %collective-permute-start.4 = (bf16[256,3712]{1,0:T(8,128)(2,1)}, bf16[256,3712]{1,0:T(8,128)(2,1)}, u32[]{:S(2)}, u32[]{:S(2)}) collective-permute-start(bf16[256,3712]{1,0:T(8,128)(2,1)} %get-tuple-element.53.refs_1_.refs_4_), channel_id=1, source_target_pairs={{0,1},{1,0},{2,3},{3,2},{4,5},{5,4},{6,7},{7,6},{8,9},{9,8},{10,11... | collective-permute-start | bytes 5701640 | tf_op jit(solution)/shard_map/ppermute | solution.py:302
  38.7 0.7 copy-start.7
  39.4 0.7 copy-start.8
  43.9 19.8 %collective-permute-start.5 = (bf16[128,3712]{1,0:T(8,128)(2,1)}, bf16[128,3712]{1,0:T(8,128)(2,1)S(1)}, u32[]{:S(2)}, u32[]{:S(2)}) collective-permute-start(bf16[128,3712]{1,0:T(8,128)(2,1)} %get-tuple-element.54.refs_2_.refs_5_), channel_id=1, source_target_pairs={{0,1},{1,0},{2,3},{3,2},{4,5},{5,4},{6,7},{7,6},{8,9},{9,8},{10,11... | collective-permute-start | bytes 2850824 | tf_op jit(solution)/shard_map/ppermute | solution.py:302
  63.7 1.6 %copy-start.2 = (bf16[128,3712]{1,0:T(8,128)(2,1)}, bf16[128,3712]{1,0:T(8,128)(2,1)S(1)}, u32[]{:S(2)}) copy-start(bf16[128,3712]{1,0:T(8,128)(2,1)S(1)} %collective-permute-done.5.refs_4_) | copy-start | bytes 2850820
  63.7 33.2 %collective-permute-start.10 = (bf16[8,688,128]{2,1,0:T(8,128)(2,1)S(1)}, bf16[8,688,128]{2,1,0:T(8,128)(2,1)}, u32[]{:S(2)}, u32[]{:S(2)}) collective-permute-start(bf16[8,688,128]{2,1,0:T(8,128)(2,1)S(1)} %constant_dynamic-slice_fusion), channel_id=1, source_target_pairs={{0,16},{16,0},{1,17},{17,1},{2,18},{18,2},{3,19},{19,3},{4,20},{20... | collective-permute-start | bytes 4227080 | tf_op jit(solution)/shard_map/ppermute | solution.py:347
  74.4 11.4 %collective-permute-start.7 = (bf16[1368,128]{1,0:T(8,128)(2,1)}, bf16[1368,128]{1,0:T(8,128)(2,1)}, u32[]{:S(2)}, u32[]{:S(2)}) collective-permute-start(bf16[1368,128]{1,0:T(8,128)(2,1)} %get-tuple-element.71), channel_id=1, source_target_pairs={{0,2},{2,0},{1,3},{3,1},{4,6},{6,4},{5,7},{7,5},{8,10},{10,8},{9,1... | collective-permute-start | bytes 1050632 | tf_op jit(solution)/shard_map/ppermute | solution.py:371
  79.8 17.2 %copy-start.4 = (f32[1368,128]{1,0:T(8,128)S(1)}, f32[1368,128]{1,0:T(8,128)}, u32[]{:S(2)}) copy-start(f32[1368,128]{1,0:T(8,128)} %get-tuple-element.63) | copy-start | bytes 2101252
  79.8 17.2 %collective-permute-start.6 = (bf16[1368,128]{1,0:T(8,128)(2,1)}, bf16[1368,128]{1,0:T(8,128)(2,1)S(1)}, u32[]{:S(2)}, u32[]{:S(2)}) collective-permute-start(bf16[1368,128]{1,0:T(8,128)(2,1)} %get-tuple-element.64), channel_id=1, source_target_pairs={{0,2},{2,0},{1,3},{3,1},{4,6},{6,4},{5,7},{7,5},{8,10},{10,8},{9,1... | collective-permute-start | bytes 1050632 | tf_op jit(solution)/shard_map/ppermute | solution.py:371
  87.0 9.9 %collective-permute-start.8 = (bf16[1368,128]{1,0:T(8,128)(2,1)S(1)}, bf16[1368,128]{1,0:T(8,128)(2,1)S(1)}, u32[]{:S(2)}, u32[]{:S(2)}) collective-permute-start(bf16[1368,128]{1,0:T(8,128)(2,1)S(1)} %add_convert_fusion.1), channel_id=1, source_target_pairs={{0,4},{4,0},{8,12},{12,8},{1,5},{5,1},{9,13},{13,9},{2,6},{6,2},{1... | collective-permute-start | bytes 1050632 | tf_op jit(solution)/shard_map/ppermute | solution.py:385
  88.5 18.7 %collective-permute-start.12 = (bf16[2,1368,128]{2,1,0:T(8,128)(2,1)}, bf16[2,1368,128]{2,1,0:T(8,128)(2,1)S(1)}, u32[]{:S(2)}, u32[]{:S(2)}) collective-permute-start(bf16[2,1368,128]{2,1,0:T(8,128)(2,1)} %get-tuple-element.75), channel_id=1, source_target_pairs={{0,2},{2,0},{1,3},{3,1},{4,6},{6,4},{5,7},{7,5},{8,10},{10,8},{9,1... | collective-permute-start | bytes 2101256 | tf_op jit(solution)/shard_map/ppermute | solution.py:371
  96.9 13.1 %collective-permute-start.11 = (bf16[8,688,128]{2,1,0:T(8,128)(2,1)}, bf16[8,688,128]{2,1,0:T(8,128)(2,1)}, u32[]{:S(2)}, u32[]{:S(2)}) collective-permute-start(bf16[8,688,128]{2,1,0:T(8,128)(2,1)} %collective-permute-done.10.refs_2_), channel_id=1, source_target_pairs={{0,1},{1,0},{2,3},{3,2},{4,5},{5,4},{6,7},{7,6},{8,9},{9,8},{10,11... | collective-permute-start | bytes 4227080 | tf_op jit(solution)/shard_map/ppermute | solution.py:302
  97.8 9.5 %copy-start.3 = (f32[1368,128]{1,0:T(8,128)S(1)}, f32[1368,128]{1,0:T(8,128)}, u32[]{:S(2)}) copy-start(f32[1368,128]{1,0:T(8,128)} %get-tuple-element.74) | copy-start | bytes 2101252
  97.8 21.9 %collective-permute-start.9 = (bf16[1368,128]{1,0:T(8,128)(2,1)}, bf16[1368,128]{1,0:T(8,128)(2,1)}, u32[]{:S(2)}, u32[]{:S(2)}) collective-permute-start(bf16[1368,128]{1,0:T(8,128)(2,1)} %add_convert_fusion), channel_id=1, source_target_pairs={{0,8},{4,12},{8,0},{12,4},{1,9},{5,13},{9,1},{13,5},{2,10},{6,14},... | collective-permute-start | bytes 1050632 | tf_op jit(solution)/shard_map/ppermute | solution.py:385
  108.1 16.2 %collective-permute-start.13 = (bf16[1368,128]{1,0:T(8,128)(2,1)}, bf16[1368,128]{1,0:T(8,128)(2,1)}, u32[]{:S(2)}, u32[]{:S(2)}) collective-permute-start(bf16[1368,128]{1,0:T(8,128)(2,1)} %fusion.5), channel_id=1, source_target_pairs={{0,4},{4,0},{8,12},{12,8},{1,5},{5,1},{9,13},{13,9},{2,6},{6,2},{1... | collective-permute-start | bytes 1050632 | tf_op jit(solution)/shard_map/ppermute | solution.py:385
Sparse Core Ops, SparseCore 0:
  10.2 52.0 all-gather.2

commit v8 on v6

--- a/solution.py
+++ b/solution.py
@@ -142,6 +142,15 @@
         build(tabt_ref, refs[i][...], refs[2 + i], refs[4 + i])
 
 
+def square(n_x):
+    return [(b, o) for b in (1, 0) for o in reversed(range(n_x)) if (b, o) != (0, 0)]
+
+
+def placed_blocks(n_z, n_x):
+    pairs = list(reversed(range(0, n_z, 2)))
+    return [(r + b, o) for r in pairs for b, o in square(n_x)] + [(r, 0) for r in pairs]
+
+
 def grad_kernel(n_z, n_x, me_ref, *refs):
     parts, outs, flat = refs[:4], refs[4:-1], refs[-1]
     chip, core = me_ref[0] // 2, me_ref[0] % 2
@@ -173,15 +182,11 @@
         base += width * width * 128
 
     rows = outs[0].shape[0]
-    at_out = 0
-    for o in list(range(1, n_x)) + [0]:
-        for r in reversed(range(n_z)):
-            start = (((z ^ r) * n_x + (x + o) % n_x) * 2 + core) * rows
-            if rows % 8 == 0:
-                start = pl.multiple_of(start, 8)
-            ref = outs[at_out]
-            ref[...] = flat[pl.ds(start, rows), :].astype(ref.dtype)
-            at_out += 1
+    for ref, (r, o) in zip(outs, placed_blocks(n_z, n_x)):
+        start = (((z ^ r) * n_x + (x + o) % n_x) * 2 + core) * rows
+        if rows % 8 == 0:
+            start = pl.multiple_of(start, 8)
+        ref[...] = flat[pl.ds(start, rows), :].astype(ref.dtype)
 
 
 def message_kernel(w_ref, *refs):
@@ -294,7 +299,7 @@
 
     row = lambda v: v.reshape(1, n)
     here, *outbound = call(
-        send_kernel, "send", 62,
+        send_kernel, "send", 63,
         [shape((n // 2, width + 128), BF16)] + [shape((cap, width + 128), BF16)] * 4,
         [row(edge_owner), row(edge_src), row(edge_dst), row(edge_rot), node_feats],
         numbers=me.reshape(1),
@@ -307,7 +312,7 @@
     def rotate(rows_in, name, cost=None):
         slots = sum(r.shape[0] for r in rows_in)
         return call(
-            lambda *refs: rotate_kernel(len(rows_in), *refs), name, 62,
+            lambda *refs: rotate_kernel(len(rows_in), *refs), name, 63,
             [
                 shape((2 * slots, width), BF16), shape((slots, n), BF16),
                 shape((slots, n_rot), BF16),
@@ -330,44 +335,43 @@
     both_b_other = swap(both_b)
     both, hots, turns = [both_a, both_b], [hot_a, hot_b], [turn_a, turn_b]
 
-    n_send = n_z * (n_x - 1)
+    n_send, n_keep = n_z // 2 * (2 * n_x - 1), n_z // 2
     blocks = call(
-        lambda *refs: grad_kernel(n_z, n_x, *refs), "weight_terms", 62,
-        [shape((rows, 128), BF16)] * n_send + [shape((rows, 128), F32)] * n_z,
+        lambda *refs: grad_kernel(n_z, n_x, *refs), "weight_terms", 63,
+        [shape((rows, 128), BF16)] * n_send + [shape((rows, 128), F32)] * n_keep,
         both + [both_a_other, both_b_other],
         [pltpu.VMEM((rows * n_dp, 128), F32)],
         numbers=me.reshape(1),
     )
     turns, blocks = lax.optimization_barrier((turns, list(blocks)))
     mats = call(
-        back_kernel, "back", 62,
+        back_kernel, "back", 63,
         [shape((t.shape[0] // 8, 240, 256), BF16) for t in turns],
         [tabt] + turns,
         [pltpu.VMEM((30, t.shape[0], 256), F32) for t in turns],
     )
     kept = blocks[n_send:]
     kept[0], mats = lax.optimization_barrier((kept[0], mats))
-    sums = {}
-    for at, r in enumerate(reversed(range(n_z))):
+    sums, moves = {}, iter(blocks)
+    for at, r in enumerate(reversed(range(0, n_z, 2))):
         total = kept[at]
-        for o in range(1, n_x):
-            got = lax.ppermute(
-                blocks[(o - 1) * n_z + at], "x", [(s, (s + o) % n_x) for s in range(n_x)]
-            )
-            total = total + got.astype(F32)
+        for b, o in square(n_x):
+            route = [
+                (i * n_x + j, (i ^ b) * n_x + (j + o) % n_x)
+                for i in range(n_z) for j in range(n_x)
+            ]
+            total = total + lax.ppermute(next(moves), ("z", "x"), route).astype(F32)
         sums[r] = total
-    for bit in [1 << i for i in range(n_z.bit_length() - 1)]:
+    for bit in [1 << i for i in range(1, n_z.bit_length() - 1)]:
         for r in reversed(range(bit, n_z, 2 * bit)):
-            term = sums[r].astype(BF16)
-            if (bit, r) == (1, 1):
-                last_term = term
-            got = lax.ppermute(term, "z", [(s, s ^ bit) for s in range(n_z)])
+            last_term = sums[r].astype(BF16)
+            got = lax.ppermute(last_term, "z", [(s, s ^ bit) for s in range(n_z)])
             if 2 * bit < n_z:
                 sums[r ^ bit] = sums[r ^ bit] + got.astype(F32)
     weights, _ = lax.optimization_barrier((weights, last_term))
     slots = n // 2 + 4 * cap
     (node_out,) = call(
-        message_kernel, "messages", 62,
+        message_kernel, "messages", 63,
         [shape((n, width), BF16)],
         [weights, *both, *mats, *hots],
         [

time: 114 us -> 126 us (1.11)
  waiting for transfers between devices: 33.9 us -> 46.8 us
    ppermute x7, waiting for transfers between devices: 21.5 us -> 32.5 us  [the longest x6 29.8 us: on_device(): total = total + lax.ppermute(next(moves), ('z', 'x'), route).astype(F32)]
    ppermute x2, waiting for transfers between devices: 2.49 us -> 3.82 us  [swap(): return lax.ppermute(block, 'core', [(0, 1), (1, 0)])]
  transfers between devices with their start and end apart: 14 -> 14, of which waited for: 8 -> 7; matrix products, arithmetic and copies ran while one was open for 5% -> 4% of each run, Pallas kernels for 27% -> 25%
where the time goes in v8:
time: 126 us; the launch traced here: 125 us
  waiting for transfers between devices  46.8 us (37%)
  Pallas kernels  33.8 us (27%)
  starting transfers between devices  21 us (17%)
  between operations  14.1 us (11%)
  local copies, waits for them, and re-layouts  5.2 us (4%)
  other arithmetic  4.46 us (4%)
    pallas_call x6, Pallas kernels, call(): pl.pallas_call(kernel, grid=(1,), out_shape=outs, in_specs=first + [whole...  33.8 us
    ppermute x6, waiting for transfers between devices, on_device(): total = total + lax.ppermute(next(moves), ('z', 'x'), route).astype(F32)  29.8 us
    ppermute x4, starting transfers between devices, shift(): return lax.ppermute(block, ALL, route)  11.1 us
    ppermute x4, waiting for transfers between devices, shift(): return lax.ppermute(block, ALL, route)  9.88 us
    ppermute x6, starting transfers between devices, on_device(): total = total + lax.ppermute(next(moves), ('z', 'x'), route).astype(F32)  7.01 us
    ppermute x2, waiting for transfers between devices, swap(): return lax.ppermute(block, 'core', [(0, 1), (1, 0)])  3.82 us
    ppermute x1, waiting for transfers between devices, on_device(): got = lax.ppermute(last_term, 'z', [(s, s ^ bit) for s in range(n_z)])  2.64 us
  transfers between devices with their start and end apart: 14, of which 7 were waited for; matrix products, arithmetic and copies ran while one was open for 4% of the time, Pallas kernels for 25%

profile of v8, /device:TPU:0, one launch (start us, length us, event | category | flops | bytes accessed | tf_op | source)
XLA Modules:
  0.0 125.4 jit_solution(536448422473465430)
XLA Ops:
  7.2 0.0 all-gather.2.cloned.1.call-start
  7.2 0.7 all-gather.2.cloned.1.call-update
  7.9 3.1 %send.1 = (bf16[64,3840]{1,0:T(8,128)(2,1)}, bf16[32,3840]{1,0:T(8,128)(2,1)}, bf16[32,3840]{1,0:T(8,128)(2,1)}, bf16[32,3840]{1,0:T(8,128)(2,1)}, bf16[32,3840]{1,0:T(8,128)(2,1)}) custom-call(s32[1]{0:T(128)} %bitcast.me_ref.refs_0_, s32[1,128]{1,0:T(1,128)} %bitcast.14, s32[1,128]{1,0:T(1,128)} %bitcast.15, s32[1,128]{1,0:T(1,128)} %bitcast.16, ...), custom_call_target="tpu_custom_call" | custom-call | tf_op jit(solution)/shard_map/send/pallas_call | solution.py:262
  11.0 1.3 %collective-permute-start = (bf16[32,3840]{1,0:T(8,128)(2,1)}, bf16[32,3840]{1,0:T(8,128)(2,1)S(1)}, u32[]{:S(2)}, u32[]{:S(2)}) collective-permute-start(bf16[32,3840]{1,0:T(8,128)(2,1)} %get-tuple-element.43), channel_id=1, source_target_pairs={{2,0},{3,1},{4,2},{5,3},{6,4},{7,5},{10,8},{11,9},{12,10},{13,11},... | collective-permute-start | bytes 737288 | tf_op jit(solution)/shard_map/ppermute | solution.py:293
  12.2 5.5 %collective-permute-start.1 = (bf16[32,3840]{1,0:T(8,128)(2,1)}, bf16[32,3840]{1,0:T(8,128)(2,1)S(1)}, u32[]{:S(2)}, u32[]{:S(2)}) collective-permute-start(bf16[32,3840]{1,0:T(8,128)(2,1)} %get-tuple-element.44), channel_id=1, source_target_pairs={{0,2},{1,3},{2,4},{3,5},{4,6},{5,7},{8,10},{9,11},{10,12},{11,13},... | collective-permute-start | bytes 737288 | tf_op jit(solution)/shard_map/ppermute | solution.py:293
  17.7 1.3 %collective-permute-start.2 = (bf16[32,3840]{1,0:T(8,128)(2,1)}, bf16[32,3840]{1,0:T(8,128)(2,1)S(1)}, u32[]{:S(2)}, u32[]{:S(2)}) collective-permute-start(bf16[32,3840]{1,0:T(8,128)(2,1)} %get-tuple-element.46), channel_id=1, source_target_pairs={{1,0},{2,1},{3,2},{4,3},{5,4},{6,5},{7,6},{9,8},{10,9},{11,10},{12... | collective-permute-start | bytes 737288 | tf_op jit(solution)/shard_map/ppermute | solution.py:293
  19.0 3.0 %collective-permute-start.3 = (bf16[32,3840]{1,0:T(8,128)(2,1)}, bf16[32,3840]{1,0:T(8,128)(2,1)S(1)}, u32[]{:S(2)}, u32[]{:S(2)}) collective-permute-start(bf16[32,3840]{1,0:T(8,128)(2,1)} %get-tuple-element.47), channel_id=1, source_target_pairs={{0,1},{1,2},{2,3},{3,4},{4,5},{5,6},{6,7},{8,9},{9,10},{10,11},{11... | collective-permute-start | bytes 737288 | tf_op jit(solution)/shard_map/ppermute | solution.py:293
  22.1 2.0 %copy.10 = bf16[29,64,29]{2,1,0:T(8,128)(2,1)} copy(bf16[29,64,29]{1,2,0:T(8,128)(2,1)} %bitcast.12) | data formatting | bytes 215296 | tf_op jit(solution)/shard_map/transpose | solution.py:309
  24.1 0.0 collective-permute-done.refs_1_
  24.1 0.0 copy-start.2
  24.1 9.9 %collective-permute-done.1.refs_2_ = bf16[32,3840]{1,0:T(8,128)(2,1)S(1)} collective-permute-done((bf16[32,3840]{1,0:T(8,128)(2,1)}, bf16[32,3840]{1,0:T(8,128)(2,1)S(1)}, u32[]{:S(2)}, u32[]{:S(2)}) %collective-permute-start.1) | collective-permute-done | bytes 245792 | tf_op jit(solution)/shard_map/ppermute | solution.py:293
  34.0 0.0 copy-start.3
  34.0 0.0 copy-done.2
  34.0 0.7 copy-done.3
  34.7 5.0 %rotate_first.1 = (bf16[256,3712]{1,0:T(8,128)(2,1)}, bf16[128,128]{1,0:T(8,128)(2,1)}, bf16[128,64]{1,0:T(8,128)(2,1)}) custom-call(bf16[64,3840]{1,0:T(8,128)(2,1)} %get-tuple-element.42.refs_0_, bf16[32,3840]{1,0:T(8,128)(2,1)} %copy-done.2, bf16[32,3840]{1,0:T(8,128)(2,1)} %copy-done.3, bf16[1856,29]{1,0:T(8,128)(2,1)} %bitcast.9, bf16[128,3712]{1,0:T(8,128)(2,1)} %refs_3_.1), custom_call_target="tpu_custom_call" | custom-call | tf_op jit(solution)/shard_map/rotate_first/pallas_call | solution.py:262
  39.6 0.0 collective-permute-start.4
  39.6 0.0 collective-permute-done.2.refs_0_
  39.7 0.0 copy-start.4
  39.7 0.0 collective-permute-done.3.refs_1_
  39.7 0.7 copy-done.4
  40.4 0.0 copy-start.5
  40.4 0.7 copy-done.5
  41.1 3.8 %rotate_last.1 = (bf16[128,3712]{1,0:T(8,128)(2,1)}, bf16[64,128]{1,0:T(8,128)(2,1)}, bf16[64,64]{1,0:T(8,128)(2,1)}) custom-call(bf16[32,3840]{1,0:T(8,128)(2,1)} %copy-done.4, bf16[32,3840]{1,0:T(8,128)(2,1)} %copy-done.5, bf16[1856,29]{1,0:T(8,128)(2,1)} %bitcast.10, bf16[128,3712]{1,0:T(8,128)(2,1)} %refs_3_.1), custom_call_target="tpu_custom_call" | custom-call | flops 10000000000 | bytes 100000000 | tf_op jit(solution)/shard_map/rotate_last/pallas_call | solution.py:262
  44.9 0.0 copy-start
  44.9 0.5 collective-permute-start.5
  45.4 3.8 %collective-permute-done.5.refs_4_ = bf16[128,3712]{1,0:T(8,128)(2,1)} collective-permute-done((bf16[128,3712]{1,0:T(8,128)(2,1)}, bf16[128,3712]{1,0:T(8,128)(2,1)}, u32[]{:S(2)}, u32[]{:S(2)}) %collective-permute-start.5) | collective-permute-done | bytes 950304 | tf_op jit(solution)/shard_map/ppermute | solution.py:296
  49.2 0.0 collective-permute-done.4.refs_3_
  49.2 8.9 %weight_terms.1 = (bf16[1368,128]{1,0:T(8,128)(2,1)}, bf16[1368,128]{1,0:T(8,128)(2,1)}, bf16[1368,128]{1,0:T(8,128)(2,1)}, bf16[1368,128]{1,0:T(8,128)(2,1)}, b...) custom-call(s32[1]{0:T(128)} %bitcast.me_ref.refs_0_, ...), custom_call_target="tpu_custom_call" | custom-call | tf_op jit(solution)/shard_map/weight_terms/pallas_call | solution.py:262
  58.1 0.0 collective-permute-start.6
  58.1 3.5 %collective-permute-start.7 = (bf16[1368,128]{1,0:T(8,128)(2,1)}, bf16[1368,128]{1,0:T(8,128)(2,1)S(1)}, u32[]{:S(2)}, u32[]{:S(2)}) collective-permute-start(bf16[1368,128]{1,0:T(8,128)(2,1)} %get-tuple-element.69), channel_id=1, source_target_pairs={{0,4},{2,6},{4,0},{6,2},{8,12},{10,14},{12,8},{14,10},{1,5},{3,7},... | collective-permute-start | bytes 1050632 | tf_op jit(solution)/shard_map/ppermute | solution.py:363
  61.6 0.0 collective-permute-start.8
  61.6 0.0 copy-done
  61.6 1.1 copy.11
  62.8 3.7 %back.1 = (bf16[16,240,256]{2,1,0:T(8,128)(2,1)}, bf16[8,240,256]{2,1,0:T(8,128)(2,1)}) custom-call(bf16[1856,29]{1,0:T(8,128)(2,1)} %bitcast.11, bf16[128,64]{1,0:T(8,128)(2,1)} %get-tuple-element.63.refs_0_, bf16[64,64]{1,0:T(8,128)(2,1)} %get-tuple-element.64.refs_1_), custom_call_target="tpu_custom_call" | custom-call | tf_op jit(solution)/shard_map/back/pallas_call | solution.py:262
  66.4 11.4 %collective-permute-done.6 = bf16[1368,128]{1,0:T(8,128)(2,1)S(1)} collective-permute-done((bf16[1368,128]{1,0:T(8,128)(2,1)}, bf16[1368,128]{1,0:T(8,128)(2,1)S(1)}, u32[]{:S(2)}, u32[]{:S(2)}) %collective-permute-start.6) | collective-permute-done | bytes 350240 | tf_op jit(solution)/shard_map/ppermute | solution.py:363
  77.9 8.7 %collective-permute-done.7 = bf16[1368,128]{1,0:T(8,128)(2,1)S(1)} collective-permute-done((bf16[1368,128]{1,0:T(8,128)(2,1)}, bf16[1368,128]{1,0:T(8,128)(2,1)S(1)}, u32[]{:S(2)}, u32[]{:S(2)}) %collective-permute-start.7) | collective-permute-done | bytes 350240 | tf_op jit(solution)/shard_map/ppermute | solution.py:363
  86.6 0.0 collective-permute-done.8
  86.6 2.1 %add_convert_fusion = bf16[1368,128]{1,0:T(8,128)(2,1)} fusion(bf16[1368,128]{1,0:T(8,128)(2,1)} %collective-permute-done.8, bf16[1368,128]{1,0:T(8,128)(2,1)S(1)} %collective-permute-done.7, f32[1368,128]{1,0:T(8,128)} %get-tuple-element.67, bf16[1368,128]{1,0:T(8,128)(2,1)S(1)} %collective-permute-done.6), kind=kLoop, calls=%fused_computation.1 | loop fusion | flops 1225728 | bytes 2101248 | tf_op jit(solution)/shard_map/convert_element_type | solution.py:367
  88.7 2.3 %collective-permute-start.9 = (bf16[1368,128]{1,0:T(8,128)(2,1)}, bf16[1368,128]{1,0:T(8,128)(2,1)}, u32[]{:S(2)}, u32[]{:S(2)}) collective-permute-start(bf16[1368,128]{1,0:T(8,128)(2,1)} %add_convert_fusion), channel_id=1, source_target_pairs={{0,8},{4,12},{8,0},{12,4},{1,9},{5,13},{9,1},{13,5},{2,10},{6,14},... | collective-permute-start | bytes 1050632 | tf_op jit(solution)/shard_map/ppermute | solution.py:368
  91.1 0.6 collective-permute-start.10
  91.7 1.5 %collective-permute-start.11 = (bf16[1368,128]{1,0:T(8,128)(2,1)}, bf16[1368,128]{1,0:T(8,128)(2,1)}, u32[]{:S(2)}, u32[]{:S(2)}) collective-permute-start(bf16[1368,128]{1,0:T(8,128)(2,1)} %get-tuple-element.79), channel_id=1, source_target_pairs={{0,4},{2,6},{4,0},{6,2},{8,12},{10,14},{12,8},{14,10},{1,5},{3,7},... | collective-permute-start | bytes 1050632 | tf_op jit(solution)/shard_map/ppermute | solution.py:363
  93.2 1.3 %collective-permute-start.12 = (bf16[1368,128]{1,0:T(8,128)(2,1)}, bf16[1368,128]{1,0:T(8,128)(2,1)}, u32[]{:S(2)}, u32[]{:S(2)}) collective-permute-start(bf16[1368,128]{1,0:T(8,128)(2,1)} %get-tuple-element.80), channel_id=1, source_target_pairs={{0,2},{2,0},{4,6},{6,4},{8,10},{10,8},{12,14},{14,12},{1,3},{3,1},... | collective-permute-start | bytes 1050632 | tf_op jit(solution)/shard_map/ppermute | solution.py:363
  94.5 0.0 all-gather.2.cloned.1.call-done.w_ref
  94.6 0.0 copy-start.1
  94.6 9.3 %messages.1 = bf16[128,3712]{1,0:T(8,128)(2,1)} custom-call(bf16[21888,128]{1,0:T(8,128)(2,1)} %all-gather.2.cloned.1.call-done.w_ref, bf16[256,3712]{1,0:T(8,128)(2,1)} %get-tuple-element.52.refs_1_.refs_0_, bf16[128,3712]{1,0:T(8,128)(2,1)} %get-tuple-element.53.refs_2_.refs_1_, bf16[16,240,256]{2,1,0:T(8,128)(2,1)} %get-tuple-element.72.refs_2_, ...), custom_call_target="tpu_custom_call" | custom-call | tf_op jit(solution)/shard_map/messages/pallas_call | solution.py:262
  103.9 2.6 %collective-permute-done.9 = bf16[1368,128]{1,0:T(8,128)(2,1)} collective-permute-done((bf16[1368,128]{1,0:T(8,128)(2,1)}, bf16[1368,128]{1,0:T(8,128)(2,1)}, u32[]{:S(2)}, u32[]{:S(2)}) %collective-permute-start.9) | collective-permute-done | bytes 350240 | tf_op jit(solution)/shard_map/ppermute | solution.py:368
  106.5 4.3 %collective-permute-done.10 = bf16[1368,128]{1,0:T(8,128)(2,1)} collective-permute-done((bf16[1368,128]{1,0:T(8,128)(2,1)}, bf16[1368,128]{1,0:T(8,128)(2,1)}, u32[]{:S(2)}, u32[]{:S(2)}) %collective-permute-start.10) | collective-permute-done | bytes 350240 | tf_op jit(solution)/shard_map/ppermute | solution.py:363
  110.8 5.3 %collective-permute-done.11 = bf16[1368,128]{1,0:T(8,128)(2,1)} collective-permute-done((bf16[1368,128]{1,0:T(8,128)(2,1)}, bf16[1368,128]{1,0:T(8,128)(2,1)}, u32[]{:S(2)}, u32[]{:S(2)}) %collective-permute-start.11) | collective-permute-done | bytes 350240 | tf_op jit(solution)/shard_map/ppermute | solution.py:363
  116.2 0.0 collective-permute-done.12
  116.2 0.0 copy-done.1
  116.2 2.4 %add_multiply_fusion = f32[1368,128]{1,0:T(8,128)} fusion(bf16[1368,128]{1,0:T(8,128)(2,1)} %collective-permute-done.9, bf16[1368,128]{1,0:T(8,128)(2,1)} %collective-permute-done.12, bf16[1368,128]{1,0:T(8,128)(2,1)} %collective-permute-done.11, f32[1368,128]{1,0:T(8,128)S(1)} %copy-done.1, bf16[1368,128]{1,0:T(8,128)(2,1)} %collective-permute-done.10), kind=kLoop, calls=%fused_computation | loop fusion | flops 1575936 | bytes 2801664 | tf_op jit(solution)/shard_map/mul | solution.py:384
Async XLA Ops:
  7.2 87.4 %all-gather.2.cloned.1.call-start = ((), (), s32[]{:S(2)}) async-start(), calls=%async_computation | async-start | bytes 5953536 | tf_op jit(solution)/shard_map/all_gather | solution.py:298
  11.0 13.1 %collective-permute-start = (bf16[32,3840]{1,0:T(8,128)(2,1)}, bf16[32,3840]{1,0:T(8,128)(2,1)S(1)}, u32[]{:S(2)}, u32[]{:S(2)}) collective-permute-start(bf16[32,3840]{1,0:T(8,128)(2,1)} %get-tuple-element.43), channel_id=1, source_target_pairs={{2,0},{3,1},{4,2},{5,3},{6,4},{7,5},{10,8},{11,9},{12,10},{13,11},... | collective-permute-start | bytes 737288 | tf_op jit(solution)/shard_map/ppermute | solution.py:293
  12.2 21.7 %collective-permute-start.1 = (bf16[32,3840]{1,0:T(8,128)(2,1)}, bf16[32,3840]{1,0:T(8,128)(2,1)S(1)}, u32[]{:S(2)}, u32[]{:S(2)}) collective-permute-start(bf16[32,3840]{1,0:T(8,128)(2,1)} %get-tuple-element.44), channel_id=1, source_target_pairs={{0,2},{1,3},{2,4},{3,5},{4,6},{5,7},{8,10},{9,11},{10,12},{11,13},... | collective-permute-start | bytes 737288 | tf_op jit(solution)/shard_map/ppermute | solution.py:293
  17.7 21.9 %collective-permute-start.2 = (bf16[32,3840]{1,0:T(8,128)(2,1)}, bf16[32,3840]{1,0:T(8,128)(2,1)S(1)}, u32[]{:S(2)}, u32[]{:S(2)}) collective-permute-start(bf16[32,3840]{1,0:T(8,128)(2,1)} %get-tuple-element.46), channel_id=1, source_target_pairs={{1,0},{2,1},{3,2},{4,3},{5,4},{6,5},{7,6},{9,8},{10,9},{11,10},{12... | collective-permute-start | bytes 737288 | tf_op jit(solution)/shard_map/ppermute | solution.py:293
  19.0 20.6 %collective-permute-start.3 = (bf16[32,3840]{1,0:T(8,128)(2,1)}, bf16[32,3840]{1,0:T(8,128)(2,1)S(1)}, u32[]{:S(2)}, u32[]{:S(2)}) collective-permute-start(bf16[32,3840]{1,0:T(8,128)(2,1)} %get-tuple-element.47), channel_id=1, source_target_pairs={{0,1},{1,2},{2,3},{3,4},{4,5},{5,6},{6,7},{8,9},{9,10},{10,11},{11... | collective-permute-start | bytes 737288 | tf_op jit(solution)/shard_map/ppermute | solution.py:293
  24.1 9.9 %copy-start.2 = (bf16[32,3840]{1,0:T(8,128)(2,1)}, bf16[32,3840]{1,0:T(8,128)(2,1)S(1)}, u32[]{:S(2)}) copy-start(bf16[32,3840]{1,0:T(8,128)(2,1)S(1)} %collective-permute-done.refs_1_) | copy-start | bytes 737284
  34.0 0.7 copy-start.3
  39.6 9.6 %collective-permute-start.4 = (bf16[256,3712]{1,0:T(8,128)(2,1)}, bf16[256,3712]{1,0:T(8,128)(2,1)}, u32[]{:S(2)}, u32[]{:S(2)}) collective-permute-start(bf16[256,3712]{1,0:T(8,128)(2,1)} %get-tuple-element.52.refs_1_.refs_0_), channel_id=1, source_target_pairs={{0,1},{1,0},{2,3},{3,2},{4,5},{5,4},{6,7},{7,6},{8,9},{9,8},{10,11... | collective-permute-start | bytes 5701640 | tf_op jit(solution)/shard_map/ppermute | solution.py:296
  39.7 0.7 copy-start.4
  40.4 0.7 copy-start.5
  44.9 16.7 %copy-start = (bf16[64,29,29]{0,2,1:T(8,128)(2,1)S(1)}, bf16[64,29,29]{0,2,1:T(8,128)(2,1)}, u32[]{:S(2)}) copy-start(bf16[64,29,29]{0,2,1:T(8,128)(2,1)} %param.11) | copy-start | bytes 322948
  44.9 4.3 %collective-permute-start.5 = (bf16[128,3712]{1,0:T(8,128)(2,1)}, bf16[128,3712]{1,0:T(8,128)(2,1)}, u32[]{:S(2)}, u32[]{:S(2)}) collective-permute-start(bf16[128,3712]{1,0:T(8,128)(2,1)} %get-tuple-element.53.refs_2_.refs_1_), channel_id=1, source_target_pairs={{0,1},{1,0},{2,3},{3,2},{4,5},{5,4},{6,7},{7,6},{8,9},{9,8},{10,11... | collective-permute-start | bytes 2850824 | tf_op jit(solution)/shard_map/ppermute | solution.py:296
  58.1 19.8 %collective-permute-start.6 = (bf16[1368,128]{1,0:T(8,128)(2,1)}, bf16[1368,128]{1,0:T(8,128)(2,1)S(1)}, u32[]{:S(2)}, u32[]{:S(2)}) collective-permute-start(bf16[1368,128]{1,0:T(8,128)(2,1)} %get-tuple-element.68), channel_id=1, source_target_pairs={{0,6},{2,4},{4,2},{6,0},{8,14},{10,12},{12,10},{14,8},{1,7},{3,5},... | collective-permute-start | bytes 1050632 | tf_op jit(solution)/shard_map/ppermute | solution.py:363
  58.1 28.5 %collective-permute-start.7 = (bf16[1368,128]{1,0:T(8,128)(2,1)}, bf16[1368,128]{1,0:T(8,128)(2,1)S(1)}, u32[]{:S(2)}, u32[]{:S(2)}) collective-permute-start(bf16[1368,128]{1,0:T(8,128)(2,1)} %get-tuple-element.69), channel_id=1, source_target_pairs={{0,4},{2,6},{4,0},{6,2},{8,12},{10,14},{12,8},{14,10},{1,5},{3,7},... | collective-permute-start | bytes 1050632 | tf_op jit(solution)/shard_map/ppermute | solution.py:363
  61.6 25.0 %collective-permute-start.8 = (bf16[1368,128]{1,0:T(8,128)(2,1)}, bf16[1368,128]{1,0:T(8,128)(2,1)}, u32[]{:S(2)}, u32[]{:S(2)}) collective-permute-start(bf16[1368,128]{1,0:T(8,128)(2,1)} %get-tuple-element.70), channel_id=1, source_target_pairs={{0,2},{2,0},{4,6},{6,4},{8,10},{10,8},{12,14},{14,12},{1,3},{3,1},... | collective-permute-start | bytes 1050632 | tf_op jit(solution)/shard_map/ppermute | solution.py:363
  88.7 17.8 %collective-permute-start.9 = (bf16[1368,128]{1,0:T(8,128)(2,1)}, bf16[1368,128]{1,0:T(8,128)(2,1)}, u32[]{:S(2)}, u32[]{:S(2)}) collective-permute-start(bf16[1368,128]{1,0:T(8,128)(2,1)} %add_convert_fusion), channel_id=1, source_target_pairs={{0,8},{4,12},{8,0},{12,4},{1,9},{5,13},{9,1},{13,5},{2,10},{6,14},... | collective-permute-start | bytes 1050632 | tf_op jit(solution)/shard_map/ppermute | solution.py:368
  91.1 19.8 %collective-permute-start.10 = (bf16[1368,128]{1,0:T(8,128)(2,1)}, bf16[1368,128]{1,0:T(8,128)(2,1)}, u32[]{:S(2)}, u32[]{:S(2)}) collective-permute-start(bf16[1368,128]{1,0:T(8,128)(2,1)} %get-tuple-element.78), channel_id=1, source_target_pairs={{0,6},{2,4},{4,2},{6,0},{8,14},{10,12},{12,10},{14,8},{1,7},{3,5},... | collective-permute-start | bytes 1050632 | tf_op jit(solution)/shard_map/ppermute | solution.py:363
  91.7 24.5 %collective-permute-start.11 = (bf16[1368,128]{1,0:T(8,128)(2,1)}, bf16[1368,128]{1,0:T(8,128)(2,1)}, u32[]{:S(2)}, u32[]{:S(2)}) collective-permute-start(bf16[1368,128]{1,0:T(8,128)(2,1)} %get-tuple-element.79), channel_id=1, source_target_pairs={{0,4},{2,6},{4,0},{6,2},{8,12},{10,14},{12,8},{14,10},{1,5},{3,7},... | collective-permute-start | bytes 1050632 | tf_op jit(solution)/shard_map/ppermute | solution.py:363
  93.2 22.9 %collective-permute-start.12 = (bf16[1368,128]{1,0:T(8,128)(2,1)}, bf16[1368,128]{1,0:T(8,128)(2,1)}, u32[]{:S(2)}, u32[]{:S(2)}) collective-permute-start(bf16[1368,128]{1,0:T(8,128)(2,1)} %get-tuple-element.80), channel_id=1, source_target_pairs={{0,2},{2,0},{4,6},{6,4},{8,10},{10,8},{12,14},{14,12},{1,3},{3,1},... | collective-permute-start | bytes 1050632 | tf_op jit(solution)/shard_map/ppermute | solution.py:363
  94.6 21.6 %copy-start.1 = (f32[1368,128]{1,0:T(8,128)S(1)}, f32[1368,128]{1,0:T(8,128)}, u32[]{:S(2)}) copy-start(f32[1368,128]{1,0:T(8,128)} %get-tuple-element.77) | copy-start | bytes 2101252
Sparse Core Ops, SparseCore 0:
  10.2 72.0 all-gather.1

commit v9 on v6

--- a/solution.py
+++ b/solution.py
@@ -142,46 +142,71 @@
         build(tabt_ref, refs[i][...], refs[2 + i], refs[4 + i])
 
 
-def grad_kernel(n_z, n_x, me_ref, *refs):
-    parts, outs, flat = refs[:4], refs[4:-1], refs[-1]
-    chip, core = me_ref[0] // 2, me_ref[0] % 2
-    z, x = chip // n_x, chip % n_x
-
-    def left(first, width):
-        at = slice(first * 128, (first + width) * 128)
+def products(parts, flat, low, high):
+
+    def left(first, i, end):
+        at = slice((first + i) * 128, (first + end) * 128)
         return [p[: p.shape[0] // 2, at] for p in parts]
 
     def right(first, width):
         at = slice(first * 128, (first + width) * 128)
         return [p[p.shape[0] // 2 :, at] for p in parts]
 
-    def outer(lhs, rhs):
-        return lax.dot_general(lhs, rhs, (((0,), (0,)), ((), ())), preferred_element_type=F32)
-
-    def emit(base, width, res):
+    def emit(base, width, firsts, rhs):
+        unit = width * 128
+        i, end = max(0, (low - base) // unit), min(width, -(-(high - base) // unit))
+        if i >= end:
+            return
+        lhs = jnp.concatenate([v for f in firsts for v in left(f, i, end)], axis=0)
+        res = lax.dot_general(
+            lhs, jnp.concatenate(rhs(), axis=0), (((0,), (0,)), ((), ())),
+            preferred_element_type=F32,
+        )
         for b in range(width):
-            flat[pl.ds(base + b, width * 128, stride=width), :] = res[:, b * 128 : (b + 1) * 128]
-
-    emit(0, 7, outer(jnp.concatenate(left(0, 7), axis=0), jnp.concatenate(right(0, 7), axis=0)))
+            at = pl.ds(base + i * unit + b, (end - i) * 128, stride=width)
+            flat[at, :] = res[:, b * 128 : (b + 1) * 128]
+
+    emit(0, 7, (0,), lambda: right(0, 7))
     base = 49 * 128
     for first, width in ((7, 6), (19, 5)):
-        lhs = jnp.concatenate(left(first, width) + left(first + width, width), axis=0)
-        real, imag = right(first, width), right(first + width, width)
-        emit(base, width, outer(lhs, jnp.concatenate(real + imag, axis=0)))
+        mid = first + width
+        emit(base, width, (first, mid), lambda: right(first, width) + right(mid, width))
         base += width * width * 128
-        emit(base, width, outer(lhs, jnp.concatenate(imag + [-v for v in real], axis=0)))
+        emit(
+            base, width, (first, mid),
+            lambda: right(mid, width) + [-v for v in right(first, width)],
+        )
         base += width * width * 128
 
+
+def owner_row(n_x, me, r, o, rows):
+    chip, core = me // 2, me % 2
+    z, x = chip // n_x, chip % n_x
+    start = (((z ^ r) * n_x + (x + o) % n_x) * 2 + core) * rows
+    return pl.multiple_of(start, 8) if rows % 8 == 0 else start
+
+
+def first_kernel(n_z, n_x, me_ref, *refs):
+    parts, out_ref, flat = refs[:4], refs[4], refs[5]
+    rows = out_ref.shape[0]
+    start = owner_row(n_x, me_ref[0], n_z - 1, 1, rows)
+    for chip in range(n_z * n_x):
+
+        @pl.when(start // (2 * rows) == chip)
+        def _():
+            products(parts, flat, chip * 2 * rows, (chip + 1) * 2 * rows)
+
+    out_ref[...] = flat[pl.ds(start, rows), :].astype(BF16)
+
+
+def grad_kernel(n_z, n_x, me_ref, *refs):
+    parts, outs, flat = refs[:4], refs[4:-1], refs[-1]
+    products(parts, flat, 0, flat.shape[0])
     rows = outs[0].shape[0]
-    at_out = 0
-    for o in list(range(1, n_x)) + [0]:
-        for r in reversed(range(n_z)):
-            start = (((z ^ r) * n_x + (x + o) % n_x) * 2 + core) * rows
-            if rows % 8 == 0:
-                start = pl.multiple_of(start, 8)
-            ref = outs[at_out]
-            ref[...] = flat[pl.ds(start, rows), :].astype(ref.dtype)
-            at_out += 1
+    order = [(r, o) for o in list(range(1, n_x)) + [0] for r in reversed(range(n_z))]
+    for ref, (r, o) in zip(outs, order[1:]):
+        start = owner_row(n_x, me_ref[0], r, o, rows)
+        ref[...] = flat[pl.ds(start, rows), :].astype(ref.dtype)
 
 
 def message_kernel(w_ref, *refs):
@@ -331,22 +356,29 @@
     both, hots, turns = [both_a, both_b], [hot_a, hot_b], [turn_a, turn_b]
 
     n_send = n_z * (n_x - 1)
-    blocks = call(
-        lambda *refs: grad_kernel(n_z, n_x, *refs), "weight_terms", 62,
-        [shape((rows, 128), BF16)] * n_send + [shape((rows, 128), F32)] * n_z,
-        both + [both_a_other, both_b_other],
-        [pltpu.VMEM((rows * n_dp, 128), F32)],
+    terms = both + [both_a_other, both_b_other]
+    (first_block,) = call(
+        lambda *refs: first_kernel(n_z, n_x, *refs), "first_terms", 63,
+        [shape((rows, 128), BF16)], terms, [pltpu.VMEM((rows * n_dp, 128), F32)],
         numbers=me.reshape(1),
     )
-    turns, blocks = lax.optimization_barrier((turns, list(blocks)))
+    terms, first_block = lax.optimization_barrier((terms, first_block))
+    others = call(
+        lambda *refs: grad_kernel(n_z, n_x, *refs), "weight_terms", 63,
+        [shape((rows, 128), BF16)] * (n_send - 1) + [shape((rows, 128), F32)] * n_z,
+        terms, [pltpu.VMEM((rows * n_dp, 128), F32)],
+        numbers=me.reshape(1),
+    )
+    turns, others = lax.optimization_barrier((turns, list(others)))
     mats = call(
         back_kernel, "back", 62,
         [shape((t.shape[0] // 8, 240, 256), BF16) for t in turns],
         [tabt] + turns,
         [pltpu.VMEM((30, t.shape[0], 256), F32) for t in turns],
     )
+    blocks = [first_block] + others
     kept = blocks[n_send:]
-    kept[0], mats = lax.optimization_barrier((kept[0], mats))
+    kept[1], mats = lax.optimization_barrier((kept[1], mats))
     sums = {}
     for at, r in enumerate(reversed(range(n_z))):
         total = kept[at]

time: 114 us -> 117 us (1.026)
  Pallas kernels: 34.1 us -> 38.4 us
  starting transfers between devices: 21 us -> 17.4 us
  other arithmetic: 4.23 us -> 6.04 us
    pallas_call x6 -> x7, Pallas kernels: 34.1 us -> 38.4 us  [call(): pl.pallas_call(kernel, grid=(1,), out_shape=outs, in_specs=first + [whole...]
    ppermute x4, waiting for transfers between devices: 8.61 us -> 5.23 us  [on_device(): lax.ppermute(blocks[(o - 1) * n_z + at], 'x', [(s, (s + o) % n_x) for s i...]
    ppermute x3, starting transfers between devices: 4.23 us -> 1.55 us  [on_device(): got = lax.ppermute(term, 'z', [(s, s ^ bit) for s in range(n_z)])]
    ppermute x3, waiting for transfers between devices: 12.9 us -> 15.4 us  [on_device(): got = lax.ppermute(term, 'z', [(s, s ^ bit) for s in range(n_z)])]
    convert_element_type x3, other arithmetic: 2.13 us -> 3.91 us  [on_device(): term = sums[r].astype(BF16)]
    ppermute x2, waiting for transfers between devices: 2.49 us -> 3.69 us  [swap(): return lax.ppermute(block, 'core', [(0, 1), (1, 0)])]
    unnamed x12 -> x18, local copies, waits for them, and re-layouts: 1.96 us -> 3.02 us
  transfers between devices with their start and end apart: 14 -> 14, of which waited for: 8 -> 5; matrix products, arithmetic and copies ran while one was open for 5% -> 6% of each run, Pallas kernels for 27% -> 30%
where the time goes in v9:
time: 117 us
  Pallas kernels  38.4 us (33%)
  waiting for transfers between devices  34.9 us (30%)
  starting transfers between devices  17.4 us (15%)
  between operations  14.1 us (12%)
  local copies, waits for them, and re-layouts  6.13 us (5%)
  other arithmetic  6.04 us (5%)
    pallas_call x7, Pallas kernels, call(): pl.pallas_call(kernel, grid=(1,), out_shape=outs, in_specs=first + [whole...  38.4 us
    ppermute x3, waiting for transfers between devices, on_device(): got = lax.ppermute(term, 'z', [(s, s ^ bit) for s in range(n_z)])  15.4 us
    ppermute x4, starting transfers between devices, shift(): return lax.ppermute(block, ALL, route)  11.1 us
    ppermute x4, waiting for transfers between devices, shift(): return lax.ppermute(block, ALL, route)  9.88 us
    ppermute x4, waiting for transfers between devices, on_device(): lax.ppermute(blocks[(o - 1) * n_z + at], 'x', [(s, (s + o) % n_x) for s i...  5.23 us
    ppermute x4, starting transfers between devices, on_device(): lax.ppermute(blocks[(o - 1) * n_z + at], 'x', [(s, (s + o) % n_x) for s i...  4.19 us
    convert_element_type x3, other arithmetic, on_device(): term = sums[r].astype(BF16)  3.91 us
    ppermute x2, waiting for transfers between devices, swap(): return lax.ppermute(block, 'core', [(0, 1), (1, 0)])  3.69 us
  transfers between devices with their start and end apart: 14, of which 5 were waited for; matrix products, arithmetic and copies ran while one was open for 6% of the time, Pallas kernels for 30%

profile of v9, /device:TPU:0, one launch (start us, length us, event | category | flops | bytes accessed | tf_op | source)
XLA Modules:
  0.0 117.0 jit_solution(17494584418362573592)
XLA Ops:
  7.2 0.0 all-gather.2.cloned.1.call-start
  7.2 0.7 all-gather.2.cloned.1.call-update
  7.9 3.1 %send.1 = (bf16[64,3840]{1,0:T(8,128)(2,1)}, bf16[32,3840]{1,0:T(8,128)(2,1)}, bf16[32,3840]{1,0:T(8,128)(2,1)}, bf16[32,3840]{1,0:T(8,128)(2,1)}, bf16[32,3840]{1,0:T(8,128)(2,1)}) custom-call(s32[1]{0:T(128)} %bitcast.me_ref.refs_0_, s32[1,128]{1,0:T(1,128)} %bitcast.14, s32[1,128]{1,0:T(1,128)} %bitcast.15, s32[1,128]{1,0:T(1,128)} %bitcast.16, ...), custom_call_target="tpu_custom_call" | custom-call | tf_op jit(solution)/shard_map/send/pallas_call | solution.py:282
  11.0 1.3 %collective-permute-start = (bf16[32,3840]{1,0:T(8,128)(2,1)}, bf16[32,3840]{1,0:T(8,128)(2,1)S(1)}, u32[]{:S(2)}, u32[]{:S(2)}) collective-permute-start(bf16[32,3840]{1,0:T(8,128)(2,1)} %get-tuple-element.46), channel_id=1, source_target_pairs={{2,0},{3,1},{4,2},{5,3},{6,4},{7,5},{10,8},{11,9},{12,10},{13,11},... | collective-permute-start | bytes 737288 | tf_op jit(solution)/shard_map/ppermute | solution.py:313
  12.3 5.5 %collective-permute-start.1 = (bf16[32,3840]{1,0:T(8,128)(2,1)}, bf16[32,3840]{1,0:T(8,128)(2,1)S(1)}, u32[]{:S(2)}, u32[]{:S(2)}) collective-permute-start(bf16[32,3840]{1,0:T(8,128)(2,1)} %get-tuple-element.47), channel_id=1, source_target_pairs={{0,2},{1,3},{2,4},{3,5},{4,6},{5,7},{8,10},{9,11},{10,12},{11,13},... | collective-permute-start | bytes 737288 | tf_op jit(solution)/shard_map/ppermute | solution.py:313
  17.7 1.3 %collective-permute-start.2 = (bf16[32,3840]{1,0:T(8,128)(2,1)}, bf16[32,3840]{1,0:T(8,128)(2,1)S(1)}, u32[]{:S(2)}, u32[]{:S(2)}) collective-permute-start(bf16[32,3840]{1,0:T(8,128)(2,1)} %get-tuple-element.49), channel_id=1, source_target_pairs={{1,0},{2,1},{3,2},{4,3},{5,4},{6,5},{7,6},{9,8},{10,9},{11,10},{12... | collective-permute-start | bytes 737288 | tf_op jit(solution)/shard_map/ppermute | solution.py:313
  19.0 3.0 %collective-permute-start.3 = (bf16[32,3840]{1,0:T(8,128)(2,1)}, bf16[32,3840]{1,0:T(8,128)(2,1)S(1)}, u32[]{:S(2)}, u32[]{:S(2)}) collective-permute-start(bf16[32,3840]{1,0:T(8,128)(2,1)} %get-tuple-element.50), channel_id=1, source_target_pairs={{0,1},{1,2},{2,3},{3,4},{4,5},{5,6},{6,7},{8,9},{9,10},{10,11},{11... | collective-permute-start | bytes 737288 | tf_op jit(solution)/shard_map/ppermute | solution.py:313
  22.1 2.0 %copy.10 = bf16[29,64,29]{2,1,0:T(8,128)(2,1)} copy(bf16[29,64,29]{1,2,0:T(8,128)(2,1)} %bitcast.12) | data formatting | bytes 215296 | tf_op jit(solution)/shard_map/transpose | solution.py:329
  24.1 0.0 collective-permute-done.refs_1_
  24.1 0.0 copy-start.5
  24.1 9.9 %collective-permute-done.1.refs_2_ = bf16[32,3840]{1,0:T(8,128)(2,1)S(1)} collective-permute-done((bf16[32,3840]{1,0:T(8,128)(2,1)}, bf16[32,3840]{1,0:T(8,128)(2,1)S(1)}, u32[]{:S(2)}, u32[]{:S(2)}) %collective-permute-start.1) | collective-permute-done | bytes 245792 | tf_op jit(solution)/shard_map/ppermute | solution.py:313
  34.0 0.0 copy-start.6
  34.0 0.0 copy-done.5
  34.0 0.7 copy-done.6
  34.7 5.0 %rotate_first.1 = (bf16[256,3712]{1,0:T(8,128)(2,1)}, bf16[128,128]{1,0:T(8,128)(2,1)}, bf16[128,64]{1,0:T(8,128)(2,1)}) custom-call(bf16[64,3840]{1,0:T(8,128)(2,1)} %get-tuple-element.45.refs_0_, bf16[32,3840]{1,0:T(8,128)(2,1)} %copy-done.5, bf16[32,3840]{1,0:T(8,128)(2,1)} %copy-done.6, bf16[1856,29]{1,0:T(8,128)(2,1)} %bitcast.9, bf16[128,3712]{1,0:T(8,128)(2,1)} %refs_3_.1), custom_call_target="tpu_custom_call" | custom-call | tf_op jit(solution)/shard_map/rotate_first/pallas_call | solution.py:282
  39.6 0.0 collective-permute-start.4
  39.6 0.0 collective-permute-done.2.refs_0_
  39.6 0.0 copy-start.7
  39.7 0.0 collective-permute-done.3.refs_1_
  39.7 0.7 copy-done.7
  40.3 0.0 copy-start.8
  40.3 0.7 copy-done.8
  41.0 3.8 %rotate_last.1 = (bf16[128,3712]{1,0:T(8,128)(2,1)}, bf16[64,128]{1,0:T(8,128)(2,1)}, bf16[64,64]{1,0:T(8,128)(2,1)}) custom-call(bf16[32,3840]{1,0:T(8,128)(2,1)} %copy-done.7, bf16[32,3840]{1,0:T(8,128)(2,1)} %copy-done.8, bf16[1856,29]{1,0:T(8,128)(2,1)} %bitcast.10, bf16[128,3712]{1,0:T(8,128)(2,1)} %refs_3_.1), custom_call_target="tpu_custom_call" | custom-call | flops 10000000000 | bytes 100000000 | tf_op jit(solution)/shard_map/rotate_last/pallas_call | solution.py:282
  44.8 0.5 collective-permute-start.5
  45.3 3.7 %collective-permute-done.5.refs_4_ = bf16[128,3712]{1,0:T(8,128)(2,1)S(1)} collective-permute-done((bf16[128,3712]{1,0:T(8,128)(2,1)}, bf16[128,3712]{1,0:T(8,128)(2,1)S(1)}, u32[]{:S(2)}, u32[]{:S(2)}) %collective-permute-start.5) | collective-permute-done | bytes 950304 | tf_op jit(solution)/shard_map/ppermute | solution.py:316
  49.0 0.0 copy-start
  49.0 0.0 collective-permute-done.4.refs_3_
  49.0 0.9 copy-done
  50.0 4.6 %first_terms.1 = bf16[1368,128]{1,0:T(8,128)(2,1)} custom-call(s32[1]{0:T(128)} %bitcast.me_ref.refs_0_, bf16[256,3712]{1,0:T(8,128)(2,1)} %get-tuple-element.57.refs_1_.refs_0_, bf16[128,3712]{1,0:T(8,128)(2,1)} %get-tuple-element.58.refs_2_.refs_1_, bf16[256,3712]{1,0:T(8,128)(2,1)} %collective-permute-done.4.refs_3_, bf16[128,3712]{1,0:T(8,128)(2,1)} %copy-done), custom_call_target="tpu_custom_call" | custom-call | tf_op jit(solution)/shard_map/first_terms/pallas_call | solution.py:282
  54.5 0.0 copy-start.1
  54.5 2.1 %collective-permute-start.7 = (bf16[1368,128]{1,0:T(8,128)(2,1)}, bf16[1368,128]{1,0:T(8,128)(2,1)}, u32[]{:S(2)}, u32[]{:S(2)}) collective-permute-start(bf16[1368,128]{1,0:T(8,128)(2,1)} %first_terms.1), channel_id=1, source_target_pairs={{0,2},{2,0},{1,3},{3,1},{4,6},{6,4},{5,7},{7,5},{8,10},{10,8},{9,1... | collective-permute-start | bytes 1050632 | tf_op jit(solution)/shard_map/ppermute | solution.py:386
  56.6 9.0 %weight_terms.1 = (bf16[1368,128]{1,0:T(8,128)(2,1)}, bf16[1368,128]{1,0:T(8,128)(2,1)}, bf16[1368,128]{1,0:T(8,128)(2,1)}, f32[1368,128]{1,0:T(8,128)}, f32[136...) custom-call(s32[1]{0:T(128)} %bitcast.me_ref.refs_0_, ...), custom_call_target="tpu_custom_call" | custom-call | tf_op jit(solution)/shard_map/weight_terms/pallas_call | solution.py:282
  65.7 0.0 copy-start.4
  65.7 0.0 copy-start.3
  65.7 0.1 collective-permute-start.6
  65.7 5.2 %collective-permute-done.7 = bf16[1368,128]{1,0:T(8,128)(2,1)} collective-permute-done((bf16[1368,128]{1,0:T(8,128)(2,1)}, bf16[1368,128]{1,0:T(8,128)(2,1)}, u32[]{:S(2)}, u32[]{:S(2)}) %collective-permute-start.7) | collective-permute-done | bytes 350240 | tf_op jit(solution)/shard_map/ppermute | solution.py:386
  71.0 2.0 %add_convert_fusion.2 = bf16[1368,128]{1,0:T(8,128)(2,1)} fusion(f32[1368,128]{1,0:T(8,128)} %get-tuple-element.75, bf16[1368,128]{1,0:T(8,128)(2,1)} %collective-permute-done.7), kind=kLoop, calls=%fused_computation.3 | loop fusion | flops 525312 | bytes 1400832 | tf_op jit(solution)/shard_map/convert_element_type | solution.py:393
  73.0 0.2 collective-permute-start.8
  73.2 0.0 copy-done.1
  73.2 1.1 copy.11
  74.3 3.7 %back.1 = (bf16[16,240,256]{2,1,0:T(8,128)(2,1)}, bf16[8,240,256]{2,1,0:T(8,128)(2,1)}) custom-call(bf16[1856,29]{1,0:T(8,128)(2,1)} %bitcast.11, bf16[128,64]{1,0:T(8,128)(2,1)} %get-tuple-element.69.refs_0_, bf16[64,64]{1,0:T(8,128)(2,1)} %get-tuple-element.70.refs_1_), custom_call_target="tpu_custom_call" | custom-call | tf_op jit(solution)/shard_map/back/pallas_call | solution.py:282
  78.0 0.2 collective-permute-start.10
  78.2 1.8 %collective-permute-start.11 = (bf16[1368,128]{1,0:T(8,128)(2,1)}, bf16[1368,128]{1,0:T(8,128)(2,1)}, u32[]{:S(2)}, u32[]{:S(2)}) collective-permute-start(bf16[1368,128]{1,0:T(8,128)(2,1)} %get-tuple-element.86), channel_id=1, source_target_pairs={{0,2},{2,0},{1,3},{3,1},{4,6},{6,4},{5,7},{7,5},{8,10},{10,8},{9,1... | collective-permute-start | bytes 1050632 | tf_op jit(solution)/shard_map/ppermute | solution.py:386
  80.0 0.0 collective-permute-done.6
  80.0 8.4 %collective-permute-done.8 = bf16[1368,128]{1,0:T(8,128)(2,1)} collective-permute-done((bf16[1368,128]{1,0:T(8,128)(2,1)}, bf16[1368,128]{1,0:T(8,128)(2,1)}, u32[]{:S(2)}, u32[]{:S(2)}) %collective-permute-start.8) | collective-permute-done | bytes 350240 | tf_op jit(solution)/shard_map/ppermute | solution.py:396
  88.4 0.0 copy-done.4
  88.4 1.8 %add_convert_fusion.1 = bf16[1368,128]{1,0:T(8,128)(2,1)} fusion(bf16[1368,128]{1,0:T(8,128)(2,1)} %collective-permute-done.8, f32[1368,128]{1,0:T(8,128)S(1)} %copy-done.4, bf16[1368,128]{1,0:T(8,128)(2,1)S(1)} %collective-permute-done.6), kind=kLoop, calls=%fused_computation.2 | loop fusion | flops 875520 | bytes 1751040 | tf_op jit(solution)/shard_map/convert_element_type | solution.py:393
  90.3 0.0 collective-permute-start.9
  90.3 0.0 collective-permute-done.10
  90.3 0.0 copy-done.3
  90.3 0.1 add_convert_fusion
  90.4 1.3 %collective-permute-start.12 = (bf16[1368,128]{1,0:T(8,128)(2,1)S(1)}, bf16[1368,128]{1,0:T(8,128)(2,1)S(1)}, u32[]{:S(2)}, u32[]{:S(2)}) collective-permute-start(bf16[1368,128]{1,0:T(8,128)(2,1)S(1)} %add_convert_fusion), channel_id=1, source_target_pairs={{0,4},{4,0},{8,12},{12,8},{1,5},{5,1},{9,13},{13,9},{2,6},{6,2},{1... | collective-permute-start | bytes 1050632 | tf_op jit(solution)/shard_map/ppermute | solution.py:396
  91.7 0.0 all-gather.2.cloned.1.call-done.w_ref
  91.7 0.0 copy-start.2
  91.7 9.3 %messages.1 = bf16[128,3712]{1,0:T(8,128)(2,1)} custom-call(bf16[21888,128]{1,0:T(8,128)(2,1)} %all-gather.2.cloned.1.call-done.w_ref, bf16[256,3712]{1,0:T(8,128)(2,1)} %get-tuple-element.57.refs_1_.refs_0_, bf16[128,3712]{1,0:T(8,128)(2,1)} %get-tuple-element.58.refs_2_.refs_1_, bf16[16,240,256]{2,1,0:T(8,128)(2,1)} %get-tuple-element.80.refs_2_, ...), custom_call_target="tpu_custom_call" | custom-call | tf_op jit(solution)/shard_map/messages/pallas_call | solution.py:282
  101.0 7.0 %collective-permute-done.9 = bf16[1368,128]{1,0:T(8,128)(2,1)} collective-permute-done((bf16[1368,128]{1,0:T(8,128)(2,1)}, bf16[1368,128]{1,0:T(8,128)(2,1)}, u32[]{:S(2)}, u32[]{:S(2)}) %collective-permute-start.9) | collective-permute-done | bytes 350240 | tf_op jit(solution)/shard_map/ppermute | solution.py:396
  108.0 0.0 collective-permute-done.11
  108.0 0.0 collective-permute-done.12
  108.0 0.0 copy-done.2
  108.0 2.1 %add_multiply_fusion = f32[1368,128]{1,0:T(8,128)} fusion(bf16[1368,128]{1,0:T(8,128)(2,1)} %collective-permute-done.9, bf16[1368,128]{1,0:T(8,128)(2,1)S(1)} %collective-permute-done.12, f32[1368,128]{1,0:T(8,128)S(1)} %copy-done.2, bf16[1368,128]{1,0:T(8,128)(2,1)} %collective-permute-done.11), kind=kLoop, calls=%fused_computation | loop fusion | flops 1225728 | bytes 2451456 | tf_op jit(solution)/shard_map/mul | solution.py:412
Async XLA Ops:
  7.2 84.5 %all-gather.2.cloned.1.call-start = ((), (), s32[]{:S(2)}) async-start(), calls=%async_computation | async-start | bytes 5953536 | tf_op jit(solution)/shard_map/all_gather | solution.py:318
  11.0 13.1 %collective-permute-start = (bf16[32,3840]{1,0:T(8,128)(2,1)}, bf16[32,3840]{1,0:T(8,128)(2,1)S(1)}, u32[]{:S(2)}, u32[]{:S(2)}) collective-permute-start(bf16[32,3840]{1,0:T(8,128)(2,1)} %get-tuple-element.46), channel_id=1, source_target_pairs={{2,0},{3,1},{4,2},{5,3},{6,4},{7,5},{10,8},{11,9},{12,10},{13,11},... | collective-permute-start | bytes 737288 | tf_op jit(solution)/shard_map/ppermute | solution.py:313
  12.3 21.7 %collective-permute-start.1 = (bf16[32,3840]{1,0:T(8,128)(2,1)}, bf16[32,3840]{1,0:T(8,128)(2,1)S(1)}, u32[]{:S(2)}, u32[]{:S(2)}) collective-permute-start(bf16[32,3840]{1,0:T(8,128)(2,1)} %get-tuple-element.47), channel_id=1, source_target_pairs={{0,2},{1,3},{2,4},{3,5},{4,6},{5,7},{8,10},{9,11},{10,12},{11,13},... | collective-permute-start | bytes 737288 | tf_op jit(solution)/shard_map/ppermute | solution.py:313
  17.7 21.9 %collective-permute-start.2 = (bf16[32,3840]{1,0:T(8,128)(2,1)}, bf16[32,3840]{1,0:T(8,128)(2,1)S(1)}, u32[]{:S(2)}, u32[]{:S(2)}) collective-permute-start(bf16[32,3840]{1,0:T(8,128)(2,1)} %get-tuple-element.49), channel_id=1, source_target_pairs={{1,0},{2,1},{3,2},{4,3},{5,4},{6,5},{7,6},{9,8},{10,9},{11,10},{12... | collective-permute-start | bytes 737288 | tf_op jit(solution)/shard_map/ppermute | solution.py:313
  19.0 20.6 %collective-permute-start.3 = (bf16[32,3840]{1,0:T(8,128)(2,1)}, bf16[32,3840]{1,0:T(8,128)(2,1)S(1)}, u32[]{:S(2)}, u32[]{:S(2)}) collective-permute-start(bf16[32,3840]{1,0:T(8,128)(2,1)} %get-tuple-element.50), channel_id=1, source_target_pairs={{0,1},{1,2},{2,3},{3,4},{4,5},{5,6},{6,7},{8,9},{9,10},{10,11},{11... | collective-permute-start | bytes 737288 | tf_op jit(solution)/shard_map/ppermute | solution.py:313
  24.1 9.9 %copy-start.5 = (bf16[32,3840]{1,0:T(8,128)(2,1)}, bf16[32,3840]{1,0:T(8,128)(2,1)S(1)}, u32[]{:S(2)}) copy-start(bf16[32,3840]{1,0:T(8,128)(2,1)S(1)} %collective-permute-done.refs_1_) | copy-start | bytes 737284
  34.0 0.7 copy-start.6
  39.6 9.4 %collective-permute-start.4 = (bf16[256,3712]{1,0:T(8,128)(2,1)}, bf16[256,3712]{1,0:T(8,128)(2,1)}, u32[]{:S(2)}, u32[]{:S(2)}) collective-permute-start(bf16[256,3712]{1,0:T(8,128)(2,1)} %get-tuple-element.57.refs_1_.refs_0_), channel_id=1, source_target_pairs={{0,1},{1,0},{2,3},{3,2},{4,5},{5,4},{6,7},{7,6},{8,9},{9,8},{10,11... | collective-permute-start | bytes 5701640 | tf_op jit(solution)/shard_map/ppermute | solution.py:316
  39.6 0.7 copy-start.7
  40.3 0.7 copy-start.8
  44.8 4.2 %collective-permute-start.5 = (bf16[128,3712]{1,0:T(8,128)(2,1)}, bf16[128,3712]{1,0:T(8,128)(2,1)S(1)}, u32[]{:S(2)}, u32[]{:S(2)}) collective-permute-start(bf16[128,3712]{1,0:T(8,128)(2,1)} %get-tuple-element.58.refs_2_.refs_1_), channel_id=1, source_target_pairs={{0,1},{1,0},{2,3},{3,2},{4,5},{5,4},{6,7},{7,6},{8,9},{9,8},{10,11... | collective-permute-start | bytes 2850824 | tf_op jit(solution)/shard_map/ppermute | solution.py:316
  49.0 0.9 copy-start
  54.5 18.7 %copy-start.1 = (bf16[64,29,29]{0,2,1:T(8,128)(2,1)S(1)}, bf16[64,29,29]{0,2,1:T(8,128)(2,1)}, u32[]{:S(2)}) copy-start(bf16[64,29,29]{0,2,1:T(8,128)(2,1)} %param.11) | copy-start | bytes 322948
  54.5 16.4 %collective-permute-start.7 = (bf16[1368,128]{1,0:T(8,128)(2,1)}, bf16[1368,128]{1,0:T(8,128)(2,1)}, u32[]{:S(2)}, u32[]{:S(2)}) collective-permute-start(bf16[1368,128]{1,0:T(8,128)(2,1)} %first_terms.1), channel_id=1, source_target_pairs={{0,2},{2,0},{1,3},{3,1},{4,6},{6,4},{5,7},{7,5},{8,10},{10,8},{9,1... | collective-permute-start | bytes 1050632 | tf_op jit(solution)/shard_map/ppermute | solution.py:386
  65.7 22.8 %copy-start.4 = (f32[1368,128]{1,0:T(8,128)S(1)}, f32[1368,128]{1,0:T(8,128)}, u32[]{:S(2)}) copy-start(f32[1368,128]{1,0:T(8,128)} %get-tuple-element.73) | copy-start | bytes 2101252
  65.7 24.6 %copy-start.3 = (f32[1368,128]{1,0:T(8,128)S(1)}, f32[1368,128]{1,0:T(8,128)}, u32[]{:S(2)}) copy-start(f32[1368,128]{1,0:T(8,128)} %get-tuple-element.77) | copy-start | bytes 2101252
  65.7 14.4 %collective-permute-start.6 = (bf16[1368,128]{1,0:T(8,128)(2,1)}, bf16[1368,128]{1,0:T(8,128)(2,1)S(1)}, u32[]{:S(2)}, u32[]{:S(2)}) collective-permute-start(bf16[1368,128]{1,0:T(8,128)(2,1)} %get-tuple-element.74), channel_id=1, source_target_pairs={{0,2},{2,0},{1,3},{3,1},{4,6},{6,4},{5,7},{7,5},{8,10},{10,8},{9,1... | collective-permute-start | bytes 1050632 | tf_op jit(solution)/shard_map/ppermute | solution.py:386
  73.0 15.5 %collective-permute-start.8 = (bf16[1368,128]{1,0:T(8,128)(2,1)}, bf16[1368,128]{1,0:T(8,128)(2,1)}, u32[]{:S(2)}, u32[]{:S(2)}) collective-permute-start(bf16[1368,128]{1,0:T(8,128)(2,1)} %add_convert_fusion.2), channel_id=1, source_target_pairs={{0,4},{4,0},{8,12},{12,8},{1,5},{5,1},{9,13},{13,9},{2,6},{6,2},{1... | collective-permute-start | bytes 1050632 | tf_op jit(solution)/shard_map/ppermute | solution.py:396
  78.0 12.3 %collective-permute-start.10 = (bf16[1368,128]{1,0:T(8,128)(2,1)}, bf16[1368,128]{1,0:T(8,128)(2,1)S(1)}, u32[]{:S(2)}, u32[]{:S(2)}) collective-permute-start(bf16[1368,128]{1,0:T(8,128)(2,1)} %get-tuple-element.78), channel_id=1, source_target_pairs={{0,2},{2,0},{1,3},{3,1},{4,6},{6,4},{5,7},{7,5},{8,10},{10,8},{9,1... | collective-permute-start | bytes 1050632 | tf_op jit(solution)/shard_map/ppermute | solution.py:386
  78.2 29.8 %collective-permute-start.11 = (bf16[1368,128]{1,0:T(8,128)(2,1)}, bf16[1368,128]{1,0:T(8,128)(2,1)}, u32[]{:S(2)}, u32[]{:S(2)}) collective-permute-start(bf16[1368,128]{1,0:T(8,128)(2,1)} %get-tuple-element.86), channel_id=1, source_target_pairs={{0,2},{2,0},{1,3},{3,1},{4,6},{6,4},{5,7},{7,5},{8,10},{10,8},{9,1... | collective-permute-start | bytes 1050632 | tf_op jit(solution)/shard_map/ppermute | solution.py:386
  90.3 17.8 %collective-permute-start.9 = (bf16[1368,128]{1,0:T(8,128)(2,1)}, bf16[1368,128]{1,0:T(8,128)(2,1)}, u32[]{:S(2)}, u32[]{:S(2)}) collective-permute-start(bf16[1368,128]{1,0:T(8,128)(2,1)} %add_convert_fusion.1), channel_id=1, source_target_pairs={{0,8},{4,12},{8,0},{12,4},{1,9},{5,13},{9,1},{13,5},{2,10},{6,14},... | collective-permute-start | bytes 1050632 | tf_op jit(solution)/shard_map/ppermute | solution.py:396
  90.4 17.7 %collective-permute-start.12 = (bf16[1368,128]{1,0:T(8,128)(2,1)S(1)}, bf16[1368,128]{1,0:T(8,128)(2,1)S(1)}, u32[]{:S(2)}, u32[]{:S(2)}) collective-permute-start(bf16[1368,128]{1,0:T(8,128)(2,1)S(1)} %add_convert_fusion), channel_id=1, source_target_pairs={{0,4},{4,0},{8,12},{12,8},{1,5},{5,1},{9,13},{13,9},{2,6},{6,2},{1... | collective-permute-start | bytes 1050632 | tf_op jit(solution)/shard_map/ppermute | solution.py:396
  91.7 16.3 %copy-start.2 = (f32[1368,128]{1,0:T(8,128)S(1)}, f32[1368,128]{1,0:T(8,128)}, u32[]{:S(2)}) copy-start(f32[1368,128]{1,0:T(8,128)} %get-tuple-element.85) | copy-start | bytes 2101252
Sparse Core Ops, SparseCore 0:
  10.2 76.2 all-gather.1

commit v10 on v6

--- a/solution.py
+++ b/solution.py
@@ -142,6 +142,10 @@
         build(tabt_ref, refs[i][...], refs[2 + i], refs[4 + i])
 
 
+def leaving(n_z):
+    return sorted(range(n_z), key=lambda r: (r % 2 == 0, -r))
+
+
 def grad_kernel(n_z, n_x, me_ref, *refs):
     parts, outs, flat = refs[:4], refs[4:-1], refs[-1]
     chip, core = me_ref[0] // 2, me_ref[0] % 2
@@ -175,7 +179,7 @@
     rows = outs[0].shape[0]
     at_out = 0
     for o in list(range(1, n_x)) + [0]:
-        for r in reversed(range(n_z)):
+        for r in leaving(n_z):
             start = (((z ^ r) * n_x + (x + o) % n_x) * 2 + core) * rows
             if rows % 8 == 0:
                 start = pl.multiple_of(start, 8)
@@ -332,8 +336,8 @@
 
     n_send = n_z * (n_x - 1)
     blocks = call(
-        lambda *refs: grad_kernel(n_z, n_x, *refs), "weight_terms", 62,
-        [shape((rows, 128), BF16)] * n_send + [shape((rows, 128), F32)] * n_z,
+        lambda *refs: grad_kernel(n_z, n_x, *refs), "weight_terms", 63,
+        [shape((rows, 128), BF16)] * (n_send + n_z),
         both + [both_a_other, both_b_other],
         [pltpu.VMEM((rows * n_dp, 128), F32)],
         numbers=me.reshape(1),
@@ -348,8 +352,8 @@
     kept = blocks[n_send:]
     kept[0], mats = lax.optimization_barrier((kept[0], mats))
     sums = {}
-    for at, r in enumerate(reversed(range(n_z))):
-        total = kept[at]
+    for at, r in enumerate(leaving(n_z)):
+        total = kept[at].astype(F32)
         for o in range(1, n_x):
             got = lax.ppermute(
                 blocks[(o - 1) * n_z + at], "x", [(s, (s + o) % n_x) for s in range(n_x)]
@@ -358,10 +362,8 @@
         sums[r] = total
     for bit in [1 << i for i in range(n_z.bit_length() - 1)]:
         for r in reversed(range(bit, n_z, 2 * bit)):
-            term = sums[r].astype(BF16)
-            if (bit, r) == (1, 1):
-                last_term = term
-            got = lax.ppermute(term, "z", [(s, s ^ bit) for s in range(n_z)])
+            last_term = sums[r].astype(BF16)
+            got = lax.ppermute(last_term, "z", [(s, s ^ bit) for s in range(n_z)])
             if 2 * bit < n_z:
                 sums[r ^ bit] = sums[r ^ bit] + got.astype(F32)
     weights, _ = lax.optimization_barrier((weights, last_term))

time: 114 us -> 113 us (level)
  waiting for transfers between devices: 33.9 us -> 37.1 us
  starting transfers between devices: 21 us -> 19.2 us
    ppermute x2, waiting for transfers between devices: 2.49 us -> 3.82 us  [swap(): return lax.ppermute(block, 'core', [(0, 1), (1, 0)])]
  transfers between devices with their start and end apart: 14 -> 14, of which waited for: 8 -> 8; matrix products, arithmetic and copies ran while one was open for 5% -> 4% of each run, Pallas kernels for 27% -> 27%
where the time goes in v10:
time: 113 us; the launch traced here: 112 us
  waiting for transfers between devices  37.1 us (33%)
  Pallas kernels  33.5 us (30%)
  starting transfers between devices  19.2 us (17%)
  between operations  14.1 us (12%)
  local copies, waits for them, and re-layouts  5.21 us (5%)
  other arithmetic  3.32 us (3%)
    pallas_call x6, Pallas kernels, call(): pl.pallas_call(kernel, grid=(1,), out_shape=outs, in_specs=first + [whole...  33.5 us
    ppermute x3, waiting for transfers between devices, on_device(): got = lax.ppermute(last_term, 'z', [(s, s ^ bit) for s in range(n_z)])  13 us
    ppermute x4, starting transfers between devices, shift(): return lax.ppermute(block, ALL, route)  11.1 us
    ppermute x4, waiting for transfers between devices, shift(): return lax.ppermute(block, ALL, route)  9.88 us
    ppermute x4, waiting for transfers between devices, on_device(): lax.ppermute(blocks[(o - 1) * n_z + at], 'x', [(s, (s + o) % n_x) for s i...  9.64 us
    ppermute x4, starting transfers between devices, on_device(): lax.ppermute(blocks[(o - 1) * n_z + at], 'x', [(s, (s + o) % n_x) for s i...  4.16 us
    ppermute x2, waiting for transfers between devices, swap(): return lax.ppermute(block, 'core', [(0, 1), (1, 0)])  3.82 us
    ppermute x3, starting transfers between devices, on_device(): got = lax.ppermute(last_term, 'z', [(s, s ^ bit) for s in range(n_z)])  3.35 us
  transfers between devices with their start and end apart: 14, of which 8 were waited for; matrix products, arithmetic and copies ran while one was open for 4% of the time, Pallas kernels for 27%

profile of v10, /device:TPU:0, one launch (start us, length us, event | category | flops | bytes accessed | tf_op | source)
XLA Modules:
  0.0 112.4 jit_solution(9427169199754626353)
XLA Ops:
  7.2 0.0 all-gather.2.cloned.1.call-start
  7.2 0.7 all-gather.2.cloned.1.call-update
  7.9 3.1 %send.1 = (bf16[64,3840]{1,0:T(8,128)(2,1)}, bf16[32,3840]{1,0:T(8,128)(2,1)}, bf16[32,3840]{1,0:T(8,128)(2,1)}, bf16[32,3840]{1,0:T(8,128)(2,1)}, bf16[32,3840]{1,0:T(8,128)(2,1)}) custom-call(s32[1]{0:T(128)} %bitcast.me_ref.refs_0_, s32[1,128]{1,0:T(1,128)} %bitcast.14, s32[1,128]{1,0:T(1,128)} %bitcast.15, s32[1,128]{1,0:T(1,128)} %bitcast.16, ...), custom_call_target="tpu_custom_call" | custom-call | tf_op jit(solution)/shard_map/send/pallas_call | solution.py:261
  11.0 1.3 %collective-permute-start = (bf16[32,3840]{1,0:T(8,128)(2,1)}, bf16[32,3840]{1,0:T(8,128)(2,1)S(1)}, u32[]{:S(2)}, u32[]{:S(2)}) collective-permute-start(bf16[32,3840]{1,0:T(8,128)(2,1)} %get-tuple-element.43), channel_id=1, source_target_pairs={{2,0},{3,1},{4,2},{5,3},{6,4},{7,5},{10,8},{11,9},{12,10},{13,11},... | collective-permute-start | bytes 737288 | tf_op jit(solution)/shard_map/ppermute | solution.py:292
  12.3 5.5 %collective-permute-start.1 = (bf16[32,3840]{1,0:T(8,128)(2,1)}, bf16[32,3840]{1,0:T(8,128)(2,1)S(1)}, u32[]{:S(2)}, u32[]{:S(2)}) collective-permute-start(bf16[32,3840]{1,0:T(8,128)(2,1)} %get-tuple-element.44), channel_id=1, source_target_pairs={{0,2},{1,3},{2,4},{3,5},{4,6},{5,7},{8,10},{9,11},{10,12},{11,13},... | collective-permute-start | bytes 737288 | tf_op jit(solution)/shard_map/ppermute | solution.py:292
  17.7 1.3 %collective-permute-start.2 = (bf16[32,3840]{1,0:T(8,128)(2,1)}, bf16[32,3840]{1,0:T(8,128)(2,1)S(1)}, u32[]{:S(2)}, u32[]{:S(2)}) collective-permute-start(bf16[32,3840]{1,0:T(8,128)(2,1)} %get-tuple-element.46), channel_id=1, source_target_pairs={{1,0},{2,1},{3,2},{4,3},{5,4},{6,5},{7,6},{9,8},{10,9},{11,10},{12... | collective-permute-start | bytes 737288 | tf_op jit(solution)/shard_map/ppermute | solution.py:292
  19.0 3.0 %collective-permute-start.3 = (bf16[32,3840]{1,0:T(8,128)(2,1)}, bf16[32,3840]{1,0:T(8,128)(2,1)S(1)}, u32[]{:S(2)}, u32[]{:S(2)}) collective-permute-start(bf16[32,3840]{1,0:T(8,128)(2,1)} %get-tuple-element.47), channel_id=1, source_target_pairs={{0,1},{1,2},{2,3},{3,4},{4,5},{5,6},{6,7},{8,9},{9,10},{10,11},{11... | collective-permute-start | bytes 737288 | tf_op jit(solution)/shard_map/ppermute | solution.py:292
  22.1 2.0 %copy.10 = bf16[29,64,29]{2,1,0:T(8,128)(2,1)} copy(bf16[29,64,29]{1,2,0:T(8,128)(2,1)} %bitcast.12) | data formatting | bytes 215296 | tf_op jit(solution)/shard_map/transpose | solution.py:308
  24.1 0.0 collective-permute-done.refs_1_
  24.1 0.0 copy-start.4
  24.1 9.9 %collective-permute-done.1.refs_2_ = bf16[32,3840]{1,0:T(8,128)(2,1)S(1)} collective-permute-done((bf16[32,3840]{1,0:T(8,128)(2,1)}, bf16[32,3840]{1,0:T(8,128)(2,1)S(1)}, u32[]{:S(2)}, u32[]{:S(2)}) %collective-permute-start.1) | collective-permute-done | bytes 245792 | tf_op jit(solution)/shard_map/ppermute | solution.py:292
  34.0 0.0 copy-start.5
  34.0 0.0 copy-done.4
  34.0 0.7 copy-done.5
  34.7 5.0 %rotate_first.1 = (bf16[256,3712]{1,0:T(8,128)(2,1)}, bf16[128,128]{1,0:T(8,128)(2,1)}, bf16[128,64]{1,0:T(8,128)(2,1)}) custom-call(bf16[64,3840]{1,0:T(8,128)(2,1)} %get-tuple-element.42.refs_0_, bf16[32,3840]{1,0:T(8,128)(2,1)} %copy-done.4, bf16[32,3840]{1,0:T(8,128)(2,1)} %copy-done.5, bf16[1856,29]{1,0:T(8,128)(2,1)} %bitcast.9, bf16[128,3712]{1,0:T(8,128)(2,1)} %refs_3_.1), custom_call_target="tpu_custom_call" | custom-call | tf_op jit(solution)/shard_map/rotate_first/pallas_call | solution.py:261
  39.6 0.0 collective-permute-start.4
  39.6 0.0 collective-permute-done.2.refs_0_
  39.6 0.0 copy-start.7
  39.7 0.0 collective-permute-done.3.refs_1_
  39.7 0.7 copy-done.7
  40.3 0.0 copy-start.8
  40.3 0.7 copy-done.8
  41.0 3.8 %rotate_last.1 = (bf16[128,3712]{1,0:T(8,128)(2,1)}, bf16[64,128]{1,0:T(8,128)(2,1)}, bf16[64,64]{1,0:T(8,128)(2,1)}) custom-call(bf16[32,3840]{1,0:T(8,128)(2,1)} %copy-done.7, bf16[32,3840]{1,0:T(8,128)(2,1)} %copy-done.8, bf16[1856,29]{1,0:T(8,128)(2,1)} %bitcast.10, bf16[128,3712]{1,0:T(8,128)(2,1)} %refs_3_.1), custom_call_target="tpu_custom_call" | custom-call | flops 10000000000 | bytes 100000000 | tf_op jit(solution)/shard_map/rotate_last/pallas_call | solution.py:261
  44.9 0.0 copy-start
  44.9 0.5 collective-permute-start.5
  45.4 3.8 %collective-permute-done.5.refs_4_ = bf16[128,3712]{1,0:T(8,128)(2,1)} collective-permute-done((bf16[128,3712]{1,0:T(8,128)(2,1)}, bf16[128,3712]{1,0:T(8,128)(2,1)}, u32[]{:S(2)}, u32[]{:S(2)}) %collective-permute-start.5) | collective-permute-done | bytes 950304 | tf_op jit(solution)/shard_map/ppermute | solution.py:295
  49.2 0.0 collective-permute-done.4.refs_3_
  49.2 8.7 %weight_terms.1 = (bf16[1368,128]{1,0:T(8,128)(2,1)}, bf16[1368,128]{1,0:T(8,128)(2,1)}, bf16[1368,128]{1,0:T(8,128)(2,1)}, bf16[1368,128]{1,0:T(8,128)(2,1)}, b...) custom-call(s32[1]{0:T(128)} %bitcast.me_ref.refs_0_, ...), custom_call_target="tpu_custom_call" | custom-call | tf_op jit(solution)/shard_map/weight_terms/pallas_call | solution.py:261
  57.9 0.0 copy-start.6
  57.9 0.0 copy-start.1
  57.9 0.0 copy-start.2
  57.9 2.1 %collective-permute-start.7 = (bf16[1368,128]{1,0:T(8,128)(2,1)}, bf16[1368,128]{1,0:T(8,128)(2,1)S(1)}, u32[]{:S(2)}, u32[]{:S(2)}) collective-permute-start(bf16[1368,128]{1,0:T(8,128)(2,1)} %get-tuple-element.70), channel_id=1, source_target_pairs={{0,2},{2,0},{1,3},{3,1},{4,6},{6,4},{5,7},{7,5},{8,10},{10,8},{9,1... | collective-permute-start | bytes 1050632 | tf_op jit(solution)/shard_map/ppermute | solution.py:358
  60.0 0.0 copy-done
  60.0 1.1 %copy.11 = bf16[29,64,29]{2,1,0:T(8,128)(2,1)} copy(bf16[29,64,29]{1,0,2:T(8,128)(2,1)S(1)} %bitcast.13) | data formatting | bytes 215296 | tf_op jit(solution)/shard_map/transpose | solution.py:309
  61.1 3.7 %back.1 = (bf16[16,240,256]{2,1,0:T(8,128)(2,1)}, bf16[8,240,256]{2,1,0:T(8,128)(2,1)}) custom-call(bf16[1856,29]{1,0:T(8,128)(2,1)} %bitcast.11, bf16[128,64]{1,0:T(8,128)(2,1)} %get-tuple-element.65.refs_0_, bf16[64,64]{1,0:T(8,128)(2,1)} %get-tuple-element.66.refs_1_), custom_call_target="tpu_custom_call" | custom-call | tf_op jit(solution)/shard_map/back/pallas_call | solution.py:261
  64.8 0.0 collective-permute-start.6
  64.8 6.0 %collective-permute-done.7 = bf16[1368,128]{1,0:T(8,128)(2,1)S(1)} collective-permute-done((bf16[1368,128]{1,0:T(8,128)(2,1)}, bf16[1368,128]{1,0:T(8,128)(2,1)S(1)}, u32[]{:S(2)}, u32[]{:S(2)}) %collective-permute-start.7) | collective-permute-done | bytes 350240 | tf_op jit(solution)/shard_map/ppermute | solution.py:358
  70.9 1.1 add_convert_fusion.2
  71.9 1.6 %collective-permute-start.8 = (bf16[1368,128]{1,0:T(8,128)(2,1)S(1)}, bf16[1368,128]{1,0:T(8,128)(2,1)S(1)}, u32[]{:S(2)}, u32[]{:S(2)}) collective-permute-start(bf16[1368,128]{1,0:T(8,128)(2,1)S(1)} %add_convert_fusion.2), channel_id=1, source_target_pairs={{0,4},{4,0},{8,12},{12,8},{1,5},{5,1},{9,13},{13,9},{2,6},{6,2},{1... | collective-permute-start | bytes 1050632 | tf_op jit(solution)/shard_map/ppermute | solution.py:366
  73.6 0.0 copy-done.6
  73.6 0.5 collective-permute-start.11
  74.1 1.5 %collective-permute-start.10 = (bf16[1368,128]{1,0:T(8,128)(2,1)}, bf16[1368,128]{1,0:T(8,128)(2,1)S(1)}, u32[]{:S(2)}, u32[]{:S(2)}) collective-permute-start(bf16[1368,128]{1,0:T(8,128)(2,1)} %get-tuple-element.78), channel_id=1, source_target_pairs={{0,2},{2,0},{1,3},{3,1},{4,6},{6,4},{5,7},{7,5},{8,10},{10,8},{9,1... | collective-permute-start | bytes 1050632 | tf_op jit(solution)/shard_map/ppermute | solution.py:358
  75.6 2.8 %collective-permute-done.6 = bf16[1368,128]{1,0:T(8,128)(2,1)S(1)} collective-permute-done((bf16[1368,128]{1,0:T(8,128)(2,1)}, bf16[1368,128]{1,0:T(8,128)(2,1)S(1)}, u32[]{:S(2)}, u32[]{:S(2)}) %collective-permute-start.6) | collective-permute-done | bytes 350240 | tf_op jit(solution)/shard_map/ppermute | solution.py:358
  78.4 6.4 %collective-permute-done.8 = bf16[1368,128]{1,0:T(8,128)(2,1)S(1)} collective-permute-done((bf16[1368,128]{1,0:T(8,128)(2,1)S(1)}, bf16[1368,128]{1,0:T(8,128)(2,1)S(1)}, u32[]{:S(2)}, u32[]{:S(2)}) %collective-permute-start.8) | collective-permute-done | bytes 350240 | tf_op jit(solution)/shard_map/ppermute | solution.py:366
  84.8 0.0 copy-done.1
  84.8 0.1 add_convert_fusion.1
  84.9 0.1 collective-permute-start.9
  85.0 0.8 collective-permute-done.11
  85.9 0.0 copy-done.2
  85.9 0.1 add_convert_fusion
  86.0 1.6 %collective-permute-start.12 = (bf16[1368,128]{1,0:T(8,128)(2,1)S(1)}, bf16[1368,128]{1,0:T(8,128)(2,1)S(1)}, u32[]{:S(2)}, u32[]{:S(2)}) collective-permute-start(bf16[1368,128]{1,0:T(8,128)(2,1)S(1)} %add_convert_fusion), channel_id=1, source_target_pairs={{0,4},{4,0},{8,12},{12,8},{1,5},{5,1},{9,13},{13,9},{2,6},{6,2},{1... | collective-permute-start | bytes 1050632 | tf_op jit(solution)/shard_map/ppermute | solution.py:366
  87.6 0.0 all-gather.2.cloned.1.call-done.w_ref
  87.6 0.0 copy-start.3
  87.6 9.3 %messages.1 = bf16[128,3712]{1,0:T(8,128)(2,1)} custom-call(bf16[21888,128]{1,0:T(8,128)(2,1)} %all-gather.2.cloned.1.call-done.w_ref, bf16[256,3712]{1,0:T(8,128)(2,1)} %get-tuple-element.52.refs_1_.refs_0_, bf16[128,3712]{1,0:T(8,128)(2,1)} %get-tuple-element.53.refs_2_.refs_1_, bf16[16,240,256]{2,1,0:T(8,128)(2,1)} %get-tuple-element.72.refs_2_, ...), custom_call_target="tpu_custom_call" | custom-call | tf_op jit(solution)/shard_map/messages/pallas_call | solution.py:261
  96.9 5.8 %collective-permute-done.9 = bf16[1368,128]{1,0:T(8,128)(2,1)} collective-permute-done((bf16[1368,128]{1,0:T(8,128)(2,1)S(1)}, bf16[1368,128]{1,0:T(8,128)(2,1)}, u32[]{:S(2)}, u32[]{:S(2)}) %collective-permute-start.9) | collective-permute-done | bytes 350240 | tf_op jit(solution)/shard_map/ppermute | solution.py:366
  102.7 0.0 collective-permute-done.10
  102.7 0.8 collective-permute-done.12
  103.5 0.0 copy-done.3
  103.5 2.0 %add_multiply_fusion = f32[1368,128]{1,0:T(8,128)} fusion(bf16[1368,128]{1,0:T(8,128)(2,1)} %collective-permute-done.9, bf16[1368,128]{1,0:T(8,128)(2,1)S(1)} %collective-permute-done.12, bf16[1368,128]{1,0:T(8,128)(2,1)S(1)} %collective-permute-done.10, bf16[1368,128]{1,0:T(8,128)(2,1)S(1)} %copy-done.3), kind=kLoop, calls=%fused_computation | loop fusion | flops 1400832 | bytes 2101248 | tf_op jit(solution)/shard_map/mul | solution.py:382
Async XLA Ops:
  7.2 80.4 %all-gather.2.cloned.1.call-start = ((), (), s32[]{:S(2)}) async-start(), calls=%async_computation | async-start | bytes 5953536 | tf_op jit(solution)/shard_map/all_gather | solution.py:297
  11.0 13.1 %collective-permute-start = (bf16[32,3840]{1,0:T(8,128)(2,1)}, bf16[32,3840]{1,0:T(8,128)(2,1)S(1)}, u32[]{:S(2)}, u32[]{:S(2)}) collective-permute-start(bf16[32,3840]{1,0:T(8,128)(2,1)} %get-tuple-element.43), channel_id=1, source_target_pairs={{2,0},{3,1},{4,2},{5,3},{6,4},{7,5},{10,8},{11,9},{12,10},{13,11},... | collective-permute-start | bytes 737288 | tf_op jit(solution)/shard_map/ppermute | solution.py:292
  12.3 21.7 %collective-permute-start.1 = (bf16[32,3840]{1,0:T(8,128)(2,1)}, bf16[32,3840]{1,0:T(8,128)(2,1)S(1)}, u32[]{:S(2)}, u32[]{:S(2)}) collective-permute-start(bf16[32,3840]{1,0:T(8,128)(2,1)} %get-tuple-element.44), channel_id=1, source_target_pairs={{0,2},{1,3},{2,4},{3,5},{4,6},{5,7},{8,10},{9,11},{10,12},{11,13},... | collective-permute-start | bytes 737288 | tf_op jit(solution)/shard_map/ppermute | solution.py:292
  17.7 21.9 %collective-permute-start.2 = (bf16[32,3840]{1,0:T(8,128)(2,1)}, bf16[32,3840]{1,0:T(8,128)(2,1)S(1)}, u32[]{:S(2)}, u32[]{:S(2)}) collective-permute-start(bf16[32,3840]{1,0:T(8,128)(2,1)} %get-tuple-element.46), channel_id=1, source_target_pairs={{1,0},{2,1},{3,2},{4,3},{5,4},{6,5},{7,6},{9,8},{10,9},{11,10},{12... | collective-permute-start | bytes 737288 | tf_op jit(solution)/shard_map/ppermute | solution.py:292
  19.0 20.6 %collective-permute-start.3 = (bf16[32,3840]{1,0:T(8,128)(2,1)}, bf16[32,3840]{1,0:T(8,128)(2,1)S(1)}, u32[]{:S(2)}, u32[]{:S(2)}) collective-permute-start(bf16[32,3840]{1,0:T(8,128)(2,1)} %get-tuple-element.47), channel_id=1, source_target_pairs={{0,1},{1,2},{2,3},{3,4},{4,5},{5,6},{6,7},{8,9},{9,10},{10,11},{11... | collective-permute-start | bytes 737288 | tf_op jit(solution)/shard_map/ppermute | solution.py:292
  24.1 9.9 %copy-start.4 = (bf16[32,3840]{1,0:T(8,128)(2,1)}, bf16[32,3840]{1,0:T(8,128)(2,1)S(1)}, u32[]{:S(2)}) copy-start(bf16[32,3840]{1,0:T(8,128)(2,1)S(1)} %collective-permute-done.refs_1_) | copy-start | bytes 737284
  34.0 0.7 copy-start.5
  39.6 9.5 %collective-permute-start.4 = (bf16[256,3712]{1,0:T(8,128)(2,1)}, bf16[256,3712]{1,0:T(8,128)(2,1)}, u32[]{:S(2)}, u32[]{:S(2)}) collective-permute-start(bf16[256,3712]{1,0:T(8,128)(2,1)} %get-tuple-element.52.refs_1_.refs_0_), channel_id=1, source_target_pairs={{0,1},{1,0},{2,3},{3,2},{4,5},{5,4},{6,7},{7,6},{8,9},{9,8},{10,11... | collective-permute-start | bytes 5701640 | tf_op jit(solution)/shard_map/ppermute | solution.py:295
  39.6 0.7 copy-start.7
  40.3 0.7 copy-start.8
  44.9 15.1 %copy-start = (bf16[64,29,29]{0,2,1:T(8,128)(2,1)S(1)}, bf16[64,29,29]{0,2,1:T(8,128)(2,1)}, u32[]{:S(2)}) copy-start(bf16[64,29,29]{0,2,1:T(8,128)(2,1)} %param.11) | copy-start | bytes 322948
  44.9 4.3 %collective-permute-start.5 = (bf16[128,3712]{1,0:T(8,128)(2,1)}, bf16[128,3712]{1,0:T(8,128)(2,1)}, u32[]{:S(2)}, u32[]{:S(2)}) collective-permute-start(bf16[128,3712]{1,0:T(8,128)(2,1)} %get-tuple-element.53.refs_2_.refs_1_), channel_id=1, source_target_pairs={{0,1},{1,0},{2,3},{3,2},{4,5},{5,4},{6,7},{7,6},{8,9},{9,8},{10,11... | collective-permute-start | bytes 2850824 | tf_op jit(solution)/shard_map/ppermute | solution.py:295
  57.9 15.7 %copy-start.6 = (bf16[1368,128]{1,0:T(8,128)(2,1)S(1)}, bf16[1368,128]{1,0:T(8,128)(2,1)}, u32[]{:S(2)}) copy-start(bf16[1368,128]{1,0:T(8,128)(2,1)} %get-tuple-element.80) | copy-start | bytes 1050628
  57.9 26.9 %copy-start.1 = (bf16[1368,128]{1,0:T(8,128)(2,1)S(1)}, bf16[1368,128]{1,0:T(8,128)(2,1)}, u32[]{:S(2)}) copy-start(bf16[1368,128]{1,0:T(8,128)(2,1)} %get-tuple-element.62) | copy-start | bytes 1050628
  57.9 28.0 %copy-start.2 = (bf16[1368,128]{1,0:T(8,128)(2,1)S(1)}, bf16[1368,128]{1,0:T(8,128)(2,1)}, u32[]{:S(2)}) copy-start(bf16[1368,128]{1,0:T(8,128)(2,1)} %get-tuple-element.79) | copy-start | bytes 1050628
  57.9 13.0 %collective-permute-start.7 = (bf16[1368,128]{1,0:T(8,128)(2,1)}, bf16[1368,128]{1,0:T(8,128)(2,1)S(1)}, u32[]{:S(2)}, u32[]{:S(2)}) collective-permute-start(bf16[1368,128]{1,0:T(8,128)(2,1)} %get-tuple-element.70), channel_id=1, source_target_pairs={{0,2},{2,0},{1,3},{3,1},{4,6},{6,4},{5,7},{7,5},{8,10},{10,8},{9,1... | collective-permute-start | bytes 1050632 | tf_op jit(solution)/shard_map/ppermute | solution.py:358
  64.8 13.6 %collective-permute-start.6 = (bf16[1368,128]{1,0:T(8,128)(2,1)}, bf16[1368,128]{1,0:T(8,128)(2,1)S(1)}, u32[]{:S(2)}, u32[]{:S(2)}) collective-permute-start(bf16[1368,128]{1,0:T(8,128)(2,1)} %get-tuple-element.63), channel_id=1, source_target_pairs={{0,2},{2,0},{1,3},{3,1},{4,6},{6,4},{5,7},{7,5},{8,10},{10,8},{9,1... | collective-permute-start | bytes 1050632 | tf_op jit(solution)/shard_map/ppermute | solution.py:358
  71.9 12.9 %collective-permute-start.8 = (bf16[1368,128]{1,0:T(8,128)(2,1)S(1)}, bf16[1368,128]{1,0:T(8,128)(2,1)S(1)}, u32[]{:S(2)}, u32[]{:S(2)}) collective-permute-start(bf16[1368,128]{1,0:T(8,128)(2,1)S(1)} %add_convert_fusion.2), channel_id=1, source_target_pairs={{0,4},{4,0},{8,12},{12,8},{1,5},{5,1},{9,13},{13,9},{2,6},{6,2},{1... | collective-permute-start | bytes 1050632 | tf_op jit(solution)/shard_map/ppermute | solution.py:366
  73.6 12.3 %collective-permute-start.11 = (bf16[1368,128]{1,0:T(8,128)(2,1)S(1)}, bf16[1368,128]{1,0:T(8,128)(2,1)S(1)}, u32[]{:S(2)}, u32[]{:S(2)}) collective-permute-start(bf16[1368,128]{1,0:T(8,128)(2,1)S(1)} %copy-done.6), channel_id=1, source_target_pairs={{0,2},{2,0},{1,3},{3,1},{4,6},{6,4},{5,7},{7,5},{8,10},{10,8},{9,1... | collective-permute-start | bytes 1050632 | tf_op jit(solution)/shard_map/ppermute | solution.py:358
  74.1 28.6 %collective-permute-start.10 = (bf16[1368,128]{1,0:T(8,128)(2,1)}, bf16[1368,128]{1,0:T(8,128)(2,1)S(1)}, u32[]{:S(2)}, u32[]{:S(2)}) collective-permute-start(bf16[1368,128]{1,0:T(8,128)(2,1)} %get-tuple-element.78), channel_id=1, source_target_pairs={{0,2},{2,0},{1,3},{3,1},{4,6},{6,4},{5,7},{7,5},{8,10},{10,8},{9,1... | collective-permute-start | bytes 1050632 | tf_op jit(solution)/shard_map/ppermute | solution.py:358
  84.9 17.8 %collective-permute-start.9 = (bf16[1368,128]{1,0:T(8,128)(2,1)S(1)}, bf16[1368,128]{1,0:T(8,128)(2,1)}, u32[]{:S(2)}, u32[]{:S(2)}) collective-permute-start(bf16[1368,128]{1,0:T(8,128)(2,1)S(1)} %add_convert_fusion.1), channel_id=1, source_target_pairs={{0,8},{4,12},{8,0},{12,4},{1,9},{5,13},{9,1},{13,5},{2,10},{6,14},... | collective-permute-start | bytes 1050632 | tf_op jit(solution)/shard_map/ppermute | solution.py:366
  86.0 17.6 %collective-permute-start.12 = (bf16[1368,128]{1,0:T(8,128)(2,1)S(1)}, bf16[1368,128]{1,0:T(8,128)(2,1)S(1)}, u32[]{:S(2)}, u32[]{:S(2)}) collective-permute-start(bf16[1368,128]{1,0:T(8,128)(2,1)S(1)} %add_convert_fusion), channel_id=1, source_target_pairs={{0,4},{4,0},{8,12},{12,8},{1,5},{5,1},{9,13},{13,9},{2,6},{6,2},{1... | collective-permute-start | bytes 1050632 | tf_op jit(solution)/shard_map/ppermute | solution.py:366
  87.6 15.9 %copy-start.3 = (bf16[1368,128]{1,0:T(8,128)(2,1)S(1)}, bf16[1368,128]{1,0:T(8,128)(2,1)}, u32[]{:S(2)}) copy-start(bf16[1368,128]{1,0:T(8,128)(2,1)} %get-tuple-element.77) | copy-start | bytes 1050628
Sparse Core Ops, SparseCore 0:
  10.2 71.4 all-gather.1
